TPU v7x, 256 devices: a whole 4x4x8 slice. The times are simulated.
256 devices in a mesh: pipe: 4 (over x), expert: 16 (over z, core), dp: 4 (over y).
Axes of the slice: x: 4, y: 4, z: 8, core: 2. Of those that a mesh axis runs over, the one named last changes fastest.
Arguments:
- seed_grads: bfloat16 [2, 4096, 3584], P(None, ('expert', 'dp')), may hold values from -6 to 6
- expert_routes: int32 [2, 4, 4096, 2], P(None, 'pipe', ('expert', 'dp')), may hold values from 0 to 15, all different within a row; in each aligned block of 64 rows (0 to 63, 64 to 127, ..., all dimensions but the last counted through in order) at most 9 rows name the same one
- route_weights: float32 [2, 4, 4096, 2], P(None, 'pipe', ('expert', 'dp')), may hold values from 0.1 to 1
- saved_gate: bfloat16 [2, 4, 4, 16, 144, 1024], P(None, 'pipe', 'dp', 'expert'), may hold values from -6 to 6
- saved_up: bfloat16 [2, 4, 4, 16, 144, 1024], P(None, 'pipe', 'dp', 'expert'), may hold values from -6 to 6
- w_gate: bfloat16 [4, 16, 3584, 1024], P('pipe', 'expert', 'dp'), may hold values from -0.09375 to 0.09375
- w_up: bfloat16 [4, 16, 3584, 1024], P('pipe', 'expert', 'dp'), may hold values from -0.09375 to 0.09375
- w_down: bfloat16 [4, 16, 1024, 3584], P('pipe', 'expert', 'dp'), may hold values from -0.1875 to 0.1875
Outputs:
- input_grads: bfloat16 [2, 4, 4096, 3584], P(None, 'pipe', ('expert', 'dp'))
- down_grads: bfloat16 [4, 16, 1024, 3584], P('pipe', 'expert', 'dp')
Inputs may be any that keep to these rules, and one draw needn't show every extreme that they name: `expert_routes`: each row names 2 different experts; among the 64 rows of one device no expert is named more than 9 times, and in every draw some device names some expert exactly 9 times.
All inputs are finite; a program needn't handle non-finite values.
Results may differ from a plain program's by a relative error of at most 0.015.
Values may be sent and summed in bfloat16 or wider, within the bound.
No kernel may reach another device: no remote copies, remote signals or barrier semaphores. Data moves between devices by JAX's collectives and lax.ppermute only.
A program may use at most 320 MiB of HBM per device.

v0:
```python
import jax
import jax.numpy as jnp
from jax import lax
from jax.sharding import PartitionSpec as P


def from_behind(value, axis, steps):
    count = lax.axis_size(axis)
    initial, last = (max(0, -steps), min(count, count - steps))
    return lax.ppermute(value, axis, [(source, source + steps) for source in range(initial, last)])


def slot_targets(routes_sel, groups, capacity):
    flattened = routes_sel.reshape(-1)
    experts = jnp.arange(groups, dtype=jnp.int32)
    onehot = (flattened[:, None] == experts[None, :]).astype(jnp.int32)
    rank_in = jnp.sum((jnp.cumsum(onehot, axis=0) - onehot) * onehot, axis=1)
    return flattened * capacity + rank_in


def expert_pass(received, gate_saved, up_saved, gate_full, up_full, down_full):
    contract = (((1,), (1,)), ((), ()))
    gate_pre = gate_saved.astype(jnp.float32)
    up_pre = up_saved.astype(jnp.float32)
    d_hidden = lax.dot_general(received, down_full, contract, preferred_element_type=jnp.float32)
    sigmoid_gate = jax.nn.sigmoid(gate_pre)
    activated = gate_pre * sigmoid_gate
    hidden = (activated * up_pre).astype(jnp.bfloat16)
    d_up = (d_hidden * activated).astype(jnp.bfloat16)
    d_gate = (d_hidden * up_pre * sigmoid_gate * (1.0 + gate_pre * (1.0 - sigmoid_gate))).astype(
        jnp.bfloat16
    )
    d_input = lax.dot_general(d_gate, gate_full, contract, preferred_element_type=jnp.float32)
    d_input = d_input + lax.dot_general(d_up, up_full, contract, preferred_element_type=jnp.float32)
    return (d_input.astype(jnp.bfloat16), hidden)


def per_device(
    seed_grads, expert_routes, route_weights, saved_gate, saved_up, w_gate, w_up, w_down
):
    sections = lax.axis_size("pipe")
    section_at = lax.axis_index("pipe")
    groups = lax.axis_size("expert")
    slots = saved_gate.shape[4]
    capacity = slots // groups
    width = seed_grads.shape[2]
    token_rows = seed_grads.shape[1]
    top_count = expert_routes.shape[3]
    gate_full, up_full, down_full = (
        lax.all_gather(w_gate[0, 0], "dp", axis=0, tiled=True),
        lax.all_gather(w_up[0, 0], "dp", axis=0, tiled=True),
        lax.all_gather(w_down[0, 0], "dp", axis=0, tiled=True),
    )
    hidden_units = gate_full.shape[1]
    contract_rows = (((0,), (0,)), ((), ()))

    def run_held(received, gate_saved, up_saved):
        return expert_pass(received, gate_saved, up_saved, gate_full, up_full, down_full)

    def skip_held(received, gate_saved, up_saved):
        return (
            jnp.zeros((slots, width), jnp.bfloat16),
            jnp.zeros((slots, hidden_units), jnp.bfloat16),
        )

    grad_down = seed_grads[0]
    grad_up = seed_grads[1]
    out_down = jnp.zeros_like(grad_down)
    out_up = jnp.zeros_like(grad_up)
    held_down_hidden = jnp.zeros((slots, hidden_units), jnp.bfloat16)
    held_up_hidden = jnp.zeros((slots, hidden_units), jnp.bfloat16)
    held_down_rows = jnp.zeros((slots, width), jnp.bfloat16)
    held_up_rows = jnp.zeros((slots, width), jnp.bfloat16)
    for step in range(sections):
        going_up = section_at == step
        going_down = section_at == sections - 1 - step
        working = jnp.logical_or(going_up, going_down)
        current = jnp.where(going_up, grad_up, grad_down)
        routes_sel = jnp.where(going_up, expert_routes[1, 0], expert_routes[0, 0])
        weights_sel = jnp.where(going_up, route_weights[1, 0], route_weights[0, 0])
        gate_saved = jnp.where(going_up, saved_gate[1, 0, 0, 0], saved_gate[0, 0, 0, 0])
        up_saved = jnp.where(going_up, saved_up[1, 0, 0, 0], saved_up[0, 0, 0, 0])
        targets = slot_targets(routes_sel, groups, capacity)
        scaled = (weights_sel[:, :, None] * current[:, None, :].astype(jnp.float32)).astype(
            jnp.bfloat16
        )
        outgoing = (
            jnp.zeros((slots, width), jnp.bfloat16).at[targets].set(scaled.reshape(-1, width))
        )
        received = lax.all_to_all(
            outgoing.reshape(groups, capacity, width),
            "expert",
            split_axis=0,
            concat_axis=0,
            tiled=True,
        ).reshape(slots, width)
        d_input, hidden = lax.cond(working, run_held, skip_held, received, gate_saved, up_saved)
        held_down_hidden = jnp.where(going_down, hidden, held_down_hidden)
        held_down_rows = jnp.where(going_down, received, held_down_rows)
        held_up_hidden = jnp.where(going_up, hidden, held_up_hidden)
        held_up_rows = jnp.where(going_up, received, held_up_rows)
        returned = lax.all_to_all(
            d_input.reshape(groups, capacity, width),
            "expert",
            split_axis=0,
            concat_axis=0,
            tiled=True,
        ).reshape(slots, width)
        gathered = jnp.sum(
            returned[targets].reshape(token_rows, top_count, width).astype(jnp.float32), axis=1
        )
        result = (current.astype(jnp.float32) + gathered).astype(jnp.bfloat16)
        out_down = jnp.where(going_down, result, out_down)
        out_up = jnp.where(going_up, result, out_up)
        if step + 1 < sections:
            grad_down = from_behind(result, "pipe", -1)
            grad_up = from_behind(result, "pipe", 1)
    weight_sum = lax.dot_general(
        held_down_hidden, held_down_rows, contract_rows, preferred_element_type=jnp.float32
    )
    weight_sum = weight_sum + lax.dot_general(
        held_up_hidden, held_up_rows, contract_rows, preferred_element_type=jnp.float32
    )
    shares = lax.psum_scatter(
        weight_sum.astype(jnp.bfloat16), "dp", scatter_dimension=0, tiled=True
    )
    down_grads = shares[None, None]
    input_grads = jnp.stack([out_down, out_up])[:, None]
    return (input_grads, down_grads)


def solution(mesh):
    return jax.shard_map(
        per_device,
        mesh=mesh,
        in_specs=(
            P(None, ("expert", "dp"), None),
            P(None, "pipe", ("expert", "dp"), None),
            P(None, "pipe", ("expert", "dp"), None),
            P(None, "pipe", "dp", "expert", None, None),
            P(None, "pipe", "dp", "expert", None, None),
            P("pipe", "expert", "dp", None),
            P("pipe", "expert", "dp", None),
            P("pipe", "expert", "dp", None),
        ),
        out_specs=(P(None, "pipe", ("expert", "dp"), None), P("pipe", "expert", "dp", None)),
        check_vma=False,
    )
```

profile of v0, /device:TPU:1, one launch (start us, length us, event | category | flops | bytes accessed | tf_op | source)
XLA Modules:
  0.0 836.1 jit_solution(6932138100712816910)
XLA Ops:
  12.4 2.6 mul.245
  15.2 2.2 scatter_custom_fusion
  18.8 10.1 %all-to-all-start = ((bf16[16,9,3584]{2,1,0:T(8,128)(2,1)}), bf16[16,9,3584]{2,1,0:T(8,128)(2,1)}, u32[]{:S(2)}, u32[]{:S(2)}) async-start(bf16[16,9,3584]{2,1,0:T(8,128)(2,1)} %reshape.349), calls=%async_computation | async-start | bytes 3670016 | tf_op jit(solution)/shard_map/all_to_all | solution.py:90
  29.1 43.6 %all-to-all-done = bf16[16,9,3584]{2,1,0:T(8,128)(2,1)} async-done(((bf16[16,9,3584]{2,1,0:T(8,128)(2,1)}), bf16[16,9,3584]{2,1,0:T(8,128)(2,1)}, u32[]{:S(2)}, u32[]{:S(2)}) %all-to-all-start) | async-done | bytes 1032224 | tf_op jit(solution)/shard_map/all_to_all | solution.py:90
  74.4 16.2 %all-gather.11.cloned.1.call-done = bf16[1,1,3584,1024]{3,2,1,0:T(8,128)(2,1)} async-done(((bf16[1,1,896,1024]{3,2,1,0:T(8,128)(2,1)}), bf16[1,1,3584,1024]{3,2,1,0:T(8,128)(2,1)}) %all-gather.11.cloned.1.call-update) | async-done | bytes 7340048 | tf_op jit(solution)/shard_map/all_gather | solution.py:51
  90.6 79.6 %all-gather.7.cloned.1.call-done = bf16[1,1,1024,3584]{3,2,1,0:T(8,128)(2,1)} async-done(((bf16[1,1,256,3584]{3,2,1,0:T(8,128)(2,1)}), bf16[1,1,1024,3584]{3,2,1,0:T(8,128)(2,1)}) %all-gather.7.cloned.1.call-update) | async-done | bytes 7340048 | tf_op jit(solution)/shard_map/all_gather | solution.py:52
  170.2 79.7 %all-gather.9.cloned.1.call-done = bf16[1,1,3584,1024]{3,2,1,0:T(8,128)(2,1)} async-done(((bf16[1,1,896,1024]{3,2,1,0:T(8,128)(2,1)}), bf16[1,1,3584,1024]{3,2,1,0:T(8,128)(2,1)}) %all-gather.9.cloned.1.call-update) | async-done | bytes 7340048 | tf_op jit(solution)/shard_map/all_gather | solution.py:50
  249.9 12.3 %conditional.4 = (bf16[144,3584]{1,0:T(8,128)(2,1)S(1)}, bf16[144,1024]{1,0:T(8,128)(2,1)}) conditional(s32[]{:T(128)} %convert_element_type.200, () %tuple.52, (bf16[144,3584]{1,0:T(8,128)(2,1)S(1)}, bf16[1024,3584]{1,0:T(8,128)(2,1)}, pred[]{:T(512)}, bf16[144,1024]{1,0:T(8,128)(2,1)S(1)}, bf16[144,1024]{1,0:T(8,128)(2,1)S(1)}, ...), branch_computations={%region_3.4_spmd, %region_4.5_spmd} | conditional | flops 3176349696 | bytes 84312152 | solution.py:97
  250.9 6.1 fusion.115
  257.0 2.6 fusion.9
  259.6 2.6 fusion
  263.7 8.1 all-to-all-start.1
  272.0 43.3 %all-to-all-done.1 = bf16[16,9,3584]{2,1,0:T(8,128)(2,1)} async-done(((bf16[16,9,3584]{2,1,0:T(8,128)(2,1)}), bf16[16,9,3584]{2,1,0:T(8,128)(2,1)}, u32[]{:S(2)}, u32[]{:S(2)}) %all-to-all-start.1) | async-done | bytes 1032224 | tf_op jit(solution)/shard_map/all_to_all | solution.py:102
  317.1 2.0 gather_fusion
  319.1 3.2 reshape.366
  322.3 4.6 reduce_sum.82
  332.1 7.9 collective-permute-done
  340.8 3.3 collective-permute-done.1
  347.9 3.4 mul.252
  351.3 3.2 scatter_custom_fusion.1
  356.0 5.0 all-to-all-start.2
  361.0 43.8 %all-to-all-done.2 = bf16[16,9,3584]{2,1,0:T(8,128)(2,1)} async-done(((bf16[16,9,3584]{2,1,0:T(8,128)(2,1)}), bf16[16,9,3584]{2,1,0:T(8,128)(2,1)}, u32[]{:S(2)}, u32[]{:S(2)}) %all-to-all-start.2) | async-done | bytes 1032224 | tf_op jit(solution)/shard_map/all_to_all | solution.py:90
  406.5 2.2 conditional.5
  408.7 2.5 reshape.355
  411.2 4.7 all-to-all-start.3
  416.1 43.5 %all-to-all-done.3 = bf16[16,9,3584]{2,1,0:T(8,128)(2,1)} async-done(((bf16[16,9,3584]{2,1,0:T(8,128)(2,1)}), bf16[16,9,3584]{2,1,0:T(8,128)(2,1)}, u32[]{:S(2)}, u32[]{:S(2)}) %all-to-all-start.3) | async-done | bytes 1032224 | tf_op jit(solution)/shard_map/all_to_all | solution.py:102
  461.3 2.1 gather_fusion.1
  463.4 3.2 reshape.367
  466.5 4.7 reduce_sum.85
  471.2 2.0 add_convert_fusion.3
  473.3 15.8 %collective-permute-start.2 = (bf16[64,3584]{1,0:T(8,128)(2,1)}, bf16[64,3584]{1,0:T(8,128)(2,1)S(1)}, u32[]{:S(2)}, u32[]{:S(2)}) collective-permute-start(bf16[64,3584]{1,0:T(8,128)(2,1)} %add_convert_fusion.3), channel_id=1, source_target_pairs={{0,64},{64,128},{128,192},{1,65},{65,129},{129,193},{2,66},{66,130... | collective-permute-start | bytes 1376264 | tf_op jit(solution)/shard_map/ppermute | solution.py:10
  491.5 7.9 collective-permute-done.2
  499.4 3.7 collective-permute-done.3
  506.0 3.4 mul.259
  509.4 3.2 scatter_custom_fusion.2
  514.0 5.3 all-to-all-start.4
  519.4 43.7 %all-to-all-done.4 = bf16[16,9,3584]{2,1,0:T(8,128)(2,1)} async-done(((bf16[16,9,3584]{2,1,0:T(8,128)(2,1)}), bf16[16,9,3584]{2,1,0:T(8,128)(2,1)}, u32[]{:S(2)}, u32[]{:S(2)}) %all-to-all-start.4) | async-done | bytes 1032224 | tf_op jit(solution)/shard_map/all_to_all | solution.py:90
  563.1 2.5 reshape.358
  567.5 2.5 reshape.359
  569.9 5.0 all-to-all-start.5
  575.2 43.3 %all-to-all-done.5 = bf16[16,9,3584]{2,1,0:T(8,128)(2,1)} async-done(((bf16[16,9,3584]{2,1,0:T(8,128)(2,1)}), bf16[16,9,3584]{2,1,0:T(8,128)(2,1)}, u32[]{:S(2)}, u32[]{:S(2)}) %all-to-all-start.5) | async-done | bytes 1032224 | tf_op jit(solution)/shard_map/all_to_all | solution.py:102
  620.3 2.1 gather_fusion.2
  622.3 3.2 reshape.368
  625.5 4.7 reduce_sum.88
  630.2 2.1 add_convert_fusion.2
  632.3 15.2 %collective-permute-start.4 = (bf16[64,3584]{1,0:T(8,128)(2,1)}, bf16[64,3584]{1,0:T(8,128)(2,1)S(1)}, u32[]{:S(2)}, u32[]{:S(2)}) collective-permute-start(bf16[64,3584]{1,0:T(8,128)(2,1)} %add_convert_fusion.2), channel_id=1, source_target_pairs={{0,64},{64,128},{128,192},{1,65},{65,129},{129,193},{2,66},{66,130... | collective-permute-start | bytes 1376264 | tf_op jit(solution)/shard_map/ppermute | solution.py:10
  649.7 8.0 collective-permute-done.4
  657.7 3.7 collective-permute-done.5
  664.3 3.4 mul.266
  667.7 3.2 scatter_custom_fusion.3
  672.3 5.4 all-to-all-start.6
  677.7 43.7 %all-to-all-done.6 = bf16[16,9,3584]{2,1,0:T(8,128)(2,1)} async-done(((bf16[16,9,3584]{2,1,0:T(8,128)(2,1)}), bf16[16,9,3584]{2,1,0:T(8,128)(2,1)}, u32[]{:S(2)}, u32[]{:S(2)}) %all-to-all-start.6) | async-done | bytes 1032224 | tf_op jit(solution)/shard_map/all_to_all | solution.py:90
  723.1 16.8 %conditional.7 = (bf16[144,3584]{1,0:T(8,128)(2,1)}, bf16[144,1024]{1,0:T(8,128)(2,1)S(1)}) conditional(s32[]{:T(128)} %convert_element_type.200, () %tuple.58, (bf16[144,3584]{1,0:T(8,128)(2,1)S(1)}, bf16[1024,3584]{1,0:T(8,128)(2,1)}, pred[]{:T(512)}, bf16[144,1024]{1,0:T(8,128)(2,1)}, bf16[144,1024]{1,0:T(8,128)(2,1)}, ...), branch_computations={%region_21.22_spmd, %region_22.23_spmd} | conditional | flops 3176349696 | bytes 57311352 | solution.py:97
  724.7 5.7 fusion.118
  730.4 5.9 fusion.51
  736.3 3.6 fusion.42
  740.6 7.4 fusion.60
  748.0 10.4 %add_convert_fusion = bf16[1024,3584]{1,0:T(8,128)(2,1)} fusion(f32[1024,3584]{1,0:T(8,128)} %fusion.60, bf16[144,3584]{1,0:T(8,128)(2,1)S(1)} %reshape.362, bf16[144,3584]{1,0:T(8,128)(2,1)} %reshape.358, bf16[144,3584]{1,0:T(8,128)(2,1)S(1)} %reshape.354, bf16[144,3584]{1,0:T(8,128)(2,1)S(1)} %reshape.350, pred[]{:T(512)} %eq.33, pred[]{:T(512)} %eq.34, ...), kind=kOutput, calls=%fused_computation.96 | convolution fusion | flops 1066958848 | bytes 27328516 | tf_op jit(solution)/shard_map/dot_general | solution.py:121
  758.4 2.5 reshape.363
  760.9 5.1 all-to-all-start.7
  766.0 43.6 %all-to-all-done.7 = bf16[16,9,3584]{2,1,0:T(8,128)(2,1)} async-done(((bf16[16,9,3584]{2,1,0:T(8,128)(2,1)}), bf16[16,9,3584]{2,1,0:T(8,128)(2,1)}, u32[]{:S(2)}, u32[]{:S(2)}) %all-to-all-start.7) | async-done | bytes 1032224 | tf_op jit(solution)/shard_map/all_to_all | solution.py:102
  812.4 2.4 reshape.369
  814.8 3.8 reduce_sum.91
  819.9 9.1 %reduce-scatter.2.cloned.1.call-done = bf16[256,3584]{1,0:T(8,128)(2,1)} async-done(((bf16[1024,3584]{1,0:T(8,128)(2,1)}), bf16[256,3584]{1,0:T(8,128)(2,1)}) %reduce-scatter.2.cloned.1.call-update) | async-done | bytes 1835024 | tf_op jit(solution)/shard_map/reduce_scatter | solution.py:124
  (149 shorter events, 56.2 us)
Async XLA Ops:
  7.2 83.4 %all-gather.11.cloned.1.call-start = ((), (), s32[]{:S(2)}) async-start(), calls=%async_computation.12 | async-start | bytes 9175040 | tf_op jit(solution)/shard_map/all_gather | solution.py:51
  7.9 1.5 copy-start.21
  7.9 2.3 copy-start.22
  7.9 2.5 copy-start.16
  7.9 162.3 %all-gather.7.cloned.1.call-start = ((), (), s32[]{:S(2)}) async-start(), calls=%async_computation.10 | async-start | bytes 9175040 | tf_op jit(solution)/shard_map/all_gather | solution.py:52
  8.7 241.2 %all-gather.9.cloned.1.call-start = ((), (), s32[]{:S(2)}) async-start(), calls=%async_computation.11 | async-start | bytes 9175040 | tf_op jit(solution)/shard_map/all_gather | solution.py:50
  18.8 10.1 %copy-start.18 = (bf16[2,1,1,1,144,1024]{5,4,3,2,1,0:T(8,128)(2,1)S(1)}, bf16[2,1,1,1,144,1024]{5,4,3,2,1,0:T(8,128)(2,1)}, u32[]{:S(2)}) copy-start(bf16[2,1,1,1,144,1024]{5,4,3,2,1,0:T(8,128)(2,1)} %param.19) | copy-start | bytes 1769476
  18.8 10.1 %copy-start.19 = (bf16[2,1,1,1,144,1024]{5,4,3,2,1,0:T(8,128)(2,1)S(1)}, bf16[2,1,1,1,144,1024]{5,4,3,2,1,0:T(8,128)(2,1)}, u32[]{:S(2)}) copy-start(bf16[2,1,1,1,144,1024]{5,4,3,2,1,0:T(8,128)(2,1)} %param.20) | copy-start | bytes 1769476
  18.8 53.9 %all-to-all-start = ((bf16[16,9,3584]{2,1,0:T(8,128)(2,1)}), bf16[16,9,3584]{2,1,0:T(8,128)(2,1)}, u32[]{:S(2)}, u32[]{:S(2)}) async-start(bf16[16,9,3584]{2,1,0:T(8,128)(2,1)} %reshape.349), calls=%async_computation | async-start | bytes 3670016 | tf_op jit(solution)/shard_map/all_to_all | solution.py:90
  29.1 377.4 %copy-start.6 = (bf16[144,1024]{1,0:T(8,128)(2,1)}, bf16[144,1024]{1,0:T(8,128)(2,1)S(1)}, u32[]{:S(2)}) copy-start(bf16[144,1024]{1,0:T(8,128)(2,1)S(1)} %get-tuple-element.233) | copy-start | bytes 884740
  29.1 377.4 %copy-start.8 = (bf16[144,1024]{1,0:T(8,128)(2,1)}, bf16[144,1024]{1,0:T(8,128)(2,1)S(1)}, u32[]{:S(2)}) copy-start(bf16[144,1024]{1,0:T(8,128)(2,1)S(1)} %get-tuple-element.246) | copy-start | bytes 884740
  29.1 377.4 %copy-start.11 = (bf16[144,1024]{1,0:T(8,128)(2,1)}, bf16[144,1024]{1,0:T(8,128)(2,1)S(1)}, u32[]{:S(2)}) copy-start(bf16[144,1024]{1,0:T(8,128)(2,1)S(1)} %get-tuple-element.247) | copy-start | bytes 884740
  249.9 7.1 copy-start.23
  250.9 8.7 %slice-start = ((s8[7340032]{0:T(1024)(128)(4,1)}), s8[4194304]{0:T(1024)(128)(4,1)S(1)}, s32[]{:S(2)}) async-start(s8[7340032]{0:T(1024)(128)(4,1)} %bitcast.91), calls=%async_computation.13 | async-start | bytes 8388608 | tf_op jit(solution)/shard_map/cond
  257.0 2.6 slice-start.1
  263.7 51.7 %all-to-all-start.1 = ((bf16[16,9,3584]{2,1,0:T(8,128)(2,1)}), bf16[16,9,3584]{2,1,0:T(8,128)(2,1)}, u32[]{:S(2)}, u32[]{:S(2)}) async-start(bf16[16,9,3584]{2,1,0:T(8,128)(2,1)} %reshape.351), calls=%async_computation.1 | async-start | bytes 3670016 | tf_op jit(solution)/shard_map/all_to_all | solution.py:102
  328.5 11.5 %copy-start.14 = (bf16[64,3584]{1,0:T(8,128)(2,1)}, bf16[64,3584]{1,0:T(8,128)(2,1)S(1)}, u32[]{:S(2)}) copy-start(bf16[64,3584]{1,0:T(8,128)(2,1)S(1)} %add_convert_fusion.4) | copy-start | bytes 1376260
  328.5 11.5 %collective-permute-start = (bf16[64,3584]{1,0:T(8,128)(2,1)S(1)}, bf16[64,3584]{1,0:T(8,128)(2,1)S(1)}, u32[]{:S(2)}, u32[]{:S(2)}) collective-permute-start(bf16[64,3584]{1,0:T(8,128)(2,1)S(1)} %add_convert_fusion.4), channel_id=1, source_target_pairs={{0,64},{64,128},{128,192},{1,65},{65,129},{129,193},{2,66},{66,130... | collective-permute-start | bytes 1376264 | tf_op jit(solution)/shard_map/ppermute | solution.py:10
  329.8 14.2 %collective-permute-start.1 = (bf16[64,3584]{1,0:T(8,128)(2,1)S(1)}, bf16[64,3584]{1,0:T(8,128)(2,1)}, u32[]{:S(2)}, u32[]{:S(2)}) collective-permute-start(bf16[64,3584]{1,0:T(8,128)(2,1)S(1)} %add_convert_fusion.4), channel_id=1, source_target_pairs={{64,0},{128,64},{192,128},{65,1},{129,65},{193,129},{66,2},{130,66... | collective-permute-start | bytes 1376264 | tf_op jit(solution)/shard_map/ppermute | solution.py:10
  340.0 0.8 copy-start.20
  345.1 0.9 copy-start.2
  356.0 48.8 %all-to-all-start.2 = ((bf16[16,9,3584]{2,1,0:T(8,128)(2,1)}), bf16[16,9,3584]{2,1,0:T(8,128)(2,1)}, u32[]{:S(2)}, u32[]{:S(2)}) async-start(bf16[16,9,3584]{2,1,0:T(8,128)(2,1)} %reshape.353), calls=%async_computation.2 | async-start | bytes 3670016 | tf_op jit(solution)/shard_map/all_to_all | solution.py:90
  411.2 48.4 %all-to-all-start.3 = ((bf16[16,9,3584]{2,1,0:T(8,128)(2,1)}), bf16[16,9,3584]{2,1,0:T(8,128)(2,1)}, u32[]{:S(2)}, u32[]{:S(2)}) async-start(bf16[16,9,3584]{2,1,0:T(8,128)(2,1)} %reshape.355), calls=%async_computation.3 | async-start | bytes 3670016 | tf_op jit(solution)/shard_map/all_to_all | solution.py:102
  466.5 4.7 copy-start.3
  473.3 26.1 %collective-permute-start.2 = (bf16[64,3584]{1,0:T(8,128)(2,1)}, bf16[64,3584]{1,0:T(8,128)(2,1)S(1)}, u32[]{:S(2)}, u32[]{:S(2)}) collective-permute-start(bf16[64,3584]{1,0:T(8,128)(2,1)} %add_convert_fusion.3), channel_id=1, source_target_pairs={{0,64},{64,128},{128,192},{1,65},{65,129},{129,193},{2,66},{66,130... | collective-permute-start | bytes 1376264 | tf_op jit(solution)/shard_map/ppermute | solution.py:10
  489.1 14.0 %collective-permute-start.3 = (bf16[64,3584]{1,0:T(8,128)(2,1)}, bf16[64,3584]{1,0:T(8,128)(2,1)S(1)}, u32[]{:S(2)}, u32[]{:S(2)}) collective-permute-start(bf16[64,3584]{1,0:T(8,128)(2,1)} %add_convert_fusion.3), channel_id=1, source_target_pairs={{64,0},{128,64},{192,128},{65,1},{129,65},{193,129},{66,2},{130,66... | collective-permute-start | bytes 1376264 | tf_op jit(solution)/shard_map/ppermute | solution.py:10
  503.2 0.9 copy-start.4
  514.0 49.1 %all-to-all-start.4 = ((bf16[16,9,3584]{2,1,0:T(8,128)(2,1)}), bf16[16,9,3584]{2,1,0:T(8,128)(2,1)}, u32[]{:S(2)}, u32[]{:S(2)}) async-start(bf16[16,9,3584]{2,1,0:T(8,128)(2,1)} %reshape.357), calls=%async_computation.4 | async-start | bytes 3670016 | tf_op jit(solution)/shard_map/all_to_all | solution.py:90
  519.3 46.3 %copy-start.7 = (bf16[144,1024]{1,0:T(8,128)(2,1)S(1)}, bf16[144,1024]{1,0:T(8,128)(2,1)}, u32[]{:S(2)}) copy-start(bf16[144,1024]{1,0:T(8,128)(2,1)} %copy-done.6) | copy-start | bytes 884740
  519.3 46.3 %copy-start.9 = (bf16[144,1024]{1,0:T(8,128)(2,1)S(1)}, bf16[144,1024]{1,0:T(8,128)(2,1)}, u32[]{:S(2)}) copy-start(bf16[144,1024]{1,0:T(8,128)(2,1)} %copy-done.8) | copy-start | bytes 884740
  519.4 46.3 %copy-start.12 = (bf16[144,1024]{1,0:T(8,128)(2,1)S(1)}, bf16[144,1024]{1,0:T(8,128)(2,1)}, u32[]{:S(2)}) copy-start(bf16[144,1024]{1,0:T(8,128)(2,1)} %copy-done.11) | copy-start | bytes 884740
  569.9 48.6 %all-to-all-start.5 = ((bf16[16,9,3584]{2,1,0:T(8,128)(2,1)}), bf16[16,9,3584]{2,1,0:T(8,128)(2,1)}, u32[]{:S(2)}, u32[]{:S(2)}) async-start(bf16[16,9,3584]{2,1,0:T(8,128)(2,1)} %reshape.359), calls=%async_computation.5 | async-start | bytes 3670016 | tf_op jit(solution)/shard_map/all_to_all | solution.py:102
  625.5 4.7 copy-start.5
  632.3 25.4 %collective-permute-start.4 = (bf16[64,3584]{1,0:T(8,128)(2,1)}, bf16[64,3584]{1,0:T(8,128)(2,1)S(1)}, u32[]{:S(2)}, u32[]{:S(2)}) collective-permute-start(bf16[64,3584]{1,0:T(8,128)(2,1)} %add_convert_fusion.2), channel_id=1, source_target_pairs={{0,64},{64,128},{128,192},{1,65},{65,129},{129,193},{2,66},{66,130... | collective-permute-start | bytes 1376264 | tf_op jit(solution)/shard_map/ppermute | solution.py:10
  647.4 14.0 %collective-permute-start.5 = (bf16[64,3584]{1,0:T(8,128)(2,1)}, bf16[64,3584]{1,0:T(8,128)(2,1)S(1)}, u32[]{:S(2)}, u32[]{:S(2)}) collective-permute-start(bf16[64,3584]{1,0:T(8,128)(2,1)} %add_convert_fusion.2), channel_id=1, source_target_pairs={{64,0},{128,64},{192,128},{65,1},{129,65},{193,129},{66,2},{130,66... | collective-permute-start | bytes 1376264 | tf_op jit(solution)/shard_map/ppermute | solution.py:10
  661.5 0.9 copy-start
  672.3 49.1 %all-to-all-start.6 = ((bf16[16,9,3584]{2,1,0:T(8,128)(2,1)}), bf16[16,9,3584]{2,1,0:T(8,128)(2,1)}, u32[]{:S(2)}, u32[]{:S(2)}) async-start(bf16[16,9,3584]{2,1,0:T(8,128)(2,1)} %reshape.361), calls=%async_computation.6 | async-start | bytes 3670016 | tf_op jit(solution)/shard_map/all_to_all | solution.py:90
  677.7 151.4 %reduce-scatter.2.cloned.1.call-start = ((), (), s32[]{:S(2)}) async-start(), calls=%async_computation.9 | async-start | bytes 9175040 | tf_op jit(solution)/shard_map/reduce_scatter | solution.py:124
  724.6 5.8 copy-start.10
  724.7 5.8 copy-start.13
  724.7 11.7 %slice-start.6 = ((s8[7340032]{0:T(1024)(128)(4,1)}), s8[4194304]{0:T(1024)(128)(4,1)S(1)}, s32[]{:S(2)}) async-start(s8[7340032]{0:T(1024)(128)(4,1)} %bitcast.97), calls=%async_computation.19 | async-start | bytes 8388608 | tf_op jit(solution)/shard_map/cond
  730.4 5.9 slice-start.7
  739.9 0.7 copy-start.17
  760.9 48.7 %all-to-all-start.7 = ((bf16[16,9,3584]{2,1,0:T(8,128)(2,1)}), bf16[16,9,3584]{2,1,0:T(8,128)(2,1)}, u32[]{:S(2)}, u32[]{:S(2)}) async-start(bf16[16,9,3584]{2,1,0:T(8,128)(2,1)} %reshape.363), calls=%async_computation.7 | async-start | bytes 3670016 | tf_op jit(solution)/shard_map/all_to_all | solution.py:102
  814.8 3.8 copy-start.1
  814.8 3.8 copy-start.15
Sparse Core Ops, SparseCore 0:
  9.8 80.7 all-gather.10
  92.4 77.7 all-gather.6
  172.1 77.7 all-gather.8
  758.5 70.4 reduce-scatter.1
where the time goes:
time: 846 us; the launch traced here: 836 us
  waiting for transfers between devices  570 us (67%)
  starting transfers between devices  85.2 us (10%)
  local copies, waits for them, and re-layouts  79.5 us (9%)
  matrix products  44.2 us (5%)
  other arithmetic  41.7 us (5%)
  between operations  14.9 us (2%)
    all_to_all x4, waiting for transfers between devices, per_device(): lax.all_to_all(outgoing.reshape(groups, capacity, width), 'expert', split...  175 us
    all_to_all x4, waiting for transfers between devices, per_device(): lax.all_to_all(d_input.reshape(groups, capacity, width), 'expert', split_...  174 us
    all_gather x1, waiting for transfers between devices, per_device(): lax.all_gather(w_gate[0, 0], 'dp', axis=0, tiled=True)  79.7 us
    all_gather x1, waiting for transfers between devices, per_device(): lax.all_gather(w_down[0, 0], 'dp', axis=0, tiled=True)  79.6 us
    ppermute x6, starting transfers between devices, from_behind(): lax.ppermute(value, axis, [(source, source + steps) for source in range(i...  36.4 us
    ppermute x6, waiting for transfers between devices, from_behind(): lax.ppermute(value, axis, [(source, source + steps) for source in range(i...  34.5 us
    all_to_all x4, starting transfers between devices, per_device(): lax.all_to_all(outgoing.reshape(groups, capacity, width), 'expert', split...  25.8 us
    all_to_all x4, starting transfers between devices, per_device(): lax.all_to_all(d_input.reshape(groups, capacity, width), 'expert', split_...  22.9 us
  transfers between devices with their start and end apart: 18, of which 18 were waited for; matrix products, arithmetic and copies ran while one was open for 3% of the time, Pallas kernels for 0%

commit v1 on v0

v1 whole, which is shorter than its diff:
```python
import functools
import jax
import jax.numpy as jnp
from jax import lax
from jax.experimental import pallas as pl
from jax.experimental.pallas import tpu as pltpu
from jax.sharding import PartitionSpec as P

BF = jnp.bfloat16
F32 = jnp.float32
I32 = jnp.int32
D = 3584
FF = 1024
TOK = 64
EXP = 16
CAP = 9
SLOTS = 144
MAIN = 128
CH = 896
PCH = 1024
NCH = 4
PIECES = 7
NT = (((1,), (1,)), ((), ()))
NN = (((1,), (0,)), ((), ()))


def dot(a, b, dims=NN):
    return lax.dot_general(a, b, dims, preferred_element_type=F32)


def ones_where(mask):
    return jnp.where(mask, 1.0, 0.0).astype(BF)


def prep_kernel(order_ref, gate_ref, up_ref, fup_ref, fgate_ref, hidden_ref):
    row = lax.broadcasted_iota(I32, (SLOTS, SLOTS), 0)
    col = lax.broadcasted_iota(I32, (SLOTS, SLOTS), 1)
    slot = jnp.where(row < MAIN, (row >> 3) * CAP + (row & 7), (row - MAIN) * CAP + 8)
    perm = ones_where(col == slot)
    gate = dot(perm, gate_ref[0])
    up = dot(perm, up_ref[0])
    sig = 1.0 / (1.0 + jnp.exp(-gate))
    act = gate * sig
    fup_ref[0] = act
    fgate_ref[0] = up * sig * (1.0 + gate * (1.0 - sig))
    hidden_ref[0] = (act * up).astype(BF)


def prep(order, gate, up):
    spec_in = pl.BlockSpec((1, SLOTS, FF), lambda i, o: (o[i], 0, 0))
    spec_out = pl.BlockSpec((1, SLOTS, FF), lambda i, o: (i, 0, 0))
    return pl.pallas_call(
        prep_kernel,
        out_shape=(
            jax.ShapeDtypeStruct((2, SLOTS, FF), F32),
            jax.ShapeDtypeStruct((2, SLOTS, FF), F32),
            jax.ShapeDtypeStruct((2, SLOTS, FF), BF),
        ),
        grid_spec=pltpu.PrefetchScalarGridSpec(
            num_scalar_prefetch=1,
            grid=(2,),
            in_specs=[spec_in, spec_in],
            out_specs=[spec_out, spec_out, spec_out],
        ),
        compiler_params=pltpu.CompilerParams(vmem_limit_bytes=24 << 20),
        cost_estimate=pl.CostEstimate(flops=170_000_000, bytes_accessed=4_700_000, transcendentals=300_000),
        name="prep",
    )(order, gate, up)


def pre_kernel(t_ref, w_ref, cur_ref, out_ref):
    c = lax.broadcasted_iota(I32, (MAIN, TOK), 0)
    e9 = (c >> 3) * CAP
    t0 = t_ref[0:1, :]
    t1 = t_ref[1:2, :]
    w0 = w_ref[0:1, :]
    w1 = w_ref[1:2, :]

    def pick(slot):
        m0 = t0 == slot
        m1 = t1 == slot
        scale = jnp.sum(jnp.where(m0, w0, 0.0) + jnp.where(m1, w1, 0.0), axis=1, keepdims=True)
        return ones_where(jnp.logical_or(m0, m1)), scale

    main, scale_main = pick(e9 + (c & 7))
    last, scale_last = pick(e9 + 8)
    piece = lax.broadcasted_iota(I32, (MAIN, 128), 0) & 7
    for j in range(NCH):
        x = cur_ref[:, j * CH : (j + 1) * CH]
        out_ref[:, j * PCH : j * PCH + CH] = (dot(main, x) * scale_main).astype(BF)
        full = dot(last, x)
        part = jnp.zeros((MAIN, 128), F32)
        for k in range(PIECES):
            part = jnp.where(piece == k, full[:, k * 128 : (k + 1) * 128], part)
        out_ref[:, j * PCH + CH : (j + 1) * PCH] = (part * scale_last).astype(BF)


def pre(targets_t, weights_t, cur):
    return pl.pallas_call(
        pre_kernel,
        out_shape=jax.ShapeDtypeStruct((MAIN, NCH * PCH), BF),
        compiler_params=pltpu.CompilerParams(vmem_limit_bytes=16 << 20),
        cost_estimate=pl.CostEstimate(flops=120_000_000, bytes_accessed=1_600_000, transcendentals=0),
        name="pre",
    )(targets_t, weights_t, cur)


def post_kernel(t_ref, cur_ref, buf_ref, out_ref):
    c = lax.broadcasted_iota(I32, (TOK, MAIN), 1)
    e9 = (c >> 3) * CAP
    s = c & 7
    t0 = t_ref[:, 0:1]
    t1 = t_ref[:, 1:2]

    def pick(slot):
        return jnp.logical_or(t0 == slot, t1 == slot)

    main = ones_where(pick(e9 + s))
    last = pick(e9 + 8)
    tail = jnp.concatenate(
        [ones_where(jnp.logical_and(last, s == k)) for k in range(PIECES)], axis=0
    )
    for j in range(NCH):
        if len(buf_ref.shape) == 3:
            packed = buf_ref[j]
        else:
            packed = buf_ref[:, j * PCH : (j + 1) * PCH]
        acc = dot(main, packed[:, :CH])
        nin = dot(tail, packed[:, CH:])
        for k in range(PIECES):
            lo = j * CH + k * 128
            out_ref[:, lo : lo + 128] = (
                cur_ref[:, lo : lo + 128].astype(F32)
                + (acc[:, k * 128 : (k + 1) * 128] + nin[k * TOK : (k + 1) * TOK, :])
            ).astype(BF)


def post(targets, cur, buf):
    return pl.pallas_call(
        post_kernel,
        out_shape=jax.ShapeDtypeStruct((TOK, D), BF),
        compiler_params=pltpu.CompilerParams(vmem_limit_bytes=16 << 20),
        cost_estimate=pl.CostEstimate(flops=120_000_000, bytes_accessed=2_000_000, transcendentals=0),
        name="post",
    )(targets, cur, buf)


def unpack_rows(buf_ref, rows_ref):
    r = lax.broadcasted_iota(I32, (128, MAIN), 0)
    c = lax.broadcasted_iota(I32, (128, MAIN), 1)
    spread = ones_where(c == (r & 15) * 8 + (r >> 4))
    for j in range(NCH):
        rows_ref[0:MAIN, j * CH : (j + 1) * CH] = buf_ref[:, j * PCH : j * PCH + CH]
        nin = dot(spread, buf_ref[:, j * PCH + CH : (j + 1) * PCH]).astype(BF)
        for k in range(PIECES):
            lo = j * CH + k * 128
            rows_ref[MAIN:SLOTS, lo : lo + 128] = nin[k * 16 : (k + 1) * 16, :]


def pack_chunk(grads, out_ref):
    c = lax.broadcasted_iota(I32, (MAIN, 128), 0)
    r = lax.broadcasted_iota(I32, (MAIN, 128), 1)
    fold = ones_where(r == (c & 7) * 16 + (c >> 3))
    out_ref[:, 0:CH] = grads[0:MAIN]
    pieces = [grads[MAIN:SLOTS, k * 128 : (k + 1) * 128] for k in range(PIECES)]
    pieces.append(jnp.zeros((16, 128), BF))
    out_ref[:, CH:PCH] = dot(fold, jnp.concatenate(pieces, axis=0)).astype(BF)


def hidden_block(rows_ref, wd_ref, fup_ref, fgate_ref):
    d_hidden = dot(rows_ref[...], wd_ref[...], NT)
    return (d_hidden * fgate_ref[...]).astype(BF), (d_hidden * fup_ref[...]).astype(BF)


def grads_block(dg, du, wg_ref, wu_ref):
    total = None
    for q in range(4):
        cols = slice(q * 256, (q + 1) * 256)
        term = dot(dg[q], wg_ref[:, cols], NT) + dot(du[q], wu_ref[:, cols], NT)
        total = term if total is None else total + term
    return total.astype(BF)


def hidden_kernel(buf_ref, wd_ref, fup_ref, fgate_ref, rows_ref, dg_ref, du_ref):
    @pl.when(pl.program_id(0) == 0)
    def _():
        unpack_rows(buf_ref, rows_ref)

    dg_ref[0], du_ref[0] = hidden_block(rows_ref, wd_ref, fup_ref, fgate_ref)


def hidden_pass(buf, wd, fup, fgate):
    return pl.pallas_call(
        hidden_kernel,
        grid=(4,),
        in_specs=[
            pl.BlockSpec((MAIN, NCH * PCH), lambda i: (0, 0)),
            pl.BlockSpec((256, D), lambda i: (i, 0)),
            pl.BlockSpec((SLOTS, 256), lambda i: (0, i)),
            pl.BlockSpec((SLOTS, 256), lambda i: (0, i)),
        ],
        out_specs=[
            pl.BlockSpec((SLOTS, D), lambda i: (0, 0)),
            pl.BlockSpec((1, SLOTS, 256), lambda i: (i, 0, 0)),
            pl.BlockSpec((1, SLOTS, 256), lambda i: (i, 0, 0)),
        ],
        out_shape=(
            jax.ShapeDtypeStruct((SLOTS, D), BF),
            jax.ShapeDtypeStruct((4, SLOTS, 256), BF),
            jax.ShapeDtypeStruct((4, SLOTS, 256), BF),
        ),
        compiler_params=pltpu.CompilerParams(vmem_limit_bytes=24 << 20),
        cost_estimate=pl.CostEstimate(flops=1_060_000_000, bytes_accessed=11_000_000, transcendentals=0),
        name="hidden_pass",
    )(buf, wd, fup, fgate)


def grads_kernel(dg_ref, du_ref, wg_ref, wu_ref, out_ref):
    dg = [dg_ref[q] for q in range(4)]
    du = [du_ref[q] for q in range(4)]
    pack_chunk(grads_block(dg, du, wg_ref, wu_ref), out_ref)


def grads_pass(dg, du, wg, wu):
    return pl.pallas_call(
        grads_kernel,
        grid=(4,),
        in_specs=[
            pl.BlockSpec((4, SLOTS, 256), lambda i: (0, 0, 0)),
            pl.BlockSpec((4, SLOTS, 256), lambda i: (0, 0, 0)),
            pl.BlockSpec((CH, FF), lambda i: (i, 0)),
            pl.BlockSpec((CH, FF), lambda i: (i, 0)),
        ],
        out_specs=pl.BlockSpec((MAIN, PCH), lambda i: (0, i)),
        out_shape=jax.ShapeDtypeStruct((MAIN, NCH * PCH), BF),
        compiler_params=pltpu.CompilerParams(vmem_limit_bytes=28 << 20),
        cost_estimate=pl.CostEstimate(flops=2_120_000_000, bytes_accessed=17_000_000, transcendentals=0),
        name="grads_pass",
    )(dg, du, wg, wu)


def expert_kernel(
    buf_ref, wd_ref, fup_ref, fgate_ref, wg_ref, wu_ref, rows_ref, out_ref, dg_ref, du_ref
):
    i = pl.program_id(0)

    @pl.when(i == 0)
    def _():
        unpack_rows(buf_ref, rows_ref)

    @pl.when(i < 4)
    def _():
        dg_ref[i], du_ref[i] = hidden_block(rows_ref, wd_ref, fup_ref, fgate_ref)

    @pl.when(i >= 4)
    def _():
        dg = [dg_ref[q] for q in range(4)]
        du = [du_ref[q] for q in range(4)]
        pack_chunk(grads_block(dg, du, wg_ref, wu_ref), out_ref)


def expert_pass(buf, wd, fup, fgate, wg, wu):
    first = lambda i: jnp.minimum(i, 3)
    second = lambda i: jnp.maximum(i - 4, 0)
    return pl.pallas_call(
        expert_kernel,
        grid=(8,),
        in_specs=[
            pl.BlockSpec((MAIN, NCH * PCH), lambda i: (0, 0)),
            pl.BlockSpec((256, D), lambda i: (first(i), 0)),
            pl.BlockSpec((SLOTS, 256), lambda i: (0, first(i))),
            pl.BlockSpec((SLOTS, 256), lambda i: (0, first(i))),
            pl.BlockSpec((CH, FF), lambda i: (second(i), 0)),
            pl.BlockSpec((CH, FF), lambda i: (second(i), 0)),
        ],
        out_specs=[
            pl.BlockSpec((SLOTS, D), lambda i: (0, 0)),
            pl.BlockSpec((MAIN, PCH), lambda i: (0, second(i))),
        ],
        out_shape=(
            jax.ShapeDtypeStruct((SLOTS, D), BF),
            jax.ShapeDtypeStruct((MAIN, NCH * PCH), BF),
        ),
        scratch_shapes=[pltpu.VMEM((4, SLOTS, 256), BF), pltpu.VMEM((4, SLOTS, 256), BF)],
        compiler_params=pltpu.CompilerParams(vmem_limit_bytes=36 << 20),
        cost_estimate=pl.CostEstimate(flops=3_200_000_000, bytes_accessed=28_000_000, transcendentals=0),
        name="expert_pass",
    )(buf, wd, fup, fgate, wg, wu)


def exchange(buf):
    return lax.all_to_all(
        buf.reshape(EXP, 8, NCH * PCH), "expert", split_axis=0, concat_axis=0, tiled=True
    ).reshape(MAIN, NCH * PCH)


def slot_targets(routes):
    flat = routes.reshape(2, TOK * 2)
    n = TOK * 2
    row = lax.broadcasted_iota(I32, (n, n), 0)
    col = lax.broadcasted_iota(I32, (n, n), 1)
    same = jnp.logical_and(flat[:, :, None] == flat[:, None, :], (col < row)[None])
    return (flat * CAP + jnp.sum(same.astype(I32), axis=2)).reshape(2, TOK, 2)


def per_device(
    seed_grads, expert_routes, route_weights, saved_gate, saved_up, w_gate, w_up, w_down
):
    section = lax.axis_index("pipe")
    first_up = section < 2
    first = jnp.where(first_up, 1, 0).astype(I32)
    order = jnp.stack([first, 1 - first])

    def gather(x):
        return lax.all_gather(x, "dp", axis=0, tiled=True)

    wd_full = gather(w_down[0, 0])
    wg_in, wu_in = w_gate[0, 0], w_up[0, 0]
    wg_full = gather(wg_in)
    wu_full = gather(wu_in)

    def ordered(x):
        return jnp.where(first_up, x[1], x[0]), jnp.where(first_up, x[0], x[1])

    targets = slot_targets(expert_routes[:, 0])
    tgt = ordered(targets)
    wts = ordered(route_weights[:, 0])
    tgt_t = [t.T for t in tgt]
    wts_t = [w.T for w in wts]
    cur = jnp.where(first_up, seed_grads[1], seed_grads[0])
    fup, fgate, hidden = prep(order, saved_gate[:, 0, 0, 0], saved_up[:, 0, 0, 0])

    moves = [[(0, 1), (3, 2)], [(1, 2), (2, 1)], [(2, 3), (1, 0)]]
    results = []
    held_rows = []
    for step in range(4):
        at = step // 2
        buf = exchange(pre(tgt_t[at], wts_t[at], cur))
        if step == 0:
            rows, dg, du = hidden_pass(buf, wd_full, fup[at], fgate[at])
            packed = grads_pass(dg, du, wg_full, wu_full)
        else:
            rows, packed = expert_pass(buf, wd_full, fup[at], fgate[at], wg_full, wu_full)
        held_rows.append(rows)
        result = post(tgt[at], cur, exchange(packed))
        results.append(result)
        if step < 3:
            cur = lax.ppermute(result, "pipe", moves[step])

    edge = jnp.logical_or(section == 0, section == 3)
    res_first = jnp.where(edge, results[0], results[1])
    res_second = jnp.where(edge, results[3], results[2])
    input_grads = jnp.where(
        first_up, jnp.stack([res_second, res_first]), jnp.stack([res_first, res_second])
    )[:, None]

    mine = lax.axis_index("dp") * 256
    hidden_all = lax.all_gather(hidden, "dp", axis=0)
    hidden_mine = lax.dynamic_slice_in_dim(hidden_all, mine, 256, axis=3)
    rows_first = jnp.where(edge, held_rows[0], held_rows[1])
    rows_second = jnp.where(edge, held_rows[3], held_rows[2])
    contract = (((0,), (0,)), ((), ()))
    total = dot(hidden_mine[:, 0].reshape(4 * SLOTS, 256), gather(rows_first), contract)
    total = total + dot(hidden_mine[:, 1].reshape(4 * SLOTS, 256), gather(rows_second), contract)
    return input_grads, total.astype(BF)[None, None]


def solution(mesh):
    return jax.shard_map(
        per_device,
        mesh=mesh,
        in_specs=(
            P(None, ("expert", "dp"), None),
            P(None, "pipe", ("expert", "dp"), None),
            P(None, "pipe", ("expert", "dp"), None),
            P(None, "pipe", "dp", "expert", None, None),
            P(None, "pipe", "dp", "expert", None, None),
            P("pipe", "expert", "dp", None),
            P("pipe", "expert", "dp", None),
            P("pipe", "expert", "dp", None),
        ),
        out_specs=(P(None, "pipe", ("expert", "dp"), None), P("pipe", "expert", "dp", None)),
        check_vma=False,
    )
```

time: 846 us -> 609 us (0.72); the launches traced: 836 us -> 608 us
  waiting for transfers between devices: 570 us -> 337 us
  blocking collectives: 0 us -> 132 us
  starting transfers between devices: 85.2 us -> 26 us
  Pallas kernels: 0 us -> 55.3 us
  local copies, waits for them, and re-layouts: 79.5 us -> 25.2 us
  other arithmetic: 41.7 us -> 5.81 us
  matrix products: 44.2 us -> 12.3 us
    all_to_all x8 -> x4, waiting for transfers between devices: 349 us -> 95.8 us  [exchange(): lax.all_to_all(buf.reshape(EXP, 8, NCH * PCH), 'expert', split_axis=0, co...]
    all_to_all x0 -> x4, blocking collectives: none -> 132 us  [exchange(): lax.all_to_all(buf.reshape(EXP, 8, NCH * PCH), 'expert', split_axis=0, co...]
    pallas_call x0 -> x14, Pallas kernels: none -> 55.3 us  [the longest x3 37.7 us: expert_pass(): pl.pallas_call(expert_kernel, grid=(8,), in_specs=[pl.BlockSpec((MAIN, NC...]
    dot_general x8 -> x2, matrix products: 44.2 us -> 12.3 us  [dot(): return lax.dot_general(a, b, dims, preferred_element_type=F32)]
    ppermute x6 -> x3, starting transfers between devices: 36.4 us -> 5.1 us  [per_device(): cur = lax.ppermute(result, 'pipe', moves[step])]
    reshape x16 -> x0, local copies, waits for them, and re-layouts: 29.2 us -> none  [the longest x4 8.94 us: per_device(): d_input.reshape(groups, capacity, width)]
    all_gather x3 -> x6, waiting for transfers between devices: 175 us -> 204 us  [the longest x5 204 us: gather(): return lax.all_gather(x, 'dp', axis=0, tiled=True)]
    all_to_all x8 -> x4, starting transfers between devices: 48.7 us -> 20.7 us  [exchange(): lax.all_to_all(buf.reshape(EXP, 8, NCH * PCH), 'expert', split_axis=0, co...]
  transfers between devices with their start and end apart: 18 -> 13, of which waited for: 18 -> 10; matrix products, arithmetic and copies ran while one was open for 3% -> 2% of each run, Pallas kernels for 0% -> 6%
where the time goes in v1:
time: 609 us; the launch traced here: 608 us
  waiting for transfers between devices  337 us (55%)
  blocking collectives  132 us (22%)
  Pallas kernels  55.3 us (9%)
  starting transfers between devices  26 us (4%)
  local copies, waits for them, and re-layouts  25.2 us (4%)
  between operations  14.4 us (2%)
  matrix products  12.3 us (2%)
    all_gather x5, waiting for transfers between devices, gather(): return lax.all_gather(x, 'dp', axis=0, tiled=True)  204 us
    all_to_all x4, blocking collectives, exchange(): lax.all_to_all(buf.reshape(EXP, 8, NCH * PCH), 'expert', split_axis=0, co...  132 us
    all_to_all x4, waiting for transfers between devices, exchange(): lax.all_to_all(buf.reshape(EXP, 8, NCH * PCH), 'expert', split_axis=0, co...  95.8 us
    pallas_call x3, Pallas kernels, expert_pass(): pl.pallas_call(expert_kernel, grid=(8,), in_specs=[pl.BlockSpec((MAIN, NC...  37.7 us
    ppermute x3, waiting for transfers between devices, per_device(): cur = lax.ppermute(result, 'pipe', moves[step])  35 us
    unnamed x55, local copies, waits for them, and re-layouts  22.6 us
    all_to_all x4, starting transfers between devices, exchange(): lax.all_to_all(buf.reshape(EXP, 8, NCH * PCH), 'expert', split_axis=0, co...  20.7 us
    dot_general x2, matrix products, dot(): return lax.dot_general(a, b, dims, preferred_element_type=F32)  12.3 us
  transfers between devices with their start and end apart: 13, of which 10 were waited for; matrix products, arithmetic and copies ran while one was open for 2% of the time, Pallas kernels for 6%

profile of v1, /device:TPU:1, one launch (start us, length us, event | category | flops | bytes accessed | tf_op | source)
XLA Modules:
  0.0 608.1 jit_solution(16993646182211825274)
XLA Ops:
  7.2 0.7 all-gather.15.cloned.1.call-update
  8.0 0.7 all-gather.17.cloned.1.call-update
  8.7 0.7 all-gather.19.cloned.1.call-update
  9.6 0.1 reshape_squeeze.9
  9.7 0.2 convert_reduce_fusion
  10.2 1.6 pre.4
  11.9 0.8 copy-done.4
  12.6 10.0 %all-to-all-start = ((bf16[16,8,4096]{2,1,0:T(8,128)(2,1)}), bf16[16,8,4096]{2,1,0:T(8,128)(2,1)S(1)}, u32[]{:S(2)}, u32[]{:S(2)}) async-start(bf16[16,8,4096]{2,1,0:T(8,128)(2,1)} %bitcast.4), calls=%async_computation | async-start | bytes 2097152 | tf_op jit(solution)/shard_map/all_to_all | solution.py:292
  22.7 2.3 prep.1
  25.0 0.2 slice_bitcast_fusion
  25.1 25.4 %all-to-all-done = bf16[16,8,4096]{2,1,0:T(8,128)(2,1)S(1)} async-done(((bf16[16,8,4096]{2,1,0:T(8,128)(2,1)}), bf16[16,8,4096]{2,1,0:T(8,128)(2,1)S(1)}, u32[]{:S(2)}, u32[]{:S(2)}) %all-to-all-start) | async-done | bytes 1048608 | tf_op jit(solution)/shard_map/all_to_all | solution.py:292
  50.5 40.1 %all-gather.15.cloned.1.call-done = bf16[1,1,1024,3584]{3,2,1,0:T(8,128)(2,1)} async-done(((bf16[1,1,256,3584]{3,2,1,0:T(8,128)(2,1)}), bf16[1,1,1024,3584]{3,2,1,0:T(8,128)(2,1)}) %all-gather.15.cloned.1.call-update) | async-done | bytes 7340048 | tf_op jit(solution)/shard_map/all_gather | solution.py:315
  90.6 3.1 copy-done
  93.7 3.3 hidden_pass.1
  97.1 1.0 copy-done.12
  98.0 0.7 copy-done.16
  98.7 0.7 copy-done.18
  99.4 70.8 %all-gather.17.cloned.1.call-done = bf16[1,1,3584,1024]{3,2,1,0:T(8,128)(2,1)} async-done(((bf16[1,1,896,1024]{3,2,1,0:T(8,128)(2,1)}), bf16[1,1,3584,1024]{3,2,1,0:T(8,128)(2,1)}) %all-gather.17.cloned.1.call-update) | async-done | bytes 7340048 | tf_op jit(solution)/shard_map/all_gather | solution.py:315
  170.3 79.7 %all-gather.19.cloned.1.call-done = bf16[1,1,3584,1024]{3,2,1,0:T(8,128)(2,1)} async-done(((bf16[1,1,896,1024]{3,2,1,0:T(8,128)(2,1)}), bf16[1,1,3584,1024]{3,2,1,0:T(8,128)(2,1)}) %all-gather.19.cloned.1.call-update) | async-done | bytes 7340048 | tf_op jit(solution)/shard_map/all_gather | solution.py:315
  249.9 3.2 copy-done.2
  253.2 3.2 copy-done.3
  256.4 1.0 copy-done.17
  257.3 1.0 copy-done.19
  258.3 5.6 grads_pass.1
  263.9 36.1 %all_to_all.40 = bf16[16,8,4096]{2,1,0:T(8,128)(2,1)S(1)} all-to-all(bf16[16,8,4096]{2,1,0:T(8,128)(2,1)S(1)} %bitcast.78), channel_id=1, replica_groups=mesh['pipe'=4,'expert'=16,'dp'=4] {'expert'}, dimensions={0} | all-to-all | bytes 2097152 | tf_op jit(solution)/shard_map/all_to_all | solution.py:292
  300.0 0.5 post.4
  300.5 3.1 collective-permute-start
  303.6 9.6 %collective-permute-done.cur_ref = bf16[64,3584]{1,0:T(8,128)(2,1)S(1)} collective-permute-done((bf16[64,3584]{1,0:T(8,128)(2,1)S(1)}, bf16[64,3584]{1,0:T(8,128)(2,1)S(1)}, u32[]{:S(2)}, u32[]{:S(2)}) %collective-permute-start) | collective-permute-done | bytes 458784 | tf_op jit(solution)/shard_map/ppermute | solution.py:348
  313.1 0.6 pre.5
  313.8 0.2 copy-done.8
  314.0 32.0 %all_to_all.41 = bf16[16,8,4096]{2,1,0:T(8,128)(2,1)S(1)} all-to-all(bf16[16,8,4096]{2,1,0:T(8,128)(2,1)S(1)} %bitcast.82), channel_id=1, replica_groups=mesh['pipe'=4,'expert'=16,'dp'=4] {'expert'}, dimensions={0} | all-to-all | bytes 2097152 | tf_op jit(solution)/shard_map/all_to_all | solution.py:292
  345.9 12.5 %expert_pass.3 = (bf16[144,3584]{1,0:T(8,128)(2,1)S(1)}, bf16[128,4096]{1,0:T(8,128)(2,1)S(1)}) custom-call(bf16[128,4096]{1,0:T(8,128)(2,1)S(1)} %bitcast.77, bf16[1024,3584]{1,0:T(8,128)(2,1)S(1)} %bitcast.63, f32[144,1024]{1,0:T(8,128)S(1)} %get-tuple-element.36.fup_ref, f32[144,1024]{1,0:T(8,128)S(1)} %get-tuple-element.31.fgate_ref, ...), custom_call_target="tpu_custom_call" | custom-call | flops 3200000000 | bytes 28000000 | tf_op jit(solution)/shard_map/expert_pass/pallas_call | solution.py:265
  358.4 1.0 copy-done.13
  359.4 1.0 copy-done.11
  360.3 3.6 all-to-all-start.3
  363.9 0.5 all-gather.21.cloned.1.call-update
  364.5 26.7 %all-to-all-done.3 = bf16[16,8,4096]{2,1,0:T(8,128)(2,1)S(1)} async-done(((bf16[16,8,4096]{2,1,0:T(8,128)(2,1)}), bf16[16,8,4096]{2,1,0:T(8,128)(2,1)S(1)}, u32[]{:S(2)}, u32[]{:S(2)}) %all-to-all-start.3) | async-done | bytes 1048608 | tf_op jit(solution)/shard_map/all_to_all | solution.py:292
  391.2 1.0 copy-done.9
  392.2 0.5 post.5
  392.7 0.7 collective-permute-start.1
  393.6 1.6 pre.6
  395.2 3.6 all-to-all-start.4
  398.8 2.4 broadcast_select_fusion.1
  401.3 25.4 %all-to-all-done.4 = bf16[16,8,4096]{2,1,0:T(8,128)(2,1)S(1)} async-done(((bf16[16,8,4096]{2,1,0:T(8,128)(2,1)}), bf16[16,8,4096]{2,1,0:T(8,128)(2,1)S(1)}, u32[]{:S(2)}, u32[]{:S(2)}) %all-to-all-start.4) | async-done | bytes 1048608 | tf_op jit(solution)/shard_map/all_to_all | solution.py:292
  426.7 3.7 copy-done.1
  430.4 12.8 %expert_pass.4 = (bf16[144,3584]{1,0:T(8,128)(2,1)S(1)}, bf16[128,4096]{1,0:T(8,128)(2,1)S(1)}) custom-call(bf16[128,4096]{1,0:T(8,128)(2,1)S(1)} %bitcast.74, bf16[1024,3584]{1,0:T(8,128)(2,1)S(1)} %bitcast.64, f32[144,1024]{1,0:T(8,128)S(1)} %get-tuple-element.37.fup_ref, f32[144,1024]{1,0:T(8,128)S(1)} %get-tuple-element.30.fgate_ref, ...), custom_call_target="tpu_custom_call" | custom-call | flops 3200000000 | bytes 28000000 | tf_op jit(solution)/shard_map/expert_pass/pallas_call | solution.py:265
  443.2 31.2 %all_to_all.42 = bf16[16,8,4096]{2,1,0:T(8,128)(2,1)S(1)} all-to-all(bf16[16,8,4096]{2,1,0:T(8,128)(2,1)S(1)} %bitcast.87), channel_id=1, replica_groups=mesh['pipe'=4,'expert'=16,'dp'=4] {'expert'}, dimensions={0} | all-to-all | bytes 2097152 | tf_op jit(solution)/shard_map/all_to_all | solution.py:292
  474.5 0.5 post.6
  475.0 1.3 collective-permute-start.2
  476.3 25.4 %collective-permute-done.2.cur_ref = bf16[64,3584]{1,0:T(8,128)(2,1)S(1)} collective-permute-done((bf16[64,3584]{1,0:T(8,128)(2,1)S(1)}, bf16[64,3584]{1,0:T(8,128)(2,1)S(1)}, u32[]{:S(2)}, u32[]{:S(2)}) %collective-permute-start.2) | collective-permute-done | bytes 458784 | tf_op jit(solution)/shard_map/ppermute | solution.py:348
  501.7 0.6 pre.7
  502.3 32.6 %all_to_all.43 = bf16[16,8,4096]{2,1,0:T(8,128)(2,1)S(1)} all-to-all(bf16[16,8,4096]{2,1,0:T(8,128)(2,1)S(1)} %bitcast.84), channel_id=1, replica_groups=mesh['pipe'=4,'expert'=16,'dp'=4] {'expert'}, dimensions={0} | all-to-all | bytes 2097152 | tf_op jit(solution)/shard_map/all_to_all | solution.py:292
  534.9 12.4 %expert_pass.5 = (bf16[144,3584]{1,0:T(8,128)(2,1)S(1)}, bf16[128,4096]{1,0:T(8,128)(2,1)S(1)}) custom-call(bf16[128,4096]{1,0:T(8,128)(2,1)S(1)} %bitcast.76, bf16[1024,3584]{1,0:T(8,128)(2,1)S(1)} %bitcast.65, f32[144,1024]{1,0:T(8,128)S(1)} %get-tuple-element.37.fup_ref, f32[144,1024]{1,0:T(8,128)S(1)} %get-tuple-element.30.fgate_ref, ...), custom_call_target="tpu_custom_call" | custom-call | flops 3200000000 | bytes 28000000 | tf_op jit(solution)/shard_map/expert_pass/pallas_call | solution.py:265
  547.3 1.0 copy-done.10
  548.3 1.2 broadcast_select_fusion
  549.5 3.6 all-to-all-start.7
  553.1 1.9 constant_dynamic-slice_fusion.1
  555.0 0.8 select_bitcast_fusion
  555.8 6.2 %fusion.4 = f32[256,3584]{1,0:T(8,128)} fusion(bf16[576,256]{1,0:T(8,128)(2,1)} %bitcast.94, bf16[576,3584]{1,0:T(8,128)(2,1)} %all-gather.11.cloned.1.call-done), kind=kOutput, calls=%fused_computation.25 | convolution fusion | flops 1056964608 | bytes 8093696 | tf_op jit(solution)/shard_map/dot_general | solution.py:28
  562.0 18.3 %all-to-all-done.7 = bf16[16,8,4096]{2,1,0:T(8,128)(2,1)S(1)} async-done(((bf16[16,8,4096]{2,1,0:T(8,128)(2,1)}), bf16[16,8,4096]{2,1,0:T(8,128)(2,1)S(1)}, u32[]{:S(2)}, u32[]{:S(2)}) %all-to-all-start.7) | async-done | bytes 1048608 | tf_op jit(solution)/shard_map/all_to_all | solution.py:292
  580.3 0.5 post.7
  580.9 1.1 maximum_select_fusion
  582.0 13.1 %all-gather.13.cloned.1.call-done = bf16[576,3584]{1,0:T(8,128)(2,1)} async-done(((bf16[144,3584]{1,0:T(8,128)(2,1)}), bf16[576,3584]{1,0:T(8,128)(2,1)}) %all-gather.13.cloned.1.call-update) | async-done | bytes 4128784 | tf_op jit(solution)/shard_map/all_gather | solution.py:315
  595.1 6.1 %fusion.1 = bf16[1,1,256,3584]{3,2,1,0:T(8,128)(2,1)} fusion(f32[256,3584]{1,0:T(8,128)} %fusion.4, bf16[576,256]{1,0:T(8,128)(2,1)S(1)} %bitcast.95, bf16[576,3584]{1,0:T(8,128)(2,1)} %all-gather.13.cloned.1.call-done), kind=kOutput, calls=%fused_computation.2 | convolution fusion | flops 1058799616 | bytes 9928704 | tf_op jit(solution)/shard_map/dot_general | solution.py:28
  (63 shorter events, 1.1 us)
Async XLA Ops:
  7.2 2.3 copy-start.23
  7.2 3.0 copy-start.24
  7.2 3.0 copy-start.22
  7.2 83.4 %all-gather.15.cloned.1.call-start = ((), (), s32[]{:S(2)}) async-start(), calls=%async_computation.10 | async-start | bytes 9175040 | tf_op jit(solution)/shard_map/all_gather | solution.py:315
  7.9 162.3 %all-gather.17.cloned.1.call-start = ((), (), s32[]{:S(2)}) async-start(), calls=%async_computation.11 | async-start | bytes 9175040 | tf_op jit(solution)/shard_map/all_gather | solution.py:315
  8.7 14.0 %copy-start.14 = (bf16[2,1,1,1,144,1024]{5,4,3,2,1,0:T(8,128)(2,1)S(1)}, bf16[2,1,1,1,144,1024]{5,4,3,2,1,0:T(8,128)(2,1)}, u32[]{:S(2)}) copy-start(bf16[2,1,1,1,144,1024]{5,4,3,2,1,0:T(8,128)(2,1)} %param.11) | copy-start | bytes 1769476
  8.7 14.0 %copy-start.15 = (bf16[2,1,1,1,144,1024]{5,4,3,2,1,0:T(8,128)(2,1)S(1)}, bf16[2,1,1,1,144,1024]{5,4,3,2,1,0:T(8,128)(2,1)}, u32[]{:S(2)}) copy-start(bf16[2,1,1,1,144,1024]{5,4,3,2,1,0:T(8,128)(2,1)} %param.12) | copy-start | bytes 1769476
  8.7 241.2 %all-gather.19.cloned.1.call-start = ((), (), s32[]{:S(2)}) async-start(), calls=%async_computation.12 | async-start | bytes 9175040 | tf_op jit(solution)/shard_map/all_gather | solution.py:315
  11.8 0.8 copy-start.4
  12.6 37.9 %all-to-all-start = ((bf16[16,8,4096]{2,1,0:T(8,128)(2,1)}), bf16[16,8,4096]{2,1,0:T(8,128)(2,1)S(1)}, u32[]{:S(2)}, u32[]{:S(2)}) async-start(bf16[16,8,4096]{2,1,0:T(8,128)(2,1)} %bitcast.4), calls=%async_computation | async-start | bytes 2097152 | tf_op jit(solution)/shard_map/all_to_all | solution.py:292
  90.6 3.1 copy-start
  97.0 1.0 copy-start.12
  98.0 0.7 copy-start.16
  98.7 0.7 copy-start.18
  249.9 96.0 %slice-start = ((s8[7340032]{0:T(1024)(128)(4,1)}), s8[4194304]{0:T(1024)(128)(4,1)S(1)}, s32[]{:S(2)}) async-start(s8[7340032]{0:T(1024)(128)(4,1)} %bitcast.61), calls=%async_computation.14 | async-start | bytes 8388608
  249.9 3.2 copy-start.2
  253.2 3.2 copy-start.3
  256.4 1.0 copy-start.17
  257.3 1.0 copy-start.19
  258.3 41.7 %copy-start.5 = (bf16[64,3584]{1,0:T(8,128)(2,1)S(1)}, bf16[64,3584]{1,0:T(8,128)(2,1)}, u32[]{:S(2)}) copy-start(bf16[64,3584]{1,0:T(8,128)(2,1)} %copy-done.4) | copy-start | bytes 1376260
  258.3 87.6 %slice-start.1 = ((s8[7340032]{0:T(1024)(128)(4,1)}), s8[3145728]{0:T(1024)(128)(4,1)S(1)}, s32[]{:S(2)}) async-start(s8[7340032]{0:T(1024)(128)(4,1)} %bitcast.61), calls=%async_computation.15 | async-start | bytes 6291456
  300.5 12.7 %collective-permute-start = (bf16[64,3584]{1,0:T(8,128)(2,1)S(1)}, bf16[64,3584]{1,0:T(8,128)(2,1)S(1)}, u32[]{:S(2)}, u32[]{:S(2)}) collective-permute-start(bf16[64,3584]{1,0:T(8,128)(2,1)S(1)} %post.4), channel_id=1, source_target_pairs={{0,64},{192,128},{1,65},{193,129},{2,66},{194,130},{3,67},{195,131... | collective-permute-start | bytes 1376264 | tf_op jit(solution)/shard_map/ppermute | solution.py:348
  313.1 0.8 copy-start.8
  358.4 1.0 copy-start.13
  359.4 1.0 copy-start.11
  360.3 30.8 %all-to-all-start.3 = ((bf16[16,8,4096]{2,1,0:T(8,128)(2,1)}), bf16[16,8,4096]{2,1,0:T(8,128)(2,1)S(1)}, u32[]{:S(2)}, u32[]{:S(2)}) async-start(bf16[16,8,4096]{2,1,0:T(8,128)(2,1)} %bitcast.86), calls=%async_computation.3 | async-start | bytes 2097152 | tf_op jit(solution)/shard_map/all_to_all | solution.py:292
  363.9 189.2 %all-gather.21.cloned.1.call-start = ((), (), s32[]{:S(2)}) async-start(), calls=%async_computation.13 | async-start | bytes 2949120 | tf_op jit(solution)/shard_map/all_gather | solution.py:358
  391.2 1.0 copy-start.9
  392.7 0.9 collective-permute-start.1
  393.6 1.6 copy-start.6
  395.2 31.5 %all-to-all-start.4 = ((bf16[16,8,4096]{2,1,0:T(8,128)(2,1)}), bf16[16,8,4096]{2,1,0:T(8,128)(2,1)S(1)}, u32[]{:S(2)}, u32[]{:S(2)}) async-start(bf16[16,8,4096]{2,1,0:T(8,128)(2,1)} %bitcast.25), calls=%async_computation.4 | async-start | bytes 2097152 | tf_op jit(solution)/shard_map/all_to_all | solution.py:292
  398.8 157.1 %all-gather.11.cloned.1.call-start = ((), (), s32[]{:S(2)}) async-start(), calls=%async_computation.8 | async-start | bytes 5160960 | tf_op jit(solution)/shard_map/all_gather | solution.py:315
  401.2 193.9 %all-gather.13.cloned.1.call-start = ((), (), s32[]{:S(2)}) async-start(), calls=%async_computation.9 | async-start | bytes 5160960 | tf_op jit(solution)/shard_map/all_gather | solution.py:315
  426.7 3.7 copy-start.1
  430.4 44.1 %copy-start.7 = (bf16[64,3584]{1,0:T(8,128)(2,1)S(1)}, bf16[64,3584]{1,0:T(8,128)(2,1)}, u32[]{:S(2)}) copy-start(bf16[64,3584]{1,0:T(8,128)(2,1)} %copy-done.6) | copy-start | bytes 1376260
  475.0 26.7 %collective-permute-start.2 = (bf16[64,3584]{1,0:T(8,128)(2,1)S(1)}, bf16[64,3584]{1,0:T(8,128)(2,1)S(1)}, u32[]{:S(2)}, u32[]{:S(2)}) collective-permute-start(bf16[64,3584]{1,0:T(8,128)(2,1)S(1)} %post.6), channel_id=1, source_target_pairs={{128,192},{64,0},{129,193},{65,1},{130,194},{66,2},{131,195},{67,3... | collective-permute-start | bytes 1376264 | tf_op jit(solution)/shard_map/ppermute | solution.py:348
  547.3 1.0 copy-start.10
  549.5 30.9 %all-to-all-start.7 = ((bf16[16,8,4096]{2,1,0:T(8,128)(2,1)}), bf16[16,8,4096]{2,1,0:T(8,128)(2,1)S(1)}, u32[]{:S(2)}, u32[]{:S(2)}) async-start(bf16[16,8,4096]{2,1,0:T(8,128)(2,1)} %bitcast.85), calls=%async_computation.7 | async-start | bytes 2097152 | tf_op jit(solution)/shard_map/all_to_all | solution.py:292
  562.0 18.8 %copy-start.20 = (bf16[1,1,64,3584]{3,2,1,0:T(8,128)(2,1)S(1)}, bf16[1,1,64,3584]{3,2,1,0:T(8,128)(2,1)}, u32[]{:S(2)}) copy-start(bf16[1,1,64,3584]{3,2,1,0:T(8,128)(2,1)} %select_bitcast_fusion) | copy-start | bytes 1376260
  562.0 33.0 %copy-start.21 = (bf16[4,1,144,256]{3,2,1,0:T(8,128)(2,1)S(1)}, bf16[4,1,144,256]{3,2,1,0:T(8,128)(2,1)}, u32[]{:S(2)}) copy-start(bf16[4,1,144,256]{3,2,1,0:T(8,128)(2,1)} %get-tuple-element.28) | copy-start | bytes 884740
Sparse Core Ops, SparseCore 0:
  9.8 80.7 all-gather.14
  92.4 77.7 all-gather.16
  172.1 77.7 all-gather.18
  366.8 36.2 all-gather.20
  404.8 61.8 all-gather.10
  549.6 45.4 all-gather.12

commit v2 on v1

--- a/solution.py
+++ b/solution.py
@@ -157,135 +157,223 @@
             rows_ref[MAIN:SLOTS, lo : lo + 128] = nin[k * 16 : (k + 1) * 16, :]
 
 
-def pack_chunk(grads, out_ref):
+def put_chunk(grads, out_ref, lead, base):
     c = lax.broadcasted_iota(I32, (MAIN, 128), 0)
     r = lax.broadcasted_iota(I32, (MAIN, 128), 1)
     fold = ones_where(r == (c & 7) * 16 + (c >> 3))
-    out_ref[:, 0:CH] = grads[0:MAIN]
     pieces = [grads[MAIN:SLOTS, k * 128 : (k + 1) * 128] for k in range(PIECES)]
     pieces.append(jnp.zeros((16, 128), BF))
-    out_ref[:, CH:PCH] = dot(fold, jnp.concatenate(pieces, axis=0)).astype(BF)
-
-
-def hidden_block(rows_ref, wd_ref, fup_ref, fgate_ref):
-    d_hidden = dot(rows_ref[...], wd_ref[...], NT)
-    return (d_hidden * fgate_ref[...]).astype(BF), (d_hidden * fup_ref[...]).astype(BF)
-
-
-def grads_block(dg, du, wg_ref, wu_ref):
-    total = None
-    for q in range(4):
-        cols = slice(q * 256, (q + 1) * 256)
-        term = dot(dg[q], wg_ref[:, cols], NT) + dot(du[q], wu_ref[:, cols], NT)
-        total = term if total is None else total + term
-    return total.astype(BF)
-
-
-def hidden_kernel(buf_ref, wd_ref, fup_ref, fgate_ref, rows_ref, dg_ref, du_ref):
-    @pl.when(pl.program_id(0) == 0)
-    def _():
-        unpack_rows(buf_ref, rows_ref)
-
-    dg_ref[0], du_ref[0] = hidden_block(rows_ref, wd_ref, fup_ref, fgate_ref)
-
-
-def hidden_pass(buf, wd, fup, fgate):
+    tail = dot(fold, jnp.concatenate(pieces, axis=0)).astype(BF)
+    if lead is None:
+        out_ref[:, pl.ds(base, CH)] = grads[0:MAIN]
+        out_ref[:, pl.ds(base + CH, 128)] = tail
+    else:
+        out_ref[lead, :, 0:CH] = grads[0:MAIN]
+        out_ref[lead, :, CH:PCH] = tail
+
+
+def hidden_part(rows_ref, wd, fup_ref, fgate_ref, lo, width):
+    d_hidden = dot(rows_ref[...], wd, NT)
+    cols = pl.ds(lo, width)
+    return (d_hidden * fgate_ref[:, cols]).astype(BF), (d_hidden * fup_ref[:, cols]).astype(BF)
+
+
+def shard_plan(shard):
+    half = shard // 2
+    return [(0, 0, shard), (3, 0, shard), (1, 0, shard), (2, 0, half), (2, half, half)]
+
+
+def fetch(src, dst, sem):
+    copy = pltpu.make_async_copy(src, dst, sem)
+    copy.start()
+    return copy
+
+
+def fetch_shards(srcs, dst_ref, plan, sems):
+    out = []
+    at = 0
+    for n, (_, _, width) in enumerate(plan):
+        out.append((fetch(srcs[n], dst_ref.at[pl.ds(at, width)], sems.at[n]), at))
+        at += width
+    return out
+
+
+def hidden_kernel(at_dir, me_ref, buf_hbm, fup_hbm, fgate_hbm, *rest):
+    wd_refs, rest = rest[:5], rest[5:]
+    rows_hbm, dgu_ref, buf_ref, rows_ref, wd_ref, fup_ref, fgate_ref, sems, f_sems = rest
+    plan = shard_plan(256)
+    buf_copy = fetch(buf_hbm, buf_ref, f_sems.at[2])
+    f_copies = [
+        fetch(fup_hbm.at[at_dir], fup_ref, f_sems.at[0]),
+        fetch(fgate_hbm.at[at_dir], fgate_ref, f_sems.at[1]),
+    ]
+    copies = fetch_shards(wd_refs, wd_ref, plan, sems)
+    buf_copy.wait()
+    unpack_rows(buf_ref, rows_ref)
+    rows_copy = fetch(rows_ref, rows_hbm, f_sems.at[3])
+    for copy in f_copies:
+        copy.wait()
+    for n, (shift, row, width) in enumerate(plan):
+        copy, at = copies[n]
+        copy.wait()
+        lo = pl.multiple_of(((me_ref[0] + shift) & 3) * 256 + row, 128)
+        dg, du = hidden_part(rows_ref, wd_ref[at : at + width], fup_ref, fgate_ref, lo, width)
+        dgu_ref[0, :, pl.ds(lo, width)] = dg
+        dgu_ref[1, :, pl.ds(lo, width)] = du
+    rows_copy.wait()
+
+
+IN_HBM = pl.BlockSpec(memory_space=pl.ANY)
+IN_SMEM = pl.BlockSpec(memory_space=pltpu.SMEM)
+IN_VMEM = pl.BlockSpec(memory_space=pltpu.VMEM)
+
+
+def hidden_pass(at_dir, me, buf, fup, fgate, wd):
     return pl.pallas_call(
-        hidden_kernel,
-        grid=(4,),
-        in_specs=[
-            pl.BlockSpec((MAIN, NCH * PCH), lambda i: (0, 0)),
-            pl.BlockSpec((256, D), lambda i: (i, 0)),
-            pl.BlockSpec((SLOTS, 256), lambda i: (0, i)),
-            pl.BlockSpec((SLOTS, 256), lambda i: (0, i)),
-        ],
-        out_specs=[
-            pl.BlockSpec((SLOTS, D), lambda i: (0, 0)),
-            pl.BlockSpec((1, SLOTS, 256), lambda i: (i, 0, 0)),
-            pl.BlockSpec((1, SLOTS, 256), lambda i: (i, 0, 0)),
-        ],
+        functools.partial(hidden_kernel, at_dir),
+        in_specs=[IN_SMEM] + [IN_HBM] * 8,
+        out_specs=[IN_HBM, IN_VMEM],
         out_shape=(
             jax.ShapeDtypeStruct((SLOTS, D), BF),
-            jax.ShapeDtypeStruct((4, SLOTS, 256), BF),
-            jax.ShapeDtypeStruct((4, SLOTS, 256), BF),
+            jax.ShapeDtypeStruct((2, SLOTS, FF), BF),
         ),
-        compiler_params=pltpu.CompilerParams(vmem_limit_bytes=24 << 20),
+        scratch_shapes=[
+            pltpu.VMEM((MAIN, NCH * PCH), BF),
+            pltpu.VMEM((SLOTS, D), BF),
+            pltpu.VMEM((FF, D), BF),
+            pltpu.VMEM((SLOTS, FF), F32),
+            pltpu.VMEM((SLOTS, FF), F32),
+            pltpu.SemaphoreType.DMA((5,)),
+            pltpu.SemaphoreType.DMA((4,)),
+        ],
+        compiler_params=pltpu.CompilerParams(vmem_limit_bytes=60 << 20),
         cost_estimate=pl.CostEstimate(flops=1_060_000_000, bytes_accessed=11_000_000, transcendentals=0),
         name="hidden_pass",
-    )(buf, wd, fup, fgate)
-
-
-def grads_kernel(dg_ref, du_ref, wg_ref, wu_ref, out_ref):
-    dg = [dg_ref[q] for q in range(4)]
-    du = [du_ref[q] for q in range(4)]
-    pack_chunk(grads_block(dg, du, wg_ref, wu_ref), out_ref)
-
-
-def grads_pass(dg, du, wg, wu):
+    )(me, buf, fup, fgate, *wd)
+
+
+def own_grads_kernel(me_ref, own, left, right, far_g, far_u, wg_hbm, wu_hbm, out_ref, d_ref, wg_ref, wu_ref, sems):
+    weights = [fetch(wg_hbm, wg_ref, sems.at[0]), fetch(wu_hbm, wu_ref, sems.at[1])]
+    copies = [
+        [fetch(own, d_ref.at[0], sems.at[2])],
+        [fetch(left, d_ref.at[1], sems.at[3])],
+        [fetch(right, d_ref.at[2], sems.at[4])],
+        [
+            fetch(far_g, d_ref.at[3, pl.ds(0, 1)], sems.at[5]),
+            fetch(far_u, d_ref.at[3, pl.ds(1, 1)], sems.at[6]),
+        ],
+    ]
+    for copy in weights:
+        copy.wait()
+    for n, shift in enumerate((0, 3, 1, 2)):
+        for copy in copies[n]:
+            copy.wait()
+        total = dot(d_ref[n, 0], wg_ref[...], NT) + dot(d_ref[n, 1], wu_ref[...], NT)
+        put_chunk(total.astype(BF), out_ref, (me_ref[0] + shift) & 3, None)
+
+
+def own_grads(me, own, left, right, far_g, far_u, wg, wu):
     return pl.pallas_call(
-        grads_kernel,
-        grid=(4,),
-        in_specs=[
-            pl.BlockSpec((4, SLOTS, 256), lambda i: (0, 0, 0)),
-            pl.BlockSpec((4, SLOTS, 256), lambda i: (0, 0, 0)),
-            pl.BlockSpec((CH, FF), lambda i: (i, 0)),
-            pl.BlockSpec((CH, FF), lambda i: (i, 0)),
+        own_grads_kernel,
+        in_specs=[IN_SMEM] + [IN_HBM] * 7,
+        out_specs=IN_VMEM,
+        out_shape=jax.ShapeDtypeStruct((4, MAIN, PCH), BF),
+        scratch_shapes=[
+            pltpu.VMEM((4, 2, SLOTS, FF), BF),
+            pltpu.VMEM((CH, FF), BF),
+            pltpu.VMEM((CH, FF), BF),
+            pltpu.SemaphoreType.DMA((7,)),
         ],
-        out_specs=pl.BlockSpec((MAIN, PCH), lambda i: (0, i)),
-        out_shape=jax.ShapeDtypeStruct((MAIN, NCH * PCH), BF),
-        compiler_params=pltpu.CompilerParams(vmem_limit_bytes=28 << 20),
-        cost_estimate=pl.CostEstimate(flops=2_120_000_000, bytes_accessed=17_000_000, transcendentals=0),
-        name="grads_pass",
-    )(dg, du, wg, wu)
-
-
-def expert_kernel(
-    buf_ref, wd_ref, fup_ref, fgate_ref, wg_ref, wu_ref, rows_ref, out_ref, dg_ref, du_ref
-):
-    i = pl.program_id(0)
-
-    @pl.when(i == 0)
-    def _():
-        unpack_rows(buf_ref, rows_ref)
-
-    @pl.when(i < 4)
-    def _():
-        dg_ref[i], du_ref[i] = hidden_block(rows_ref, wd_ref, fup_ref, fgate_ref)
-
-    @pl.when(i >= 4)
-    def _():
-        dg = [dg_ref[q] for q in range(4)]
-        du = [du_ref[q] for q in range(4)]
-        pack_chunk(grads_block(dg, du, wg_ref, wu_ref), out_ref)
-
-
-def expert_pass(buf, wd, fup, fgate, wg, wu):
-    first = lambda i: jnp.minimum(i, 3)
-    second = lambda i: jnp.maximum(i - 4, 0)
+        compiler_params=pltpu.CompilerParams(vmem_limit_bytes=60 << 20),
+        cost_estimate=pl.CostEstimate(flops=2_120_000_000, bytes_accessed=8_000_000, transcendentals=0),
+        name="own_grads",
+    )(me, own, left, right, far_g, far_u, wg, wu)
+
+
+def expert_kernel(at_dir, whole, me_ref, buf_hbm, fup_hbm, fgate_hbm, *rest):
+    wd_refs = rest[:5]
+    me = me_ref[0]
+    if whole:
+        wg_full, wu_full = rest[5:7]
+        rest = rest[7:]
+        gplan = [(k, 0, CH) for k in range(4)]
+        g_src = [wg_full.at[pl.ds(k * CH, CH)] for k in range(4)]
+        u_src = [wu_full.at[pl.ds(k * CH, CH)] for k in range(4)]
+    else:
+        g_src, wu_full = rest[5:10], rest[10]
+        rest = rest[11:]
+        gplan = shard_plan(CH)
+        u_src = [
+            wu_full.at[pl.ds(pl.multiple_of(((me + shift) & 3) * CH + row, 64), width)]
+            for shift, row, width in gplan
+        ]
+    (
+        rows_hbm, out_ref, buf_ref, rows_ref, wd_ref, wg_ref, wu_ref, fup_ref, fgate_ref, dg_ref, du_ref,
+        f_sems, d_sems, g_sems, u_sems,
+    ) = rest
+    plan = shard_plan(256)
+    buf_copy = fetch(buf_hbm, buf_ref, f_sems.at[2])
+    f_copies = [
+        fetch(fup_hbm.at[at_dir], fup_ref, f_sems.at[0]),
+        fetch(fgate_hbm.at[at_dir], fgate_ref, f_sems.at[1]),
+    ]
+    d_copies = fetch_shards(wd_refs, wd_ref, plan, d_sems)
+    g_copies = fetch_shards(g_src, wg_ref, gplan, g_sems)
+    u_copies = fetch_shards(u_src, wu_ref, gplan, u_sems)
+    buf_copy.wait()
+    unpack_rows(buf_ref, rows_ref)
+    rows_copy = fetch(rows_ref, rows_hbm, f_sems.at[3])
+    for copy in f_copies:
+        copy.wait()
+    for n, (shift, row, width) in enumerate(plan):
+        copy, at = d_copies[n]
+        copy.wait()
+        lo = pl.multiple_of(((me + shift) & 3) * 256 + row, 128)
+        dg, du = hidden_part(rows_ref, wd_ref[at : at + width], fup_ref, fgate_ref, lo, width)
+        dg_ref[:, pl.ds(lo, width)] = dg
+        du_ref[:, pl.ds(lo, width)] = du
+    for n in range(4):
+        shift = gplan[n][0]
+        last = (n, 4) if n == 3 and not whole else (n,)
+        for m in last:
+            g_copies[m][0].wait()
+            u_copies[m][0].wait()
+        at = g_copies[n][1]
+        total = dot(dg_ref[...], wg_ref[at : at + CH], NT) + dot(du_ref[...], wu_ref[at : at + CH], NT)
+        base = shift * PCH if whole else pl.multiple_of(((me + shift) & 3) * PCH, 128)
+        put_chunk(total.astype(BF), out_ref, None, base)
+    rows_copy.wait()
+
+
+def expert_pass(at_dir, me, buf, fup, fgate, wd, wg, wu):
+    whole = len(wg) == 1
     return pl.pallas_call(
-        expert_kernel,
-        grid=(8,),
-        in_specs=[
-            pl.BlockSpec((MAIN, NCH * PCH), lambda i: (0, 0)),
-            pl.BlockSpec((256, D), lambda i: (first(i), 0)),
-            pl.BlockSpec((SLOTS, 256), lambda i: (0, first(i))),
-            pl.BlockSpec((SLOTS, 256), lambda i: (0, first(i))),
-            pl.BlockSpec((CH, FF), lambda i: (second(i), 0)),
-            pl.BlockSpec((CH, FF), lambda i: (second(i), 0)),
-        ],
-        out_specs=[
-            pl.BlockSpec((SLOTS, D), lambda i: (0, 0)),
-            pl.BlockSpec((MAIN, PCH), lambda i: (0, second(i))),
-        ],
+        functools.partial(expert_kernel, at_dir, whole),
+        in_specs=[IN_SMEM] + [IN_HBM] * (9 + len(wg)),
+        out_specs=[IN_HBM, IN_VMEM],
         out_shape=(
             jax.ShapeDtypeStruct((SLOTS, D), BF),
             jax.ShapeDtypeStruct((MAIN, NCH * PCH), BF),
         ),
-        scratch_shapes=[pltpu.VMEM((4, SLOTS, 256), BF), pltpu.VMEM((4, SLOTS, 256), BF)],
-        compiler_params=pltpu.CompilerParams(vmem_limit_bytes=36 << 20),
+        scratch_shapes=[
+            pltpu.VMEM((MAIN, NCH * PCH), BF),
+            pltpu.VMEM((SLOTS, D), BF),
+            pltpu.VMEM((FF, D), BF),
+            pltpu.VMEM((D, FF), BF),
+            pltpu.VMEM((D, FF), BF),
+            pltpu.VMEM((SLOTS, FF), F32),
+            pltpu.VMEM((SLOTS, FF), F32),
+            pltpu.VMEM((SLOTS, FF), BF),
+            pltpu.VMEM((SLOTS, FF), BF),
+            pltpu.SemaphoreType.DMA((4,)),
+            pltpu.SemaphoreType.DMA((5,)),
+            pltpu.SemaphoreType.DMA((5,)),
+            pltpu.SemaphoreType.DMA((5,)),
+        ],
+        compiler_params=pltpu.CompilerParams(vmem_limit_bytes=60 << 20),
         cost_estimate=pl.CostEstimate(flops=3_200_000_000, bytes_accessed=28_000_000, transcendentals=0),
         name="expert_pass",
-    )(buf, wd, fup, fgate, wg, wu)
+    )(me, buf, fup, fgate, *wd, *wg, wu)
 
 
 def exchange(buf):
@@ -303,21 +391,39 @@
     return (flat * CAP + jnp.sum(same.astype(I32), axis=2)).reshape(2, TOK, 2)
 
 
+def shift_dp(value, step, sections):
+    pairs = [(s * 4 + i, s * 4 + (i + step) % 4) for s in sections for i in range(4)]
+    return lax.ppermute(value, ("pipe", "dp"), pairs)
+
+
+def tie(value, *others):
+    return lax.optimization_barrier((value,) + others)[0]
+
+
 def per_device(
     seed_grads, expert_routes, route_weights, saved_gate, saved_up, w_gate, w_up, w_down
 ):
     section = lax.axis_index("pipe")
+    dp = lax.axis_index("dp").astype(I32)
+    me = dp.reshape(1)
     first_up = section < 2
     first = jnp.where(first_up, 1, 0).astype(I32)
     order = jnp.stack([first, 1 - first])
+    every, outer, inner = (0, 1, 2, 3), (0, 3), (1, 2)
 
     def gather(x):
         return lax.all_gather(x, "dp", axis=0, tiled=True)
 
-    wd_full = gather(w_down[0, 0])
-    wg_in, wu_in = w_gate[0, 0], w_up[0, 0]
-    wg_full = gather(wg_in)
-    wu_full = gather(wu_in)
+    def near(x, sections):
+        return shift_dp(x, 1, sections), shift_dp(x, -1, sections)
+
+    def far(left, right, sections):
+        half = left.shape[0] // 2
+        return shift_dp(left[:half], 1, sections), shift_dp(right[half:], -1, sections)
+
+    wd_own, wg_own, wu_own = w_down[0, 0], w_gate[0, 0], w_up[0, 0]
+    wd_near = near(wd_own, every)
+    wg_near = near(tie(wg_own, *wd_near), inner)
 
     def ordered(x):
         return jnp.where(first_up, x[1], x[0]), jnp.where(first_up, x[0], x[1])
@@ -333,16 +439,36 @@
     moves = [[(0, 1), (3, 2)], [(1, 2), (2, 1)], [(2, 3), (1, 0)]]
     results = []
     held_rows = []
+    wg = None
     for step in range(4):
         at = step // 2
-        buf = exchange(pre(tgt_t[at], wts_t[at], cur))
+        outgoing = pre(tgt_t[at], wts_t[at], cur)
+        if step == 1:
+            outgoing = tie(outgoing, *wg)
+        buf = exchange(outgoing)
         if step == 0:
-            rows, dg, du = hidden_pass(buf, wd_full, fup[at], fgate[at])
-            packed = grads_pass(dg, du, wg_full, wu_full)
+            wd = (wd_own,) + wd_near + far(*[tie(w, buf) for w in wd_near], every)
+            rows, dgu = hidden_pass(at, me, buf, fup, fgate, wd)
+            dgu_near = near(tie(dgu, *wg_near), outer)
+            dgu_far = far(*dgu_near, outer)
+            sent = own_grads(
+                me, dgu, *dgu_near, *dgu_far, wg_own, wu_own
+            )
+            wu_full = gather(tie(wu_own, sent))
+            wg = (wg_own,) + wg_near + far(*[tie(w, sent) for w in wg_near], inner)
+            home = lax.all_to_all(
+                sent.reshape(4 * EXP, 8, PCH), ("dp", "expert"), split_axis=0, concat_axis=0, tiled=True
+            ).reshape(4, MAIN, PCH)
+            result = post(tgt[at], cur, home)
         else:
-            rows, packed = expert_pass(buf, wd_full, fup[at], fgate[at], wg_full, wu_full)
+            if step == 1:
+                hidden_all = lax.all_gather(tie(hidden, buf), "dp", axis=0)
+                wg_full = (gather(tie(wg_own, buf)),)
+            if step == 3:
+                wg = wg_full
+            rows, packed = expert_pass(at, me, buf, fup, fgate, wd, wg, wu_full)
+            result = post(tgt[at], cur, exchange(packed))
         held_rows.append(rows)
-        result = post(tgt[at], cur, exchange(packed))
         results.append(result)
         if step < 3:
             cur = lax.ppermute(result, "pipe", moves[step])
@@ -354,9 +480,7 @@
         first_up, jnp.stack([res_second, res_first]), jnp.stack([res_first, res_second])
     )[:, None]
 
-    mine = lax.axis_index("dp") * 256
-    hidden_all = lax.all_gather(hidden, "dp", axis=0)
-    hidden_mine = lax.dynamic_slice_in_dim(hidden_all, mine, 256, axis=3)
+    hidden_mine = lax.dynamic_slice_in_dim(hidden_all, dp * 256, 256, axis=3)
     rows_first = jnp.where(edge, held_rows[0], held_rows[1])
     rows_second = jnp.where(edge, held_rows[3], held_rows[2])
     contract = (((0,), (0,)), ((), ()))

time: 609 us -> 590 us (0.969); the launches traced: 608 us -> 581 us
  waiting for transfers between devices: 337 us -> 243 us
  starting transfers between devices: 26 us -> 75 us
  Pallas kernels: 55.3 us -> 84.1 us
  local copies, waits for them, and re-layouts: 25.2 us -> 16.8 us
    all_gather x5 -> x4, waiting for transfers between devices: 204 us -> 58.8 us  [gather(): return lax.all_gather(x, 'dp', axis=0, tiled=True)]
    ppermute x0 -> x12, waiting for transfers between devices: none -> 51.3 us  [shift_dp(): return lax.ppermute(value, ('pipe', 'dp'), pairs)]
    all_to_all x4 -> x3, waiting for transfers between devices: 95.8 us -> 53.5 us  [exchange(): lax.all_to_all(buf.reshape(EXP, 8, NCH * PCH), 'expert', split_axis=0, co...]
    pallas_call x5, Pallas kernels: 46.6 us -> 75.4 us  [the longest x3 57.2 us: expert_pass(): pl.pallas_call(functools.partial(expert_kernel, at_dir, whole), in_specs=...]
    ppermute x0 -> x12, starting transfers between devices: none -> 25.6 us  [shift_dp(): return lax.ppermute(value, ('pipe', 'dp'), pairs)]
    ppermute x3, waiting for transfers between devices: 35 us -> 58 us  [per_device(): cur = lax.ppermute(result, 'pipe', moves[step])]
    all_to_all x0 -> x1, waiting for transfers between devices: none -> 21.7 us  [per_device(): lax.all_to_all(sent.reshape(4 * EXP, 8, PCH), ('dp', 'expert'), split_axi...]
    all_to_all x0 -> x1, starting transfers between devices: none -> 18.3 us  [per_device(): lax.all_to_all(sent.reshape(4 * EXP, 8, PCH), ('dp', 'expert'), split_axi...]
  transfers between devices with their start and end apart: 13 -> 24, of which waited for: 10 -> 14; matrix products, arithmetic and copies ran while one was open for 2% -> 4% of each run, Pallas kernels for 6% -> 13%
where the time goes in v2:
time: 590 us; the launch traced here: 581 us
  waiting for transfers between devices  243 us (41%)
  blocking collectives  128 us (22%)
  Pallas kernels  84.1 us (14%)
  starting transfers between devices  75 us (13%)
  local copies, waits for them, and re-layouts  16.8 us (3%)
  between operations  14.6 us (2%)
  matrix products  11.8 us (2%)
  other arithmetic  6.89 us (1%)
    all_to_all x4, blocking collectives, exchange(): lax.all_to_all(buf.reshape(EXP, 8, NCH * PCH), 'expert', split_axis=0, co...  128 us
    all_gather x4, waiting for transfers between devices, gather(): return lax.all_gather(x, 'dp', axis=0, tiled=True)  58.8 us
    ppermute x3, waiting for transfers between devices, per_device(): cur = lax.ppermute(result, 'pipe', moves[step])  58 us
    pallas_call x3, Pallas kernels, expert_pass(): pl.pallas_call(functools.partial(expert_kernel, at_dir, whole), in_specs=...  57.2 us
    all_to_all x3, waiting for transfers between devices, exchange(): lax.all_to_all(buf.reshape(EXP, 8, NCH * PCH), 'expert', split_axis=0, co...  53.5 us
    ppermute x12, waiting for transfers between devices, shift_dp(): return lax.ppermute(value, ('pipe', 'dp'), pairs)  51.3 us
    ppermute x12, starting transfers between devices, shift_dp(): return lax.ppermute(value, ('pipe', 'dp'), pairs)  25.6 us
    all_to_all x1, waiting for transfers between devices, per_device(): lax.all_to_all(sent.reshape(4 * EXP, 8, PCH), ('dp', 'expert'), split_axi...  21.7 us
  transfers between devices with their start and end apart: 24, of which 14 were waited for; matrix products, arithmetic and copies ran while one was open for 4% of the time, Pallas kernels for 13%

profile of v2, /device:TPU:1, one launch (start us, length us, event | category | flops | bytes accessed | tf_op | source)
XLA Modules:
  0.0 580.8 jit_solution(12519915935053753519)
XLA Ops:
  7.2 2.2 collective-permute-start
  9.4 1.5 collective-permute-start.1
  10.9 0.8 copy.18
  12.3 0.7 select_bitcast_fusion.3
  13.0 1.2 select_bitcast_fusion.2.cur_ref
  14.2 1.6 pre.4
  15.8 9.6 %all-to-all-start = ((bf16[16,8,4096]{2,1,0:T(8,128)(2,1)}), bf16[16,8,4096]{2,1,0:T(8,128)(2,1)S(1)}, u32[]{:S(2)}, u32[]{:S(2)}) async-start(bf16[16,8,4096]{2,1,0:T(8,128)(2,1)} %bitcast.5), calls=%async_computation | async-start | bytes 2097152 | tf_op jit(solution)/shard_map/all_to_all | solution.py:380
  25.4 23.4 %collective-permute-done.rest_1_ = bf16[256,3584]{1,0:T(8,128)(2,1)} collective-permute-done((bf16[256,3584]{1,0:T(8,128)(2,1)}, bf16[256,3584]{1,0:T(8,128)(2,1)}, u32[]{:S(2)}, u32[]{:S(2)}) %collective-permute-start) | collective-permute-done | bytes 1835040 | tf_op jit(solution)/shard_map/ppermute | solution.py:396
  48.8 1.2 collective-permute-done.1.rest_2_
  50.0 2.0 collective-permute-start.4
  51.9 1.9 collective-permute-start.5
  53.8 1.0 copy-done.6
  54.8 2.2 slice.56
  57.0 1.6 collective-permute-start.2
  58.6 2.2 slice.57
  60.8 1.1 collective-permute-start.3
  62.0 2.3 prep.1
  64.2 1.0 copy-done
  65.2 1.0 copy-done.1
  66.2 11.9 %collective-permute-done.2.rest_3_ = bf16[128,3584]{1,0:T(8,128)(2,1)S(1)} collective-permute-done((bf16[128,3584]{1,0:T(8,128)(2,1)}, bf16[128,3584]{1,0:T(8,128)(2,1)S(1)}, u32[]{:S(2)}, u32[]{:S(2)}) %collective-permute-start.2) | collective-permute-done | bytes 917536 | tf_op jit(solution)/shard_map/ppermute | solution.py:396
  78.1 2.6 collective-permute-done.3.rest_4_
  80.8 9.1 %hidden_pass.1 = (bf16[144,3584]{1,0:T(8,128)(2,1)}, bf16[2,144,1024]{2,1,0:T(8,128)(2,1)}) custom-call(s32[1]{0:T(128)} %bitcast.1.me_ref, bf16[128,4096]{1,0:T(8,128)(2,1)} %bitcast.80, f32[2,144,1024]{2,1,0:T(8,128)} %copy-done, f32[2,144,1024]{2,1,0:T(8,128)} %copy-done.1, bf16[256,3584]{1,0:T(8,128)(2,1)} %bitcast.67, ...), custom_call_target="tpu_custom_call" | custom-call | flops 1060000000 | bytes 11000000 | tf_op jit(solution)/shard_map/hidden_pass/pallas_call | solution.py:232
  89.9 2.9 collective-permute-start.6
  92.8 3.6 collective-permute-start.7
  96.4 8.6 %collective-permute-done.6.left = bf16[2,144,1024]{2,1,0:T(8,128)(2,1)S(1)} collective-permute-done((bf16[2,144,1024]{2,1,0:T(8,128)(2,1)}, bf16[2,144,1024]{2,1,0:T(8,128)(2,1)S(1)}, u32[]{:S(2)}, u32[]{:S(2)}) %collective-permute-start.6) | collective-permute-done | bytes 589856 | tf_op jit(solution)/shard_map/ppermute | solution.py:396
  105.0 1.9 collective-permute-start.8
  107.0 4.6 collective-permute-start.9
  111.6 2.1 collective-permute-done.8.far_g
  113.7 1.5 collective-permute-done.9.far_u
  115.2 0.7 copy-done.14
  115.9 9.1 %own_grads.1 = bf16[4,128,1024]{2,1,0:T(8,128)(2,1)} custom-call(s32[1]{0:T(128)} %bitcast.1.me_ref, bf16[2,144,1024]{2,1,0:T(8,128)(2,1)} %get-tuple-element.29.own, bf16[2,144,1024]{2,1,0:T(8,128)(2,1)} %copy-done.11, bf16[2,144,1024]{2,1,0:T(8,128)(2,1)} %copy-done.12, bf16[1,144,1024]{2,1,0:T(8,128)(2,1)} %copy-done.13, ...), custom_call_target="tpu_custom_call" | custom-call | flops 2120000000 | bytes 8000000 | tf_op jit(solution)/shard_map/own_grads/pallas_call | solution.py:276
  125.1 18.3 %all-to-all-start.1 = ((bf16[64,8,1024]{2,1,0:T(8,128)(2,1)}), bf16[64,8,1024]{2,1,0:T(8,128)(2,1)S(1)}, u32[]{:S(2)}, u32[]{:S(2)}) async-start(bf16[64,8,1024]{2,1,0:T(8,128)(2,1)} %bitcast.86), calls=%async_computation.1 | async-start | bytes 2097152 | tf_op jit(solution)/shard_map/all_to_all | solution.py:459
  143.4 2.2 slice.60
  145.6 0.7 collective-permute-start.11
  146.3 2.2 slice.61
  148.5 1.6 collective-permute-start.12
  150.1 21.7 %all-to-all-done.1 = bf16[64,8,1024]{2,1,0:T(8,128)(2,1)S(1)} async-done(((bf16[64,8,1024]{2,1,0:T(8,128)(2,1)}), bf16[64,8,1024]{2,1,0:T(8,128)(2,1)S(1)}, u32[]{:S(2)}, u32[]{:S(2)}) %all-to-all-start.1) | async-done | bytes 1048608 | tf_op jit(solution)/shard_map/all_to_all | solution.py:459
  172.3 11.6 %collective-permute-start.10 = (bf16[64,3584]{1,0:T(8,128)(2,1)S(1)}, bf16[64,3584]{1,0:T(8,128)(2,1)S(1)}, u32[]{:S(2)}, u32[]{:S(2)}) collective-permute-start(bf16[64,3584]{1,0:T(8,128)(2,1)S(1)} %post.4), channel_id=1, source_target_pairs={{0,64},{192,128},{1,65},{193,129},{2,66},{194,130},{3,67},{195,131... | collective-permute-start | bytes 1376264 | tf_op jit(solution)/shard_map/ppermute | solution.py:474
  183.9 9.8 %collective-permute-done.10.cur_ref = bf16[64,3584]{1,0:T(8,128)(2,1)S(1)} collective-permute-done((bf16[64,3584]{1,0:T(8,128)(2,1)S(1)}, bf16[64,3584]{1,0:T(8,128)(2,1)S(1)}, u32[]{:S(2)}, u32[]{:S(2)}) %collective-permute-start.10) | collective-permute-done | bytes 458784 | tf_op jit(solution)/shard_map/ppermute | solution.py:474
  194.4 33.6 %all_to_all.40 = bf16[16,8,4096]{2,1,0:T(8,128)(2,1)} all-to-all(bf16[16,8,4096]{2,1,0:T(8,128)(2,1)S(1)} %bitcast.55), channel_id=1, replica_groups=mesh['pipe'=4,'expert'=16,'dp'=4] {'expert'}, dimensions={0} | all-to-all | bytes 2097152 | tf_op jit(solution)/shard_map/all_to_all | solution.py:380
  228.1 19.2 %expert_pass.3 = (bf16[144,3584]{1,0:T(8,128)(2,1)}, bf16[128,4096]{1,0:T(8,128)(2,1)}) custom-call(s32[1]{0:T(128)} %bitcast.1.me_ref, bf16[128,4096]{1,0:T(8,128)(2,1)} %bitcast.78, f32[2,144,1024]{2,1,0:T(8,128)} %copy-done, f32[2,144,1024]{2,1,0:T(8,128)} %copy-done.1, bf16[256,3584]{1,0:T(8,128)(2,1)} %bitcast.68, ...), custom_call_target="tpu_custom_call" | custom-call | flops 3200000000 | bytes 28000000 | tf_op jit(solution)/shard_map/expert_pass/pallas_call | solution.py:350
  247.3 31.4 %all_to_all.41 = bf16[16,8,4096]{2,1,0:T(8,128)(2,1)S(1)} all-to-all(bf16[16,8,4096]{2,1,0:T(8,128)(2,1)} %bitcast.88), channel_id=1, replica_groups=mesh['pipe'=4,'expert'=16,'dp'=4] {'expert'}, dimensions={0} | all-to-all | bytes 2097152 | tf_op jit(solution)/shard_map/all_to_all | solution.py:380
  279.2 0.7 collective-permute-start.13
  280.1 0.6 pre.6
  280.8 31.6 %all_to_all.42 = bf16[16,8,4096]{2,1,0:T(8,128)(2,1)} all-to-all(bf16[16,8,4096]{2,1,0:T(8,128)(2,1)S(1)} %bitcast.58), channel_id=1, replica_groups=mesh['pipe'=4,'expert'=16,'dp'=4] {'expert'}, dimensions={0} | all-to-all | bytes 2097152 | tf_op jit(solution)/shard_map/all_to_all | solution.py:380
  312.3 19.2 %expert_pass.4 = (bf16[144,3584]{1,0:T(8,128)(2,1)}, bf16[128,4096]{1,0:T(8,128)(2,1)}) custom-call(s32[1]{0:T(128)} %bitcast.1.me_ref, bf16[128,4096]{1,0:T(8,128)(2,1)} %bitcast.79, f32[2,144,1024]{2,1,0:T(8,128)} %copy-done, f32[2,144,1024]{2,1,0:T(8,128)} %copy-done.1, bf16[256,3584]{1,0:T(8,128)(2,1)} %bitcast.69, ...), custom_call_target="tpu_custom_call" | custom-call | flops 3200000000 | bytes 28000000 | tf_op jit(solution)/shard_map/expert_pass/pallas_call | solution.py:350
  331.6 31.6 %all_to_all.43 = bf16[16,8,4096]{2,1,0:T(8,128)(2,1)S(1)} all-to-all(bf16[16,8,4096]{2,1,0:T(8,128)(2,1)} %bitcast.87), channel_id=1, replica_groups=mesh['pipe'=4,'expert'=16,'dp'=4] {'expert'}, dimensions={0} | all-to-all | bytes 2097152 | tf_op jit(solution)/shard_map/all_to_all | solution.py:380
  363.7 1.3 collective-permute-start.14
  365.0 48.2 %collective-permute-done.14.cur_ref = bf16[64,3584]{1,0:T(8,128)(2,1)S(1)} collective-permute-done((bf16[64,3584]{1,0:T(8,128)(2,1)S(1)}, bf16[64,3584]{1,0:T(8,128)(2,1)S(1)}, u32[]{:S(2)}, u32[]{:S(2)}) %collective-permute-start.14) | collective-permute-done | bytes 458784 | tf_op jit(solution)/shard_map/ppermute | solution.py:474
  413.2 1.6 pre.7
  414.8 4.1 all-to-all-start.6
  419.2 27.6 %all-to-all-done.6 = bf16[16,8,4096]{2,1,0:T(8,128)(2,1)S(1)} async-done(((bf16[16,8,4096]{2,1,0:T(8,128)(2,1)}), bf16[16,8,4096]{2,1,0:T(8,128)(2,1)S(1)}, u32[]{:S(2)}, u32[]{:S(2)}) %all-to-all-start.6) | async-done | bytes 1048608 | tf_op jit(solution)/shard_map/all_to_all | solution.py:380
  446.8 1.0 copy-done.5
  447.8 18.7 %expert_pass.5 = (bf16[144,3584]{1,0:T(8,128)(2,1)}, bf16[128,4096]{1,0:T(8,128)(2,1)}) custom-call(s32[1]{0:T(128)} %bitcast.1.me_ref, bf16[128,4096]{1,0:T(8,128)(2,1)} %bitcast.77, f32[2,144,1024]{2,1,0:T(8,128)} %copy-done, f32[2,144,1024]{2,1,0:T(8,128)} %copy-done.1, bf16[256,3584]{1,0:T(8,128)(2,1)} %bitcast.70, ...), custom_call_target="tpu_custom_call" | custom-call | flops 3200000000 | bytes 28000000 | tf_op jit(solution)/shard_map/expert_pass/pallas_call | solution.py:350
  466.5 2.4 broadcast_select_fusion
  469.0 1.1 broadcast_select_fusion.1
  470.1 3.6 all-to-all-start.7
  473.7 1.9 constant_dynamic-slice_fusion
  475.7 25.9 %all-to-all-done.7 = bf16[16,8,4096]{2,1,0:T(8,128)(2,1)S(1)} async-done(((bf16[16,8,4096]{2,1,0:T(8,128)(2,1)}), bf16[16,8,4096]{2,1,0:T(8,128)(2,1)S(1)}, u32[]{:S(2)}, u32[]{:S(2)}) %all-to-all-start.7) | async-done | bytes 1048608 | tf_op jit(solution)/shard_map/all_to_all | solution.py:380
  502.1 1.1 maximum_select_fusion
  503.2 12.2 %all-gather.13.cloned.1.call-done = bf16[576,3584]{1,0:T(8,128)(2,1)} async-done(((bf16[144,3584]{1,0:T(8,128)(2,1)}), bf16[576,3584]{1,0:T(8,128)(2,1)}) %all-gather.13.cloned.1.call-update) | async-done | bytes 4128784 | tf_op jit(solution)/shard_map/all_gather | solution.py:415
  515.4 5.7 fusion.4
  521.1 46.6 %all-gather.11.cloned.1.call-done = bf16[576,3584]{1,0:T(8,128)(2,1)} async-done(((bf16[144,3584]{1,0:T(8,128)(2,1)}), bf16[576,3584]{1,0:T(8,128)(2,1)}) %all-gather.11.cloned.1.call-update) | async-done | bytes 4128784 | tf_op jit(solution)/shard_map/all_gather | solution.py:415
  567.7 6.1 %fusion.1 = bf16[1,1,256,3584]{3,2,1,0:T(8,128)(2,1)} fusion(f32[256,3584]{1,0:T(8,128)} %fusion.4, bf16[576,256]{1,0:T(8,128)(2,1)S(1)} %bitcast.84, bf16[576,3584]{1,0:T(8,128)(2,1)} %all-gather.11.cloned.1.call-done), kind=kOutput, calls=%fused_computation.2 | convolution fusion | flops 1058799616 | bytes 9928704 | tf_op jit(solution)/shard_map/dot_general | solution.py:28
  (64 shorter events, 4.2 us)
Async XLA Ops:
  7.2 41.7 %collective-permute-start = (bf16[256,3584]{1,0:T(8,128)(2,1)}, bf16[256,3584]{1,0:T(8,128)(2,1)}, u32[]{:S(2)}, u32[]{:S(2)}) collective-permute-start(bf16[256,3584]{1,0:T(8,128)(2,1)} %bitcast.65), channel_id=1, source_target_pairs={{0,1},{1,2},{2,3},{3,0},{64,65},{65,66},{66,67},{67,64},{128,129},... | collective-permute-start | bytes 5505032 | tf_op jit(solution)/shard_map/ppermute | solution.py:396
  9.4 40.6 %collective-permute-start.1 = (bf16[256,3584]{1,0:T(8,128)(2,1)}, bf16[256,3584]{1,0:T(8,128)(2,1)}, u32[]{:S(2)}, u32[]{:S(2)}) collective-permute-start(bf16[256,3584]{1,0:T(8,128)(2,1)} %bitcast.66), channel_id=1, source_target_pairs={{0,3},{1,0},{2,1},{3,2},{64,67},{65,64},{66,65},{67,66},{128,131},... | collective-permute-start | bytes 5505032 | tf_op jit(solution)/shard_map/ppermute | solution.py:396
  14.2 47.7 %copy-start.2 = (bf16[2,1,1,1,144,1024]{5,4,3,2,1,0:T(8,128)(2,1)S(1)}, bf16[2,1,1,1,144,1024]{5,4,3,2,1,0:T(8,128)(2,1)}, u32[]{:S(2)}) copy-start(bf16[2,1,1,1,144,1024]{5,4,3,2,1,0:T(8,128)(2,1)} %param.11) | copy-start | bytes 1769476
  14.2 47.7 %copy-start.3 = (bf16[2,1,1,1,144,1024]{5,4,3,2,1,0:T(8,128)(2,1)S(1)}, bf16[2,1,1,1,144,1024]{5,4,3,2,1,0:T(8,128)(2,1)}, u32[]{:S(2)}) copy-start(bf16[2,1,1,1,144,1024]{5,4,3,2,1,0:T(8,128)(2,1)} %param.12) | copy-start | bytes 1769476
  15.8 38.0 %all-to-all-start = ((bf16[16,8,4096]{2,1,0:T(8,128)(2,1)}), bf16[16,8,4096]{2,1,0:T(8,128)(2,1)S(1)}, u32[]{:S(2)}, u32[]{:S(2)}) async-start(bf16[16,8,4096]{2,1,0:T(8,128)(2,1)} %bitcast.5), calls=%async_computation | async-start | bytes 2097152 | tf_op jit(solution)/shard_map/all_to_all | solution.py:380
  25.4 202.7 %all-gather.7.cloned.1.call-start = ((), (), s32[]{:S(2)}) async-start(), calls=%async_computation.8 | async-start | bytes 9175040 | tf_op jit(solution)/shard_map/all_gather | solution.py:415
  50.0 39.9 %collective-permute-start.4 = (bf16[896,1024]{1,0:T(8,128)(2,1)}, bf16[896,1024]{1,0:T(8,128)(2,1)}, u32[]{:S(2)}, u32[]{:S(2)}) collective-permute-start(bf16[896,1024]{1,0:T(8,128)(2,1)} %bitcast.71), channel_id=1, source_target_pairs={{64,65},{65,66},{66,67},{67,64},{128,129},{129,130},{130,131},{131... | collective-permute-start | bytes 5505032 | tf_op jit(solution)/shard_map/ppermute | solution.py:396
  51.9 38.0 %collective-permute-start.5 = (bf16[896,1024]{1,0:T(8,128)(2,1)}, bf16[896,1024]{1,0:T(8,128)(2,1)}, u32[]{:S(2)}, u32[]{:S(2)}) collective-permute-start(bf16[896,1024]{1,0:T(8,128)(2,1)} %bitcast.72), channel_id=1, source_target_pairs={{64,67},{65,64},{66,65},{67,66},{128,131},{129,128},{130,129},{131... | collective-permute-start | bytes 5505032 | tf_op jit(solution)/shard_map/ppermute | solution.py:396
  53.8 1.0 copy-start.6
  57.0 21.1 %collective-permute-start.2 = (bf16[128,3584]{1,0:T(8,128)(2,1)}, bf16[128,3584]{1,0:T(8,128)(2,1)S(1)}, u32[]{:S(2)}, u32[]{:S(2)}) collective-permute-start(bf16[128,3584]{1,0:T(8,128)(2,1)} %slice.56), channel_id=1, source_target_pairs={{0,1},{1,2},{2,3},{3,0},{64,65},{65,66},{66,67},{67,64},{128,129},... | collective-permute-start | bytes 2752520 | tf_op jit(solution)/shard_map/ppermute | solution.py:396
  60.8 20.0 %collective-permute-start.3 = (bf16[128,3584]{1,0:T(8,128)(2,1)}, bf16[128,3584]{1,0:T(8,128)(2,1)}, u32[]{:S(2)}, u32[]{:S(2)}) collective-permute-start(bf16[128,3584]{1,0:T(8,128)(2,1)} %slice.57), channel_id=1, source_target_pairs={{0,3},{1,0},{2,1},{3,2},{64,67},{65,64},{66,65},{67,66},{128,131},... | collective-permute-start | bytes 2752520 | tf_op jit(solution)/shard_map/ppermute | solution.py:396
  64.2 1.0 copy-start
  65.2 1.0 copy-start.1
  78.1 2.6 copy-start.4
  89.9 15.1 %collective-permute-start.6 = (bf16[2,144,1024]{2,1,0:T(8,128)(2,1)}, bf16[2,144,1024]{2,1,0:T(8,128)(2,1)S(1)}, u32[]{:S(2)}, u32[]{:S(2)}) collective-permute-start(bf16[2,144,1024]{2,1,0:T(8,128)(2,1)} %get-tuple-element.29.own), channel_id=1, source_target_pairs={{0,1},{1,2},{2,3},{3,0},{192,193},{193,194},{194,195},{195,192},{4... | collective-permute-start | bytes 1769480 | tf_op jit(solution)/shard_map/ppermute | solution.py:396
  92.8 14.1 %collective-permute-start.7 = (bf16[2,144,1024]{2,1,0:T(8,128)(2,1)}, bf16[2,144,1024]{2,1,0:T(8,128)(2,1)S(1)}, u32[]{:S(2)}, u32[]{:S(2)}) collective-permute-start(bf16[2,144,1024]{2,1,0:T(8,128)(2,1)} %get-tuple-element.29.own), channel_id=1, source_target_pairs={{0,3},{1,0},{2,1},{3,2},{192,195},{193,192},{194,193},{195,194},{4... | collective-permute-start | bytes 1769480 | tf_op jit(solution)/shard_map/ppermute | solution.py:396
  105.0 10.2 %copy-start.11 = (bf16[2,144,1024]{2,1,0:T(8,128)(2,1)}, bf16[2,144,1024]{2,1,0:T(8,128)(2,1)S(1)}, u32[]{:S(2)}) copy-start(bf16[2,144,1024]{2,1,0:T(8,128)(2,1)S(1)} %collective-permute-done.6.left) | copy-start | bytes 1769476
  105.0 8.7 %collective-permute-start.8 = (bf16[1,144,1024]{2,1,0:T(8,128)(2,1)S(1)}, bf16[1,144,1024]{2,1,0:T(8,128)(2,1)S(1)}, u32[]{:S(2)}, u32[]{:S(2)}) collective-permute-start(bf16[1,144,1024]{2,1,0:T(8,128)(2,1)S(1)} %slice.64), channel_id=1, source_target_pairs={{0,1},{1,2},{2,3},{3,0},{192,193},{193,194},{194,195},{195,192},{4... | collective-permute-start | bytes 884744 | tf_op jit(solution)/shard_map/ppermute | solution.py:396
  107.0 8.3 %copy-start.12 = (bf16[2,144,1024]{2,1,0:T(8,128)(2,1)}, bf16[2,144,1024]{2,1,0:T(8,128)(2,1)S(1)}, u32[]{:S(2)}) copy-start(bf16[2,144,1024]{2,1,0:T(8,128)(2,1)S(1)} %collective-permute-done.7.right) | copy-start | bytes 1769476
  107.0 8.2 %collective-permute-start.9 = (bf16[1,144,1024]{2,1,0:T(8,128)(2,1)S(1)}, bf16[1,144,1024]{2,1,0:T(8,128)(2,1)S(1)}, u32[]{:S(2)}, u32[]{:S(2)}) collective-permute-start(bf16[1,144,1024]{2,1,0:T(8,128)(2,1)S(1)} %slice.65), channel_id=1, source_target_pairs={{0,3},{1,0},{2,1},{3,2},{192,195},{193,192},{194,193},{195,194},{4... | collective-permute-start | bytes 884744 | tf_op jit(solution)/shard_map/ppermute | solution.py:396
  113.7 1.5 copy-start.13
  115.2 0.7 copy-start.14
  125.1 46.7 %all-to-all-start.1 = ((bf16[64,8,1024]{2,1,0:T(8,128)(2,1)}), bf16[64,8,1024]{2,1,0:T(8,128)(2,1)S(1)}, u32[]{:S(2)}, u32[]{:S(2)}) async-start(bf16[64,8,1024]{2,1,0:T(8,128)(2,1)} %bitcast.86), calls=%async_computation.1 | async-start | bytes 2097152 | tf_op jit(solution)/shard_map/all_to_all | solution.py:459
  143.4 275.8 %all-gather.9.cloned.1.call-start = ((), (), s32[]{:S(2)}) async-start(), calls=%async_computation.9 | async-start | bytes 9175040 | tf_op jit(solution)/shard_map/all_gather | solution.py:415
  145.6 48.8 %collective-permute-start.11 = (bf16[448,1024]{1,0:T(8,128)(2,1)}, bf16[448,1024]{1,0:T(8,128)(2,1)S(1)}, u32[]{:S(2)}, u32[]{:S(2)}) collective-permute-start(bf16[448,1024]{1,0:T(8,128)(2,1)} %slice.60), channel_id=1, source_target_pairs={{64,65},{65,66},{66,67},{67,64},{128,129},{129,130},{130,131},{131... | collective-permute-start | bytes 2752520 | tf_op jit(solution)/shard_map/ppermute | solution.py:396
  148.5 45.9 %collective-permute-start.12 = (bf16[448,1024]{1,0:T(8,128)(2,1)}, bf16[448,1024]{1,0:T(8,128)(2,1)}, u32[]{:S(2)}, u32[]{:S(2)}) collective-permute-start(bf16[448,1024]{1,0:T(8,128)(2,1)} %slice.61), channel_id=1, source_target_pairs={{64,67},{65,64},{66,65},{67,66},{128,131},{129,128},{130,129},{131... | collective-permute-start | bytes 2752520 | tf_op jit(solution)/shard_map/ppermute | solution.py:396
  172.3 21.4 %collective-permute-start.10 = (bf16[64,3584]{1,0:T(8,128)(2,1)S(1)}, bf16[64,3584]{1,0:T(8,128)(2,1)S(1)}, u32[]{:S(2)}, u32[]{:S(2)}) collective-permute-start(bf16[64,3584]{1,0:T(8,128)(2,1)S(1)} %post.4), channel_id=1, source_target_pairs={{0,64},{192,128},{1,65},{193,129},{2,66},{194,130},{3,67},{195,131... | collective-permute-start | bytes 1376264 | tf_op jit(solution)/shard_map/ppermute | solution.py:474
  194.4 33.7 %copy-start.7 = (bf16[448,1024]{1,0:T(8,128)(2,1)}, bf16[448,1024]{1,0:T(8,128)(2,1)S(1)}, u32[]{:S(2)}) copy-start(bf16[448,1024]{1,0:T(8,128)(2,1)S(1)} %collective-permute-done.11.rest_8_) | copy-start | bytes 2752516
  228.0 245.7 %all-gather.15.cloned.1.call-start = ((), (), s32[]{:S(2)}) async-start(), calls=%async_computation.12 | async-start | bytes 2949120 | tf_op jit(solution)/shard_map/all_gather | solution.py:465
  279.2 0.9 collective-permute-start.13
  363.7 49.5 %collective-permute-start.14 = (bf16[64,3584]{1,0:T(8,128)(2,1)S(1)}, bf16[64,3584]{1,0:T(8,128)(2,1)S(1)}, u32[]{:S(2)}, u32[]{:S(2)}) collective-permute-start(bf16[64,3584]{1,0:T(8,128)(2,1)S(1)} %post.6), channel_id=1, source_target_pairs={{128,192},{64,0},{129,193},{65,1},{130,194},{66,2},{131,195},{67,3... | collective-permute-start | bytes 1376264 | tf_op jit(solution)/shard_map/ppermute | solution.py:474
  414.8 32.0 %all-to-all-start.6 = ((bf16[16,8,4096]{2,1,0:T(8,128)(2,1)}), bf16[16,8,4096]{2,1,0:T(8,128)(2,1)S(1)}, u32[]{:S(2)}, u32[]{:S(2)}) async-start(bf16[16,8,4096]{2,1,0:T(8,128)(2,1)} %bitcast.29), calls=%async_computation.6 | async-start | bytes 2097152 | tf_op jit(solution)/shard_map/all_to_all | solution.py:380
  418.8 96.5 %all-gather.13.cloned.1.call-start = ((), (), s32[]{:S(2)}) async-start(), calls=%async_computation.11 | async-start | bytes 5160960 | tf_op jit(solution)/shard_map/all_gather | solution.py:415
  446.8 1.0 copy-start.5
  466.5 2.5 copy-start.10
  468.9 98.8 %all-gather.11.cloned.1.call-start = ((), (), s32[]{:S(2)}) async-start(), calls=%async_computation.10 | async-start | bytes 5160960 | tf_op jit(solution)/shard_map/all_gather | solution.py:415
  470.1 31.5 %all-to-all-start.7 = ((bf16[16,8,4096]{2,1,0:T(8,128)(2,1)}), bf16[16,8,4096]{2,1,0:T(8,128)(2,1)S(1)}, u32[]{:S(2)}, u32[]{:S(2)}) async-start(bf16[16,8,4096]{2,1,0:T(8,128)(2,1)} %bitcast.85), calls=%async_computation.7 | async-start | bytes 2097152 | tf_op jit(solution)/shard_map/all_to_all | solution.py:380
  475.7 39.7 %copy-start.8 = (bf16[4,1,144,256]{3,2,1,0:T(8,128)(2,1)S(1)}, bf16[4,1,144,256]{3,2,1,0:T(8,128)(2,1)}, u32[]{:S(2)}) copy-start(bf16[4,1,144,256]{3,2,1,0:T(8,128)(2,1)} %get-tuple-element.47) | copy-start | bytes 884740
  515.4 52.3 %copy-start.9 = (bf16[4,1,144,256]{3,2,1,0:T(8,128)(2,1)S(1)}, bf16[4,1,144,256]{3,2,1,0:T(8,128)(2,1)}, u32[]{:S(2)}) copy-start(bf16[4,1,144,256]{3,2,1,0:T(8,128)(2,1)} %get-tuple-element.46) | copy-start | bytes 884740
Sparse Core Ops, SparseCore 0:
  125.2 99.4 all-gather.6
  228.1 98.5 all-gather.8
  365.1 68.9 all-gather.14
  469.0 46.2 all-gather.12
  517.0 50.6 all-gather.10

commit v3 on v2

--- a/solution.py
+++ b/solution.py
@@ -178,49 +178,48 @@
     return (d_hidden * fgate_ref[:, cols]).astype(BF), (d_hidden * fup_ref[:, cols]).astype(BF)
 
 
-def shard_plan(shard):
+def halves_plan(shard):
     half = shard // 2
-    return [(0, 0, shard), (3, 0, shard), (1, 0, shard), (2, 0, half), (2, half, half)]
-
-
-def fetch(src, dst, sem):
-    copy = pltpu.make_async_copy(src, dst, sem)
-    copy.start()
-    return copy
-
-
-def fetch_shards(srcs, dst_ref, plan, sems):
-    out = []
-    at = 0
-    for n, (_, _, width) in enumerate(plan):
-        out.append((fetch(srcs[n], dst_ref.at[pl.ds(at, width)], sems.at[n]), at))
-        at += width
-    return out
-
-
-def hidden_kernel(at_dir, me_ref, buf_hbm, fup_hbm, fgate_hbm, *rest):
-    wd_refs, rest = rest[:5], rest[5:]
-    rows_hbm, dgu_ref, buf_ref, rows_ref, wd_ref, fup_ref, fgate_ref, sems, f_sems = rest
-    plan = shard_plan(256)
-    buf_copy = fetch(buf_hbm, buf_ref, f_sems.at[2])
-    f_copies = [
-        fetch(fup_hbm.at[at_dir], fup_ref, f_sems.at[0]),
-        fetch(fgate_hbm.at[at_dir], fgate_ref, f_sems.at[1]),
-    ]
-    copies = fetch_shards(wd_refs, wd_ref, plan, sems)
-    buf_copy.wait()
-    unpack_rows(buf_ref, rows_ref)
-    rows_copy = fetch(rows_ref, rows_hbm, f_sems.at[3])
-    for copy in f_copies:
-        copy.wait()
-    for n, (shift, row, width) in enumerate(plan):
-        copy, at = copies[n]
-        copy.wait()
-        lo = pl.multiple_of(((me_ref[0] + shift) & 3) * 256 + row, 128)
-        dg, du = hidden_part(rows_ref, wd_ref[at : at + width], fup_ref, fgate_ref, lo, width)
-        dgu_ref[0, :, pl.ds(lo, width)] = dg
-        dgu_ref[1, :, pl.ds(lo, width)] = du
-    rows_copy.wait()
+    pieces = [(0, 0, shard)]
+    groups = [(0, [0])]
+    for shift, parts in ((3, False), (1, False), (2, True)):
+        mine = []
+        for row, width in ((0, half), (half, half)) if parts else ((0, shard),):
+            mine.append(len(pieces))
+            pieces.append((shift, row, width))
+        groups.append((shift, mine))
+    return pieces, groups
+
+
+class Stream:
+    def __init__(self, sems, ahead):
+        self.sems, self.ahead, self.todo, self.flying, self.done = sems, ahead, [], [], 0
+
+    def add(self, src, dst):
+        self.todo.append((src, dst))
+        return len(self.todo) - 1
+
+    def start(self, upto):
+        while len(self.flying) < min(upto, len(self.todo)):
+            n = len(self.flying)
+            copy = pltpu.make_async_copy(*self.todo[n], self.sems.at[n])
+            copy.start()
+            self.flying.append(copy)
+
+    def wait(self, n):
+        self.start(n + 1 + self.ahead)
+        while self.done <= n:
+            self.flying[self.done].wait()
+            self.done += 1
+
+
+def hidden_stage(stream, groups, ids, me, rows_ref, wd_ref, fup_ref, fgate_ref, store):
+    for n, (shift, members) in enumerate(groups):
+        for m in members:
+            stream.wait(ids[m])
+        lo = pl.multiple_of(((me + shift) & 3) * 256, 128)
+        dg, du = hidden_part(rows_ref, wd_ref[n * 256 : (n + 1) * 256], fup_ref, fgate_ref, lo, 256)
+        store(lo, dg, du)
 
 
 IN_HBM = pl.BlockSpec(memory_space=pl.ANY)
@@ -228,23 +227,49 @@
 IN_VMEM = pl.BlockSpec(memory_space=pltpu.VMEM)
 
 
+def add_shards(stream, srcs, pieces, dst_ref):
+    at = 0
+    ids = []
+    for src, (_, _, width) in zip(srcs, pieces):
+        ids.append(stream.add(src, dst_ref.at[pl.ds(at, width)]))
+        at += width
+    return ids
+
+
+def hidden_kernel(at_dir, me_ref, buf_hbm, fup_hbm, fgate_hbm, *rest):
+    pieces, groups = halves_plan(256)
+    wd_refs, rest = rest[: len(pieces)], rest[len(pieces) :]
+    dgu_ref, buf_ref, rows_ref, wd_ref, fup_ref, fgate_ref, sems = rest
+    stream = Stream(sems, 4)
+    first = stream.add(buf_hbm, buf_ref)
+    ids = add_shards(stream, wd_refs[:1], pieces[:1], wd_ref)
+    stream.add(fup_hbm.at[at_dir], fup_ref)
+    act = stream.add(fgate_hbm.at[at_dir], fgate_ref)
+    ids += add_shards(stream, wd_refs[1:], pieces[1:], wd_ref.at[pl.ds(256, FF - 256)])
+    stream.wait(first)
+    unpack_rows(buf_ref, rows_ref)
+    stream.wait(act)
+
+    def store(lo, dg, du):
+        dgu_ref[0, :, pl.ds(lo, 256)] = dg
+        dgu_ref[1, :, pl.ds(lo, 256)] = du
+
+    hidden_stage(stream, groups, ids, me_ref[0], rows_ref, wd_ref, fup_ref, fgate_ref, store)
+
+
 def hidden_pass(at_dir, me, buf, fup, fgate, wd):
     return pl.pallas_call(
         functools.partial(hidden_kernel, at_dir),
-        in_specs=[IN_SMEM] + [IN_HBM] * 8,
-        out_specs=[IN_HBM, IN_VMEM],
-        out_shape=(
-            jax.ShapeDtypeStruct((SLOTS, D), BF),
-            jax.ShapeDtypeStruct((2, SLOTS, FF), BF),
-        ),
+        in_specs=[IN_SMEM] + [IN_HBM] * (3 + len(wd)),
+        out_specs=IN_VMEM,
+        out_shape=jax.ShapeDtypeStruct((2, SLOTS, FF), BF),
         scratch_shapes=[
             pltpu.VMEM((MAIN, NCH * PCH), BF),
             pltpu.VMEM((SLOTS, D), BF),
             pltpu.VMEM((FF, D), BF),
             pltpu.VMEM((SLOTS, FF), F32),
             pltpu.VMEM((SLOTS, FF), F32),
-            pltpu.SemaphoreType.DMA((5,)),
-            pltpu.SemaphoreType.DMA((4,)),
+            pltpu.SemaphoreType.DMA((3 + len(wd),)),
         ],
         compiler_params=pltpu.CompilerParams(vmem_limit_bytes=60 << 20),
         cost_estimate=pl.CostEstimate(flops=1_060_000_000, bytes_accessed=11_000_000, transcendentals=0),
@@ -253,23 +278,20 @@
 
 
 def own_grads_kernel(me_ref, own, left, right, far_g, far_u, wg_hbm, wu_hbm, out_ref, d_ref, wg_ref, wu_ref, sems):
-    weights = [fetch(wg_hbm, wg_ref, sems.at[0]), fetch(wu_hbm, wu_ref, sems.at[1])]
-    copies = [
-        [fetch(own, d_ref.at[0], sems.at[2])],
-        [fetch(left, d_ref.at[1], sems.at[3])],
-        [fetch(right, d_ref.at[2], sems.at[4])],
-        [
-            fetch(far_g, d_ref.at[3, pl.ds(0, 1)], sems.at[5]),
-            fetch(far_u, d_ref.at[3, pl.ds(1, 1)], sems.at[6]),
-        ],
-    ]
-    for copy in weights:
-        copy.wait()
+    srcs = [own.at[0], left.at[0], right.at[0], far_g.at[0], own.at[1], left.at[1], right.at[1], far_u.at[0]]
+    stream = Stream(sems, 10)
+    stream.add(wg_hbm, wg_ref)
+    for n in range(4):
+        stream.add(srcs[n], d_ref.at[0, pl.ds(n * SLOTS, SLOTS)])
+    stream.add(wu_hbm, wu_ref)
+    for n in range(4):
+        stream.add(srcs[4 + n], d_ref.at[1, pl.ds(n * SLOTS, SLOTS)])
+    stream.wait(4)
+    total = dot(d_ref[0], wg_ref[...], NT)
+    stream.wait(9)
+    total = (total + dot(d_ref[1], wu_ref[...], NT)).astype(BF)
     for n, shift in enumerate((0, 3, 1, 2)):
-        for copy in copies[n]:
-            copy.wait()
-        total = dot(d_ref[n, 0], wg_ref[...], NT) + dot(d_ref[n, 1], wu_ref[...], NT)
-        put_chunk(total.astype(BF), out_ref, (me_ref[0] + shift) & 3, None)
+        put_chunk(total[n * SLOTS : (n + 1) * SLOTS], out_ref, (me_ref[0] + shift) & 3, None)
 
 
 def own_grads(me, own, left, right, far_g, far_u, wg, wu):
@@ -279,10 +301,10 @@
         out_specs=IN_VMEM,
         out_shape=jax.ShapeDtypeStruct((4, MAIN, PCH), BF),
         scratch_shapes=[
-            pltpu.VMEM((4, 2, SLOTS, FF), BF),
+            pltpu.VMEM((2, 4 * SLOTS, FF), BF),
             pltpu.VMEM((CH, FF), BF),
             pltpu.VMEM((CH, FF), BF),
-            pltpu.SemaphoreType.DMA((7,)),
+            pltpu.SemaphoreType.DMA((10,)),
         ],
         compiler_params=pltpu.CompilerParams(vmem_limit_bytes=60 << 20),
         cost_estimate=pl.CostEstimate(flops=2_120_000_000, bytes_accessed=8_000_000, transcendentals=0),
@@ -291,70 +313,58 @@
 
 
 def expert_kernel(at_dir, whole, me_ref, buf_hbm, fup_hbm, fgate_hbm, *rest):
-    wd_refs = rest[:5]
+    pieces, groups = halves_plan(256)
+    wd_refs, rest = rest[: len(pieces)], rest[len(pieces) :]
     me = me_ref[0]
+    gpieces, ggroups = halves_plan(CH)
+    count = 1 if whole else len(gpieces)
+    g_src, wu_full, rest = rest[:count], rest[count], rest[count + 1 :]
     if whole:
-        wg_full, wu_full = rest[5:7]
-        rest = rest[7:]
-        gplan = [(k, 0, CH) for k in range(4)]
-        g_src = [wg_full.at[pl.ds(k * CH, CH)] for k in range(4)]
-        u_src = [wu_full.at[pl.ds(k * CH, CH)] for k in range(4)]
+        gpieces, ggroups = [(k, 0, CH) for k in range(4)], [(k, [k]) for k in range(4)]
+        starts = [k * CH for k in range(4)]
+        g_src = [g_src[0].at[pl.ds(row, CH)] for row in starts]
     else:
-        g_src, wu_full = rest[5:10], rest[10]
-        rest = rest[11:]
-        gplan = shard_plan(CH)
-        u_src = [
-            wu_full.at[pl.ds(pl.multiple_of(((me + shift) & 3) * CH + row, 64), width)]
-            for shift, row, width in gplan
-        ]
-    (
-        rows_hbm, out_ref, buf_ref, rows_ref, wd_ref, wg_ref, wu_ref, fup_ref, fgate_ref, dg_ref, du_ref,
-        f_sems, d_sems, g_sems, u_sems,
-    ) = rest
-    plan = shard_plan(256)
-    buf_copy = fetch(buf_hbm, buf_ref, f_sems.at[2])
-    f_copies = [
-        fetch(fup_hbm.at[at_dir], fup_ref, f_sems.at[0]),
-        fetch(fgate_hbm.at[at_dir], fgate_ref, f_sems.at[1]),
-    ]
-    d_copies = fetch_shards(wd_refs, wd_ref, plan, d_sems)
-    g_copies = fetch_shards(g_src, wg_ref, gplan, g_sems)
-    u_copies = fetch_shards(u_src, wu_ref, gplan, u_sems)
-    buf_copy.wait()
+        starts = [pl.multiple_of(((me + shift) & 3) * CH + row, 64) for shift, row, _ in gpieces]
+    u_src = [wu_full.at[pl.ds(row, width)] for row, (_, _, width) in zip(starts, gpieces)]
+    out_ref, buf_ref, rows_ref, wd_ref, wg_ref, wu_ref, fup_ref, fgate_ref, dg_ref, du_ref, sems = rest
+    stream = Stream(sems, 4)
+    first = stream.add(buf_hbm, buf_ref)
+    ids = add_shards(stream, wd_refs[:1], pieces[:1], wd_ref)
+    stream.add(fup_hbm.at[at_dir], fup_ref)
+    act = stream.add(fgate_hbm.at[at_dir], fgate_ref)
+    ids += add_shards(stream, wd_refs[1:], pieces[1:], wd_ref.at[pl.ds(256, FF - 256)])
+    grad_ids = []
+    at = 0
+    for n, (_, _, width) in enumerate(gpieces):
+        place = pl.ds(at, width)
+        grad_ids.append((stream.add(g_src[n], wg_ref.at[place]), stream.add(u_src[n], wu_ref.at[place])))
+        at += width
+    stream.wait(first)
     unpack_rows(buf_ref, rows_ref)
-    rows_copy = fetch(rows_ref, rows_hbm, f_sems.at[3])
-    for copy in f_copies:
-        copy.wait()
-    for n, (shift, row, width) in enumerate(plan):
-        copy, at = d_copies[n]
-        copy.wait()
-        lo = pl.multiple_of(((me + shift) & 3) * 256 + row, 128)
-        dg, du = hidden_part(rows_ref, wd_ref[at : at + width], fup_ref, fgate_ref, lo, width)
-        dg_ref[:, pl.ds(lo, width)] = dg
-        du_ref[:, pl.ds(lo, width)] = du
-    for n in range(4):
-        shift = gplan[n][0]
-        last = (n, 4) if n == 3 and not whole else (n,)
-        for m in last:
-            g_copies[m][0].wait()
-            u_copies[m][0].wait()
-        at = g_copies[n][1]
-        total = dot(dg_ref[...], wg_ref[at : at + CH], NT) + dot(du_ref[...], wu_ref[at : at + CH], NT)
+    stream.wait(act)
+
+    def store(lo, dg, du):
+        dg_ref[:, pl.ds(lo, 256)] = dg
+        du_ref[:, pl.ds(lo, 256)] = du
+
+    hidden_stage(stream, groups, ids, me, rows_ref, wd_ref, fup_ref, fgate_ref, store)
+    for n, (shift, members) in enumerate(ggroups):
+        for m in members:
+            stream.wait(grad_ids[m][1])
+        at = slice(n * CH, (n + 1) * CH)
+        total = dot(dg_ref[...], wg_ref[at], NT) + dot(du_ref[...], wu_ref[at], NT)
         base = shift * PCH if whole else pl.multiple_of(((me + shift) & 3) * PCH, 128)
         put_chunk(total.astype(BF), out_ref, None, base)
-    rows_copy.wait()
 
 
 def expert_pass(at_dir, me, buf, fup, fgate, wd, wg, wu):
     whole = len(wg) == 1
+    copies = 3 + len(wd) + 2 * (4 if whole else len(wg))
     return pl.pallas_call(
         functools.partial(expert_kernel, at_dir, whole),
-        in_specs=[IN_SMEM] + [IN_HBM] * (9 + len(wg)),
-        out_specs=[IN_HBM, IN_VMEM],
-        out_shape=(
-            jax.ShapeDtypeStruct((SLOTS, D), BF),
-            jax.ShapeDtypeStruct((MAIN, NCH * PCH), BF),
-        ),
+        in_specs=[IN_SMEM] + [IN_HBM] * (4 + len(wd) + len(wg)),
+        out_specs=IN_VMEM,
+        out_shape=jax.ShapeDtypeStruct((MAIN, NCH * PCH), BF),
         scratch_shapes=[
             pltpu.VMEM((MAIN, NCH * PCH), BF),
             pltpu.VMEM((SLOTS, D), BF),
@@ -365,15 +375,46 @@
             pltpu.VMEM((SLOTS, FF), F32),
             pltpu.VMEM((SLOTS, FF), BF),
             pltpu.VMEM((SLOTS, FF), BF),
-            pltpu.SemaphoreType.DMA((4,)),
-            pltpu.SemaphoreType.DMA((5,)),
-            pltpu.SemaphoreType.DMA((5,)),
-            pltpu.SemaphoreType.DMA((5,)),
+            pltpu.SemaphoreType.DMA((copies,)),
         ],
         compiler_params=pltpu.CompilerParams(vmem_limit_bytes=60 << 20),
         cost_estimate=pl.CostEstimate(flops=3_200_000_000, bytes_accessed=28_000_000, transcendentals=0),
         name="expert_pass",
     )(me, buf, fup, fgate, *wd, *wg, wu)
+
+
+def down_kernel(ha_ref, hb_ref, bufa_ref, bufb_ref, out_ref, rows_ref):
+    r = lax.broadcasted_iota(I32, (128, MAIN), 0)
+    c = lax.broadcasted_iota(I32, (128, MAIN), 1)
+    spread = ones_where(c == (r & 15) * 8 + (r >> 4))
+    total = None
+    for h_ref, buf_ref in ((ha_ref, bufa_ref), (hb_ref, bufb_ref)):
+        for rep in range(4):
+            lo = rep * SLOTS
+            block = slice(rep * MAIN, (rep + 1) * MAIN)
+            rows_ref[lo : lo + MAIN, :] = buf_ref[block, 0:CH]
+            nin = dot(spread, buf_ref[block, CH:PCH]).astype(BF)
+            for k in range(PIECES):
+                rows_ref[lo + MAIN : lo + SLOTS, k * 128 : (k + 1) * 128] = nin[k * 16 : (k + 1) * 16, :]
+        term = dot(h_ref[...], rows_ref[...])
+        total = term if total is None else total + term
+    out_ref[...] = total.astype(BF)
+
+
+def down_pass(ha, hb, bufa, bufb):
+    packed = pl.BlockSpec((4 * MAIN, PCH), lambda j: (0, j))
+    whole = pl.BlockSpec((256, 4 * SLOTS), lambda j: (0, 0))
+    return pl.pallas_call(
+        down_kernel,
+        grid=(NCH,),
+        in_specs=[whole, whole, packed, packed],
+        out_specs=pl.BlockSpec((256, CH), lambda j: (0, j)),
+        out_shape=jax.ShapeDtypeStruct((256, D), BF),
+        scratch_shapes=[pltpu.VMEM((4 * SLOTS, CH), BF)],
+        compiler_params=pltpu.CompilerParams(vmem_limit_bytes=60 << 20),
+        cost_estimate=pl.CostEstimate(flops=2_120_000_000, bytes_accessed=11_000_000, transcendentals=0),
+        name="down_pass",
+    )(ha, hb, bufa, bufb)
 
 
 def exchange(buf):
@@ -423,7 +464,6 @@
 
     wd_own, wg_own, wu_own = w_down[0, 0], w_gate[0, 0], w_up[0, 0]
     wd_near = near(wd_own, every)
-    wg_near = near(tie(wg_own, *wd_near), inner)
 
     def ordered(x):
         return jnp.where(first_up, x[1], x[0]), jnp.where(first_up, x[0], x[1])
@@ -435,26 +475,28 @@
     wts_t = [w.T for w in wts]
     cur = jnp.where(first_up, seed_grads[1], seed_grads[0])
     fup, fgate, hidden = prep(order, saved_gate[:, 0, 0, 0], saved_up[:, 0, 0, 0])
-
+    wg_near = near(tie(wg_own, hidden, *wd_near), inner)
+
+    edge = jnp.logical_or(section == 0, section == 3)
     moves = [[(0, 1), (3, 2)], [(1, 2), (2, 1)], [(2, 3), (1, 0)]]
     results = []
-    held_rows = []
-    wg = None
+    bufs = []
     for step in range(4):
         at = step // 2
         outgoing = pre(tgt_t[at], wts_t[at], cur)
         if step == 1:
             outgoing = tie(outgoing, *wg)
+        if step == 2:
+            outgoing = tie(outgoing, buf_first)
         buf = exchange(outgoing)
+        bufs.append(buf)
         if step == 0:
             wd = (wd_own,) + wd_near + far(*[tie(w, buf) for w in wd_near], every)
-            rows, dgu = hidden_pass(at, me, buf, fup, fgate, wd)
+            dgu = hidden_pass(at, me, buf, fup, fgate, wd)
             dgu_near = near(tie(dgu, *wg_near), outer)
             dgu_far = far(*dgu_near, outer)
-            sent = own_grads(
-                me, dgu, *dgu_near, *dgu_far, wg_own, wu_own
-            )
-            wu_full = gather(tie(wu_own, sent))
+            sent = own_grads(me, dgu, *dgu_near, *dgu_far, wg_own, wu_own)
+            wu_full = gather(tie(wu_own, *dgu_far))
             wg = (wg_own,) + wg_near + far(*[tie(w, sent) for w in wg_near], inner)
             home = lax.all_to_all(
                 sent.reshape(4 * EXP, 8, PCH), ("dp", "expert"), split_axis=0, concat_axis=0, tiled=True
@@ -462,18 +504,19 @@
             result = post(tgt[at], cur, home)
         else:
             if step == 1:
-                hidden_all = lax.all_gather(tie(hidden, buf), "dp", axis=0)
                 wg_full = (gather(tie(wg_own, buf)),)
+                buf_first = jnp.where(edge, bufs[0], bufs[1])
+                all_first = gather(buf_first)
+                hidden_all = lax.all_gather(tie(hidden, buf_first), "dp", axis=0)
             if step == 3:
                 wg = wg_full
-            rows, packed = expert_pass(at, me, buf, fup, fgate, wd, wg, wu_full)
+                all_second = gather(jnp.where(edge, bufs[3], bufs[2]))
+            packed = expert_pass(at, me, buf, fup, fgate, wd, wg, wu_full)
             result = post(tgt[at], cur, exchange(packed))
-        held_rows.append(rows)
         results.append(result)
         if step < 3:
             cur = lax.ppermute(result, "pipe", moves[step])
 
-    edge = jnp.logical_or(section == 0, section == 3)
     res_first = jnp.where(edge, results[0], results[1])
     res_second = jnp.where(edge, results[3], results[2])
     input_grads = jnp.where(
@@ -481,12 +524,9 @@
     )[:, None]
 
     hidden_mine = lax.dynamic_slice_in_dim(hidden_all, dp * 256, 256, axis=3)
-    rows_first = jnp.where(edge, held_rows[0], held_rows[1])
-    rows_second = jnp.where(edge, held_rows[3], held_rows[2])
-    contract = (((0,), (0,)), ((), ()))
-    total = dot(hidden_mine[:, 0].reshape(4 * SLOTS, 256), gather(rows_first), contract)
-    total = total + dot(hidden_mine[:, 1].reshape(4 * SLOTS, 256), gather(rows_second), contract)
-    return input_grads, total.astype(BF)[None, None]
+    hidden_t = hidden_mine.transpose(1, 3, 0, 2).reshape(2, 256, 4 * SLOTS)
+    down_grads = down_pass(hidden_t[0], hidden_t[1], all_first, all_second)
+    return input_grads, down_grads[None, None]
 
 
 def solution(mesh):

time: 590 us -> 493 us (0.84); the launches traced: 581 us -> 492 us
  waiting for transfers between devices: 243 us -> 204 us
  blocking collectives: 128 us -> 98 us
  Pallas kernels: 84.1 us -> 71.7 us
  matrix products: 11.8 us -> 0 us
    all_gather x4, waiting for transfers between devices: 58.8 us -> 0.03 us  [gather(): return lax.all_gather(x, 'dp', axis=0, tiled=True)]
    all_to_all x4 -> x3, blocking collectives: 128 us -> 98 us  [exchange(): lax.all_to_all(buf.reshape(EXP, 8, NCH * PCH), 'expert', split_axis=0, co...]
    all_to_all x3 -> x4, waiting for transfers between devices: 53.5 us -> 76.1 us  [exchange(): lax.all_to_all(buf.reshape(EXP, 8, NCH * PCH), 'expert', split_axis=0, co...]
    pallas_call x3, Pallas kernels: 57.2 us -> 41.1 us  [expert_pass(): pl.pallas_call(functools.partial(expert_kernel, at_dir, whole), in_specs=...]
    dot_general x2 -> x0, matrix products: 11.8 us -> none  [dot(): return lax.dot_general(a, b, dims, preferred_element_type=F32)]
    pallas_call x0 -> x1, Pallas kernels: none -> 7.89 us  [down_pass(): pl.pallas_call(down_kernel, grid=(NCH,), in_specs=[whole, whole, packed,...]
    all_to_all x3 -> x4, starting transfers between devices: 17.2 us -> 20.4 us  [exchange(): lax.all_to_all(buf.reshape(EXP, 8, NCH * PCH), 'expert', split_axis=0, co...]
  transfers between devices with their start and end apart: 24 -> 25, of which waited for: 14 -> 13; matrix products, arithmetic and copies ran while one was open for 4% -> 4% of each run, Pallas kernels for 13% -> 13%
where the time goes in v3:
time: 493 us; the launch traced here: 492 us
  waiting for transfers between devices  204 us (41%)
  blocking collectives  98 us (20%)
  starting transfers between devices  78.9 us (16%)
  Pallas kernels  71.7 us (15%)
  local copies, waits for them, and re-layouts  18.2 us (4%)
  between operations  14.2 us (3%)
  other arithmetic  6.96 us (1%)
    all_to_all x3, blocking collectives, exchange(): lax.all_to_all(buf.reshape(EXP, 8, NCH * PCH), 'expert', split_axis=0, co...  98 us
    all_to_all x4, waiting for transfers between devices, exchange(): lax.all_to_all(buf.reshape(EXP, 8, NCH * PCH), 'expert', split_axis=0, co...  76.1 us
    ppermute x3, waiting for transfers between devices, per_device(): cur = lax.ppermute(result, 'pipe', moves[step])  54.6 us
    ppermute x12, waiting for transfers between devices, shift_dp(): return lax.ppermute(value, ('pipe', 'dp'), pairs)  51.1 us
    pallas_call x3, Pallas kernels, expert_pass(): pl.pallas_call(functools.partial(expert_kernel, at_dir, whole), in_specs=...  41.1 us
    ppermute x12, starting transfers between devices, shift_dp(): return lax.ppermute(value, ('pipe', 'dp'), pairs)  25.5 us
    all_to_all x1, waiting for transfers between devices, per_device(): lax.all_to_all(sent.reshape(4 * EXP, 8, PCH), ('dp', 'expert'), split_axi...  21.7 us
    all_to_all x4, starting transfers between devices, exchange(): lax.all_to_all(buf.reshape(EXP, 8, NCH * PCH), 'expert', split_axis=0, co...  20.4 us
  transfers between devices with their start and end apart: 25, of which 13 were waited for; matrix products, arithmetic and copies ran while one was open for 4% of the time, Pallas kernels for 13%

profile of v3, /device:TPU:1, one launch (start us, length us, event | category | flops | bytes accessed | tf_op | source)
XLA Modules:
  0.0 492.2 jit_solution(5650304173046439317)
XLA Ops:
  7.2 2.2 collective-permute-start
  9.4 1.5 collective-permute-start.1
  10.9 0.8 copy.29
  12.3 0.7 select_bitcast_fusion.3
  13.0 1.2 select_bitcast_fusion.2.cur_ref
  14.2 1.6 pre.4
  15.9 9.6 %all-to-all-start = ((bf16[16,8,4096]{2,1,0:T(8,128)(2,1)}), bf16[16,8,4096]{2,1,0:T(8,128)(2,1)S(1)}, u32[]{:S(2)}, u32[]{:S(2)}) async-start(bf16[16,8,4096]{2,1,0:T(8,128)(2,1)} %bitcast.5), calls=%async_computation | async-start | bytes 2097152 | tf_op jit(solution)/shard_map/all_to_all | solution.py:421
  25.6 2.3 prep.1
  27.8 1.0 copy-done
  28.8 1.1 copy-done.1
  29.9 18.9 %collective-permute-done.rest_1_ = bf16[256,3584]{1,0:T(8,128)(2,1)} collective-permute-done((bf16[256,3584]{1,0:T(8,128)(2,1)}, bf16[256,3584]{1,0:T(8,128)(2,1)}, u32[]{:S(2)}, u32[]{:S(2)}) %collective-permute-start) | collective-permute-done | bytes 1835040 | tf_op jit(solution)/shard_map/ppermute | solution.py:437
  48.8 1.2 collective-permute-done.1.rest_2_
  50.0 1.9 collective-permute-start.4
  51.9 1.9 collective-permute-start.5
  53.8 2.5 slice.58
  56.3 1.6 collective-permute-start.2
  57.9 2.2 slice.59
  60.1 1.1 collective-permute-start.3
  61.2 16.3 %collective-permute-done.2.rest_3_ = bf16[128,3584]{1,0:T(8,128)(2,1)S(1)} collective-permute-done((bf16[128,3584]{1,0:T(8,128)(2,1)}, bf16[128,3584]{1,0:T(8,128)(2,1)S(1)}, u32[]{:S(2)}, u32[]{:S(2)}) %collective-permute-start.2) | collective-permute-done | bytes 917536 | tf_op jit(solution)/shard_map/ppermute | solution.py:437
  77.5 2.5 collective-permute-done.3.rest_4_
  80.0 0.9 copy-done.5
  80.9 7.5 %hidden_pass.1.own = bf16[2,144,1024]{2,1,0:T(8,128)(2,1)} custom-call(s32[1]{0:T(128)} %bitcast.1.me_ref, bf16[128,4096]{1,0:T(8,128)(2,1)} %bitcast.81, f32[2,144,1024]{2,1,0:T(8,128)} %copy-done, f32[2,144,1024]{2,1,0:T(8,128)} %copy-done.1, bf16[256,3584]{1,0:T(8,128)(2,1)} %bitcast.68, bf16[256,3584]{1,0:T(8,128)(2,1)} %collective-permute-done.rest_1_, ...), custom_call_target="tpu_custom_call" | custom-call | flops 1060000000 | bytes 11000000 | tf_op jit(solution)/shard_map/hidden_pass/pallas_call | solution.py:261
  88.5 2.9 collective-permute-start.6
  91.4 3.6 collective-permute-start.7
  95.0 8.6 %collective-permute-done.6.left = bf16[2,144,1024]{2,1,0:T(8,128)(2,1)S(1)} collective-permute-done((bf16[2,144,1024]{2,1,0:T(8,128)(2,1)}, bf16[2,144,1024]{2,1,0:T(8,128)(2,1)S(1)}, u32[]{:S(2)}, u32[]{:S(2)}) %collective-permute-start.6) | collective-permute-done | bytes 589856 | tf_op jit(solution)/shard_map/ppermute | solution.py:437
  103.6 1.9 collective-permute-start.8
  105.5 4.6 collective-permute-start.9
  110.1 2.1 collective-permute-done.8.far_g
  112.2 1.5 collective-permute-done.9.far_u
  113.8 0.7 copy-done.15
  114.5 6.5 %own_grads.1 = bf16[4,128,1024]{2,1,0:T(8,128)(2,1)} custom-call(s32[1]{0:T(128)} %bitcast.1.me_ref, bf16[2,144,1024]{2,1,0:T(8,128)(2,1)} %hidden_pass.1.own, bf16[2,144,1024]{2,1,0:T(8,128)(2,1)} %copy-done.12, bf16[2,144,1024]{2,1,0:T(8,128)(2,1)} %copy-done.13, bf16[1,144,1024]{2,1,0:T(8,128)(2,1)} %copy-done.14, bf16[1,144,1024]{2,1,0:T(8,128)(2,1)} %copy-done.15, ...), custom_call_target="tpu_custom_call" | custom-call | flops 2120000000 | bytes 8000000 | tf_op jit(solution)/shard_map/own_grads/pallas_call | solution.py:298
  121.0 18.0 %all-to-all-start.1 = ((bf16[64,8,1024]{2,1,0:T(8,128)(2,1)}), bf16[64,8,1024]{2,1,0:T(8,128)(2,1)S(1)}, u32[]{:S(2)}, u32[]{:S(2)}) async-start(bf16[64,8,1024]{2,1,0:T(8,128)(2,1)} %bitcast.90), calls=%async_computation.1 | async-start | bytes 2097152 | tf_op jit(solution)/shard_map/all_to_all | solution.py:501
  139.0 2.2 slice.62
  141.2 0.7 collective-permute-start.11
  141.9 2.3 slice.63
  144.2 1.6 collective-permute-start.12
  145.8 21.7 %all-to-all-done.1 = bf16[64,8,1024]{2,1,0:T(8,128)(2,1)S(1)} async-done(((bf16[64,8,1024]{2,1,0:T(8,128)(2,1)}), bf16[64,8,1024]{2,1,0:T(8,128)(2,1)S(1)}, u32[]{:S(2)}, u32[]{:S(2)}) %all-to-all-start.1) | async-done | bytes 1048608 | tf_op jit(solution)/shard_map/all_to_all | solution.py:501
  168.0 12.5 %collective-permute-start.10 = (bf16[64,3584]{1,0:T(8,128)(2,1)S(1)}, bf16[64,3584]{1,0:T(8,128)(2,1)S(1)}, u32[]{:S(2)}, u32[]{:S(2)}) collective-permute-start(bf16[64,3584]{1,0:T(8,128)(2,1)S(1)} %post.4), channel_id=1, source_target_pairs={{0,64},{192,128},{1,65},{193,129},{2,66},{194,130},{3,67},{195,131... | collective-permute-start | bytes 1376264 | tf_op jit(solution)/shard_map/ppermute | solution.py:518
  180.5 9.6 %collective-permute-done.10.cur_ref = bf16[64,3584]{1,0:T(8,128)(2,1)S(1)} collective-permute-done((bf16[64,3584]{1,0:T(8,128)(2,1)S(1)}, bf16[64,3584]{1,0:T(8,128)(2,1)S(1)}, u32[]{:S(2)}, u32[]{:S(2)}) %collective-permute-start.10) | collective-permute-done | bytes 458784 | tf_op jit(solution)/shard_map/ppermute | solution.py:518
  190.8 33.6 %all_to_all.40 = bf16[16,8,4096]{2,1,0:T(8,128)(2,1)} all-to-all(bf16[16,8,4096]{2,1,0:T(8,128)(2,1)S(1)} %bitcast.57), channel_id=1, replica_groups=mesh['pipe'=4,'expert'=16,'dp'=4] {'expert'}, dimensions={0} | all-to-all | bytes 2097152 | tf_op jit(solution)/shard_map/all_to_all | solution.py:421
  224.5 13.7 %expert_pass.3 = bf16[128,4096]{1,0:T(8,128)(2,1)} custom-call(s32[1]{0:T(128)} %bitcast.1.me_ref, bf16[128,4096]{1,0:T(8,128)(2,1)} %bitcast.79, f32[2,144,1024]{2,1,0:T(8,128)} %copy-done, f32[2,144,1024]{2,1,0:T(8,128)} %copy-done.1, bf16[256,3584]{1,0:T(8,128)(2,1)} %bitcast.69, bf16[256,3584]{1,0:T(8,128)(2,1)} %collective-permute-done.rest_1_, ...), custom_call_target="tpu_custom_call" | custom-call | flops 3200000000 | bytes 28000000 | tf_op jit(solution)/shard_map/expert_pass/pallas_call | solution.py:363
  238.2 3.7 all-to-all-start.3
  242.0 2.4 broadcast_select_fusion.1
  244.4 24.8 %all-to-all-done.3 = bf16[16,8,4096]{2,1,0:T(8,128)(2,1)S(1)} async-done(((bf16[16,8,4096]{2,1,0:T(8,128)(2,1)}), bf16[16,8,4096]{2,1,0:T(8,128)(2,1)S(1)}, u32[]{:S(2)}, u32[]{:S(2)}) %all-to-all-start.3) | async-done | bytes 1048608 | tf_op jit(solution)/shard_map/all_to_all | solution.py:421
  269.7 0.7 collective-permute-start.13
  270.6 1.6 pre.6
  272.2 3.5 all-to-all-start.4
  276.6 27.1 %all-to-all-done.4 = bf16[16,8,4096]{2,1,0:T(8,128)(2,1)S(1)} async-done(((bf16[16,8,4096]{2,1,0:T(8,128)(2,1)}), bf16[16,8,4096]{2,1,0:T(8,128)(2,1)S(1)}, u32[]{:S(2)}, u32[]{:S(2)}) %all-to-all-start.4) | async-done | bytes 1048608 | tf_op jit(solution)/shard_map/all_to_all | solution.py:421
  303.7 1.0 copy-done.6
  304.6 13.7 %expert_pass.4 = bf16[128,4096]{1,0:T(8,128)(2,1)} custom-call(s32[1]{0:T(128)} %bitcast.1.me_ref, bf16[128,4096]{1,0:T(8,128)(2,1)} %bitcast.78, f32[2,144,1024]{2,1,0:T(8,128)} %copy-done, f32[2,144,1024]{2,1,0:T(8,128)} %copy-done.1, bf16[256,3584]{1,0:T(8,128)(2,1)} %bitcast.70, bf16[256,3584]{1,0:T(8,128)(2,1)} %collective-permute-done.rest_1_, ...), custom_call_target="tpu_custom_call" | custom-call | flops 3200000000 | bytes 28000000 | tf_op jit(solution)/shard_map/expert_pass/pallas_call | solution.py:363
  318.3 32.2 %all_to_all.41 = bf16[16,8,4096]{2,1,0:T(8,128)(2,1)S(1)} all-to-all(bf16[16,8,4096]{2,1,0:T(8,128)(2,1)} %bitcast.84), channel_id=1, replica_groups=mesh['pipe'=4,'expert'=16,'dp'=4] {'expert'}, dimensions={0} | all-to-all | bytes 2097152 | tf_op jit(solution)/shard_map/all_to_all | solution.py:421
  351.0 1.4 collective-permute-start.14
  352.4 44.9 %collective-permute-done.14.cur_ref = bf16[64,3584]{1,0:T(8,128)(2,1)S(1)} collective-permute-done((bf16[64,3584]{1,0:T(8,128)(2,1)S(1)}, bf16[64,3584]{1,0:T(8,128)(2,1)S(1)}, u32[]{:S(2)}, u32[]{:S(2)}) %collective-permute-start.14) | collective-permute-done | bytes 458784 | tf_op jit(solution)/shard_map/ppermute | solution.py:518
  397.4 0.6 pre.7
  398.0 32.3 %all_to_all.42 = bf16[16,8,4096]{2,1,0:T(8,128)(2,1)S(1)} all-to-all(bf16[16,8,4096]{2,1,0:T(8,128)(2,1)S(1)} %bitcast.59), channel_id=1, replica_groups=mesh['pipe'=4,'expert'=16,'dp'=4] {'expert'}, dimensions={0} | all-to-all | bytes 2097152 | tf_op jit(solution)/shard_map/all_to_all | solution.py:421
  430.3 1.2 broadcast_select_fusion
  431.6 13.7 %expert_pass.5 = bf16[128,4096]{1,0:T(8,128)(2,1)} custom-call(s32[1]{0:T(128)} %bitcast.1.me_ref, bf16[128,4096]{1,0:T(8,128)(2,1)} %bitcast.80, f32[2,144,1024]{2,1,0:T(8,128)} %copy-done, f32[2,144,1024]{2,1,0:T(8,128)} %copy-done.1, bf16[256,3584]{1,0:T(8,128)(2,1)} %bitcast.71, bf16[256,3584]{1,0:T(8,128)(2,1)} %collective-permute-done.rest_1_, ...), custom_call_target="tpu_custom_call" | custom-call | flops 3200000000 | bytes 28000000 | tf_op jit(solution)/shard_map/expert_pass/pallas_call | solution.py:363
  445.3 3.6 all-to-all-start.7
  448.9 1.1 dynamic-slice_bitcast_fusion
  450.1 0.9 copy.32.ha_ref
  451.0 0.9 copy.33.hb_ref
  451.9 24.2 %all-to-all-done.7 = bf16[16,8,4096]{2,1,0:T(8,128)(2,1)S(1)} async-done(((bf16[16,8,4096]{2,1,0:T(8,128)(2,1)}), bf16[16,8,4096]{2,1,0:T(8,128)(2,1)S(1)}, u32[]{:S(2)}, u32[]{:S(2)}) %all-to-all-start.7) | async-done | bytes 1048608 | tf_op jit(solution)/shard_map/all_to_all | solution.py:421
  476.7 1.1 maximum_select_fusion
  477.8 7.9 %down_pass.1 = bf16[256,3584]{1,0:T(8,128)(2,1)} custom-call(bf16[256,576]{1,0:T(8,128)(2,1)} %copy.32.ha_ref, bf16[256,576]{1,0:T(8,128)(2,1)} %copy.33.hb_ref, bf16[512,4096]{1,0:T(8,128)(2,1)} %all-gather.11.cloned.1.call-done.bufa_ref, bf16[512,4096]{1,0:T(8,128)(2,1)} %all-gather.13.cloned.1.call-done.bufb_ref), custom_call_target="tpu_custom_call" | custom-call | flops 2120000000 | bytes 11000000 | tf_op jit(solution)/shard_map/down_pass/pallas_call | solution.py:407
  (69 shorter events, 4.8 us)
Async XLA Ops:
  7.2 41.7 %collective-permute-start = (bf16[256,3584]{1,0:T(8,128)(2,1)}, bf16[256,3584]{1,0:T(8,128)(2,1)}, u32[]{:S(2)}, u32[]{:S(2)}) collective-permute-start(bf16[256,3584]{1,0:T(8,128)(2,1)} %bitcast.66), channel_id=1, source_target_pairs={{0,1},{1,2},{2,3},{3,0},{64,65},{65,66},{66,67},{67,64},{128,129},... | collective-permute-start | bytes 5505032 | tf_op jit(solution)/shard_map/ppermute | solution.py:437
  9.4 40.6 %collective-permute-start.1 = (bf16[256,3584]{1,0:T(8,128)(2,1)}, bf16[256,3584]{1,0:T(8,128)(2,1)}, u32[]{:S(2)}, u32[]{:S(2)}) collective-permute-start(bf16[256,3584]{1,0:T(8,128)(2,1)} %bitcast.67), channel_id=1, source_target_pairs={{0,3},{1,0},{2,1},{3,2},{64,67},{65,64},{66,65},{67,66},{128,131},... | collective-permute-start | bytes 5505032 | tf_op jit(solution)/shard_map/ppermute | solution.py:437
  14.2 11.4 %copy-start.2 = (bf16[2,1,1,1,144,1024]{5,4,3,2,1,0:T(8,128)(2,1)S(1)}, bf16[2,1,1,1,144,1024]{5,4,3,2,1,0:T(8,128)(2,1)}, u32[]{:S(2)}) copy-start(bf16[2,1,1,1,144,1024]{5,4,3,2,1,0:T(8,128)(2,1)} %param.11) | copy-start | bytes 1769476
  14.2 11.3 %copy-start.3 = (bf16[2,1,1,1,144,1024]{5,4,3,2,1,0:T(8,128)(2,1)S(1)}, bf16[2,1,1,1,144,1024]{5,4,3,2,1,0:T(8,128)(2,1)}, u32[]{:S(2)}) copy-start(bf16[2,1,1,1,144,1024]{5,4,3,2,1,0:T(8,128)(2,1)} %param.12) | copy-start | bytes 1769476
  15.9 37.9 %all-to-all-start = ((bf16[16,8,4096]{2,1,0:T(8,128)(2,1)}), bf16[16,8,4096]{2,1,0:T(8,128)(2,1)S(1)}, u32[]{:S(2)}, u32[]{:S(2)}) async-start(bf16[16,8,4096]{2,1,0:T(8,128)(2,1)} %bitcast.5), calls=%async_computation | async-start | bytes 2097152 | tf_op jit(solution)/shard_map/all_to_all | solution.py:421
  25.4 199.0 %all-gather.7.cloned.1.call-start = ((), (), s32[]{:S(2)}) async-start(), calls=%async_computation.8 | async-start | bytes 9175040 | tf_op jit(solution)/shard_map/all_gather | solution.py:456
  27.8 1.0 copy-start
  28.8 1.1 copy-start.1
  50.0 38.5 %collective-permute-start.4 = (bf16[896,1024]{1,0:T(8,128)(2,1)}, bf16[896,1024]{1,0:T(8,128)(2,1)}, u32[]{:S(2)}, u32[]{:S(2)}) collective-permute-start(bf16[896,1024]{1,0:T(8,128)(2,1)} %bitcast.72), channel_id=1, source_target_pairs={{64,65},{65,66},{66,67},{67,64},{128,129},{129,130},{130,131},{131... | collective-permute-start | bytes 5505032 | tf_op jit(solution)/shard_map/ppermute | solution.py:437
  51.9 36.6 %collective-permute-start.5 = (bf16[896,1024]{1,0:T(8,128)(2,1)}, bf16[896,1024]{1,0:T(8,128)(2,1)}, u32[]{:S(2)}, u32[]{:S(2)}) collective-permute-start(bf16[896,1024]{1,0:T(8,128)(2,1)} %bitcast.73), channel_id=1, source_target_pairs={{64,67},{65,64},{66,65},{67,66},{128,131},{129,128},{130,129},{131... | collective-permute-start | bytes 5505032 | tf_op jit(solution)/shard_map/ppermute | solution.py:437
  53.8 4.1 copy-start.10
  56.3 21.1 %collective-permute-start.2 = (bf16[128,3584]{1,0:T(8,128)(2,1)}, bf16[128,3584]{1,0:T(8,128)(2,1)S(1)}, u32[]{:S(2)}, u32[]{:S(2)}) collective-permute-start(bf16[128,3584]{1,0:T(8,128)(2,1)} %slice.58), channel_id=1, source_target_pairs={{0,1},{1,2},{2,3},{3,0},{64,65},{65,66},{66,67},{67,64},{128,129},... | collective-permute-start | bytes 2752520 | tf_op jit(solution)/shard_map/ppermute | solution.py:437
  60.1 19.9 %collective-permute-start.3 = (bf16[128,3584]{1,0:T(8,128)(2,1)}, bf16[128,3584]{1,0:T(8,128)(2,1)S(1)}, u32[]{:S(2)}, u32[]{:S(2)}) collective-permute-start(bf16[128,3584]{1,0:T(8,128)(2,1)} %slice.59), channel_id=1, source_target_pairs={{0,3},{1,0},{2,1},{3,2},{64,67},{65,64},{66,65},{67,66},{128,131},... | collective-permute-start | bytes 2752520 | tf_op jit(solution)/shard_map/ppermute | solution.py:437
  77.5 2.5 copy-start.4
  80.0 0.9 copy-start.5
  88.5 15.1 %collective-permute-start.6 = (bf16[2,144,1024]{2,1,0:T(8,128)(2,1)}, bf16[2,144,1024]{2,1,0:T(8,128)(2,1)S(1)}, u32[]{:S(2)}, u32[]{:S(2)}) collective-permute-start(bf16[2,144,1024]{2,1,0:T(8,128)(2,1)} %hidden_pass.1.own), channel_id=1, source_target_pairs={{0,1},{1,2},{2,3},{3,0},{192,193},{193,194},{194,195},{195,192},{4... | collective-permute-start | bytes 1769480 | tf_op jit(solution)/shard_map/ppermute | solution.py:437
  91.4 14.1 %collective-permute-start.7 = (bf16[2,144,1024]{2,1,0:T(8,128)(2,1)}, bf16[2,144,1024]{2,1,0:T(8,128)(2,1)S(1)}, u32[]{:S(2)}, u32[]{:S(2)}) collective-permute-start(bf16[2,144,1024]{2,1,0:T(8,128)(2,1)} %hidden_pass.1.own), channel_id=1, source_target_pairs={{0,3},{1,0},{2,1},{3,2},{192,195},{193,192},{194,193},{195,194},{4... | collective-permute-start | bytes 1769480 | tf_op jit(solution)/shard_map/ppermute | solution.py:437
  103.5 10.3 %copy-start.12 = (bf16[2,144,1024]{2,1,0:T(8,128)(2,1)}, bf16[2,144,1024]{2,1,0:T(8,128)(2,1)S(1)}, u32[]{:S(2)}) copy-start(bf16[2,144,1024]{2,1,0:T(8,128)(2,1)S(1)} %collective-permute-done.6.left) | copy-start | bytes 1769476
  103.6 8.7 %collective-permute-start.8 = (bf16[1,144,1024]{2,1,0:T(8,128)(2,1)S(1)}, bf16[1,144,1024]{2,1,0:T(8,128)(2,1)S(1)}, u32[]{:S(2)}, u32[]{:S(2)}) collective-permute-start(bf16[1,144,1024]{2,1,0:T(8,128)(2,1)S(1)} %slice.66), channel_id=1, source_target_pairs={{0,1},{1,2},{2,3},{3,0},{192,193},{193,194},{194,195},{195,192},{4... | collective-permute-start | bytes 884744 | tf_op jit(solution)/shard_map/ppermute | solution.py:437
  105.5 8.3 %copy-start.13 = (bf16[2,144,1024]{2,1,0:T(8,128)(2,1)}, bf16[2,144,1024]{2,1,0:T(8,128)(2,1)S(1)}, u32[]{:S(2)}) copy-start(bf16[2,144,1024]{2,1,0:T(8,128)(2,1)S(1)} %collective-permute-done.7.right) | copy-start | bytes 1769476
  105.5 8.2 %collective-permute-start.9 = (bf16[1,144,1024]{2,1,0:T(8,128)(2,1)S(1)}, bf16[1,144,1024]{2,1,0:T(8,128)(2,1)S(1)}, u32[]{:S(2)}, u32[]{:S(2)}) collective-permute-start(bf16[1,144,1024]{2,1,0:T(8,128)(2,1)S(1)} %slice.67), channel_id=1, source_target_pairs={{0,3},{1,0},{2,1},{3,2},{192,195},{193,192},{194,193},{195,194},{4... | collective-permute-start | bytes 884744 | tf_op jit(solution)/shard_map/ppermute | solution.py:437
  112.2 1.6 copy-start.14
  113.8 0.7 copy-start.15
  121.0 46.5 %all-to-all-start.1 = ((bf16[64,8,1024]{2,1,0:T(8,128)(2,1)}), bf16[64,8,1024]{2,1,0:T(8,128)(2,1)S(1)}, u32[]{:S(2)}, u32[]{:S(2)}) async-start(bf16[64,8,1024]{2,1,0:T(8,128)(2,1)} %bitcast.90), calls=%async_computation.1 | async-start | bytes 2097152 | tf_op jit(solution)/shard_map/all_to_all | solution.py:501
  139.0 292.6 %all-gather.9.cloned.1.call-start = ((), (), s32[]{:S(2)}) async-start(), calls=%async_computation.9 | async-start | bytes 9175040 | tf_op jit(solution)/shard_map/all_gather | solution.py:456
  141.2 49.6 %collective-permute-start.11 = (bf16[448,1024]{1,0:T(8,128)(2,1)}, bf16[448,1024]{1,0:T(8,128)(2,1)S(1)}, u32[]{:S(2)}, u32[]{:S(2)}) collective-permute-start(bf16[448,1024]{1,0:T(8,128)(2,1)} %slice.62), channel_id=1, source_target_pairs={{64,65},{65,66},{66,67},{67,64},{128,129},{129,130},{130,131},{131... | collective-permute-start | bytes 2752520 | tf_op jit(solution)/shard_map/ppermute | solution.py:437
  144.2 46.6 %collective-permute-start.12 = (bf16[448,1024]{1,0:T(8,128)(2,1)}, bf16[448,1024]{1,0:T(8,128)(2,1)}, u32[]{:S(2)}, u32[]{:S(2)}) collective-permute-start(bf16[448,1024]{1,0:T(8,128)(2,1)} %slice.63), channel_id=1, source_target_pairs={{64,67},{65,64},{66,65},{67,66},{128,131},{129,128},{130,129},{131... | collective-permute-start | bytes 2752520 | tf_op jit(solution)/shard_map/ppermute | solution.py:437
  168.0 22.2 %collective-permute-start.10 = (bf16[64,3584]{1,0:T(8,128)(2,1)S(1)}, bf16[64,3584]{1,0:T(8,128)(2,1)S(1)}, u32[]{:S(2)}, u32[]{:S(2)}) collective-permute-start(bf16[64,3584]{1,0:T(8,128)(2,1)S(1)} %post.4), channel_id=1, source_target_pairs={{0,64},{192,128},{1,65},{193,129},{2,66},{194,130},{3,67},{195,131... | collective-permute-start | bytes 1376264 | tf_op jit(solution)/shard_map/ppermute | solution.py:518
  190.8 33.6 %copy-start.11 = (bf16[448,1024]{1,0:T(8,128)(2,1)}, bf16[448,1024]{1,0:T(8,128)(2,1)S(1)}, u32[]{:S(2)}) copy-start(bf16[448,1024]{1,0:T(8,128)(2,1)S(1)} %collective-permute-done.11.rest_8_) | copy-start | bytes 2752516
  238.2 3.8 copy-start.8
  238.2 31.0 %all-to-all-start.3 = ((bf16[16,8,4096]{2,1,0:T(8,128)(2,1)}), bf16[16,8,4096]{2,1,0:T(8,128)(2,1)S(1)}, u32[]{:S(2)}, u32[]{:S(2)}) async-start(bf16[16,8,4096]{2,1,0:T(8,128)(2,1)} %bitcast.83), calls=%async_computation.3 | async-start | bytes 2097152 | tf_op jit(solution)/shard_map/all_to_all | solution.py:421
  241.9 207.0 %all-gather.15.cloned.1.call-start = ((), (), s32[]{:S(2)}) async-start(), calls=%async_computation.12 | async-start | bytes 2949120 | tf_op jit(solution)/shard_map/all_gather | solution.py:510
  269.7 0.9 collective-permute-start.13
  272.2 31.5 %all-to-all-start.4 = ((bf16[16,8,4096]{2,1,0:T(8,128)(2,1)}), bf16[16,8,4096]{2,1,0:T(8,128)(2,1)S(1)}, u32[]{:S(2)}, u32[]{:S(2)}) async-start(bf16[16,8,4096]{2,1,0:T(8,128)(2,1)} %bitcast.24), calls=%async_computation.4 | async-start | bytes 2097152 | tf_op jit(solution)/shard_map/all_to_all | solution.py:421
  275.8 202.0 %all-gather.11.cloned.1.call-start = ((), (), s32[]{:S(2)}) async-start(), calls=%async_computation.10 | async-start | bytes 5242880 | tf_op jit(solution)/shard_map/all_gather | solution.py:456
  276.3 201.4 %all-gather.13.cloned.1.call-start = ((), (), s32[]{:S(2)}) async-start(), calls=%async_computation.11 | async-start | bytes 5242880 | tf_op jit(solution)/shard_map/all_gather | solution.py:456
  303.7 1.0 copy-start.6
  351.0 79.3 %copy-start.7 = (bf16[16,8,4096]{2,1,0:T(8,128)(2,1)S(1)}, bf16[16,8,4096]{2,1,0:T(8,128)(2,1)}, u32[]{:S(2)}) copy-start(bf16[16,8,4096]{2,1,0:T(8,128)(2,1)} %copy-done.6) | copy-start | bytes 3145732
  351.0 46.4 %collective-permute-start.14 = (bf16[64,3584]{1,0:T(8,128)(2,1)S(1)}, bf16[64,3584]{1,0:T(8,128)(2,1)S(1)}, u32[]{:S(2)}, u32[]{:S(2)}) collective-permute-start(bf16[64,3584]{1,0:T(8,128)(2,1)S(1)} %post.6), channel_id=1, source_target_pairs={{128,192},{64,0},{129,193},{65,1},{130,194},{66,2},{131,195},{67,3... | collective-permute-start | bytes 1376264 | tf_op jit(solution)/shard_map/ppermute | solution.py:518
  430.3 1.3 copy-start.9
  445.3 30.8 %all-to-all-start.7 = ((bf16[16,8,4096]{2,1,0:T(8,128)(2,1)}), bf16[16,8,4096]{2,1,0:T(8,128)(2,1)S(1)}, u32[]{:S(2)}, u32[]{:S(2)}) async-start(bf16[16,8,4096]{2,1,0:T(8,128)(2,1)} %bitcast.82), calls=%async_computation.7 | async-start | bytes 2097152 | tf_op jit(solution)/shard_map/all_to_all | solution.py:421
Sparse Core Ops, SparseCore 0:
  113.9 102.9 all-gather.6
  224.6 94.4 all-gather.8
  320.9 36.4 all-gather.14
  359.0 50.9 all-gather.10
  431.6 45.9 all-gather.12

commit v4 on v3

--- a/solution.py
+++ b/solution.py
@@ -24,6 +24,11 @@
 NN = (((1,), (0,)), ((), ()))
 
 
+IN_HBM = pl.BlockSpec(memory_space=pl.ANY)
+IN_SMEM = pl.BlockSpec(memory_space=pltpu.SMEM)
+IN_VMEM = pl.BlockSpec(memory_space=pltpu.VMEM)
+
+
 def dot(a, b, dims=NN):
     return lax.dot_general(a, b, dims, preferred_element_type=F32)
 
@@ -68,7 +73,8 @@
     )(order, gate, up)
 
 
-def pre_kernel(t_ref, w_ref, cur_ref, out_ref):
+def pre_kernel(pick_ref, t_ref, w_ref, old_ref, new_ref, out_ref):
+    keep = pick_ref[0] > 0
     c = lax.broadcasted_iota(I32, (MAIN, TOK), 0)
     e9 = (c >> 3) * CAP
     t0 = t_ref[0:1, :]
@@ -86,7 +92,8 @@
     last, scale_last = pick(e9 + 8)
     piece = lax.broadcasted_iota(I32, (MAIN, 128), 0) & 7
     for j in range(NCH):
-        x = cur_ref[:, j * CH : (j + 1) * CH]
+        cols = slice(j * CH, (j + 1) * CH)
+        x = jnp.where(keep, old_ref[:, cols], new_ref[:, cols])
         out_ref[:, j * PCH : j * PCH + CH] = (dot(main, x) * scale_main).astype(BF)
         full = dot(last, x)
         part = jnp.zeros((MAIN, 128), F32)
@@ -95,14 +102,15 @@
         out_ref[:, j * PCH + CH : (j + 1) * PCH] = (part * scale_last).astype(BF)
 
 
-def pre(targets_t, weights_t, cur):
+def pre(keep, targets_t, weights_t, old, new):
     return pl.pallas_call(
         pre_kernel,
+        in_specs=[IN_SMEM] + [IN_VMEM] * 4,
         out_shape=jax.ShapeDtypeStruct((MAIN, NCH * PCH), BF),
         compiler_params=pltpu.CompilerParams(vmem_limit_bytes=16 << 20),
         cost_estimate=pl.CostEstimate(flops=120_000_000, bytes_accessed=1_600_000, transcendentals=0),
         name="pre",
-    )(targets_t, weights_t, cur)
+    )(keep, targets_t, weights_t, old, new)
 
 
 def post_kernel(t_ref, cur_ref, buf_ref, out_ref):
@@ -220,11 +228,6 @@
         lo = pl.multiple_of(((me + shift) & 3) * 256, 128)
         dg, du = hidden_part(rows_ref, wd_ref[n * 256 : (n + 1) * 256], fup_ref, fgate_ref, lo, 256)
         store(lo, dg, du)
-
-
-IN_HBM = pl.BlockSpec(memory_space=pl.ANY)
-IN_SMEM = pl.BlockSpec(memory_space=pltpu.SMEM)
-IN_VMEM = pl.BlockSpec(memory_space=pltpu.VMEM)
 
 
 def add_shards(stream, srcs, pieces, dst_ref):
@@ -383,38 +386,49 @@
     )(me, buf, fup, fgate, *wd, *wg, wu)
 
 
-def down_kernel(ha_ref, hb_ref, bufa_ref, bufb_ref, out_ref, rows_ref):
+def down_term(h_ref, buf_ref, rows_ref):
     r = lax.broadcasted_iota(I32, (128, MAIN), 0)
     c = lax.broadcasted_iota(I32, (128, MAIN), 1)
     spread = ones_where(c == (r & 15) * 8 + (r >> 4))
-    total = None
-    for h_ref, buf_ref in ((ha_ref, bufa_ref), (hb_ref, bufb_ref)):
-        for rep in range(4):
-            lo = rep * SLOTS
-            block = slice(rep * MAIN, (rep + 1) * MAIN)
-            rows_ref[lo : lo + MAIN, :] = buf_ref[block, 0:CH]
-            nin = dot(spread, buf_ref[block, CH:PCH]).astype(BF)
-            for k in range(PIECES):
-                rows_ref[lo + MAIN : lo + SLOTS, k * 128 : (k + 1) * 128] = nin[k * 16 : (k + 1) * 16, :]
-        term = dot(h_ref[...], rows_ref[...])
-        total = term if total is None else total + term
-    out_ref[...] = total.astype(BF)
-
-
-def down_pass(ha, hb, bufa, bufb):
-    packed = pl.BlockSpec((4 * MAIN, PCH), lambda j: (0, j))
-    whole = pl.BlockSpec((256, 4 * SLOTS), lambda j: (0, 0))
-    return pl.pallas_call(
-        down_kernel,
+    for rep in range(4):
+        lo = rep * SLOTS
+        block = slice(rep * MAIN, (rep + 1) * MAIN)
+        rows_ref[lo : lo + MAIN, :] = buf_ref[block, 0:CH]
+        nin = dot(spread, buf_ref[block, CH:PCH]).astype(BF)
+        for k in range(PIECES):
+            rows_ref[lo + MAIN : lo + SLOTS, k * 128 : (k + 1) * 128] = nin[k * 16 : (k + 1) * 16, :]
+    return dot(h_ref[...], rows_ref[...])
+
+
+def down_first_kernel(h_ref, buf_ref, out_ref, rows_ref):
+    out_ref[...] = down_term(h_ref, buf_ref, rows_ref)
+
+
+def down_last_kernel(h_ref, buf_ref, sum_ref, out_ref, rows_ref):
+    out_ref[...] = (sum_ref[...] + down_term(h_ref, buf_ref, rows_ref)).astype(BF)
+
+
+def down_pass(h, buf, total=None):
+    block = pl.BlockSpec((256, CH), lambda j: (0, j))
+    specs = [
+        pl.BlockSpec((256, 4 * SLOTS), lambda j: (0, 0)),
+        pl.BlockSpec((4 * MAIN, PCH), lambda j: (0, j)),
+    ]
+    args = [h, buf]
+    if total is not None:
+        specs.append(block)
+        args.append(total)
+    return pl.pallas_call(
+        down_first_kernel if total is None else down_last_kernel,
         grid=(NCH,),
-        in_specs=[whole, whole, packed, packed],
-        out_specs=pl.BlockSpec((256, CH), lambda j: (0, j)),
-        out_shape=jax.ShapeDtypeStruct((256, D), BF),
+        in_specs=specs,
+        out_specs=block,
+        out_shape=jax.ShapeDtypeStruct((256, D), F32 if total is None else BF),
         scratch_shapes=[pltpu.VMEM((4 * SLOTS, CH), BF)],
         compiler_params=pltpu.CompilerParams(vmem_limit_bytes=60 << 20),
-        cost_estimate=pl.CostEstimate(flops=2_120_000_000, bytes_accessed=11_000_000, transcendentals=0),
+        cost_estimate=pl.CostEstimate(flops=1_060_000_000, bytes_accessed=8_000_000, transcendentals=0),
         name="down_pass",
-    )(ha, hb, bufa, bufb)
+    )(*args)
 
 
 def exchange(buf):
@@ -475,21 +489,22 @@
     wts_t = [w.T for w in wts]
     cur = jnp.where(first_up, seed_grads[1], seed_grads[0])
     fup, fgate, hidden = prep(order, saved_gate[:, 0, 0, 0], saved_up[:, 0, 0, 0])
+
     wg_near = near(tie(wg_own, hidden, *wd_near), inner)
 
     edge = jnp.logical_or(section == 0, section == 3)
+    keep_edge = edge.astype(I32).reshape(1)
+    old = cur
     moves = [[(0, 1), (3, 2)], [(1, 2), (2, 1)], [(2, 3), (1, 0)]]
     results = []
-    bufs = []
     for step in range(4):
         at = step // 2
-        outgoing = pre(tgt_t[at], wts_t[at], cur)
+        keep = keep_edge if step == 1 else 1 - keep_edge if step == 3 else 0 * keep_edge
+        outgoing = pre(keep, tgt_t[at], wts_t[at], old, cur)
+        old = cur
         if step == 1:
             outgoing = tie(outgoing, *wg)
-        if step == 2:
-            outgoing = tie(outgoing, buf_first)
         buf = exchange(outgoing)
-        bufs.append(buf)
         if step == 0:
             wd = (wd_own,) + wd_near + far(*[tie(w, buf) for w in wd_near], every)
             dgu = hidden_pass(at, me, buf, fup, fgate, wd)
@@ -505,12 +520,11 @@
         else:
             if step == 1:
                 wg_full = (gather(tie(wg_own, buf)),)
-                buf_first = jnp.where(edge, bufs[0], bufs[1])
-                all_first = gather(buf_first)
-                hidden_all = lax.all_gather(tie(hidden, buf_first), "dp", axis=0)
+                all_first = gather(buf)
+                hidden_all = lax.all_gather(tie(hidden, buf), "dp", axis=0)
             if step == 3:
                 wg = wg_full
-                all_second = gather(jnp.where(edge, bufs[3], bufs[2]))
+                all_second = gather(buf)
             packed = expert_pass(at, me, buf, fup, fgate, wd, wg, wu_full)
             result = post(tgt[at], cur, exchange(packed))
         results.append(result)
@@ -525,7 +539,7 @@
 
     hidden_mine = lax.dynamic_slice_in_dim(hidden_all, dp * 256, 256, axis=3)
     hidden_t = hidden_mine.transpose(1, 3, 0, 2).reshape(2, 256, 4 * SLOTS)
-    down_grads = down_pass(hidden_t[0], hidden_t[1], all_first, all_second)
+    down_grads = down_pass(hidden_t[1], all_second, down_pass(hidden_t[0], all_first))
     return input_grads, down_grads[None, None]
 
 

time: 493 us -> 490 us (level)
  blocking collectives: 98 us -> 130 us
  waiting for transfers between devices: 204 us -> 173 us
    all_to_all x4 -> x3, waiting for transfers between devices: 76.1 us -> 44.6 us  [exchange(): lax.all_to_all(buf.reshape(EXP, 8, NCH * PCH), 'expert', split_axis=0, co...]
    all_to_all x3 -> x4, blocking collectives: 98 us -> 130 us  [exchange(): lax.all_to_all(buf.reshape(EXP, 8, NCH * PCH), 'expert', split_axis=0, co...]
    pallas_call x5 -> x6, Pallas kernels: 12.4 us -> 17 us  [the longest x2 12.5 us: down_pass(): pl.pallas_call(down_first_kernel if total is None else down_last_kernel,...]
    all_to_all x4 -> x3, starting transfers between devices: 20.4 us -> 16.7 us  [exchange(): lax.all_to_all(buf.reshape(EXP, 8, NCH * PCH), 'expert', split_axis=0, co...]
  transfers between devices with their start and end apart: 25 -> 24, of which waited for: 13 -> 12; matrix products, arithmetic and copies ran while one was open for 4% -> 3% of each run, Pallas kernels for 13% -> 14%
where the time goes in v4:
time: 490 us; the launch traced here: 489 us
  waiting for transfers between devices  173 us (35%)
  blocking collectives  130 us (27%)
  Pallas kernels  76.3 us (16%)
  starting transfers between devices  75.1 us (15%)
  local copies, waits for them, and re-layouts  18.1 us (4%)
  between operations  14.2 us (3%)
    all_to_all x4, blocking collectives, exchange(): lax.all_to_all(buf.reshape(EXP, 8, NCH * PCH), 'expert', split_axis=0, co...  130 us
    ppermute x3, waiting for transfers between devices, per_device(): cur = lax.ppermute(result, 'pipe', moves[step])  53.8 us
    ppermute x12, waiting for transfers between devices, shift_dp(): return lax.ppermute(value, ('pipe', 'dp'), pairs)  51.1 us
    all_to_all x3, waiting for transfers between devices, exchange(): lax.all_to_all(buf.reshape(EXP, 8, NCH * PCH), 'expert', split_axis=0, co...  44.6 us
    pallas_call x3, Pallas kernels, expert_pass(): pl.pallas_call(functools.partial(expert_kernel, at_dir, whole), in_specs=...  41.1 us
    ppermute x12, starting transfers between devices, shift_dp(): return lax.ppermute(value, ('pipe', 'dp'), pairs)  25.5 us
    all_to_all x1, waiting for transfers between devices, per_device(): lax.all_to_all(sent.reshape(4 * EXP, 8, PCH), ('dp', 'expert'), split_axi...  21.7 us
    all_to_all x1, starting transfers between devices, per_device(): lax.all_to_all(sent.reshape(4 * EXP, 8, PCH), ('dp', 'expert'), split_axi...  18 us
  transfers between devices with their start and end apart: 24, of which 12 were waited for; matrix products, arithmetic and copies ran while one was open for 3% of the time, Pallas kernels for 14%

profile of v4, /device:TPU:1, one launch (start us, length us, event | category | flops | bytes accessed | tf_op | source)
XLA Modules:
  0.0 489.2 jit_solution(14134142845858573093)
XLA Ops:
  7.2 2.2 collective-permute-start
  9.4 1.5 collective-permute-start.1
  10.9 0.8 copy.29
  12.3 0.7 select_bitcast_fusion.3
  13.0 1.2 select_bitcast_fusion.2.old_ref.new_ref.cur_ref
  14.2 1.6 pre.4
  15.9 9.6 %all-to-all-start = ((bf16[16,8,4096]{2,1,0:T(8,128)(2,1)}), bf16[16,8,4096]{2,1,0:T(8,128)(2,1)S(1)}, u32[]{:S(2)}, u32[]{:S(2)}) async-start(bf16[16,8,4096]{2,1,0:T(8,128)(2,1)} %bitcast.5), calls=%async_computation | async-start | bytes 2097152 | tf_op jit(solution)/shard_map/all_to_all | solution.py:435
  25.6 2.3 prep.1
  27.8 1.0 copy-done
  28.8 1.0 copy-done.1
  29.9 19.0 %collective-permute-done.rest_1_ = bf16[256,3584]{1,0:T(8,128)(2,1)} collective-permute-done((bf16[256,3584]{1,0:T(8,128)(2,1)}, bf16[256,3584]{1,0:T(8,128)(2,1)}, u32[]{:S(2)}, u32[]{:S(2)}) %collective-permute-start) | collective-permute-done | bytes 1835040 | tf_op jit(solution)/shard_map/ppermute | solution.py:451
  48.8 1.2 collective-permute-done.1.rest_2_
  50.0 1.9 collective-permute-start.4
  51.9 1.9 collective-permute-start.5
  53.8 2.5 slice.58
  56.3 1.6 collective-permute-start.2
  57.9 2.2 slice.59
  60.0 1.1 collective-permute-start.3
  61.1 16.3 %collective-permute-done.2.rest_3_ = bf16[128,3584]{1,0:T(8,128)(2,1)S(1)} collective-permute-done((bf16[128,3584]{1,0:T(8,128)(2,1)}, bf16[128,3584]{1,0:T(8,128)(2,1)S(1)}, u32[]{:S(2)}, u32[]{:S(2)}) %collective-permute-start.2) | collective-permute-done | bytes 917536 | tf_op jit(solution)/shard_map/ppermute | solution.py:451
  77.4 2.5 collective-permute-done.3.rest_4_
  79.9 0.9 copy-done.5
  80.9 7.5 %hidden_pass.1.own = bf16[2,144,1024]{2,1,0:T(8,128)(2,1)} custom-call(s32[1]{0:T(128)} %bitcast.1.me_ref, bf16[128,4096]{1,0:T(8,128)(2,1)} %bitcast.83, f32[2,144,1024]{2,1,0:T(8,128)} %copy-done, f32[2,144,1024]{2,1,0:T(8,128)} %copy-done.1, bf16[256,3584]{1,0:T(8,128)(2,1)} %bitcast.65, bf16[256,3584]{1,0:T(8,128)(2,1)} %collective-permute-done.rest_1_, ...), custom_call_target="tpu_custom_call" | custom-call | flops 1060000000 | bytes 11000000 | tf_op jit(solution)/shard_map/hidden_pass/pallas_call | solution.py:264
  88.4 2.9 collective-permute-start.6
  91.3 3.6 collective-permute-start.7
  94.9 8.6 %collective-permute-done.6.left = bf16[2,144,1024]{2,1,0:T(8,128)(2,1)S(1)} collective-permute-done((bf16[2,144,1024]{2,1,0:T(8,128)(2,1)}, bf16[2,144,1024]{2,1,0:T(8,128)(2,1)S(1)}, u32[]{:S(2)}, u32[]{:S(2)}) %collective-permute-start.6) | collective-permute-done | bytes 589856 | tf_op jit(solution)/shard_map/ppermute | solution.py:451
  103.5 1.9 collective-permute-start.8
  105.5 4.6 collective-permute-start.9
  110.0 2.1 collective-permute-done.8.far_g
  112.2 1.5 collective-permute-done.9.far_u
  113.7 0.7 copy-done.12
  114.4 6.5 %own_grads.1 = bf16[4,128,1024]{2,1,0:T(8,128)(2,1)} custom-call(s32[1]{0:T(128)} %bitcast.1.me_ref, bf16[2,144,1024]{2,1,0:T(8,128)(2,1)} %hidden_pass.1.own, bf16[2,144,1024]{2,1,0:T(8,128)(2,1)} %copy-done.9, bf16[2,144,1024]{2,1,0:T(8,128)(2,1)} %copy-done.10, bf16[1,144,1024]{2,1,0:T(8,128)(2,1)} %copy-done.11, bf16[1,144,1024]{2,1,0:T(8,128)(2,1)} %copy-done.12, ...), custom_call_target="tpu_custom_call" | custom-call | flops 2120000000 | bytes 8000000 | tf_op jit(solution)/shard_map/own_grads/pallas_call | solution.py:301
  120.9 18.0 %all-to-all-start.1 = ((bf16[64,8,1024]{2,1,0:T(8,128)(2,1)}), bf16[64,8,1024]{2,1,0:T(8,128)(2,1)S(1)}, u32[]{:S(2)}, u32[]{:S(2)}) async-start(bf16[64,8,1024]{2,1,0:T(8,128)(2,1)} %bitcast.89), calls=%async_computation.1 | async-start | bytes 2097152 | tf_op jit(solution)/shard_map/all_to_all | solution.py:516
  139.0 2.2 slice.62
  141.1 0.7 collective-permute-start.11
  141.9 2.3 slice.63
  144.1 1.6 collective-permute-start.12
  145.8 21.7 %all-to-all-done.1 = bf16[64,8,1024]{2,1,0:T(8,128)(2,1)S(1)} async-done(((bf16[64,8,1024]{2,1,0:T(8,128)(2,1)}), bf16[64,8,1024]{2,1,0:T(8,128)(2,1)S(1)}, u32[]{:S(2)}, u32[]{:S(2)}) %all-to-all-start.1) | async-done | bytes 1048608 | tf_op jit(solution)/shard_map/all_to_all | solution.py:516
  167.9 12.5 %collective-permute-start.10 = (bf16[64,3584]{1,0:T(8,128)(2,1)S(1)}, bf16[64,3584]{1,0:T(8,128)(2,1)S(1)}, u32[]{:S(2)}, u32[]{:S(2)}) collective-permute-start(bf16[64,3584]{1,0:T(8,128)(2,1)S(1)} %post.4), channel_id=1, source_target_pairs={{0,64},{192,128},{1,65},{193,129},{2,66},{194,130},{3,67},{195,131... | collective-permute-start | bytes 1376264 | tf_op jit(solution)/shard_map/ppermute | solution.py:532
  180.5 9.6 %collective-permute-done.10.new_ref.cur_ref.old_ref = bf16[64,3584]{1,0:T(8,128)(2,1)S(1)} collective-permute-done((bf16[64,3584]{1,0:T(8,128)(2,1)S(1)}, bf16[64,3584]{1,0:T(8,128)(2,1)S(1)}, u32[]{:S(2)}, u32[]{:S(2)}) %collective-permute-start.10) | collective-permute-done | bytes 458784 | tf_op jit(solution)/shard_map/ppermute | solution.py:532
  190.1 0.6 pre.5
  190.8 33.6 %all_to_all.40 = bf16[16,8,4096]{2,1,0:T(8,128)(2,1)} all-to-all(bf16[16,8,4096]{2,1,0:T(8,128)(2,1)S(1)} %bitcast.51), channel_id=1, replica_groups=mesh['pipe'=4,'expert'=16,'dp'=4] {'expert'}, dimensions={0} | all-to-all | bytes 2097152 | tf_op jit(solution)/shard_map/all_to_all | solution.py:435
  224.4 0.7 all-gather.15.cloned.1.call-update
  225.1 13.7 %expert_pass.3 = bf16[128,4096]{1,0:T(8,128)(2,1)} custom-call(s32[1]{0:T(128)} %bitcast.1.me_ref, bf16[128,4096]{1,0:T(8,128)(2,1)} %bitcast.75, f32[2,144,1024]{2,1,0:T(8,128)} %copy-done, f32[2,144,1024]{2,1,0:T(8,128)} %copy-done.1, bf16[256,3584]{1,0:T(8,128)(2,1)} %bitcast.66, bf16[256,3584]{1,0:T(8,128)(2,1)} %collective-permute-done.rest_1_, ...), custom_call_target="tpu_custom_call" | custom-call | flops 3200000000 | bytes 28000000 | tf_op jit(solution)/shard_map/expert_pass/pallas_call | solution.py:366
  238.8 31.4 %all_to_all.41 = bf16[16,8,4096]{2,1,0:T(8,128)(2,1)S(1)} all-to-all(bf16[16,8,4096]{2,1,0:T(8,128)(2,1)} %bitcast.82), channel_id=1, replica_groups=mesh['pipe'=4,'expert'=16,'dp'=4] {'expert'}, dimensions={0} | all-to-all | bytes 2097152 | tf_op jit(solution)/shard_map/all_to_all | solution.py:435
  270.8 0.7 collective-permute-start.13
  271.7 1.6 pre.6
  273.3 3.6 all-to-all-start.4
  277.7 26.5 %all-to-all-done.4 = bf16[16,8,4096]{2,1,0:T(8,128)(2,1)S(1)} async-done(((bf16[16,8,4096]{2,1,0:T(8,128)(2,1)}), bf16[16,8,4096]{2,1,0:T(8,128)(2,1)S(1)}, u32[]{:S(2)}, u32[]{:S(2)}) %all-to-all-start.4) | async-done | bytes 1048608 | tf_op jit(solution)/shard_map/all_to_all | solution.py:435
  304.2 1.0 copy-done.6
  305.2 13.7 %expert_pass.4 = bf16[128,4096]{1,0:T(8,128)(2,1)} custom-call(s32[1]{0:T(128)} %bitcast.1.me_ref, bf16[128,4096]{1,0:T(8,128)(2,1)} %bitcast.80, f32[2,144,1024]{2,1,0:T(8,128)} %copy-done, f32[2,144,1024]{2,1,0:T(8,128)} %copy-done.1, bf16[256,3584]{1,0:T(8,128)(2,1)} %bitcast.67, bf16[256,3584]{1,0:T(8,128)(2,1)} %collective-permute-done.rest_1_, ...), custom_call_target="tpu_custom_call" | custom-call | flops 3200000000 | bytes 28000000 | tf_op jit(solution)/shard_map/expert_pass/pallas_call | solution.py:366
  318.9 32.1 %all_to_all.42 = bf16[16,8,4096]{2,1,0:T(8,128)(2,1)S(1)} all-to-all(bf16[16,8,4096]{2,1,0:T(8,128)(2,1)} %bitcast.81), channel_id=1, replica_groups=mesh['pipe'=4,'expert'=16,'dp'=4] {'expert'}, dimensions={0} | all-to-all | bytes 2097152 | tf_op jit(solution)/shard_map/all_to_all | solution.py:435
  351.5 1.3 collective-permute-start.14
  352.8 44.2 %collective-permute-done.14.new_ref.cur_ref = bf16[64,3584]{1,0:T(8,128)(2,1)S(1)} collective-permute-done((bf16[64,3584]{1,0:T(8,128)(2,1)S(1)}, bf16[64,3584]{1,0:T(8,128)(2,1)S(1)}, u32[]{:S(2)}, u32[]{:S(2)}) %collective-permute-start.14) | collective-permute-done | bytes 458784 | tf_op jit(solution)/shard_map/ppermute | solution.py:532
  397.0 0.6 pre.7
  397.7 32.4 %all_to_all.43 = bf16[16,8,4096]{2,1,0:T(8,128)(2,1)} all-to-all(bf16[16,8,4096]{2,1,0:T(8,128)(2,1)S(1)} %bitcast.52), channel_id=1, replica_groups=mesh['pipe'=4,'expert'=16,'dp'=4] {'expert'}, dimensions={0} | all-to-all | bytes 2097152 | tf_op jit(solution)/shard_map/all_to_all | solution.py:435
  430.1 13.7 %expert_pass.5 = bf16[128,4096]{1,0:T(8,128)(2,1)} custom-call(s32[1]{0:T(128)} %bitcast.1.me_ref, bf16[128,4096]{1,0:T(8,128)(2,1)} %bitcast.78, f32[2,144,1024]{2,1,0:T(8,128)} %copy-done, f32[2,144,1024]{2,1,0:T(8,128)} %copy-done.1, bf16[256,3584]{1,0:T(8,128)(2,1)} %bitcast.68, bf16[256,3584]{1,0:T(8,128)(2,1)} %collective-permute-done.rest_1_, ...), custom_call_target="tpu_custom_call" | custom-call | flops 3200000000 | bytes 28000000 | tf_op jit(solution)/shard_map/expert_pass/pallas_call | solution.py:366
  443.8 3.6 all-to-all-start.7
  447.4 1.1 dynamic-slice_bitcast_fusion
  448.5 0.9 copy.33.h_ref
  449.5 0.9 copy.32.h_ref
  450.4 6.1 %down_pass.2.sum_ref = f32[256,3584]{1,0:T(8,128)} custom-call(bf16[256,576]{1,0:T(8,128)(2,1)} %copy.32.h_ref, bf16[512,4096]{1,0:T(8,128)(2,1)} %all-gather.13.cloned.1.call-done.buf_ref), custom_call_target="tpu_custom_call" | custom-call | flops 1060000000 | bytes 8000000 | tf_op jit(solution)/shard_map/down_pass/pallas_call | solution.py:421
  456.5 18.1 %all-to-all-done.7 = bf16[16,8,4096]{2,1,0:T(8,128)(2,1)S(1)} async-done(((bf16[16,8,4096]{2,1,0:T(8,128)(2,1)}), bf16[16,8,4096]{2,1,0:T(8,128)(2,1)S(1)}, u32[]{:S(2)}, u32[]{:S(2)}) %all-to-all-start.7) | async-done | bytes 1048608 | tf_op jit(solution)/shard_map/all_to_all | solution.py:435
  475.2 1.1 maximum_select_fusion
  476.3 6.4 %down_pass.3 = bf16[256,3584]{1,0:T(8,128)(2,1)} custom-call(bf16[256,576]{1,0:T(8,128)(2,1)} %copy.33.h_ref, bf16[512,4096]{1,0:T(8,128)(2,1)} %all-gather.11.cloned.1.call-done.buf_ref, f32[256,3584]{1,0:T(8,128)} %down_pass.2.sum_ref), custom_call_target="tpu_custom_call" | custom-call | flops 1060000000 | bytes 8000000 | tf_op jit(solution)/shard_map/down_pass/pallas_call | solution.py:421
  (61 shorter events, 4.1 us)
Async XLA Ops:
  7.2 41.7 %collective-permute-start = (bf16[256,3584]{1,0:T(8,128)(2,1)}, bf16[256,3584]{1,0:T(8,128)(2,1)}, u32[]{:S(2)}, u32[]{:S(2)}) collective-permute-start(bf16[256,3584]{1,0:T(8,128)(2,1)} %bitcast.63), channel_id=1, source_target_pairs={{0,1},{1,2},{2,3},{3,0},{64,65},{65,66},{66,67},{67,64},{128,129},... | collective-permute-start | bytes 5505032 | tf_op jit(solution)/shard_map/ppermute | solution.py:451
  9.4 40.6 %collective-permute-start.1 = (bf16[256,3584]{1,0:T(8,128)(2,1)}, bf16[256,3584]{1,0:T(8,128)(2,1)}, u32[]{:S(2)}, u32[]{:S(2)}) collective-permute-start(bf16[256,3584]{1,0:T(8,128)(2,1)} %bitcast.64), channel_id=1, source_target_pairs={{0,3},{1,0},{2,1},{3,2},{64,67},{65,64},{66,65},{67,66},{128,131},... | collective-permute-start | bytes 5505032 | tf_op jit(solution)/shard_map/ppermute | solution.py:451
  14.2 11.3 %copy-start.2 = (bf16[2,1,1,1,144,1024]{5,4,3,2,1,0:T(8,128)(2,1)S(1)}, bf16[2,1,1,1,144,1024]{5,4,3,2,1,0:T(8,128)(2,1)}, u32[]{:S(2)}) copy-start(bf16[2,1,1,1,144,1024]{5,4,3,2,1,0:T(8,128)(2,1)} %param.11) | copy-start | bytes 1769476
  14.2 11.3 %copy-start.3 = (bf16[2,1,1,1,144,1024]{5,4,3,2,1,0:T(8,128)(2,1)S(1)}, bf16[2,1,1,1,144,1024]{5,4,3,2,1,0:T(8,128)(2,1)}, u32[]{:S(2)}) copy-start(bf16[2,1,1,1,144,1024]{5,4,3,2,1,0:T(8,128)(2,1)} %param.12) | copy-start | bytes 1769476
  15.9 37.9 %all-to-all-start = ((bf16[16,8,4096]{2,1,0:T(8,128)(2,1)}), bf16[16,8,4096]{2,1,0:T(8,128)(2,1)S(1)}, u32[]{:S(2)}, u32[]{:S(2)}) async-start(bf16[16,8,4096]{2,1,0:T(8,128)(2,1)} %bitcast.5), calls=%async_computation | async-start | bytes 2097152 | tf_op jit(solution)/shard_map/all_to_all | solution.py:435
  25.4 199.7 %all-gather.7.cloned.1.call-start = ((), (), s32[]{:S(2)}) async-start(), calls=%async_computation.8 | async-start | bytes 9175040 | tf_op jit(solution)/shard_map/all_gather | solution.py:470
  27.8 1.0 copy-start
  28.8 1.0 copy-start.1
  50.0 38.4 %collective-permute-start.4 = (bf16[896,1024]{1,0:T(8,128)(2,1)}, bf16[896,1024]{1,0:T(8,128)(2,1)}, u32[]{:S(2)}, u32[]{:S(2)}) collective-permute-start(bf16[896,1024]{1,0:T(8,128)(2,1)} %bitcast.69), channel_id=1, source_target_pairs={{64,65},{65,66},{66,67},{67,64},{128,129},{129,130},{130,131},{131... | collective-permute-start | bytes 5505032 | tf_op jit(solution)/shard_map/ppermute | solution.py:451
  51.9 36.5 %collective-permute-start.5 = (bf16[896,1024]{1,0:T(8,128)(2,1)}, bf16[896,1024]{1,0:T(8,128)(2,1)}, u32[]{:S(2)}, u32[]{:S(2)}) collective-permute-start(bf16[896,1024]{1,0:T(8,128)(2,1)} %bitcast.70), channel_id=1, source_target_pairs={{64,67},{65,64},{66,65},{67,66},{128,131},{129,128},{130,129},{131... | collective-permute-start | bytes 5505032 | tf_op jit(solution)/shard_map/ppermute | solution.py:451
  53.8 4.1 copy-start.7
  56.3 21.1 %collective-permute-start.2 = (bf16[128,3584]{1,0:T(8,128)(2,1)}, bf16[128,3584]{1,0:T(8,128)(2,1)S(1)}, u32[]{:S(2)}, u32[]{:S(2)}) collective-permute-start(bf16[128,3584]{1,0:T(8,128)(2,1)} %slice.58), channel_id=1, source_target_pairs={{0,1},{1,2},{2,3},{3,0},{64,65},{65,66},{66,67},{67,64},{128,129},... | collective-permute-start | bytes 2752520 | tf_op jit(solution)/shard_map/ppermute | solution.py:451
  60.0 19.9 %collective-permute-start.3 = (bf16[128,3584]{1,0:T(8,128)(2,1)}, bf16[128,3584]{1,0:T(8,128)(2,1)S(1)}, u32[]{:S(2)}, u32[]{:S(2)}) collective-permute-start(bf16[128,3584]{1,0:T(8,128)(2,1)} %slice.59), channel_id=1, source_target_pairs={{0,3},{1,0},{2,1},{3,2},{64,67},{65,64},{66,65},{67,66},{128,131},... | collective-permute-start | bytes 2752520 | tf_op jit(solution)/shard_map/ppermute | solution.py:451
  77.4 2.5 copy-start.4
  79.9 0.9 copy-start.5
  88.4 15.1 %collective-permute-start.6 = (bf16[2,144,1024]{2,1,0:T(8,128)(2,1)}, bf16[2,144,1024]{2,1,0:T(8,128)(2,1)S(1)}, u32[]{:S(2)}, u32[]{:S(2)}) collective-permute-start(bf16[2,144,1024]{2,1,0:T(8,128)(2,1)} %hidden_pass.1.own), channel_id=1, source_target_pairs={{0,1},{1,2},{2,3},{3,0},{192,193},{193,194},{194,195},{195,192},{4... | collective-permute-start | bytes 1769480 | tf_op jit(solution)/shard_map/ppermute | solution.py:451
  91.3 14.1 %collective-permute-start.7 = (bf16[2,144,1024]{2,1,0:T(8,128)(2,1)}, bf16[2,144,1024]{2,1,0:T(8,128)(2,1)S(1)}, u32[]{:S(2)}, u32[]{:S(2)}) collective-permute-start(bf16[2,144,1024]{2,1,0:T(8,128)(2,1)} %hidden_pass.1.own), channel_id=1, source_target_pairs={{0,3},{1,0},{2,1},{3,2},{192,195},{193,192},{194,193},{195,194},{4... | collective-permute-start | bytes 1769480 | tf_op jit(solution)/shard_map/ppermute | solution.py:451
  103.5 10.3 %copy-start.9 = (bf16[2,144,1024]{2,1,0:T(8,128)(2,1)}, bf16[2,144,1024]{2,1,0:T(8,128)(2,1)S(1)}, u32[]{:S(2)}) copy-start(bf16[2,144,1024]{2,1,0:T(8,128)(2,1)S(1)} %collective-permute-done.6.left) | copy-start | bytes 1769476
  103.5 8.7 %collective-permute-start.8 = (bf16[1,144,1024]{2,1,0:T(8,128)(2,1)S(1)}, bf16[1,144,1024]{2,1,0:T(8,128)(2,1)S(1)}, u32[]{:S(2)}, u32[]{:S(2)}) collective-permute-start(bf16[1,144,1024]{2,1,0:T(8,128)(2,1)S(1)} %slice.66), channel_id=1, source_target_pairs={{0,1},{1,2},{2,3},{3,0},{192,193},{193,194},{194,195},{195,192},{4... | collective-permute-start | bytes 884744 | tf_op jit(solution)/shard_map/ppermute | solution.py:451
  105.4 8.3 %copy-start.10 = (bf16[2,144,1024]{2,1,0:T(8,128)(2,1)}, bf16[2,144,1024]{2,1,0:T(8,128)(2,1)S(1)}, u32[]{:S(2)}) copy-start(bf16[2,144,1024]{2,1,0:T(8,128)(2,1)S(1)} %collective-permute-done.7.right) | copy-start | bytes 1769476
  105.5 8.2 %collective-permute-start.9 = (bf16[1,144,1024]{2,1,0:T(8,128)(2,1)S(1)}, bf16[1,144,1024]{2,1,0:T(8,128)(2,1)S(1)}, u32[]{:S(2)}, u32[]{:S(2)}) collective-permute-start(bf16[1,144,1024]{2,1,0:T(8,128)(2,1)S(1)} %slice.67), channel_id=1, source_target_pairs={{0,3},{1,0},{2,1},{3,2},{192,195},{193,192},{194,193},{195,194},{4... | collective-permute-start | bytes 884744 | tf_op jit(solution)/shard_map/ppermute | solution.py:451
  112.2 1.6 copy-start.11
  113.7 0.7 copy-start.12
  120.9 46.5 %all-to-all-start.1 = ((bf16[64,8,1024]{2,1,0:T(8,128)(2,1)}), bf16[64,8,1024]{2,1,0:T(8,128)(2,1)S(1)}, u32[]{:S(2)}, u32[]{:S(2)}) async-start(bf16[64,8,1024]{2,1,0:T(8,128)(2,1)} %bitcast.89), calls=%async_computation.1 | async-start | bytes 2097152 | tf_op jit(solution)/shard_map/all_to_all | solution.py:516
  138.9 291.2 %all-gather.9.cloned.1.call-start = ((), (), s32[]{:S(2)}) async-start(), calls=%async_computation.9 | async-start | bytes 9175040 | tf_op jit(solution)/shard_map/all_gather | solution.py:470
  141.1 49.6 %collective-permute-start.11 = (bf16[448,1024]{1,0:T(8,128)(2,1)}, bf16[448,1024]{1,0:T(8,128)(2,1)S(1)}, u32[]{:S(2)}, u32[]{:S(2)}) collective-permute-start(bf16[448,1024]{1,0:T(8,128)(2,1)} %slice.62), channel_id=1, source_target_pairs={{64,65},{65,66},{66,67},{67,64},{128,129},{129,130},{130,131},{131... | collective-permute-start | bytes 2752520 | tf_op jit(solution)/shard_map/ppermute | solution.py:451
  144.1 46.6 %collective-permute-start.12 = (bf16[448,1024]{1,0:T(8,128)(2,1)}, bf16[448,1024]{1,0:T(8,128)(2,1)}, u32[]{:S(2)}, u32[]{:S(2)}) collective-permute-start(bf16[448,1024]{1,0:T(8,128)(2,1)} %slice.63), channel_id=1, source_target_pairs={{64,67},{65,64},{66,65},{67,66},{128,131},{129,128},{130,129},{131... | collective-permute-start | bytes 2752520 | tf_op jit(solution)/shard_map/ppermute | solution.py:451
  167.9 22.1 %collective-permute-start.10 = (bf16[64,3584]{1,0:T(8,128)(2,1)S(1)}, bf16[64,3584]{1,0:T(8,128)(2,1)S(1)}, u32[]{:S(2)}, u32[]{:S(2)}) collective-permute-start(bf16[64,3584]{1,0:T(8,128)(2,1)S(1)} %post.4), channel_id=1, source_target_pairs={{0,64},{192,128},{1,65},{193,129},{2,66},{194,130},{3,67},{195,131... | collective-permute-start | bytes 1376264 | tf_op jit(solution)/shard_map/ppermute | solution.py:532
  190.7 33.6 %copy-start.8 = (bf16[448,1024]{1,0:T(8,128)(2,1)}, bf16[448,1024]{1,0:T(8,128)(2,1)S(1)}, u32[]{:S(2)}) copy-start(bf16[448,1024]{1,0:T(8,128)(2,1)S(1)} %collective-permute-done.11.rest_8_) | copy-start | bytes 2752516
  224.4 223.0 %all-gather.15.cloned.1.call-start = ((), (), s32[]{:S(2)}) async-start(), calls=%async_computation.12 | async-start | bytes 2949120 | tf_op jit(solution)/shard_map/all_gather | solution.py:524
  270.8 0.9 collective-permute-start.13
  273.3 30.9 %all-to-all-start.4 = ((bf16[16,8,4096]{2,1,0:T(8,128)(2,1)}), bf16[16,8,4096]{2,1,0:T(8,128)(2,1)S(1)}, u32[]{:S(2)}, u32[]{:S(2)}) async-start(bf16[16,8,4096]{2,1,0:T(8,128)(2,1)} %bitcast.25), calls=%async_computation.4 | async-start | bytes 2097152 | tf_op jit(solution)/shard_map/all_to_all | solution.py:435
  276.9 173.5 %all-gather.13.cloned.1.call-start = ((), (), s32[]{:S(2)}) async-start(), calls=%async_computation.11 | async-start | bytes 5242880 | tf_op jit(solution)/shard_map/all_gather | solution.py:470
  277.4 198.8 %all-gather.11.cloned.1.call-start = ((), (), s32[]{:S(2)}) async-start(), calls=%async_computation.10 | async-start | bytes 5242880 | tf_op jit(solution)/shard_map/all_gather | solution.py:470
  304.2 1.0 copy-start.6
  351.5 45.5 %collective-permute-start.14 = (bf16[64,3584]{1,0:T(8,128)(2,1)S(1)}, bf16[64,3584]{1,0:T(8,128)(2,1)S(1)}, u32[]{:S(2)}, u32[]{:S(2)}) collective-permute-start(bf16[64,3584]{1,0:T(8,128)(2,1)S(1)} %post.6), channel_id=1, source_target_pairs={{128,192},{64,0},{129,193},{65,1},{130,194},{66,2},{131,195},{67,3... | collective-permute-start | bytes 1376264 | tf_op jit(solution)/shard_map/ppermute | solution.py:532
  443.8 30.9 %all-to-all-start.7 = ((bf16[16,8,4096]{2,1,0:T(8,128)(2,1)}), bf16[16,8,4096]{2,1,0:T(8,128)(2,1)S(1)}, u32[]{:S(2)}, u32[]{:S(2)}) async-start(bf16[16,8,4096]{2,1,0:T(8,128)(2,1)} %bitcast.79), calls=%async_computation.7 | async-start | bytes 2097152 | tf_op jit(solution)/shard_map/all_to_all | solution.py:435
Sparse Core Ops, SparseCore 0:
  113.8 102.9 all-gather.6
  224.5 94.5 all-gather.8
  320.9 36.4 all-gather.14
  359.0 50.9 all-gather.12
  430.2 45.8 all-gather.10

commit v5 on v4

--- a/solution.py
+++ b/solution.py
@@ -386,6 +386,99 @@
     )(me, buf, fup, fgate, *wd, *wg, wu)
 
 
+def front_kernel(at_dir, me_ref, buf_hbm, fup_hbm, fgate_hbm, *rest):
+    pieces, groups = halves_plan(256)
+    gpieces, ggroups = halves_plan(CH)
+    wd_refs, wg_refs, rest = rest[:5], rest[5:10], rest[10:]
+    (
+        part_hbm, du_ref, buf_ref, rows_ref, wd_ref, wg_ref, fup_ref, fgate_ref, dg_ref, part_ref,
+        sems, out_sems,
+    ) = rest
+    me = me_ref[0]
+    stream = Stream(sems, 4)
+    first = stream.add(buf_hbm, buf_ref)
+    ids = add_shards(stream, wd_refs[:1], pieces[:1], wd_ref)
+    stream.add(fup_hbm.at[at_dir], fup_ref)
+    act = stream.add(fgate_hbm.at[at_dir], fgate_ref)
+    ids += add_shards(stream, wd_refs[1:], pieces[1:], wd_ref.at[pl.ds(256, FF - 256)])
+    grad_ids = add_shards(stream, wg_refs, gpieces, wg_ref)
+    stream.wait(first)
+    unpack_rows(buf_ref, rows_ref)
+    stream.wait(act)
+
+    def store(lo, dg, du):
+        dg_ref[:, pl.ds(lo, 256)] = dg
+        du_ref[:, pl.ds(lo, 256)] = du
+
+    hidden_stage(stream, groups, ids, me, rows_ref, wd_ref, fup_ref, fgate_ref, store)
+    outs = []
+    for n, (shift, members) in enumerate(ggroups):
+        for m in members:
+            stream.wait(grad_ids[m])
+        part_ref[n] = dot(dg_ref[...], wg_ref[n * CH : (n + 1) * CH], NT)
+        outs.append(pltpu.make_async_copy(part_ref.at[n], part_hbm.at[(me + shift) & 3], out_sems.at[n]))
+        outs[-1].start()
+    for copy in outs:
+        copy.wait()
+
+
+def front_pass(at_dir, me, buf, fup, fgate, wd, wg):
+    return pl.pallas_call(
+        functools.partial(front_kernel, at_dir),
+        in_specs=[IN_SMEM] + [IN_HBM] * 13,
+        out_specs=[IN_HBM, IN_VMEM],
+        out_shape=(
+            jax.ShapeDtypeStruct((NCH, SLOTS, CH), F32),
+            jax.ShapeDtypeStruct((SLOTS, FF), BF),
+        ),
+        scratch_shapes=[
+            pltpu.VMEM((MAIN, NCH * PCH), BF),
+            pltpu.VMEM((SLOTS, D), BF),
+            pltpu.VMEM((FF, D), BF),
+            pltpu.VMEM((D, FF), BF),
+            pltpu.VMEM((SLOTS, FF), F32),
+            pltpu.VMEM((SLOTS, FF), F32),
+            pltpu.VMEM((SLOTS, FF), BF),
+            pltpu.VMEM((NCH, SLOTS, CH), F32),
+            pltpu.SemaphoreType.DMA((13,)),
+            pltpu.SemaphoreType.DMA((NCH,)),
+        ],
+        compiler_params=pltpu.CompilerParams(vmem_limit_bytes=60 << 20),
+        cost_estimate=pl.CostEstimate(flops=2_100_000_000, bytes_accessed=20_000_000, transcendentals=0),
+        name="front_pass",
+    )(me, buf, fup, fgate, *wd, *wg)
+
+
+def back_kernel(du_hbm, part_hbm, wu_hbm, out_ref, du_ref, part_ref, wu_ref, sems):
+    stream = Stream(sems, 4)
+    stream.add(du_hbm, du_ref)
+    for k in range(NCH):
+        stream.add(wu_hbm.at[pl.ds(k * CH, CH)], wu_ref.at[k])
+        stream.add(part_hbm.at[k], part_ref.at[k])
+    for k in range(NCH):
+        stream.wait(2 * k + 2)
+        total = part_ref[k] + dot(du_ref[...], wu_ref[k], NT)
+        put_chunk(total.astype(BF), out_ref, None, k * PCH)
+
+
+def back_pass(du, part, wu):
+    return pl.pallas_call(
+        back_kernel,
+        in_specs=[IN_HBM] * 3,
+        out_specs=IN_VMEM,
+        out_shape=jax.ShapeDtypeStruct((MAIN, NCH * PCH), BF),
+        scratch_shapes=[
+            pltpu.VMEM((SLOTS, FF), BF),
+            pltpu.VMEM((NCH, SLOTS, CH), F32),
+            pltpu.VMEM((NCH, CH, FF), BF),
+            pltpu.SemaphoreType.DMA((1 + 2 * NCH,)),
+        ],
+        compiler_params=pltpu.CompilerParams(vmem_limit_bytes=60 << 20),
+        cost_estimate=pl.CostEstimate(flops=1_060_000_000, bytes_accessed=10_000_000, transcendentals=0),
+        name="back_pass",
+    )(du, part, wu)
+
+
 def down_term(h_ref, buf_ref, rows_ref):
     r = lax.broadcasted_iota(I32, (128, MAIN), 0)
     c = lax.broadcasted_iota(I32, (128, MAIN), 1)
@@ -404,31 +497,58 @@
     out_ref[...] = down_term(h_ref, buf_ref, rows_ref)
 
 
-def down_last_kernel(h_ref, buf_ref, sum_ref, out_ref, rows_ref):
-    out_ref[...] = (sum_ref[...] + down_term(h_ref, buf_ref, rows_ref)).astype(BF)
-
-
-def down_pass(h, buf, total=None):
-    block = pl.BlockSpec((256, CH), lambda j: (0, j))
-    specs = [
-        pl.BlockSpec((256, 4 * SLOTS), lambda j: (0, 0)),
-        pl.BlockSpec((4 * MAIN, PCH), lambda j: (0, j)),
-    ]
-    args = [h, buf]
-    if total is not None:
-        specs.append(block)
-        args.append(total)
-    return pl.pallas_call(
-        down_first_kernel if total is None else down_last_kernel,
+def down_first(h, buf):
+    return pl.pallas_call(
+        down_first_kernel,
         grid=(NCH,),
-        in_specs=specs,
-        out_specs=block,
-        out_shape=jax.ShapeDtypeStruct((256, D), F32 if total is None else BF),
+        in_specs=[
+            pl.BlockSpec((256, 4 * SLOTS), lambda j: (0, 0)),
+            pl.BlockSpec((4 * MAIN, PCH), lambda j: (0, j)),
+        ],
+        out_specs=pl.BlockSpec((256, CH), lambda j: (0, j)),
+        out_shape=jax.ShapeDtypeStruct((256, D), F32),
         scratch_shapes=[pltpu.VMEM((4 * SLOTS, CH), BF)],
         compiler_params=pltpu.CompilerParams(vmem_limit_bytes=60 << 20),
         cost_estimate=pl.CostEstimate(flops=1_060_000_000, bytes_accessed=8_000_000, transcendentals=0),
-        name="down_pass",
-    )(*args)
+        name="down_first",
+    )(h, buf)
+
+
+def down_last_kernel(h_hbm, buf_hbm, sum_hbm, out_hbm, h_ref, buf_ref, sum_ref, out_ref, rows_ref, sems, out_sems):
+    stream = Stream(sems, 9)
+    stream.add(h_hbm, h_ref)
+    for j in range(NCH):
+        stream.add(buf_hbm.at[:, pl.ds(j * PCH, PCH)], buf_ref.at[j])
+        stream.add(sum_hbm.at[:, pl.ds(j * CH, CH)], sum_ref.at[j])
+    outs = []
+    for j in range(NCH):
+        stream.wait(2 + 2 * j)
+        out_ref[j] = (sum_ref[j] + down_term(h_ref, buf_ref.at[j], rows_ref.at[j % 2])).astype(BF)
+        outs.append(pltpu.make_async_copy(out_ref.at[j], out_hbm.at[:, pl.ds(j * CH, CH)], out_sems.at[j]))
+        outs[-1].start()
+    for copy in outs:
+        copy.wait()
+
+
+def down_last(h, buf, total):
+    return pl.pallas_call(
+        down_last_kernel,
+        in_specs=[IN_HBM] * 3,
+        out_specs=IN_HBM,
+        out_shape=jax.ShapeDtypeStruct((256, D), BF),
+        scratch_shapes=[
+            pltpu.VMEM((256, 4 * SLOTS), BF),
+            pltpu.VMEM((NCH, 4 * MAIN, PCH), BF),
+            pltpu.VMEM((NCH, 256, CH), F32),
+            pltpu.VMEM((NCH, 256, CH), BF),
+            pltpu.VMEM((2, 4 * SLOTS, CH), BF),
+            pltpu.SemaphoreType.DMA((9,)),
+            pltpu.SemaphoreType.DMA((NCH,)),
+        ],
+        compiler_params=pltpu.CompilerParams(vmem_limit_bytes=60 << 20),
+        cost_estimate=pl.CostEstimate(flops=1_060_000_000, bytes_accessed=10_000_000, transcendentals=0),
+        name="down_last",
+    )(h, buf, total)
 
 
 def exchange(buf):
@@ -472,9 +592,12 @@
     def near(x, sections):
         return shift_dp(x, 1, sections), shift_dp(x, -1, sections)
 
+    def hop(top, low, sections):
+        return shift_dp(top, 1, sections), shift_dp(low, -1, sections)
+
     def far(left, right, sections):
         half = left.shape[0] // 2
-        return shift_dp(left[:half], 1, sections), shift_dp(right[half:], -1, sections)
+        return hop(left[:half], right[half:], sections)
 
     wd_own, wg_own, wu_own = w_down[0, 0], w_gate[0, 0], w_up[0, 0]
     wd_near = near(wd_own, every)
@@ -502,17 +625,18 @@
         keep = keep_edge if step == 1 else 1 - keep_edge if step == 3 else 0 * keep_edge
         outgoing = pre(keep, tgt_t[at], wts_t[at], old, cur)
         old = cur
-        if step == 1:
-            outgoing = tie(outgoing, *wg)
         buf = exchange(outgoing)
         if step == 0:
-            wd = (wd_own,) + wd_near + far(*[tie(w, buf) for w in wd_near], every)
-            dgu = hidden_pass(at, me, buf, fup, fgate, wd)
+            halves = tie(wd_near[0], buf)[:128], tie(wd_near[1], buf)[128:]
+            wd_outer = (wd_own,) + wd_near + hop(*halves, outer)
+            dgu = hidden_pass(at, me, buf, fup, fgate, wd_outer)
             dgu_near = near(tie(dgu, *wg_near), outer)
             dgu_far = far(*dgu_near, outer)
             sent = own_grads(me, dgu, *dgu_near, *dgu_far, wg_own, wu_own)
-            wu_full = gather(tie(wu_own, *dgu_far))
-            wg = (wg_own,) + wg_near + far(*[tie(w, sent) for w in wg_near], inner)
+            wd = (wd_own,) + wd_near + hop(*[tie(h, dgu) for h in halves], inner)
+            wg = (wg_own,) + wg_near + far(*wg_near, inner)
+            sent = tie(sent, *wd, *wg)
+            wu_full = gather(tie(wu_own, sent))
             home = lax.all_to_all(
                 sent.reshape(4 * EXP, 8, PCH), ("dp", "expert"), split_axis=0, concat_axis=0, tiled=True
             ).reshape(4, MAIN, PCH)
@@ -522,10 +646,13 @@
                 wg_full = (gather(tie(wg_own, buf)),)
                 all_first = gather(buf)
                 hidden_all = lax.all_gather(tie(hidden, buf), "dp", axis=0)
-            if step == 3:
-                wg = wg_full
+                part, du = front_pass(at, me, buf, fup, fgate, wd, wg)
+                packed = back_pass(du, part, wu_full)
+            elif step == 2:
+                packed = expert_pass(at, me, buf, fup, fgate, wd, wg, wu_full)
+            else:
                 all_second = gather(buf)
-            packed = expert_pass(at, me, buf, fup, fgate, wd, wg, wu_full)
+                packed = expert_pass(at, me, buf, fup, fgate, wd_outer, wg_full, wu_full)
             result = post(tgt[at], cur, exchange(packed))
         results.append(result)
         if step < 3:
@@ -539,7 +666,7 @@
 
     hidden_mine = lax.dynamic_slice_in_dim(hidden_all, dp * 256, 256, axis=3)
     hidden_t = hidden_mine.transpose(1, 3, 0, 2).reshape(2, 256, 4 * SLOTS)
-    down_grads = down_pass(hidden_t[1], all_second, down_pass(hidden_t[0], all_first))
+    down_grads = down_last(hidden_t[1], all_second, down_first(hidden_t[0], all_first))
     return input_grads, down_grads[None, None]
 
 

time: 490 us -> 483 us (0.986)
  blocking collectives: 130 us -> 174 us
  waiting for transfers between devices: 173 us -> 132 us
  starting transfers between devices: 75.1 us -> 61.1 us
    all_to_all x0 -> x1, blocking collectives: none -> 45.2 us  [per_device(): lax.all_to_all(sent.reshape(4 * EXP, 8, PCH), ('dp', 'expert'), split_axi...]
    all_to_all x1 -> x0, waiting for transfers between devices: 21.7 us -> none  [per_device(): lax.all_to_all(sent.reshape(4 * EXP, 8, PCH), ('dp', 'expert'), split_axi...]
    ppermute x3, waiting for transfers between devices: 53.8 us -> 35.8 us  [per_device(): cur = lax.ppermute(result, 'pipe', moves[step])]
    all_to_all x1 -> x0, starting transfers between devices: 18 us -> none  [per_device(): lax.all_to_all(sent.reshape(4 * EXP, 8, PCH), ('dp', 'expert'), split_axi...]
    pallas_call x2 -> x4, Pallas kernels: 12.5 us -> 29.8 us  [the longest x1 11.4 us: front_pass(): pl.pallas_call(functools.partial(front_kernel, at_dir), in_specs=[IN_SMEM...]
    pallas_call x3 -> x2, Pallas kernels: 41.1 us -> 27.4 us  [expert_pass(): pl.pallas_call(functools.partial(expert_kernel, at_dir, whole), in_specs=...]
    ppermute x12 -> x14, starting transfers between devices: 25.5 us -> 32.4 us  [shift_dp(): return lax.ppermute(value, ('pipe', 'dp'), pairs)]
    ppermute x12 -> x14, waiting for transfers between devices: 51.1 us -> 50 us  [shift_dp(): return lax.ppermute(value, ('pipe', 'dp'), pairs)]
  transfers between devices with their start and end apart: 24 -> 25, of which waited for: 12 -> 13; matrix products, arithmetic and copies ran while one was open for 3% -> 3% of each run, Pallas kernels for 14% -> 15%
where the time goes in v5:
time: 483 us; the launch traced here: 482 us
  blocking collectives  174 us (36%)
  waiting for transfers between devices  132 us (27%)
  Pallas kernels  80 us (17%)
  starting transfers between devices  61.1 us (13%)
  local copies, waits for them, and re-layouts  17.1 us (4%)
  between operations  14.2 us (3%)
    all_to_all x4, blocking collectives, exchange(): lax.all_to_all(buf.reshape(EXP, 8, NCH * PCH), 'expert', split_axis=0, co...  129 us
    ppermute x14, waiting for transfers between devices, shift_dp(): return lax.ppermute(value, ('pipe', 'dp'), pairs)  50 us
    all_to_all x1, blocking collectives, per_device(): lax.all_to_all(sent.reshape(4 * EXP, 8, PCH), ('dp', 'expert'), split_axi...  45.2 us
    all_to_all x3, waiting for transfers between devices, exchange(): lax.all_to_all(buf.reshape(EXP, 8, NCH * PCH), 'expert', split_axis=0, co...  45 us
    ppermute x3, waiting for transfers between devices, per_device(): cur = lax.ppermute(result, 'pipe', moves[step])  35.8 us
    ppermute x14, starting transfers between devices, shift_dp(): return lax.ppermute(value, ('pipe', 'dp'), pairs)  32.4 us
    pallas_call x2, Pallas kernels, expert_pass(): pl.pallas_call(functools.partial(expert_kernel, at_dir, whole), in_specs=...  27.4 us
    all_to_all x3, starting transfers between devices, exchange(): lax.all_to_all(buf.reshape(EXP, 8, NCH * PCH), 'expert', split_axis=0, co...  16.9 us
  transfers between devices with their start and end apart: 25, of which 13 were waited for; matrix products, arithmetic and copies ran while one was open for 3% of the time, Pallas kernels for 15%

profile of v5, /device:TPU:1, one launch (start us, length us, event | category | flops | bytes accessed | tf_op | source)
XLA Modules:
  0.0 482.0 jit_solution(5115612290498203909)
XLA Ops:
  7.2 2.2 collective-permute-start
  9.4 1.5 collective-permute-start.1
  10.9 0.8 copy.29
  12.3 0.7 select_bitcast_fusion.3
  13.0 1.2 select_bitcast_fusion.2.old_ref.new_ref.cur_ref
  14.2 1.6 pre.4
  15.8 9.6 %all-to-all-start = ((bf16[16,8,4096]{2,1,0:T(8,128)(2,1)}), bf16[16,8,4096]{2,1,0:T(8,128)(2,1)}, u32[]{:S(2)}, u32[]{:S(2)}) async-start(bf16[16,8,4096]{2,1,0:T(8,128)(2,1)} %bitcast.5), calls=%async_computation | async-start | bytes 2097152 | tf_op jit(solution)/shard_map/all_to_all | solution.py:555
  25.5 2.2 prep.1
  27.8 1.0 copy-done
  28.8 1.0 copy-done.1
  29.8 19.0 %collective-permute-done.rest_1_ = bf16[256,3584]{1,0:T(8,128)(2,1)} collective-permute-done((bf16[256,3584]{1,0:T(8,128)(2,1)}, bf16[256,3584]{1,0:T(8,128)(2,1)}, u32[]{:S(2)}, u32[]{:S(2)}) %collective-permute-start) | collective-permute-done | bytes 1835040 | tf_op jit(solution)/shard_map/ppermute | solution.py:571
  48.8 1.2 collective-permute-done.1.rest_2_
  50.0 0.8 collective-permute-start.4
  50.8 1.9 collective-permute-start.5
  52.6 0.8 all-to-all-done
  53.4 2.2 slice.58
  55.6 2.7 collective-permute-start.2
  58.3 2.2 slice.59
  60.4 3.8 collective-permute-start.3
  64.3 15.3 %collective-permute-done.2.rest_3_ = bf16[128,3584]{1,0:T(8,128)(2,1)} collective-permute-done((bf16[128,3584]{1,0:T(8,128)(2,1)}, bf16[128,3584]{1,0:T(8,128)(2,1)}, u32[]{:S(2)}, u32[]{:S(2)}) %collective-permute-start.2) | collective-permute-done | bytes 917536 | tf_op jit(solution)/shard_map/ppermute | solution.py:571
  79.5 3.1 collective-permute-done.3.rest_4_
  82.6 7.5 %hidden_pass.1.own = bf16[2,144,1024]{2,1,0:T(8,128)(2,1)} custom-call(s32[1]{0:T(128)} %bitcast.1.me_ref, bf16[128,4096]{1,0:T(8,128)(2,1)} %bitcast.6.buf_hbm, f32[2,144,1024]{2,1,0:T(8,128)} %copy-done, f32[2,144,1024]{2,1,0:T(8,128)} %copy-done.1, bf16[256,3584]{1,0:T(8,128)(2,1)} %bitcast.65, bf16[256,3584]{1,0:T(8,128)(2,1)} %collective-permute-done.rest_1_, ...), custom_call_target="tpu_custom_call" | custom-call | flops 1060000000 | bytes 11000000 | tf_op jit(solution)/shard_map/hidden_pass/pallas_call | solution.py:264
  90.1 2.7 collective-permute-start.6
  92.8 4.6 collective-permute-start.7
  97.4 1.6 collective-permute-start.10
  99.0 1.6 collective-permute-start.11
  100.6 1.0 slice.68
  101.6 1.6 collective-permute-start.12
  103.2 2.2 slice.69
  105.4 1.3 collective-permute-done.6.left
  106.8 0.7 collective-permute-start.13
  107.8 3.4 collective-permute-start.8
  111.2 5.9 %collective-permute-done.8.far_g = bf16[1,144,1024]{2,1,0:T(8,128)(2,1)S(1)} collective-permute-done((bf16[1,144,1024]{2,1,0:T(8,128)(2,1)S(1)}, bf16[1,144,1024]{2,1,0:T(8,128)(2,1)S(1)}, u32[]{:S(2)}, u32[]{:S(2)}) %collective-permute-start.8) | collective-permute-done | bytes 294944 | tf_op jit(solution)/shard_map/ppermute | solution.py:571
  117.1 3.4 collective-permute-start.9
  120.4 4.1 collective-permute-done.9.far_u
  124.6 0.7 copy-done.11
  125.3 6.5 %own_grads.1 = bf16[4,128,1024]{2,1,0:T(8,128)(2,1)} custom-call(s32[1]{0:T(128)} %bitcast.1.me_ref, bf16[2,144,1024]{2,1,0:T(8,128)(2,1)} %hidden_pass.1.own, bf16[2,144,1024]{2,1,0:T(8,128)(2,1)} %copy-done.8, bf16[2,144,1024]{2,1,0:T(8,128)(2,1)} %copy-done.9, bf16[1,144,1024]{2,1,0:T(8,128)(2,1)} %copy-done.10, bf16[1,144,1024]{2,1,0:T(8,128)(2,1)} %copy-done.11, ...), custom_call_target="tpu_custom_call" | custom-call | flops 2120000000 | bytes 8000000 | tf_op jit(solution)/shard_map/own_grads/pallas_call | solution.py:301
  132.0 1.4 copy-done.7
  133.4 45.2 %all_to_all.40 = bf16[64,8,1024]{2,1,0:T(8,128)(2,1)S(1)} all-to-all(bf16[64,8,1024]{2,1,0:T(8,128)(2,1)S(1)} %bitcast.88), channel_id=1, replica_groups=mesh['pipe'=4,'expert'=16,'dp'=4] {'dp','expert'}, dimensions={0} | all-to-all | bytes 2097152 | tf_op jit(solution)/shard_map/all_to_all | solution.py:640
  179.1 9.2 %collective-permute-start.14 = (bf16[64,3584]{1,0:T(8,128)(2,1)S(1)}, bf16[64,3584]{1,0:T(8,128)(2,1)S(1)}, u32[]{:S(2)}, u32[]{:S(2)}) collective-permute-start(bf16[64,3584]{1,0:T(8,128)(2,1)S(1)} %post.4), channel_id=1, source_target_pairs={{0,64},{192,128},{1,65},{193,129},{2,66},{194,130},{3,67},{195,131... | collective-permute-start | bytes 1376264 | tf_op jit(solution)/shard_map/ppermute | solution.py:659
  188.3 9.8 %collective-permute-done.14.new_ref.cur_ref.old_ref = bf16[64,3584]{1,0:T(8,128)(2,1)S(1)} collective-permute-done((bf16[64,3584]{1,0:T(8,128)(2,1)S(1)}, bf16[64,3584]{1,0:T(8,128)(2,1)S(1)}, u32[]{:S(2)}, u32[]{:S(2)}) %collective-permute-start.14) | collective-permute-done | bytes 458784 | tf_op jit(solution)/shard_map/ppermute | solution.py:659
  198.8 33.6 %all_to_all.41 = bf16[16,8,4096]{2,1,0:T(8,128)(2,1)} all-to-all(bf16[16,8,4096]{2,1,0:T(8,128)(2,1)S(1)} %bitcast.52), channel_id=1, replica_groups=mesh['pipe'=4,'expert'=16,'dp'=4] {'expert'}, dimensions={0} | all-to-all | bytes 2097152 | tf_op jit(solution)/shard_map/all_to_all | solution.py:555
  233.1 11.4 %front_pass.1 = (f32[4,144,896]{2,1,0:T(8,128)}, bf16[144,1024]{1,0:T(8,128)(2,1)}) custom-call(s32[1]{0:T(128)} %bitcast.1.me_ref, bf16[128,4096]{1,0:T(8,128)(2,1)} %bitcast.77, f32[2,144,1024]{2,1,0:T(8,128)} %copy-done, f32[2,144,1024]{2,1,0:T(8,128)} %copy-done.1, bf16[256,3584]{1,0:T(8,128)(2,1)} %bitcast.66, ...), custom_call_target="tpu_custom_call" | custom-call | flops 2100000000 | bytes 20000000 | tf_op jit(solution)/shard_map/front_pass/pallas_call | solution.py:426
  244.6 6.9 %back_pass.1 = bf16[128,4096]{1,0:T(8,128)(2,1)} custom-call(bf16[144,1024]{1,0:T(8,128)(2,1)} %get-tuple-element.27.du_hbm, f32[4,144,896]{2,1,0:T(8,128)} %get-tuple-element.28.part_hbm, bf16[3584,1024]{1,0:T(8,128)(2,1)} %all-gather.7.cloned.1.call-done.wu_hbm.rest_10_.rest_6_), custom_call_target="tpu_custom_call" | custom-call | flops 1060000000 | bytes 10000000 | tf_op jit(solution)/shard_map/back_pass/pallas_call | solution.py:465
  251.5 30.9 %all_to_all.42 = bf16[16,8,4096]{2,1,0:T(8,128)(2,1)S(1)} all-to-all(bf16[16,8,4096]{2,1,0:T(8,128)(2,1)} %bitcast.82), channel_id=1, replica_groups=mesh['pipe'=4,'expert'=16,'dp'=4] {'expert'}, dimensions={0} | all-to-all | bytes 2097152 | tf_op jit(solution)/shard_map/all_to_all | solution.py:555
  282.9 0.7 collective-permute-start.15
  283.8 1.7 pre.6
  285.5 3.6 all-to-all-start.4
  289.9 26.4 %all-to-all-done.4 = bf16[16,8,4096]{2,1,0:T(8,128)(2,1)S(1)} async-done(((bf16[16,8,4096]{2,1,0:T(8,128)(2,1)}), bf16[16,8,4096]{2,1,0:T(8,128)(2,1)S(1)}, u32[]{:S(2)}, u32[]{:S(2)}) %all-to-all-start.4) | async-done | bytes 1048608 | tf_op jit(solution)/shard_map/all_to_all | solution.py:555
  316.3 1.0 copy-done.5
  317.3 13.7 %expert_pass.2 = bf16[128,4096]{1,0:T(8,128)(2,1)} custom-call(s32[1]{0:T(128)} %bitcast.1.me_ref, bf16[128,4096]{1,0:T(8,128)(2,1)} %bitcast.80, f32[2,144,1024]{2,1,0:T(8,128)} %copy-done, f32[2,144,1024]{2,1,0:T(8,128)} %copy-done.1, bf16[256,3584]{1,0:T(8,128)(2,1)} %bitcast.67, bf16[256,3584]{1,0:T(8,128)(2,1)} %collective-permute-done.rest_1_, ...), custom_call_target="tpu_custom_call" | custom-call | flops 3200000000 | bytes 28000000 | tf_op jit(solution)/shard_map/expert_pass/pallas_call | solution.py:366
  331.0 32.1 %all_to_all.43 = bf16[16,8,4096]{2,1,0:T(8,128)(2,1)S(1)} all-to-all(bf16[16,8,4096]{2,1,0:T(8,128)(2,1)} %bitcast.81), channel_id=1, replica_groups=mesh['pipe'=4,'expert'=16,'dp'=4] {'expert'}, dimensions={0} | all-to-all | bytes 2097152 | tf_op jit(solution)/shard_map/all_to_all | solution.py:555
  363.6 1.3 collective-permute-start.16
  364.9 26.0 %collective-permute-done.16.new_ref.cur_ref = bf16[64,3584]{1,0:T(8,128)(2,1)S(1)} collective-permute-done((bf16[64,3584]{1,0:T(8,128)(2,1)S(1)}, bf16[64,3584]{1,0:T(8,128)(2,1)S(1)}, u32[]{:S(2)}, u32[]{:S(2)}) %collective-permute-start.16) | collective-permute-done | bytes 458784 | tf_op jit(solution)/shard_map/ppermute | solution.py:659
  391.6 32.4 %all_to_all.44 = bf16[16,8,4096]{2,1,0:T(8,128)(2,1)} all-to-all(bf16[16,8,4096]{2,1,0:T(8,128)(2,1)S(1)} %bitcast.51), channel_id=1, replica_groups=mesh['pipe'=4,'expert'=16,'dp'=4] {'expert'}, dimensions={0} | all-to-all | bytes 2097152 | tf_op jit(solution)/shard_map/all_to_all | solution.py:555
  424.0 13.7 %expert_pass.3 = bf16[128,4096]{1,0:T(8,128)(2,1)} custom-call(s32[1]{0:T(128)} %bitcast.1.me_ref, bf16[128,4096]{1,0:T(8,128)(2,1)} %bitcast.76, f32[2,144,1024]{2,1,0:T(8,128)} %copy-done, f32[2,144,1024]{2,1,0:T(8,128)} %copy-done.1, bf16[256,3584]{1,0:T(8,128)(2,1)} %bitcast.68, bf16[256,3584]{1,0:T(8,128)(2,1)} %collective-permute-done.rest_1_, ...), custom_call_target="tpu_custom_call" | custom-call | flops 3200000000 | bytes 28000000 | tf_op jit(solution)/shard_map/expert_pass/pallas_call | solution.py:366
  437.7 3.8 all-to-all-start.7
  441.5 1.1 dynamic-slice_bitcast_fusion
  442.7 0.9 copy.33.h_hbm
  443.6 0.9 copy.32.h_ref
  444.5 6.1 %down_first.1.sum_hbm = f32[256,3584]{1,0:T(8,128)} custom-call(bf16[256,576]{1,0:T(8,128)(2,1)} %copy.32.h_ref, bf16[512,4096]{1,0:T(8,128)(2,1)} %all-gather.13.cloned.1.call-done.buf_ref), custom_call_target="tpu_custom_call" | custom-call | flops 1060000000 | bytes 8000000 | tf_op jit(solution)/shard_map/down_first/pallas_call | solution.py:501
  450.7 17.8 %all-to-all-done.7 = bf16[16,8,4096]{2,1,0:T(8,128)(2,1)S(1)} async-done(((bf16[16,8,4096]{2,1,0:T(8,128)(2,1)}), bf16[16,8,4096]{2,1,0:T(8,128)(2,1)S(1)}, u32[]{:S(2)}, u32[]{:S(2)}) %all-to-all-start.7) | async-done | bytes 1048608 | tf_op jit(solution)/shard_map/all_to_all | solution.py:555
  469.1 1.1 maximum_select_fusion
  470.1 5.4 %down_last.1 = bf16[256,3584]{1,0:T(8,128)(2,1)} custom-call(bf16[256,576]{1,0:T(8,128)(2,1)} %copy.33.h_hbm, bf16[512,4096]{1,0:T(8,128)(2,1)} %all-gather.11.cloned.1.call-done.buf_hbm, f32[256,3584]{1,0:T(8,128)} %down_first.1.sum_hbm), custom_call_target="tpu_custom_call" | custom-call | flops 1060000000 | bytes 10000000 | tf_op jit(solution)/shard_map/down_last/pallas_call | solution.py:534
  (63 shorter events, 6.3 us)
Async XLA Ops:
  7.2 41.7 %collective-permute-start = (bf16[256,3584]{1,0:T(8,128)(2,1)}, bf16[256,3584]{1,0:T(8,128)(2,1)}, u32[]{:S(2)}, u32[]{:S(2)}) collective-permute-start(bf16[256,3584]{1,0:T(8,128)(2,1)} %bitcast.63), channel_id=1, source_target_pairs={{0,1},{1,2},{2,3},{3,0},{64,65},{65,66},{66,67},{67,64},{128,129},... | collective-permute-start | bytes 5505032 | tf_op jit(solution)/shard_map/ppermute | solution.py:571
  9.4 40.6 %collective-permute-start.1 = (bf16[256,3584]{1,0:T(8,128)(2,1)}, bf16[256,3584]{1,0:T(8,128)(2,1)}, u32[]{:S(2)}, u32[]{:S(2)}) collective-permute-start(bf16[256,3584]{1,0:T(8,128)(2,1)} %bitcast.64), channel_id=1, source_target_pairs={{0,3},{1,0},{2,1},{3,2},{64,67},{65,64},{66,65},{67,66},{128,131},... | collective-permute-start | bytes 5505032 | tf_op jit(solution)/shard_map/ppermute | solution.py:571
  14.2 11.3 %copy-start.2 = (bf16[2,1,1,1,144,1024]{5,4,3,2,1,0:T(8,128)(2,1)S(1)}, bf16[2,1,1,1,144,1024]{5,4,3,2,1,0:T(8,128)(2,1)}, u32[]{:S(2)}) copy-start(bf16[2,1,1,1,144,1024]{5,4,3,2,1,0:T(8,128)(2,1)} %param.11) | copy-start | bytes 1769476
  14.2 11.3 %copy-start.3 = (bf16[2,1,1,1,144,1024]{5,4,3,2,1,0:T(8,128)(2,1)S(1)}, bf16[2,1,1,1,144,1024]{5,4,3,2,1,0:T(8,128)(2,1)}, u32[]{:S(2)}) copy-start(bf16[2,1,1,1,144,1024]{5,4,3,2,1,0:T(8,128)(2,1)} %param.12) | copy-start | bytes 1769476
  15.8 37.6 %all-to-all-start = ((bf16[16,8,4096]{2,1,0:T(8,128)(2,1)}), bf16[16,8,4096]{2,1,0:T(8,128)(2,1)}, u32[]{:S(2)}, u32[]{:S(2)}) async-start(bf16[16,8,4096]{2,1,0:T(8,128)(2,1)} %bitcast.5), calls=%async_computation | async-start | bytes 2097152 | tf_op jit(solution)/shard_map/all_to_all | solution.py:555
  25.4 219.1 %all-gather.7.cloned.1.call-start = ((), (), s32[]{:S(2)}) async-start(), calls=%async_computation.8 | async-start | bytes 9175040 | tf_op jit(solution)/shard_map/all_gather | solution.py:590
  27.8 1.1 copy-start
  28.8 1.0 copy-start.1
  50.0 40.1 %collective-permute-start.4 = (bf16[896,1024]{1,0:T(8,128)(2,1)}, bf16[896,1024]{1,0:T(8,128)(2,1)S(1)}, u32[]{:S(2)}, u32[]{:S(2)}) collective-permute-start(bf16[896,1024]{1,0:T(8,128)(2,1)} %bitcast.69), channel_id=1, source_target_pairs={{64,65},{65,66},{66,67},{67,64},{128,129},{129,130},{130,131},{131... | collective-permute-start | bytes 5505032 | tf_op jit(solution)/shard_map/ppermute | solution.py:571
  50.8 39.4 %collective-permute-start.5 = (bf16[896,1024]{1,0:T(8,128)(2,1)}, bf16[896,1024]{1,0:T(8,128)(2,1)}, u32[]{:S(2)}, u32[]{:S(2)}) collective-permute-start(bf16[896,1024]{1,0:T(8,128)(2,1)} %bitcast.70), channel_id=1, source_target_pairs={{64,67},{65,64},{66,65},{67,66},{128,131},{129,128},{130,129},{131... | collective-permute-start | bytes 5505032 | tf_op jit(solution)/shard_map/ppermute | solution.py:571
  55.6 23.9 %collective-permute-start.2 = (bf16[128,3584]{1,0:T(8,128)(2,1)}, bf16[128,3584]{1,0:T(8,128)(2,1)}, u32[]{:S(2)}, u32[]{:S(2)}) collective-permute-start(bf16[128,3584]{1,0:T(8,128)(2,1)} %slice.58), channel_id=1, source_target_pairs={{0,1},{1,2},{2,3},{3,0},{192,193},{193,194},{194,195},{195,192},{4... | collective-permute-start | bytes 2752520 | tf_op jit(solution)/shard_map/ppermute | solution.py:571
  60.4 22.1 %collective-permute-start.3 = (bf16[128,3584]{1,0:T(8,128)(2,1)}, bf16[128,3584]{1,0:T(8,128)(2,1)}, u32[]{:S(2)}, u32[]{:S(2)}) collective-permute-start(bf16[128,3584]{1,0:T(8,128)(2,1)} %slice.59), channel_id=1, source_target_pairs={{0,3},{1,0},{2,1},{3,2},{192,195},{193,192},{194,193},{195,194},{4... | collective-permute-start | bytes 2752520 | tf_op jit(solution)/shard_map/ppermute | solution.py:571
  90.1 15.3 %copy-start.4 = (bf16[896,1024]{1,0:T(8,128)(2,1)}, bf16[896,1024]{1,0:T(8,128)(2,1)S(1)}, u32[]{:S(2)}) copy-start(bf16[896,1024]{1,0:T(8,128)(2,1)S(1)} %collective-permute-done.4.rest_6_) | copy-start | bytes 5505028
  90.1 16.6 %collective-permute-start.6 = (bf16[2,144,1024]{2,1,0:T(8,128)(2,1)}, bf16[2,144,1024]{2,1,0:T(8,128)(2,1)S(1)}, u32[]{:S(2)}, u32[]{:S(2)}) collective-permute-start(bf16[2,144,1024]{2,1,0:T(8,128)(2,1)} %hidden_pass.1.own), channel_id=1, source_target_pairs={{0,1},{1,2},{2,3},{3,0},{192,193},{193,194},{194,195},{195,192},{4... | collective-permute-start | bytes 1769480 | tf_op jit(solution)/shard_map/ppermute | solution.py:571
  92.8 15.0 %collective-permute-start.7 = (bf16[2,144,1024]{2,1,0:T(8,128)(2,1)}, bf16[2,144,1024]{2,1,0:T(8,128)(2,1)S(1)}, u32[]{:S(2)}, u32[]{:S(2)}) collective-permute-start(bf16[2,144,1024]{2,1,0:T(8,128)(2,1)} %hidden_pass.1.own), channel_id=1, source_target_pairs={{0,3},{1,0},{2,1},{3,2},{192,195},{193,192},{194,193},{195,194},{4... | collective-permute-start | bytes 1769480 | tf_op jit(solution)/shard_map/ppermute | solution.py:571
  97.4 34.4 %collective-permute-start.10 = (bf16[128,3584]{1,0:T(8,128)(2,1)}, bf16[128,3584]{1,0:T(8,128)(2,1)}, u32[]{:S(2)}, u32[]{:S(2)}) collective-permute-start(bf16[128,3584]{1,0:T(8,128)(2,1)} %slice.58), channel_id=1, source_target_pairs={{64,65},{65,66},{66,67},{67,64},{128,129},{129,130},{130,131},{131... | collective-permute-start | bytes 2752520 | tf_op jit(solution)/shard_map/ppermute | solution.py:571
  99.0 32.8 %collective-permute-start.11 = (bf16[128,3584]{1,0:T(8,128)(2,1)}, bf16[128,3584]{1,0:T(8,128)(2,1)}, u32[]{:S(2)}, u32[]{:S(2)}) collective-permute-start(bf16[128,3584]{1,0:T(8,128)(2,1)} %slice.59), channel_id=1, source_target_pairs={{64,67},{65,64},{66,65},{67,66},{128,131},{129,128},{130,129},{131... | collective-permute-start | bytes 2752520 | tf_op jit(solution)/shard_map/ppermute | solution.py:571
  101.6 30.2 %collective-permute-start.12 = (bf16[448,1024]{1,0:T(8,128)(2,1)}, bf16[448,1024]{1,0:T(8,128)(2,1)}, u32[]{:S(2)}, u32[]{:S(2)}) collective-permute-start(bf16[448,1024]{1,0:T(8,128)(2,1)} %slice.68), channel_id=1, source_target_pairs={{64,65},{65,66},{66,67},{67,64},{128,129},{129,130},{130,131},{131... | collective-permute-start | bytes 2752520 | tf_op jit(solution)/shard_map/ppermute | solution.py:571
  106.8 17.8 %copy-start.8 = (bf16[2,144,1024]{2,1,0:T(8,128)(2,1)}, bf16[2,144,1024]{2,1,0:T(8,128)(2,1)S(1)}, u32[]{:S(2)}) copy-start(bf16[2,144,1024]{2,1,0:T(8,128)(2,1)S(1)} %collective-permute-done.6.left) | copy-start | bytes 1769476
  106.8 25.1 %collective-permute-start.13 = (bf16[448,1024]{1,0:T(8,128)(2,1)}, bf16[448,1024]{1,0:T(8,128)(2,1)S(1)}, u32[]{:S(2)}, u32[]{:S(2)}) collective-permute-start(bf16[448,1024]{1,0:T(8,128)(2,1)} %slice.69), channel_id=1, source_target_pairs={{64,67},{65,64},{66,65},{67,66},{128,131},{129,128},{130,129},{131... | collective-permute-start | bytes 2752520 | tf_op jit(solution)/shard_map/ppermute | solution.py:571
  107.8 16.8 %copy-start.9 = (bf16[2,144,1024]{2,1,0:T(8,128)(2,1)}, bf16[2,144,1024]{2,1,0:T(8,128)(2,1)S(1)}, u32[]{:S(2)}) copy-start(bf16[2,144,1024]{2,1,0:T(8,128)(2,1)S(1)} %collective-permute-done.7.right) | copy-start | bytes 1769476
  107.8 9.3 %collective-permute-start.8 = (bf16[1,144,1024]{2,1,0:T(8,128)(2,1)S(1)}, bf16[1,144,1024]{2,1,0:T(8,128)(2,1)S(1)}, u32[]{:S(2)}, u32[]{:S(2)}) collective-permute-start(bf16[1,144,1024]{2,1,0:T(8,128)(2,1)S(1)} %slice.66), channel_id=1, source_target_pairs={{0,1},{1,2},{2,3},{3,0},{192,193},{193,194},{194,195},{195,192},{4... | collective-permute-start | bytes 884744 | tf_op jit(solution)/shard_map/ppermute | solution.py:571
  117.1 7.5 %copy-start.10 = (bf16[1,144,1024]{2,1,0:T(8,128)(2,1)}, bf16[1,144,1024]{2,1,0:T(8,128)(2,1)S(1)}, u32[]{:S(2)}) copy-start(bf16[1,144,1024]{2,1,0:T(8,128)(2,1)S(1)} %collective-permute-done.8.far_g) | copy-start | bytes 884740
  117.1 7.5 %collective-permute-start.9 = (bf16[1,144,1024]{2,1,0:T(8,128)(2,1)S(1)}, bf16[1,144,1024]{2,1,0:T(8,128)(2,1)S(1)}, u32[]{:S(2)}, u32[]{:S(2)}) collective-permute-start(bf16[1,144,1024]{2,1,0:T(8,128)(2,1)S(1)} %slice.67), channel_id=1, source_target_pairs={{0,3},{1,0},{2,1},{3,2},{192,195},{193,192},{194,193},{195,194},{4... | collective-permute-start | bytes 884744 | tf_op jit(solution)/shard_map/ppermute | solution.py:571
  124.5 0.7 copy-start.11
  131.8 1.6 copy-start.7
  131.9 46.7 %copy-start.6 = (bf16[448,1024]{1,0:T(8,128)(2,1)}, bf16[448,1024]{1,0:T(8,128)(2,1)S(1)}, u32[]{:S(2)}) copy-start(bf16[448,1024]{1,0:T(8,128)(2,1)S(1)} %collective-permute-done.13.rest_9_) | copy-start | bytes 2752516
  131.9 292.1 %all-gather.9.cloned.1.call-start = ((), (), s32[]{:S(2)}) async-start(), calls=%async_computation.9 | async-start | bytes 9175040 | tf_op jit(solution)/shard_map/all_gather | solution.py:590
  179.1 19.0 %collective-permute-start.14 = (bf16[64,3584]{1,0:T(8,128)(2,1)S(1)}, bf16[64,3584]{1,0:T(8,128)(2,1)S(1)}, u32[]{:S(2)}, u32[]{:S(2)}) collective-permute-start(bf16[64,3584]{1,0:T(8,128)(2,1)S(1)} %post.4), channel_id=1, source_target_pairs={{0,64},{192,128},{1,65},{193,129},{2,66},{194,130},{3,67},{195,131... | collective-permute-start | bytes 1376264 | tf_op jit(solution)/shard_map/ppermute | solution.py:659
  232.4 209.2 %all-gather.15.cloned.1.call-start = ((), (), s32[]{:S(2)}) async-start(), calls=%async_computation.12 | async-start | bytes 2949120 | tf_op jit(solution)/shard_map/all_gather | solution.py:648
  282.9 0.9 collective-permute-start.15
  285.5 30.8 %all-to-all-start.4 = ((bf16[16,8,4096]{2,1,0:T(8,128)(2,1)}), bf16[16,8,4096]{2,1,0:T(8,128)(2,1)S(1)}, u32[]{:S(2)}, u32[]{:S(2)}) async-start(bf16[16,8,4096]{2,1,0:T(8,128)(2,1)} %bitcast.25), calls=%async_computation.4 | async-start | bytes 2097152 | tf_op jit(solution)/shard_map/all_to_all | solution.py:555
  289.1 155.5 %all-gather.13.cloned.1.call-start = ((), (), s32[]{:S(2)}) async-start(), calls=%async_computation.11 | async-start | bytes 5242880 | tf_op jit(solution)/shard_map/all_gather | solution.py:590
  289.6 180.5 %all-gather.11.cloned.1.call-start = ((), (), s32[]{:S(2)}) async-start(), calls=%async_computation.10 | async-start | bytes 5242880 | tf_op jit(solution)/shard_map/all_gather | solution.py:590
  316.3 1.0 copy-start.5
  363.6 27.3 %collective-permute-start.16 = (bf16[64,3584]{1,0:T(8,128)(2,1)S(1)}, bf16[64,3584]{1,0:T(8,128)(2,1)S(1)}, u32[]{:S(2)}, u32[]{:S(2)}) collective-permute-start(bf16[64,3584]{1,0:T(8,128)(2,1)S(1)} %post.6), channel_id=1, source_target_pairs={{128,192},{64,0},{129,193},{65,1},{130,194},{66,2},{131,195},{67,3... | collective-permute-start | bytes 1376264 | tf_op jit(solution)/shard_map/ppermute | solution.py:659
  437.7 30.8 %all-to-all-start.7 = ((bf16[16,8,4096]{2,1,0:T(8,128)(2,1)}), bf16[16,8,4096]{2,1,0:T(8,128)(2,1)S(1)}, u32[]{:S(2)}, u32[]{:S(2)}) async-start(bf16[16,8,4096]{2,1,0:T(8,128)(2,1)} %bitcast.79), calls=%async_computation.7 | async-start | bytes 2097152 | tf_op jit(solution)/shard_map/all_to_all | solution.py:555
Sparse Core Ops, SparseCore 0:
  132.0 98.3 all-gather.6
  232.5 79.0 all-gather.8
  313.4 36.5 all-gather.14
  351.6 50.8 all-gather.12
  424.1 45.2 all-gather.10

commit v6 on v5

--- a/solution.py
+++ b/solution.py
@@ -280,39 +280,46 @@
     )(me, buf, fup, fgate, *wd)
 
 
-def own_grads_kernel(me_ref, own, left, right, far_g, far_u, wg_hbm, wu_hbm, out_ref, d_ref, wg_ref, wu_ref, sems):
-    srcs = [own.at[0], left.at[0], right.at[0], far_g.at[0], own.at[1], left.at[1], right.at[1], far_u.at[0]]
+def own_grads_kernel(me_ref, own, left, right, far, wg_hbm, wu_hbm, out_hbm, out_ref, d_ref, wg_ref, wu_ref, sems, out_sems):
+    srcs = [own, left, right, far]
     stream = Stream(sems, 10)
     stream.add(wg_hbm, wg_ref)
     for n in range(4):
-        stream.add(srcs[n], d_ref.at[0, pl.ds(n * SLOTS, SLOTS)])
+        stream.add(srcs[n].at[0], d_ref.at[0, pl.ds(n * SLOTS, SLOTS)])
     stream.add(wu_hbm, wu_ref)
     for n in range(4):
-        stream.add(srcs[4 + n], d_ref.at[1, pl.ds(n * SLOTS, SLOTS)])
+        stream.add(srcs[n].at[1], d_ref.at[1, pl.ds(n * SLOTS, SLOTS)])
     stream.wait(4)
     total = dot(d_ref[0], wg_ref[...], NT)
     stream.wait(9)
     total = (total + dot(d_ref[1], wu_ref[...], NT)).astype(BF)
+    outs = []
     for n, shift in enumerate((0, 3, 1, 2)):
-        put_chunk(total[n * SLOTS : (n + 1) * SLOTS], out_ref, (me_ref[0] + shift) & 3, None)
-
-
-def own_grads(me, own, left, right, far_g, far_u, wg, wu):
+        put_chunk(total[n * SLOTS : (n + 1) * SLOTS], out_ref, n, None)
+        outs.append(pltpu.make_async_copy(out_ref.at[n], out_hbm.at[(me_ref[0] + shift) & 3], out_sems.at[n]))
+        outs[-1].start()
+    for copy in outs:
+        copy.wait()
+
+
+def own_grads(me, own, left, right, far, wg, wu):
     return pl.pallas_call(
         own_grads_kernel,
-        in_specs=[IN_SMEM] + [IN_HBM] * 7,
-        out_specs=IN_VMEM,
+        in_specs=[IN_SMEM] + [IN_HBM] * 6,
+        out_specs=IN_HBM,
         out_shape=jax.ShapeDtypeStruct((4, MAIN, PCH), BF),
         scratch_shapes=[
+            pltpu.VMEM((4, MAIN, PCH), BF),
             pltpu.VMEM((2, 4 * SLOTS, FF), BF),
             pltpu.VMEM((CH, FF), BF),
             pltpu.VMEM((CH, FF), BF),
             pltpu.SemaphoreType.DMA((10,)),
+            pltpu.SemaphoreType.DMA((4,)),
         ],
         compiler_params=pltpu.CompilerParams(vmem_limit_bytes=60 << 20),
         cost_estimate=pl.CostEstimate(flops=2_120_000_000, bytes_accessed=8_000_000, transcendentals=0),
         name="own_grads",
-    )(me, own, left, right, far_g, far_u, wg, wu)
+    )(me, own, left, right, far, wg, wu)
 
 
 def expert_kernel(at_dir, whole, me_ref, buf_hbm, fup_hbm, fgate_hbm, *rest):
@@ -624,19 +631,21 @@
         at = step // 2
         keep = keep_edge if step == 1 else 1 - keep_edge if step == 3 else 0 * keep_edge
         outgoing = pre(keep, tgt_t[at], wts_t[at], old, cur)
+        if step == 1:
+            outgoing = tie(outgoing, *wg)
         old = cur
         buf = exchange(outgoing)
         if step == 0:
             halves = tie(wd_near[0], buf)[:128], tie(wd_near[1], buf)[128:]
             wd_outer = (wd_own,) + wd_near + hop(*halves, outer)
             dgu = hidden_pass(at, me, buf, fup, fgate, wd_outer)
-            dgu_near = near(tie(dgu, *wg_near), outer)
-            dgu_far = far(*dgu_near, outer)
-            sent = own_grads(me, dgu, *dgu_near, *dgu_far, wg_own, wu_own)
-            wd = (wd_own,) + wd_near + hop(*[tie(h, dgu) for h in halves], inner)
-            wg = (wg_own,) + wg_near + far(*wg_near, inner)
-            sent = tie(sent, *wd, *wg)
+            ready = tie(dgu, *wg_near)
+            others = [shift_dp(ready, step_dp, outer) for step_dp in (1, -1, 2)]
+            sent = own_grads(me, dgu, *others, wg_own, wu_own)
+            wd = (wd_own,) + wd_near + hop(*halves, inner)
+            sent = tie(sent, *wd)
             wu_full = gather(tie(wu_own, sent))
+            wg = (wg_own,) + wg_near + far(*[tie(w, sent) for w in wg_near], inner)
             home = lax.all_to_all(
                 sent.reshape(4 * EXP, 8, PCH), ("dp", "expert"), split_axis=0, concat_axis=0, tiled=True
             ).reshape(4, MAIN, PCH)

time: 483 us -> 471 us (0.975)
  blocking collectives: 174 us -> 129 us
  waiting for transfers between devices: 132 us -> 163 us
    all_to_all x1 -> x0, blocking collectives: 45.2 us -> none  [per_device(): lax.all_to_all(sent.reshape(4 * EXP, 8, PCH), ('dp', 'expert'), split_axi...]
    all_to_all x0 -> x1, waiting for transfers between devices: none -> 21.7 us  [per_device(): lax.all_to_all(sent.reshape(4 * EXP, 8, PCH), ('dp', 'expert'), split_axi...]
    all_to_all x0 -> x1, starting transfers between devices: none -> 15.3 us  [per_device(): lax.all_to_all(sent.reshape(4 * EXP, 8, PCH), ('dp', 'expert'), split_axi...]
    ppermute x3, starting transfers between devices: 11.2 us -> 3.3 us  [per_device(): cur = lax.ppermute(result, 'pipe', moves[step])]
    ppermute x14 -> x13, waiting for transfers between devices: 50 us -> 55.1 us  [shift_dp(): return lax.ppermute(value, ('pipe', 'dp'), pairs)]
    ppermute x14 -> x13, starting transfers between devices: 32.4 us -> 28.8 us  [shift_dp(): return lax.ppermute(value, ('pipe', 'dp'), pairs)]
  transfers between devices with their start and end apart: 25 -> 25, of which waited for: 13 -> 14; matrix products, arithmetic and copies ran while one was open for 3% -> 4% of each run, Pallas kernels for 15% -> 16%
where the time goes in v6:
time: 471 us; the launch traced here: 470 us
  waiting for transfers between devices  163 us (35%)
  blocking collectives  129 us (27%)
  Pallas kernels  79.4 us (17%)
  starting transfers between devices  64.9 us (14%)
  local copies, waits for them, and re-layouts  16.2 us (3%)
  between operations  14.2 us (3%)
    all_to_all x4, blocking collectives, exchange(): lax.all_to_all(buf.reshape(EXP, 8, NCH * PCH), 'expert', split_axis=0, co...  129 us
    ppermute x13, waiting for transfers between devices, shift_dp(): return lax.ppermute(value, ('pipe', 'dp'), pairs)  55.1 us
    all_to_all x3, waiting for transfers between devices, exchange(): lax.all_to_all(buf.reshape(EXP, 8, NCH * PCH), 'expert', split_axis=0, co...  45.1 us
    ppermute x3, waiting for transfers between devices, per_device(): cur = lax.ppermute(result, 'pipe', moves[step])  38.3 us
    ppermute x13, starting transfers between devices, shift_dp(): return lax.ppermute(value, ('pipe', 'dp'), pairs)  28.8 us
    pallas_call x2, Pallas kernels, expert_pass(): pl.pallas_call(functools.partial(expert_kernel, at_dir, whole), in_specs=...  27.4 us
    all_to_all x1, waiting for transfers between devices, per_device(): lax.all_to_all(sent.reshape(4 * EXP, 8, PCH), ('dp', 'expert'), split_axi...  21.7 us
    all_to_all x3, starting transfers between devices, exchange(): lax.all_to_all(buf.reshape(EXP, 8, NCH * PCH), 'expert', split_axis=0, co...  16.9 us
  transfers between devices with their start and end apart: 25, of which 14 were waited for; matrix products, arithmetic and copies ran while one was open for 4% of the time, Pallas kernels for 16%

profile of v6, /device:TPU:1, one launch (start us, length us, event | category | flops | bytes accessed | tf_op | source)
XLA Modules:
  0.0 469.8 jit_solution(7632673058576117944)
XLA Ops:
  7.2 2.2 collective-permute-start
  9.4 1.5 collective-permute-start.1
  10.9 0.8 copy.29
  12.3 0.7 select_bitcast_fusion.3
  13.0 1.2 select_bitcast_fusion.2.old_ref.new_ref.cur_ref
  14.2 1.6 pre.4
  15.8 9.6 %all-to-all-start = ((bf16[16,8,4096]{2,1,0:T(8,128)(2,1)}), bf16[16,8,4096]{2,1,0:T(8,128)(2,1)}, u32[]{:S(2)}, u32[]{:S(2)}) async-start(bf16[16,8,4096]{2,1,0:T(8,128)(2,1)} %bitcast.5), calls=%async_computation | async-start | bytes 2097152 | tf_op jit(solution)/shard_map/all_to_all | solution.py:562
  25.5 2.2 prep.1
  27.8 1.1 copy-done
  28.9 1.0 copy-done.1
  29.9 18.9 %collective-permute-done.rest_1_ = bf16[256,3584]{1,0:T(8,128)(2,1)} collective-permute-done((bf16[256,3584]{1,0:T(8,128)(2,1)}, bf16[256,3584]{1,0:T(8,128)(2,1)}, u32[]{:S(2)}, u32[]{:S(2)}) %collective-permute-start) | collective-permute-done | bytes 1835040 | tf_op jit(solution)/shard_map/ppermute | solution.py:578
  48.8 1.2 collective-permute-done.1.rest_2_
  50.0 0.8 collective-permute-start.4
  50.8 1.9 collective-permute-start.5
  52.6 0.8 all-to-all-done
  53.4 2.2 slice.52
  55.6 2.7 collective-permute-start.2
  58.3 2.2 slice.53
  60.4 3.8 collective-permute-start.3
  64.3 1.6 collective-permute-start.9
  65.9 13.6 %collective-permute-done.2.rest_3_ = bf16[128,3584]{1,0:T(8,128)(2,1)} collective-permute-done((bf16[128,3584]{1,0:T(8,128)(2,1)}, bf16[128,3584]{1,0:T(8,128)(2,1)}, u32[]{:S(2)}, u32[]{:S(2)}) %collective-permute-start.2) | collective-permute-done | bytes 917536 | tf_op jit(solution)/shard_map/ppermute | solution.py:578
  79.5 1.6 collective-permute-start.10
  81.1 1.5 collective-permute-done.3.rest_4_
  82.6 7.5 %hidden_pass.1.own = bf16[2,144,1024]{2,1,0:T(8,128)(2,1)} custom-call(s32[1]{0:T(128)} %bitcast.1.me_ref, bf16[128,4096]{1,0:T(8,128)(2,1)} %bitcast.6.buf_hbm, f32[2,144,1024]{2,1,0:T(8,128)} %copy-done, f32[2,144,1024]{2,1,0:T(8,128)} %copy-done.1, bf16[256,3584]{1,0:T(8,128)(2,1)} %bitcast.65, bf16[256,3584]{1,0:T(8,128)(2,1)} %collective-permute-done.rest_1_, ...), custom_call_target="tpu_custom_call" | custom-call | flops 1060000000 | bytes 11000000 | tf_op jit(solution)/shard_map/hidden_pass/pallas_call | solution.py:264
  90.2 2.6 collective-permute-start.6
  92.8 4.6 collective-permute-start.7
  97.4 3.1 collective-permute-start.8
  100.5 6.3 %collective-permute-done.6.left = bf16[2,144,1024]{2,1,0:T(8,128)(2,1)S(1)} collective-permute-done((bf16[2,144,1024]{2,1,0:T(8,128)(2,1)}, bf16[2,144,1024]{2,1,0:T(8,128)(2,1)S(1)}, u32[]{:S(2)}, u32[]{:S(2)}) %collective-permute-start.6) | collective-permute-done | bytes 589856 | tf_op jit(solution)/shard_map/ppermute | solution.py:578
  106.8 2.8 collective-permute-done.7.right
  109.6 10.8 %collective-permute-done.8.far = bf16[2,144,1024]{2,1,0:T(8,128)(2,1)} collective-permute-done((bf16[2,144,1024]{2,1,0:T(8,128)(2,1)}, bf16[2,144,1024]{2,1,0:T(8,128)(2,1)}, u32[]{:S(2)}, u32[]{:S(2)}) %collective-permute-start.8) | collective-permute-done | bytes 589856 | tf_op jit(solution)/shard_map/ppermute | solution.py:578
  120.4 6.5 %own_grads.1 = bf16[4,128,1024]{2,1,0:T(8,128)(2,1)} custom-call(s32[1]{0:T(128)} %bitcast.1.me_ref, bf16[2,144,1024]{2,1,0:T(8,128)(2,1)} %hidden_pass.1.own, bf16[2,144,1024]{2,1,0:T(8,128)(2,1)} %copy-done.7, bf16[2,144,1024]{2,1,0:T(8,128)(2,1)} %collective-permute-done.7.right, bf16[2,144,1024]{2,1,0:T(8,128)(2,1)} %collective-permute-done.8.far, ...), custom_call_target="tpu_custom_call" | custom-call | flops 2120000000 | bytes 8000000 | tf_op jit(solution)/shard_map/own_grads/pallas_call | solution.py:306
  127.0 15.3 %all-to-all-start.1 = ((bf16[64,8,1024]{2,1,0:T(8,128)(2,1)}), bf16[64,8,1024]{2,1,0:T(8,128)(2,1)S(1)}, u32[]{:S(2)}, u32[]{:S(2)}) async-start(bf16[64,8,1024]{2,1,0:T(8,128)(2,1)} %bitcast.14), calls=%async_computation.1 | async-start | bytes 2097152 | tf_op jit(solution)/shard_map/all_to_all | solution.py:649
  142.3 2.2 slice.54
  144.5 0.7 collective-permute-start.12
  145.2 2.3 slice.55
  147.5 1.6 collective-permute-start.13
  149.2 21.7 %all-to-all-done.1 = bf16[64,8,1024]{2,1,0:T(8,128)(2,1)S(1)} async-done(((bf16[64,8,1024]{2,1,0:T(8,128)(2,1)}), bf16[64,8,1024]{2,1,0:T(8,128)(2,1)S(1)}, u32[]{:S(2)}, u32[]{:S(2)}) %all-to-all-start.1) | async-done | bytes 1048608 | tf_op jit(solution)/shard_map/all_to_all | solution.py:649
  171.3 1.3 collective-permute-start.11
  172.7 10.0 %collective-permute-done.11.new_ref.cur_ref.old_ref = bf16[64,3584]{1,0:T(8,128)(2,1)S(1)} collective-permute-done((bf16[64,3584]{1,0:T(8,128)(2,1)S(1)}, bf16[64,3584]{1,0:T(8,128)(2,1)S(1)}, u32[]{:S(2)}, u32[]{:S(2)}) %collective-permute-start.11) | collective-permute-done | bytes 458784 | tf_op jit(solution)/shard_map/ppermute | solution.py:668
  182.7 0.6 pre.5
  183.3 33.4 %all_to_all.40 = bf16[16,8,4096]{2,1,0:T(8,128)(2,1)} all-to-all(bf16[16,8,4096]{2,1,0:T(8,128)(2,1)S(1)} %bitcast.51), channel_id=1, replica_groups=mesh['pipe'=4,'expert'=16,'dp'=4] {'expert'}, dimensions={0} | all-to-all | bytes 2097152 | tf_op jit(solution)/shard_map/all_to_all | solution.py:562
  217.5 11.4 %front_pass.1 = (f32[4,144,896]{2,1,0:T(8,128)}, bf16[144,1024]{1,0:T(8,128)(2,1)}) custom-call(s32[1]{0:T(128)} %bitcast.1.me_ref, bf16[128,4096]{1,0:T(8,128)(2,1)} %bitcast.77, f32[2,144,1024]{2,1,0:T(8,128)} %copy-done, f32[2,144,1024]{2,1,0:T(8,128)} %copy-done.1, bf16[256,3584]{1,0:T(8,128)(2,1)} %bitcast.66, ...), custom_call_target="tpu_custom_call" | custom-call | flops 2100000000 | bytes 20000000 | tf_op jit(solution)/shard_map/front_pass/pallas_call | solution.py:433
  229.0 6.4 %back_pass.1 = bf16[128,4096]{1,0:T(8,128)(2,1)} custom-call(bf16[144,1024]{1,0:T(8,128)(2,1)} %get-tuple-element.29.du_hbm, f32[4,144,896]{2,1,0:T(8,128)} %get-tuple-element.30.part_hbm, bf16[3584,1024]{1,0:T(8,128)(2,1)} %all-gather.7.cloned.1.call-done.wu_hbm.rest_10_.rest_6_), custom_call_target="tpu_custom_call" | custom-call | flops 1060000000 | bytes 10000000 | tf_op jit(solution)/shard_map/back_pass/pallas_call | solution.py:472
  235.4 31.4 %all_to_all.41 = bf16[16,8,4096]{2,1,0:T(8,128)(2,1)S(1)} all-to-all(bf16[16,8,4096]{2,1,0:T(8,128)(2,1)} %bitcast.82), channel_id=1, replica_groups=mesh['pipe'=4,'expert'=16,'dp'=4] {'expert'}, dimensions={0} | all-to-all | bytes 2097152 | tf_op jit(solution)/shard_map/all_to_all | solution.py:562
  267.3 0.7 collective-permute-start.14
  268.2 1.7 pre.6
  269.8 3.5 all-to-all-start.4
  274.3 26.5 %all-to-all-done.4 = bf16[16,8,4096]{2,1,0:T(8,128)(2,1)S(1)} async-done(((bf16[16,8,4096]{2,1,0:T(8,128)(2,1)}), bf16[16,8,4096]{2,1,0:T(8,128)(2,1)S(1)}, u32[]{:S(2)}, u32[]{:S(2)}) %all-to-all-start.4) | async-done | bytes 1048608 | tf_op jit(solution)/shard_map/all_to_all | solution.py:562
  300.7 1.0 copy-done.5
  301.7 13.7 %expert_pass.2 = bf16[128,4096]{1,0:T(8,128)(2,1)} custom-call(s32[1]{0:T(128)} %bitcast.1.me_ref, bf16[128,4096]{1,0:T(8,128)(2,1)} %bitcast.80, f32[2,144,1024]{2,1,0:T(8,128)} %copy-done, f32[2,144,1024]{2,1,0:T(8,128)} %copy-done.1, bf16[256,3584]{1,0:T(8,128)(2,1)} %bitcast.67, bf16[256,3584]{1,0:T(8,128)(2,1)} %collective-permute-done.rest_1_, ...), custom_call_target="tpu_custom_call" | custom-call | flops 3200000000 | bytes 28000000 | tf_op jit(solution)/shard_map/expert_pass/pallas_call | solution.py:373
  315.4 32.1 %all_to_all.42 = bf16[16,8,4096]{2,1,0:T(8,128)(2,1)S(1)} all-to-all(bf16[16,8,4096]{2,1,0:T(8,128)(2,1)} %bitcast.81), channel_id=1, replica_groups=mesh['pipe'=4,'expert'=16,'dp'=4] {'expert'}, dimensions={0} | all-to-all | bytes 2097152 | tf_op jit(solution)/shard_map/all_to_all | solution.py:562
  348.0 1.3 collective-permute-start.15
  349.3 28.3 %collective-permute-done.15.new_ref.cur_ref = bf16[64,3584]{1,0:T(8,128)(2,1)S(1)} collective-permute-done((bf16[64,3584]{1,0:T(8,128)(2,1)S(1)}, bf16[64,3584]{1,0:T(8,128)(2,1)S(1)}, u32[]{:S(2)}, u32[]{:S(2)}) %collective-permute-start.15) | collective-permute-done | bytes 458784 | tf_op jit(solution)/shard_map/ppermute | solution.py:668
  378.3 32.3 %all_to_all.43 = bf16[16,8,4096]{2,1,0:T(8,128)(2,1)} all-to-all(bf16[16,8,4096]{2,1,0:T(8,128)(2,1)S(1)} %bitcast.52), channel_id=1, replica_groups=mesh['pipe'=4,'expert'=16,'dp'=4] {'expert'}, dimensions={0} | all-to-all | bytes 2097152 | tf_op jit(solution)/shard_map/all_to_all | solution.py:562
  410.6 13.7 %expert_pass.3 = bf16[128,4096]{1,0:T(8,128)(2,1)} custom-call(s32[1]{0:T(128)} %bitcast.1.me_ref, bf16[128,4096]{1,0:T(8,128)(2,1)} %bitcast.76, f32[2,144,1024]{2,1,0:T(8,128)} %copy-done, f32[2,144,1024]{2,1,0:T(8,128)} %copy-done.1, bf16[256,3584]{1,0:T(8,128)(2,1)} %bitcast.68, bf16[256,3584]{1,0:T(8,128)(2,1)} %collective-permute-done.rest_1_, ...), custom_call_target="tpu_custom_call" | custom-call | flops 3200000000 | bytes 28000000 | tf_op jit(solution)/shard_map/expert_pass/pallas_call | solution.py:373
  424.3 3.8 all-to-all-start.7
  428.2 1.1 dynamic-slice_bitcast_fusion
  429.3 0.9 copy.33.h_hbm
  430.2 0.9 copy.32.h_ref
  431.1 6.1 %down_first.1.sum_hbm = f32[256,3584]{1,0:T(8,128)} custom-call(bf16[256,576]{1,0:T(8,128)(2,1)} %copy.32.h_ref, bf16[512,4096]{1,0:T(8,128)(2,1)} %all-gather.13.cloned.1.call-done.buf_ref), custom_call_target="tpu_custom_call" | custom-call | flops 1060000000 | bytes 8000000 | tf_op jit(solution)/shard_map/down_first/pallas_call | solution.py:508
  437.3 17.8 %all-to-all-done.7 = bf16[16,8,4096]{2,1,0:T(8,128)(2,1)S(1)} async-done(((bf16[16,8,4096]{2,1,0:T(8,128)(2,1)}), bf16[16,8,4096]{2,1,0:T(8,128)(2,1)S(1)}, u32[]{:S(2)}, u32[]{:S(2)}) %all-to-all-start.7) | async-done | bytes 1048608 | tf_op jit(solution)/shard_map/all_to_all | solution.py:562
  455.7 1.1 maximum_select_fusion
  456.8 1.2 all-gather.11.cloned.1.call-done.buf_hbm
  457.9 5.4 %down_last.1 = bf16[256,3584]{1,0:T(8,128)(2,1)} custom-call(bf16[256,576]{1,0:T(8,128)(2,1)} %copy.33.h_hbm, bf16[512,4096]{1,0:T(8,128)(2,1)} %all-gather.11.cloned.1.call-done.buf_hbm, f32[256,3584]{1,0:T(8,128)} %down_first.1.sum_hbm), custom_call_target="tpu_custom_call" | custom-call | flops 1060000000 | bytes 10000000 | tf_op jit(solution)/shard_map/down_last/pallas_call | solution.py:541
  (52 shorter events, 5.3 us)
Async XLA Ops:
  7.2 41.7 %collective-permute-start = (bf16[256,3584]{1,0:T(8,128)(2,1)}, bf16[256,3584]{1,0:T(8,128)(2,1)}, u32[]{:S(2)}, u32[]{:S(2)}) collective-permute-start(bf16[256,3584]{1,0:T(8,128)(2,1)} %bitcast.63), channel_id=1, source_target_pairs={{0,1},{1,2},{2,3},{3,0},{64,65},{65,66},{66,67},{67,64},{128,129},... | collective-permute-start | bytes 5505032 | tf_op jit(solution)/shard_map/ppermute | solution.py:578
  9.4 40.6 %collective-permute-start.1 = (bf16[256,3584]{1,0:T(8,128)(2,1)}, bf16[256,3584]{1,0:T(8,128)(2,1)}, u32[]{:S(2)}, u32[]{:S(2)}) collective-permute-start(bf16[256,3584]{1,0:T(8,128)(2,1)} %bitcast.64), channel_id=1, source_target_pairs={{0,3},{1,0},{2,1},{3,2},{64,67},{65,64},{66,65},{67,66},{128,131},... | collective-permute-start | bytes 5505032 | tf_op jit(solution)/shard_map/ppermute | solution.py:578
  14.2 11.3 %copy-start.2 = (bf16[2,1,1,1,144,1024]{5,4,3,2,1,0:T(8,128)(2,1)S(1)}, bf16[2,1,1,1,144,1024]{5,4,3,2,1,0:T(8,128)(2,1)}, u32[]{:S(2)}) copy-start(bf16[2,1,1,1,144,1024]{5,4,3,2,1,0:T(8,128)(2,1)} %param.11) | copy-start | bytes 1769476
  14.2 11.3 %copy-start.3 = (bf16[2,1,1,1,144,1024]{5,4,3,2,1,0:T(8,128)(2,1)S(1)}, bf16[2,1,1,1,144,1024]{5,4,3,2,1,0:T(8,128)(2,1)}, u32[]{:S(2)}) copy-start(bf16[2,1,1,1,144,1024]{5,4,3,2,1,0:T(8,128)(2,1)} %param.12) | copy-start | bytes 1769476
  15.8 37.6 %all-to-all-start = ((bf16[16,8,4096]{2,1,0:T(8,128)(2,1)}), bf16[16,8,4096]{2,1,0:T(8,128)(2,1)}, u32[]{:S(2)}, u32[]{:S(2)}) async-start(bf16[16,8,4096]{2,1,0:T(8,128)(2,1)} %bitcast.5), calls=%async_computation | async-start | bytes 2097152 | tf_op jit(solution)/shard_map/all_to_all | solution.py:562
  25.4 203.5 %all-gather.7.cloned.1.call-start = ((), (), s32[]{:S(2)}) async-start(), calls=%async_computation.8 | async-start | bytes 9175040 | tf_op jit(solution)/shard_map/all_gather | solution.py:597
  27.8 1.1 copy-start
  28.9 1.0 copy-start.1
  50.0 40.2 %collective-permute-start.4 = (bf16[896,1024]{1,0:T(8,128)(2,1)}, bf16[896,1024]{1,0:T(8,128)(2,1)S(1)}, u32[]{:S(2)}, u32[]{:S(2)}) collective-permute-start(bf16[896,1024]{1,0:T(8,128)(2,1)} %bitcast.69), channel_id=1, source_target_pairs={{64,65},{65,66},{66,67},{67,64},{128,129},{129,130},{130,131},{131... | collective-permute-start | bytes 5505032 | tf_op jit(solution)/shard_map/ppermute | solution.py:578
  50.8 39.4 %collective-permute-start.5 = (bf16[896,1024]{1,0:T(8,128)(2,1)}, bf16[896,1024]{1,0:T(8,128)(2,1)}, u32[]{:S(2)}, u32[]{:S(2)}) collective-permute-start(bf16[896,1024]{1,0:T(8,128)(2,1)} %bitcast.70), channel_id=1, source_target_pairs={{64,67},{65,64},{66,65},{67,66},{128,131},{129,128},{130,129},{131... | collective-permute-start | bytes 5505032 | tf_op jit(solution)/shard_map/ppermute | solution.py:578
  55.6 23.9 %collective-permute-start.2 = (bf16[128,3584]{1,0:T(8,128)(2,1)}, bf16[128,3584]{1,0:T(8,128)(2,1)}, u32[]{:S(2)}, u32[]{:S(2)}) collective-permute-start(bf16[128,3584]{1,0:T(8,128)(2,1)} %slice.52), channel_id=1, source_target_pairs={{0,1},{1,2},{2,3},{3,0},{192,193},{193,194},{194,195},{195,192},{4... | collective-permute-start | bytes 2752520 | tf_op jit(solution)/shard_map/ppermute | solution.py:578
  60.4 22.1 %collective-permute-start.3 = (bf16[128,3584]{1,0:T(8,128)(2,1)}, bf16[128,3584]{1,0:T(8,128)(2,1)}, u32[]{:S(2)}, u32[]{:S(2)}) collective-permute-start(bf16[128,3584]{1,0:T(8,128)(2,1)} %slice.53), channel_id=1, source_target_pairs={{0,3},{1,0},{2,1},{3,2},{192,195},{193,192},{194,193},{195,194},{4... | collective-permute-start | bytes 2752520 | tf_op jit(solution)/shard_map/ppermute | solution.py:578
  64.3 62.7 %collective-permute-start.9 = (bf16[128,3584]{1,0:T(8,128)(2,1)}, bf16[128,3584]{1,0:T(8,128)(2,1)}, u32[]{:S(2)}, u32[]{:S(2)}) collective-permute-start(bf16[128,3584]{1,0:T(8,128)(2,1)} %slice.52), channel_id=1, source_target_pairs={{64,65},{65,66},{66,67},{67,64},{128,129},{129,130},{130,131},{131... | collective-permute-start | bytes 2752520 | tf_op jit(solution)/shard_map/ppermute | solution.py:578
  79.5 47.4 %collective-permute-start.10 = (bf16[128,3584]{1,0:T(8,128)(2,1)}, bf16[128,3584]{1,0:T(8,128)(2,1)}, u32[]{:S(2)}, u32[]{:S(2)}) collective-permute-start(bf16[128,3584]{1,0:T(8,128)(2,1)} %slice.53), channel_id=1, source_target_pairs={{64,67},{65,64},{66,65},{67,66},{128,131},{129,128},{130,129},{131... | collective-permute-start | bytes 2752520 | tf_op jit(solution)/shard_map/ppermute | solution.py:578
  90.1 36.8 %copy-start.4 = (bf16[896,1024]{1,0:T(8,128)(2,1)}, bf16[896,1024]{1,0:T(8,128)(2,1)S(1)}, u32[]{:S(2)}) copy-start(bf16[896,1024]{1,0:T(8,128)(2,1)S(1)} %collective-permute-done.4.rest_6_) | copy-start | bytes 5505028
  90.2 16.6 %collective-permute-start.6 = (bf16[2,144,1024]{2,1,0:T(8,128)(2,1)}, bf16[2,144,1024]{2,1,0:T(8,128)(2,1)S(1)}, u32[]{:S(2)}, u32[]{:S(2)}) collective-permute-start(bf16[2,144,1024]{2,1,0:T(8,128)(2,1)} %hidden_pass.1.own), channel_id=1, source_target_pairs={{0,1},{1,2},{2,3},{3,0},{192,193},{193,194},{194,195},{195,192},{4... | collective-permute-start | bytes 1769480 | tf_op jit(solution)/shard_map/ppermute | solution.py:578
  92.8 16.8 %collective-permute-start.7 = (bf16[2,144,1024]{2,1,0:T(8,128)(2,1)}, bf16[2,144,1024]{2,1,0:T(8,128)(2,1)}, u32[]{:S(2)}, u32[]{:S(2)}) collective-permute-start(bf16[2,144,1024]{2,1,0:T(8,128)(2,1)} %hidden_pass.1.own), channel_id=1, source_target_pairs={{0,3},{1,0},{2,1},{3,2},{192,195},{193,192},{194,193},{195,194},{4... | collective-permute-start | bytes 1769480 | tf_op jit(solution)/shard_map/ppermute | solution.py:578
  97.4 23.0 %collective-permute-start.8 = (bf16[2,144,1024]{2,1,0:T(8,128)(2,1)}, bf16[2,144,1024]{2,1,0:T(8,128)(2,1)}, u32[]{:S(2)}, u32[]{:S(2)}) collective-permute-start(bf16[2,144,1024]{2,1,0:T(8,128)(2,1)} %hidden_pass.1.own), channel_id=1, source_target_pairs={{0,2},{1,3},{2,0},{3,1},{192,194},{193,195},{194,192},{195,193},{4... | collective-permute-start | bytes 1769480 | tf_op jit(solution)/shard_map/ppermute | solution.py:578
  106.8 13.6 %copy-start.7 = (bf16[2,144,1024]{2,1,0:T(8,128)(2,1)}, bf16[2,144,1024]{2,1,0:T(8,128)(2,1)S(1)}, u32[]{:S(2)}) copy-start(bf16[2,144,1024]{2,1,0:T(8,128)(2,1)S(1)} %collective-permute-done.6.left) | copy-start | bytes 1769476
  127.0 43.9 %all-to-all-start.1 = ((bf16[64,8,1024]{2,1,0:T(8,128)(2,1)}), bf16[64,8,1024]{2,1,0:T(8,128)(2,1)S(1)}, u32[]{:S(2)}, u32[]{:S(2)}) async-start(bf16[64,8,1024]{2,1,0:T(8,128)(2,1)} %bitcast.14), calls=%async_computation.1 | async-start | bytes 2097152 | tf_op jit(solution)/shard_map/all_to_all | solution.py:649
  142.3 268.3 %all-gather.9.cloned.1.call-start = ((), (), s32[]{:S(2)}) async-start(), calls=%async_computation.9 | async-start | bytes 9175040 | tf_op jit(solution)/shard_map/all_gather | solution.py:597
  144.5 38.8 %collective-permute-start.12 = (bf16[448,1024]{1,0:T(8,128)(2,1)}, bf16[448,1024]{1,0:T(8,128)(2,1)S(1)}, u32[]{:S(2)}, u32[]{:S(2)}) collective-permute-start(bf16[448,1024]{1,0:T(8,128)(2,1)} %slice.54), channel_id=1, source_target_pairs={{64,65},{65,66},{66,67},{67,64},{128,129},{129,130},{130,131},{131... | collective-permute-start | bytes 2752520 | tf_op jit(solution)/shard_map/ppermute | solution.py:578
  147.5 35.8 %collective-permute-start.13 = (bf16[448,1024]{1,0:T(8,128)(2,1)}, bf16[448,1024]{1,0:T(8,128)(2,1)}, u32[]{:S(2)}, u32[]{:S(2)}) collective-permute-start(bf16[448,1024]{1,0:T(8,128)(2,1)} %slice.55), channel_id=1, source_target_pairs={{64,67},{65,64},{66,65},{67,66},{128,131},{129,128},{130,129},{131... | collective-permute-start | bytes 2752520 | tf_op jit(solution)/shard_map/ppermute | solution.py:578
  171.3 11.3 %collective-permute-start.11 = (bf16[64,3584]{1,0:T(8,128)(2,1)S(1)}, bf16[64,3584]{1,0:T(8,128)(2,1)S(1)}, u32[]{:S(2)}, u32[]{:S(2)}) collective-permute-start(bf16[64,3584]{1,0:T(8,128)(2,1)S(1)} %post.4), channel_id=1, source_target_pairs={{0,64},{192,128},{1,65},{193,129},{2,66},{194,130},{3,67},{195,131... | collective-permute-start | bytes 1376264 | tf_op jit(solution)/shard_map/ppermute | solution.py:668
  183.3 33.5 %copy-start.6 = (bf16[448,1024]{1,0:T(8,128)(2,1)}, bf16[448,1024]{1,0:T(8,128)(2,1)S(1)}, u32[]{:S(2)}) copy-start(bf16[448,1024]{1,0:T(8,128)(2,1)S(1)} %collective-permute-done.12.rest_8_) | copy-start | bytes 2752516
  216.8 211.4 %all-gather.15.cloned.1.call-start = ((), (), s32[]{:S(2)}) async-start(), calls=%async_computation.12 | async-start | bytes 2949120 | tf_op jit(solution)/shard_map/all_gather | solution.py:657
  267.3 0.9 collective-permute-start.14
  269.8 30.9 %all-to-all-start.4 = ((bf16[16,8,4096]{2,1,0:T(8,128)(2,1)}), bf16[16,8,4096]{2,1,0:T(8,128)(2,1)S(1)}, u32[]{:S(2)}, u32[]{:S(2)}) async-start(bf16[16,8,4096]{2,1,0:T(8,128)(2,1)} %bitcast.25), calls=%async_computation.4 | async-start | bytes 2097152 | tf_op jit(solution)/shard_map/all_to_all | solution.py:562
  273.4 157.7 %all-gather.13.cloned.1.call-start = ((), (), s32[]{:S(2)}) async-start(), calls=%async_computation.11 | async-start | bytes 5242880 | tf_op jit(solution)/shard_map/all_gather | solution.py:597
  274.0 183.9 %all-gather.11.cloned.1.call-start = ((), (), s32[]{:S(2)}) async-start(), calls=%async_computation.10 | async-start | bytes 5242880 | tf_op jit(solution)/shard_map/all_gather | solution.py:597
  300.7 1.0 copy-start.5
  348.0 29.6 %collective-permute-start.15 = (bf16[64,3584]{1,0:T(8,128)(2,1)S(1)}, bf16[64,3584]{1,0:T(8,128)(2,1)S(1)}, u32[]{:S(2)}, u32[]{:S(2)}) collective-permute-start(bf16[64,3584]{1,0:T(8,128)(2,1)S(1)} %post.6), channel_id=1, source_target_pairs={{128,192},{64,0},{129,193},{65,1},{130,194},{66,2},{131,195},{67,3... | collective-permute-start | bytes 1376264 | tf_op jit(solution)/shard_map/ppermute | solution.py:668
  424.3 30.8 %all-to-all-start.7 = ((bf16[16,8,4096]{2,1,0:T(8,128)(2,1)}), bf16[16,8,4096]{2,1,0:T(8,128)(2,1)S(1)}, u32[]{:S(2)}, u32[]{:S(2)}) async-start(bf16[16,8,4096]{2,1,0:T(8,128)(2,1)} %bitcast.79), calls=%async_computation.7 | async-start | bytes 2097152 | tf_op jit(solution)/shard_map/all_to_all | solution.py:562
Sparse Core Ops, SparseCore 0:
  127.1 92.3 all-gather.6
  221.3 85.7 all-gather.8
  308.8 36.4 all-gather.14
  347.0 50.9 all-gather.12
  410.7 47.1 all-gather.10

commit v7 on v6

--- a/solution.py
+++ b/solution.py
@@ -239,45 +239,96 @@
     return ids
 
 
-def hidden_kernel(at_dir, me_ref, buf_hbm, fup_hbm, fgate_hbm, *rest):
+def near_kernel(at_dir, me_ref, buf_hbm, fup_hbm, fgate_hbm, *rest):
+    wd_refs, (rows_hbm, dgu_hbm, buf_ref, rows_ref, wd_ref, fup_ref, fgate_ref, dgu_ref, sems, out_sems) = rest[:3], rest[3:]
     pieces, groups = halves_plan(256)
-    wd_refs, rest = rest[: len(pieces)], rest[len(pieces) :]
-    dgu_ref, buf_ref, rows_ref, wd_ref, fup_ref, fgate_ref, sems = rest
+    pieces, groups = pieces[:3], groups[:3]
     stream = Stream(sems, 4)
     first = stream.add(buf_hbm, buf_ref)
     ids = add_shards(stream, wd_refs[:1], pieces[:1], wd_ref)
     stream.add(fup_hbm.at[at_dir], fup_ref)
     act = stream.add(fgate_hbm.at[at_dir], fgate_ref)
-    ids += add_shards(stream, wd_refs[1:], pieces[1:], wd_ref.at[pl.ds(256, FF - 256)])
+    ids += add_shards(stream, wd_refs[1:], pieces[1:], wd_ref.at[pl.ds(256, 512)])
     stream.wait(first)
     unpack_rows(buf_ref, rows_ref)
+    rows_copy = pltpu.make_async_copy(rows_ref, rows_hbm, out_sems.at[0])
+    rows_copy.start()
     stream.wait(act)
 
     def store(lo, dg, du):
         dgu_ref[0, :, pl.ds(lo, 256)] = dg
         dgu_ref[1, :, pl.ds(lo, 256)] = du
 
+    far = pl.multiple_of(((me_ref[0] + 2) & 3) * 256, 256)
+    store(far, jnp.zeros((SLOTS, 256), BF), jnp.zeros((SLOTS, 256), BF))
     hidden_stage(stream, groups, ids, me_ref[0], rows_ref, wd_ref, fup_ref, fgate_ref, store)
-
-
-def hidden_pass(at_dir, me, buf, fup, fgate, wd):
-    return pl.pallas_call(
-        functools.partial(hidden_kernel, at_dir),
-        in_specs=[IN_SMEM] + [IN_HBM] * (3 + len(wd)),
+    dgu_copy = pltpu.make_async_copy(dgu_ref, dgu_hbm, out_sems.at[1])
+    dgu_copy.start()
+    rows_copy.wait()
+    dgu_copy.wait()
+
+
+def hidden_near(at_dir, me, buf, fup, fgate, wd):
+    return pl.pallas_call(
+        functools.partial(near_kernel, at_dir),
+        in_specs=[IN_SMEM] + [IN_HBM] * 6,
+        out_specs=[IN_HBM, IN_HBM],
+        out_shape=(
+            jax.ShapeDtypeStruct((SLOTS, D), BF),
+            jax.ShapeDtypeStruct((2, SLOTS, FF), BF),
+        ),
+        scratch_shapes=[
+            pltpu.VMEM((MAIN, NCH * PCH), BF),
+            pltpu.VMEM((SLOTS, D), BF),
+            pltpu.VMEM((768, D), BF),
+            pltpu.VMEM((SLOTS, FF), F32),
+            pltpu.VMEM((SLOTS, FF), F32),
+            pltpu.VMEM((2, SLOTS, FF), BF),
+            pltpu.SemaphoreType.DMA((6,)),
+            pltpu.SemaphoreType.DMA((2,)),
+        ],
+        compiler_params=pltpu.CompilerParams(vmem_limit_bytes=60 << 20),
+        cost_estimate=pl.CostEstimate(flops=800_000_000, bytes_accessed=10_000_000, transcendentals=0),
+        name="hidden_near",
+    )(me, buf, fup, fgate, *wd)
+
+
+def far_kernel(at_dir, me_ref, rows_hbm, fup_hbm, fgate_hbm, near_hbm, top_hbm, low_hbm, dgu_ref, rows_ref, wd_ref, fup_ref, fgate_ref, sems):
+    lo = pl.multiple_of(((me_ref[0] + 2) & 3) * 256, 256)
+    cols = pl.ds(lo, 256)
+    stream = Stream(sems, 7)
+    stream.add(rows_hbm, rows_ref)
+    stream.add(top_hbm, wd_ref.at[pl.ds(0, 128)])
+    stream.add(low_hbm, wd_ref.at[pl.ds(128, 128)])
+    stream.add(fup_hbm.at[at_dir, :, cols], fup_ref)
+    stream.add(fgate_hbm.at[at_dir, :, cols], fgate_ref)
+    last = stream.add(near_hbm, dgu_ref)
+    stream.wait(last - 1)
+    d_hidden = dot(rows_ref[...], wd_ref[...], NT)
+    dg = (d_hidden * fgate_ref[...]).astype(BF)
+    du = (d_hidden * fup_ref[...]).astype(BF)
+    stream.wait(last)
+    dgu_ref[0, :, cols] = dg
+    dgu_ref[1, :, cols] = du
+
+
+def hidden_far(at_dir, me, rows, fup, fgate, near, top, low):
+    return pl.pallas_call(
+        functools.partial(far_kernel, at_dir),
+        in_specs=[IN_SMEM] + [IN_HBM] * 6,
         out_specs=IN_VMEM,
         out_shape=jax.ShapeDtypeStruct((2, SLOTS, FF), BF),
         scratch_shapes=[
-            pltpu.VMEM((MAIN, NCH * PCH), BF),
             pltpu.VMEM((SLOTS, D), BF),
-            pltpu.VMEM((FF, D), BF),
-            pltpu.VMEM((SLOTS, FF), F32),
-            pltpu.VMEM((SLOTS, FF), F32),
-            pltpu.SemaphoreType.DMA((3 + len(wd),)),
+            pltpu.VMEM((256, D), BF),
+            pltpu.VMEM((SLOTS, 256), F32),
+            pltpu.VMEM((SLOTS, 256), F32),
+            pltpu.SemaphoreType.DMA((6,)),
         ],
         compiler_params=pltpu.CompilerParams(vmem_limit_bytes=60 << 20),
-        cost_estimate=pl.CostEstimate(flops=1_060_000_000, bytes_accessed=11_000_000, transcendentals=0),
-        name="hidden_pass",
-    )(me, buf, fup, fgate, *wd)
+        cost_estimate=pl.CostEstimate(flops=270_000_000, bytes_accessed=5_000_000, transcendentals=0),
+        name="hidden_far",
+    )(me, rows, fup, fgate, near, top, low)
 
 
 def own_grads_kernel(me_ref, own, left, right, far, wg_hbm, wu_hbm, out_hbm, out_ref, d_ref, wg_ref, wu_ref, sems, out_sems):
@@ -638,11 +689,12 @@
         if step == 0:
             halves = tie(wd_near[0], buf)[:128], tie(wd_near[1], buf)[128:]
             wd_outer = (wd_own,) + wd_near + hop(*halves, outer)
-            dgu = hidden_pass(at, me, buf, fup, fgate, wd_outer)
+            rows, dgu_part = hidden_near(at, me, buf, fup, fgate, wd_outer[:3])
+            dgu = hidden_far(at, me, rows, fup, fgate, dgu_part, *wd_outer[3:])
             ready = tie(dgu, *wg_near)
             others = [shift_dp(ready, step_dp, outer) for step_dp in (1, -1, 2)]
             sent = own_grads(me, dgu, *others, wg_own, wu_own)
-            wd = (wd_own,) + wd_near + hop(*halves, inner)
+            wd = (wd_own,) + wd_near + hop(*[tie(h, dgu_part) for h in halves], inner)
             sent = tie(sent, *wd)
             wu_full = gather(tie(wu_own, sent))
             wg = (wg_own,) + wg_near + far(*[tie(w, sent) for w in wg_near], inner)

time: 471 us -> 473 us (level)
    ppermute x13, waiting for transfers between devices: 55.1 us -> 48.8 us  [shift_dp(): return lax.ppermute(value, ('pipe', 'dp'), pairs)]
    ppermute x3, waiting for transfers between devices: 38.3 us -> 44.4 us  [per_device(): cur = lax.ppermute(result, 'pipe', moves[step])]
    pallas_call x1 -> x2, Pallas kernels: 7.54 us -> 9.73 us  [the longest x1 6.27 us: hidden_near(): pl.pallas_call(functools.partial(near_kernel, at_dir), in_specs=[IN_SMEM]...]
  transfers between devices with their start and end apart: 25 -> 25, of which waited for: 14 -> 14; matrix products, arithmetic and copies ran while one was open for 4% -> 3% of each run, Pallas kernels for 16% -> 16%
where the time goes in v7:
time: 473 us; the launch traced here: 471 us
  waiting for transfers between devices  162 us (34%)
  blocking collectives  129 us (27%)
  Pallas kernels  81.6 us (17%)
  starting transfers between devices  65 us (14%)
  local copies, waits for them, and re-layouts  16.2 us (3%)
  between operations  14.2 us (3%)
    all_to_all x4, blocking collectives, exchange(): lax.all_to_all(buf.reshape(EXP, 8, NCH * PCH), 'expert', split_axis=0, co...  129 us
    ppermute x13, waiting for transfers between devices, shift_dp(): return lax.ppermute(value, ('pipe', 'dp'), pairs)  48.8 us
    all_to_all x3, waiting for transfers between devices, exchange(): lax.all_to_all(buf.reshape(EXP, 8, NCH * PCH), 'expert', split_axis=0, co...  45.1 us
    ppermute x3, waiting for transfers between devices, per_device(): cur = lax.ppermute(result, 'pipe', moves[step])  44.4 us
    ppermute x13, starting transfers between devices, shift_dp(): return lax.ppermute(value, ('pipe', 'dp'), pairs)  28.8 us
    pallas_call x2, Pallas kernels, expert_pass(): pl.pallas_call(functools.partial(expert_kernel, at_dir, whole), in_specs=...  27.4 us
    all_to_all x1, waiting for transfers between devices, per_device(): lax.all_to_all(sent.reshape(4 * EXP, 8, PCH), ('dp', 'expert'), split_axi...  21.7 us
    all_to_all x3, starting transfers between devices, exchange(): lax.all_to_all(buf.reshape(EXP, 8, NCH * PCH), 'expert', split_axis=0, co...  16.9 us
  transfers between devices with their start and end apart: 25, of which 14 were waited for; matrix products, arithmetic and copies ran while one was open for 3% of the time, Pallas kernels for 16%

profile of v7, /device:TPU:1, one launch (start us, length us, event | category | flops | bytes accessed | tf_op | source)
XLA Modules:
  0.0 471.4 jit_solution(7727484112352144130)
XLA Ops:
  7.2 2.2 collective-permute-start
  9.4 1.5 collective-permute-start.1
  10.9 0.8 copy.29
  12.3 0.7 select_bitcast_fusion.3
  13.0 1.2 select_bitcast_fusion.2.old_ref.new_ref.cur_ref
  14.2 1.6 pre.4
  15.8 9.6 %all-to-all-start = ((bf16[16,8,4096]{2,1,0:T(8,128)(2,1)}), bf16[16,8,4096]{2,1,0:T(8,128)(2,1)}, u32[]{:S(2)}, u32[]{:S(2)}) async-start(bf16[16,8,4096]{2,1,0:T(8,128)(2,1)} %bitcast.5), calls=%async_computation | async-start | bytes 2097152 | tf_op jit(solution)/shard_map/all_to_all | solution.py:613
  25.5 2.3 prep.1
  27.8 1.1 copy-done
  28.9 1.0 copy-done.1
  29.9 18.9 %collective-permute-done.rest_1_ = bf16[256,3584]{1,0:T(8,128)(2,1)} collective-permute-done((bf16[256,3584]{1,0:T(8,128)(2,1)}, bf16[256,3584]{1,0:T(8,128)(2,1)}, u32[]{:S(2)}, u32[]{:S(2)}) %collective-permute-start) | collective-permute-done | bytes 1835040 | tf_op jit(solution)/shard_map/ppermute | solution.py:629
  48.8 1.2 collective-permute-done.1.rest_2_
  50.0 0.8 collective-permute-start.4
  50.8 1.9 collective-permute-start.5
  52.7 0.8 all-to-all-done
  53.4 2.2 slice.52
  55.6 2.7 collective-permute-start.2
  58.3 2.2 slice.53
  60.5 3.8 collective-permute-start.3
  64.3 6.3 %hidden_near.1 = (bf16[144,3584]{1,0:T(8,128)(2,1)}, bf16[2,144,1024]{2,1,0:T(8,128)(2,1)}) custom-call(s32[1]{0:T(128)} %bitcast.1.me_ref, bf16[128,4096]{1,0:T(8,128)(2,1)} %bitcast.6.buf_hbm, f32[2,144,1024]{2,1,0:T(8,128)} %copy-done, f32[2,144,1024]{2,1,0:T(8,128)} %copy-done.1, bf16[256,3584]{1,0:T(8,128)(2,1)} %bitcast.65, ...), custom_call_target="tpu_custom_call" | custom-call | flops 800000000 | bytes 10000000 | tf_op jit(solution)/shard_map/hidden_near/pallas_call | solution.py:272
  70.5 1.6 collective-permute-start.9
  72.2 7.3 %collective-permute-done.2.top_hbm.rest_3_ = bf16[128,3584]{1,0:T(8,128)(2,1)} collective-permute-done((bf16[128,3584]{1,0:T(8,128)(2,1)}, bf16[128,3584]{1,0:T(8,128)(2,1)}, u32[]{:S(2)}, u32[]{:S(2)}) %collective-permute-start.2) | collective-permute-done | bytes 917536 | tf_op jit(solution)/shard_map/ppermute | solution.py:629
  79.5 1.6 collective-permute-start.10
  81.1 1.5 collective-permute-done.3.low_hbm.rest_4_
  82.6 3.5 hidden_far.1.own
  86.1 2.7 collective-permute-start.6
  88.8 4.6 collective-permute-start.7
  93.3 3.1 collective-permute-start.8
  96.4 6.3 %collective-permute-done.6.left = bf16[2,144,1024]{2,1,0:T(8,128)(2,1)S(1)} collective-permute-done((bf16[2,144,1024]{2,1,0:T(8,128)(2,1)}, bf16[2,144,1024]{2,1,0:T(8,128)(2,1)S(1)}, u32[]{:S(2)}, u32[]{:S(2)}) %collective-permute-start.6) | collective-permute-done | bytes 589856 | tf_op jit(solution)/shard_map/ppermute | solution.py:629
  102.7 2.8 collective-permute-done.7.right
  105.5 10.8 %collective-permute-done.8.far = bf16[2,144,1024]{2,1,0:T(8,128)(2,1)} collective-permute-done((bf16[2,144,1024]{2,1,0:T(8,128)(2,1)}, bf16[2,144,1024]{2,1,0:T(8,128)(2,1)}, u32[]{:S(2)}, u32[]{:S(2)}) %collective-permute-start.8) | collective-permute-done | bytes 589856 | tf_op jit(solution)/shard_map/ppermute | solution.py:629
  116.3 6.5 %own_grads.1 = bf16[4,128,1024]{2,1,0:T(8,128)(2,1)} custom-call(s32[1]{0:T(128)} %bitcast.1.me_ref, bf16[2,144,1024]{2,1,0:T(8,128)(2,1)} %hidden_far.1.own, bf16[2,144,1024]{2,1,0:T(8,128)(2,1)} %copy-done.7, bf16[2,144,1024]{2,1,0:T(8,128)(2,1)} %collective-permute-done.7.right, bf16[2,144,1024]{2,1,0:T(8,128)(2,1)} %collective-permute-done.8.far, ...), custom_call_target="tpu_custom_call" | custom-call | flops 2120000000 | bytes 8000000 | tf_op jit(solution)/shard_map/own_grads/pallas_call | solution.py:357
  122.9 15.4 %all-to-all-start.1 = ((bf16[64,8,1024]{2,1,0:T(8,128)(2,1)}), bf16[64,8,1024]{2,1,0:T(8,128)(2,1)S(1)}, u32[]{:S(2)}, u32[]{:S(2)}) async-start(bf16[64,8,1024]{2,1,0:T(8,128)(2,1)} %bitcast.14), calls=%async_computation.1 | async-start | bytes 2097152 | tf_op jit(solution)/shard_map/all_to_all | solution.py:701
  138.3 2.2 slice.54
  140.4 0.7 collective-permute-start.12
  141.2 2.3 slice.55
  143.5 1.6 collective-permute-start.13
  145.1 21.7 %all-to-all-done.1 = bf16[64,8,1024]{2,1,0:T(8,128)(2,1)S(1)} async-done(((bf16[64,8,1024]{2,1,0:T(8,128)(2,1)}), bf16[64,8,1024]{2,1,0:T(8,128)(2,1)S(1)}, u32[]{:S(2)}, u32[]{:S(2)}) %all-to-all-start.1) | async-done | bytes 1048608 | tf_op jit(solution)/shard_map/all_to_all | solution.py:701
  167.3 1.3 collective-permute-start.11
  168.6 10.0 %collective-permute-done.11.new_ref.cur_ref.old_ref = bf16[64,3584]{1,0:T(8,128)(2,1)S(1)} collective-permute-done((bf16[64,3584]{1,0:T(8,128)(2,1)S(1)}, bf16[64,3584]{1,0:T(8,128)(2,1)S(1)}, u32[]{:S(2)}, u32[]{:S(2)}) %collective-permute-start.11) | collective-permute-done | bytes 458784 | tf_op jit(solution)/shard_map/ppermute | solution.py:720
  179.3 33.4 %all_to_all.40 = bf16[16,8,4096]{2,1,0:T(8,128)(2,1)} all-to-all(bf16[16,8,4096]{2,1,0:T(8,128)(2,1)S(1)} %bitcast.51), channel_id=1, replica_groups=mesh['pipe'=4,'expert'=16,'dp'=4] {'expert'}, dimensions={0} | all-to-all | bytes 2097152 | tf_op jit(solution)/shard_map/all_to_all | solution.py:613
  213.5 11.4 %front_pass.1 = (f32[4,144,896]{2,1,0:T(8,128)}, bf16[144,1024]{1,0:T(8,128)(2,1)}) custom-call(s32[1]{0:T(128)} %bitcast.1.me_ref, bf16[128,4096]{1,0:T(8,128)(2,1)} %bitcast.77, f32[2,144,1024]{2,1,0:T(8,128)} %copy-done, f32[2,144,1024]{2,1,0:T(8,128)} %copy-done.1, bf16[256,3584]{1,0:T(8,128)(2,1)} %bitcast.66, ...), custom_call_target="tpu_custom_call" | custom-call | flops 2100000000 | bytes 20000000 | tf_op jit(solution)/shard_map/front_pass/pallas_call | solution.py:484
  224.9 6.4 %back_pass.1 = bf16[128,4096]{1,0:T(8,128)(2,1)} custom-call(bf16[144,1024]{1,0:T(8,128)(2,1)} %get-tuple-element.37.du_hbm, f32[4,144,896]{2,1,0:T(8,128)} %get-tuple-element.38.part_hbm, bf16[3584,1024]{1,0:T(8,128)(2,1)} %all-gather.7.cloned.1.call-done.wu_hbm.rest_10_.rest_6_), custom_call_target="tpu_custom_call" | custom-call | flops 1060000000 | bytes 10000000 | tf_op jit(solution)/shard_map/back_pass/pallas_call | solution.py:523
  231.3 31.4 %all_to_all.41 = bf16[16,8,4096]{2,1,0:T(8,128)(2,1)S(1)} all-to-all(bf16[16,8,4096]{2,1,0:T(8,128)(2,1)} %bitcast.82), channel_id=1, replica_groups=mesh['pipe'=4,'expert'=16,'dp'=4] {'expert'}, dimensions={0} | all-to-all | bytes 2097152 | tf_op jit(solution)/shard_map/all_to_all | solution.py:613
  263.2 0.7 collective-permute-start.14
  264.1 1.7 pre.6
  265.8 3.5 all-to-all-start.4
  270.2 26.5 %all-to-all-done.4 = bf16[16,8,4096]{2,1,0:T(8,128)(2,1)S(1)} async-done(((bf16[16,8,4096]{2,1,0:T(8,128)(2,1)}), bf16[16,8,4096]{2,1,0:T(8,128)(2,1)S(1)}, u32[]{:S(2)}, u32[]{:S(2)}) %all-to-all-start.4) | async-done | bytes 1048608 | tf_op jit(solution)/shard_map/all_to_all | solution.py:613
  296.7 1.0 copy-done.5
  297.7 13.7 %expert_pass.2 = bf16[128,4096]{1,0:T(8,128)(2,1)} custom-call(s32[1]{0:T(128)} %bitcast.1.me_ref, bf16[128,4096]{1,0:T(8,128)(2,1)} %bitcast.80, f32[2,144,1024]{2,1,0:T(8,128)} %copy-done, f32[2,144,1024]{2,1,0:T(8,128)} %copy-done.1, bf16[256,3584]{1,0:T(8,128)(2,1)} %bitcast.67, bf16[256,3584]{1,0:T(8,128)(2,1)} %collective-permute-done.rest_1_, ...), custom_call_target="tpu_custom_call" | custom-call | flops 3200000000 | bytes 28000000 | tf_op jit(solution)/shard_map/expert_pass/pallas_call | solution.py:424
  311.4 32.1 %all_to_all.42 = bf16[16,8,4096]{2,1,0:T(8,128)(2,1)S(1)} all-to-all(bf16[16,8,4096]{2,1,0:T(8,128)(2,1)} %bitcast.81), channel_id=1, replica_groups=mesh['pipe'=4,'expert'=16,'dp'=4] {'expert'}, dimensions={0} | all-to-all | bytes 2097152 | tf_op jit(solution)/shard_map/all_to_all | solution.py:613
  344.0 1.3 collective-permute-start.15
  345.3 34.4 %collective-permute-done.15.new_ref.cur_ref = bf16[64,3584]{1,0:T(8,128)(2,1)S(1)} collective-permute-done((bf16[64,3584]{1,0:T(8,128)(2,1)S(1)}, bf16[64,3584]{1,0:T(8,128)(2,1)S(1)}, u32[]{:S(2)}, u32[]{:S(2)}) %collective-permute-start.15) | collective-permute-done | bytes 458784 | tf_op jit(solution)/shard_map/ppermute | solution.py:720
  380.3 32.1 %all_to_all.43 = bf16[16,8,4096]{2,1,0:T(8,128)(2,1)} all-to-all(bf16[16,8,4096]{2,1,0:T(8,128)(2,1)S(1)} %bitcast.52), channel_id=1, replica_groups=mesh['pipe'=4,'expert'=16,'dp'=4] {'expert'}, dimensions={0} | all-to-all | bytes 2097152 | tf_op jit(solution)/shard_map/all_to_all | solution.py:613
  412.5 13.7 %expert_pass.3 = bf16[128,4096]{1,0:T(8,128)(2,1)} custom-call(s32[1]{0:T(128)} %bitcast.1.me_ref, bf16[128,4096]{1,0:T(8,128)(2,1)} %bitcast.76, f32[2,144,1024]{2,1,0:T(8,128)} %copy-done, f32[2,144,1024]{2,1,0:T(8,128)} %copy-done.1, bf16[256,3584]{1,0:T(8,128)(2,1)} %bitcast.68, bf16[256,3584]{1,0:T(8,128)(2,1)} %collective-permute-done.rest_1_, ...), custom_call_target="tpu_custom_call" | custom-call | flops 3200000000 | bytes 28000000 | tf_op jit(solution)/shard_map/expert_pass/pallas_call | solution.py:424
  426.1 3.8 all-to-all-start.7
  430.0 1.1 dynamic-slice_bitcast_fusion
  431.2 0.9 copy.33.h_hbm
  432.1 0.9 copy.32.h_ref
  433.0 6.1 %down_first.1.sum_hbm = f32[256,3584]{1,0:T(8,128)} custom-call(bf16[256,576]{1,0:T(8,128)(2,1)} %copy.32.h_ref, bf16[512,4096]{1,0:T(8,128)(2,1)} %all-gather.13.cloned.1.call-done.buf_ref), custom_call_target="tpu_custom_call" | custom-call | flops 1060000000 | bytes 8000000 | tf_op jit(solution)/shard_map/down_first/pallas_call | solution.py:559
  439.1 17.9 %all-to-all-done.7 = bf16[16,8,4096]{2,1,0:T(8,128)(2,1)S(1)} async-done(((bf16[16,8,4096]{2,1,0:T(8,128)(2,1)}), bf16[16,8,4096]{2,1,0:T(8,128)(2,1)S(1)}, u32[]{:S(2)}, u32[]{:S(2)}) %all-to-all-start.7) | async-done | bytes 1048608 | tf_op jit(solution)/shard_map/all_to_all | solution.py:613
  457.5 1.1 maximum_select_fusion
  458.6 0.9 all-gather.11.cloned.1.call-done.buf_hbm
  459.4 5.4 %down_last.1 = bf16[256,3584]{1,0:T(8,128)(2,1)} custom-call(bf16[256,576]{1,0:T(8,128)(2,1)} %copy.33.h_hbm, bf16[512,4096]{1,0:T(8,128)(2,1)} %all-gather.11.cloned.1.call-done.buf_hbm, f32[256,3584]{1,0:T(8,128)} %down_first.1.sum_hbm), custom_call_target="tpu_custom_call" | custom-call | flops 1060000000 | bytes 10000000 | tf_op jit(solution)/shard_map/down_last/pallas_call | solution.py:592
  (53 shorter events, 6.0 us)
Async XLA Ops:
  7.2 41.7 %collective-permute-start = (bf16[256,3584]{1,0:T(8,128)(2,1)}, bf16[256,3584]{1,0:T(8,128)(2,1)}, u32[]{:S(2)}, u32[]{:S(2)}) collective-permute-start(bf16[256,3584]{1,0:T(8,128)(2,1)} %bitcast.63), channel_id=1, source_target_pairs={{0,1},{1,2},{2,3},{3,0},{64,65},{65,66},{66,67},{67,64},{128,129},... | collective-permute-start | bytes 5505032 | tf_op jit(solution)/shard_map/ppermute | solution.py:629
  9.4 40.6 %collective-permute-start.1 = (bf16[256,3584]{1,0:T(8,128)(2,1)}, bf16[256,3584]{1,0:T(8,128)(2,1)}, u32[]{:S(2)}, u32[]{:S(2)}) collective-permute-start(bf16[256,3584]{1,0:T(8,128)(2,1)} %bitcast.64), channel_id=1, source_target_pairs={{0,3},{1,0},{2,1},{3,2},{64,67},{65,64},{66,65},{67,66},{128,131},... | collective-permute-start | bytes 5505032 | tf_op jit(solution)/shard_map/ppermute | solution.py:629
  14.2 11.3 %copy-start.2 = (bf16[2,1,1,1,144,1024]{5,4,3,2,1,0:T(8,128)(2,1)S(1)}, bf16[2,1,1,1,144,1024]{5,4,3,2,1,0:T(8,128)(2,1)}, u32[]{:S(2)}) copy-start(bf16[2,1,1,1,144,1024]{5,4,3,2,1,0:T(8,128)(2,1)} %param.11) | copy-start | bytes 1769476
  14.2 11.3 %copy-start.3 = (bf16[2,1,1,1,144,1024]{5,4,3,2,1,0:T(8,128)(2,1)S(1)}, bf16[2,1,1,1,144,1024]{5,4,3,2,1,0:T(8,128)(2,1)}, u32[]{:S(2)}) copy-start(bf16[2,1,1,1,144,1024]{5,4,3,2,1,0:T(8,128)(2,1)} %param.12) | copy-start | bytes 1769476
  15.8 37.6 %all-to-all-start = ((bf16[16,8,4096]{2,1,0:T(8,128)(2,1)}), bf16[16,8,4096]{2,1,0:T(8,128)(2,1)}, u32[]{:S(2)}, u32[]{:S(2)}) async-start(bf16[16,8,4096]{2,1,0:T(8,128)(2,1)} %bitcast.5), calls=%async_computation | async-start | bytes 2097152 | tf_op jit(solution)/shard_map/all_to_all | solution.py:613
  25.4 199.5 %all-gather.7.cloned.1.call-start = ((), (), s32[]{:S(2)}) async-start(), calls=%async_computation.8 | async-start | bytes 9175040 | tf_op jit(solution)/shard_map/all_gather | solution.py:648
  27.8 1.1 copy-start
  28.9 1.0 copy-start.1
  50.0 36.1 %collective-permute-start.4 = (bf16[896,1024]{1,0:T(8,128)(2,1)}, bf16[896,1024]{1,0:T(8,128)(2,1)S(1)}, u32[]{:S(2)}, u32[]{:S(2)}) collective-permute-start(bf16[896,1024]{1,0:T(8,128)(2,1)} %bitcast.69), channel_id=1, source_target_pairs={{64,65},{65,66},{66,67},{67,64},{128,129},{129,130},{130,131},{131... | collective-permute-start | bytes 5505032 | tf_op jit(solution)/shard_map/ppermute | solution.py:629
  50.8 35.3 %collective-permute-start.5 = (bf16[896,1024]{1,0:T(8,128)(2,1)}, bf16[896,1024]{1,0:T(8,128)(2,1)}, u32[]{:S(2)}, u32[]{:S(2)}) collective-permute-start(bf16[896,1024]{1,0:T(8,128)(2,1)} %bitcast.70), channel_id=1, source_target_pairs={{64,67},{65,64},{66,65},{67,66},{128,131},{129,128},{130,129},{131... | collective-permute-start | bytes 5505032 | tf_op jit(solution)/shard_map/ppermute | solution.py:629
  55.6 23.9 %collective-permute-start.2 = (bf16[128,3584]{1,0:T(8,128)(2,1)}, bf16[128,3584]{1,0:T(8,128)(2,1)}, u32[]{:S(2)}, u32[]{:S(2)}) collective-permute-start(bf16[128,3584]{1,0:T(8,128)(2,1)} %slice.52), channel_id=1, source_target_pairs={{0,1},{1,2},{2,3},{3,0},{192,193},{193,194},{194,195},{195,192},{4... | collective-permute-start | bytes 2752520 | tf_op jit(solution)/shard_map/ppermute | solution.py:629
  60.5 22.1 %collective-permute-start.3 = (bf16[128,3584]{1,0:T(8,128)(2,1)}, bf16[128,3584]{1,0:T(8,128)(2,1)}, u32[]{:S(2)}, u32[]{:S(2)}) collective-permute-start(bf16[128,3584]{1,0:T(8,128)(2,1)} %slice.53), channel_id=1, source_target_pairs={{0,3},{1,0},{2,1},{3,2},{192,195},{193,192},{194,193},{195,194},{4... | collective-permute-start | bytes 2752520 | tf_op jit(solution)/shard_map/ppermute | solution.py:629
  70.5 52.3 %collective-permute-start.9 = (bf16[128,3584]{1,0:T(8,128)(2,1)}, bf16[128,3584]{1,0:T(8,128)(2,1)}, u32[]{:S(2)}, u32[]{:S(2)}) collective-permute-start(bf16[128,3584]{1,0:T(8,128)(2,1)} %slice.52), channel_id=1, source_target_pairs={{64,65},{65,66},{66,67},{67,64},{128,129},{129,130},{130,131},{131... | collective-permute-start | bytes 2752520 | tf_op jit(solution)/shard_map/ppermute | solution.py:629
  79.5 43.3 %collective-permute-start.10 = (bf16[128,3584]{1,0:T(8,128)(2,1)}, bf16[128,3584]{1,0:T(8,128)(2,1)}, u32[]{:S(2)}, u32[]{:S(2)}) collective-permute-start(bf16[128,3584]{1,0:T(8,128)(2,1)} %slice.53), channel_id=1, source_target_pairs={{64,67},{65,64},{66,65},{67,66},{128,131},{129,128},{130,129},{131... | collective-permute-start | bytes 2752520 | tf_op jit(solution)/shard_map/ppermute | solution.py:629
  86.1 36.8 %copy-start.4 = (bf16[896,1024]{1,0:T(8,128)(2,1)}, bf16[896,1024]{1,0:T(8,128)(2,1)S(1)}, u32[]{:S(2)}) copy-start(bf16[896,1024]{1,0:T(8,128)(2,1)S(1)} %collective-permute-done.4.rest_6_) | copy-start | bytes 5505028
  86.1 16.6 %collective-permute-start.6 = (bf16[2,144,1024]{2,1,0:T(8,128)(2,1)}, bf16[2,144,1024]{2,1,0:T(8,128)(2,1)S(1)}, u32[]{:S(2)}, u32[]{:S(2)}) collective-permute-start(bf16[2,144,1024]{2,1,0:T(8,128)(2,1)} %hidden_far.1.own), channel_id=1, source_target_pairs={{0,1},{1,2},{2,3},{3,0},{192,193},{193,194},{194,195},{195,192},{4... | collective-permute-start | bytes 1769480 | tf_op jit(solution)/shard_map/ppermute | solution.py:629
  88.8 16.7 %collective-permute-start.7 = (bf16[2,144,1024]{2,1,0:T(8,128)(2,1)}, bf16[2,144,1024]{2,1,0:T(8,128)(2,1)}, u32[]{:S(2)}, u32[]{:S(2)}) collective-permute-start(bf16[2,144,1024]{2,1,0:T(8,128)(2,1)} %hidden_far.1.own), channel_id=1, source_target_pairs={{0,3},{1,0},{2,1},{3,2},{192,195},{193,192},{194,193},{195,194},{4... | collective-permute-start | bytes 1769480 | tf_op jit(solution)/shard_map/ppermute | solution.py:629
  93.3 23.0 %collective-permute-start.8 = (bf16[2,144,1024]{2,1,0:T(8,128)(2,1)}, bf16[2,144,1024]{2,1,0:T(8,128)(2,1)}, u32[]{:S(2)}, u32[]{:S(2)}) collective-permute-start(bf16[2,144,1024]{2,1,0:T(8,128)(2,1)} %hidden_far.1.own), channel_id=1, source_target_pairs={{0,2},{1,3},{2,0},{3,1},{192,194},{193,195},{194,192},{195,193},{4... | collective-permute-start | bytes 1769480 | tf_op jit(solution)/shard_map/ppermute | solution.py:629
  102.7 13.6 %copy-start.7 = (bf16[2,144,1024]{2,1,0:T(8,128)(2,1)}, bf16[2,144,1024]{2,1,0:T(8,128)(2,1)S(1)}, u32[]{:S(2)}) copy-start(bf16[2,144,1024]{2,1,0:T(8,128)(2,1)S(1)} %collective-permute-done.6.left) | copy-start | bytes 1769476
  122.9 43.9 %all-to-all-start.1 = ((bf16[64,8,1024]{2,1,0:T(8,128)(2,1)}), bf16[64,8,1024]{2,1,0:T(8,128)(2,1)S(1)}, u32[]{:S(2)}, u32[]{:S(2)}) async-start(bf16[64,8,1024]{2,1,0:T(8,128)(2,1)} %bitcast.14), calls=%async_computation.1 | async-start | bytes 2097152 | tf_op jit(solution)/shard_map/all_to_all | solution.py:701
  138.2 274.2 %all-gather.9.cloned.1.call-start = ((), (), s32[]{:S(2)}) async-start(), calls=%async_computation.9 | async-start | bytes 9175040 | tf_op jit(solution)/shard_map/all_gather | solution.py:648
  140.4 38.8 %collective-permute-start.12 = (bf16[448,1024]{1,0:T(8,128)(2,1)}, bf16[448,1024]{1,0:T(8,128)(2,1)S(1)}, u32[]{:S(2)}, u32[]{:S(2)}) collective-permute-start(bf16[448,1024]{1,0:T(8,128)(2,1)} %slice.54), channel_id=1, source_target_pairs={{64,65},{65,66},{66,67},{67,64},{128,129},{129,130},{130,131},{131... | collective-permute-start | bytes 2752520 | tf_op jit(solution)/shard_map/ppermute | solution.py:629
  143.5 35.8 %collective-permute-start.13 = (bf16[448,1024]{1,0:T(8,128)(2,1)}, bf16[448,1024]{1,0:T(8,128)(2,1)}, u32[]{:S(2)}, u32[]{:S(2)}) collective-permute-start(bf16[448,1024]{1,0:T(8,128)(2,1)} %slice.55), channel_id=1, source_target_pairs={{64,67},{65,64},{66,65},{67,66},{128,131},{129,128},{130,129},{131... | collective-permute-start | bytes 2752520 | tf_op jit(solution)/shard_map/ppermute | solution.py:629
  167.3 11.3 %collective-permute-start.11 = (bf16[64,3584]{1,0:T(8,128)(2,1)S(1)}, bf16[64,3584]{1,0:T(8,128)(2,1)S(1)}, u32[]{:S(2)}, u32[]{:S(2)}) collective-permute-start(bf16[64,3584]{1,0:T(8,128)(2,1)S(1)} %post.4), channel_id=1, source_target_pairs={{0,64},{192,128},{1,65},{193,129},{2,66},{194,130},{3,67},{195,131... | collective-permute-start | bytes 1376264 | tf_op jit(solution)/shard_map/ppermute | solution.py:720
  179.3 33.5 %copy-start.6 = (bf16[448,1024]{1,0:T(8,128)(2,1)}, bf16[448,1024]{1,0:T(8,128)(2,1)S(1)}, u32[]{:S(2)}) copy-start(bf16[448,1024]{1,0:T(8,128)(2,1)S(1)} %collective-permute-done.12.rest_8_) | copy-start | bytes 2752516
  212.7 217.3 %all-gather.15.cloned.1.call-start = ((), (), s32[]{:S(2)}) async-start(), calls=%async_computation.12 | async-start | bytes 2949120 | tf_op jit(solution)/shard_map/all_gather | solution.py:709
  263.2 0.9 collective-permute-start.14
  265.8 30.9 %all-to-all-start.4 = ((bf16[16,8,4096]{2,1,0:T(8,128)(2,1)}), bf16[16,8,4096]{2,1,0:T(8,128)(2,1)S(1)}, u32[]{:S(2)}, u32[]{:S(2)}) async-start(bf16[16,8,4096]{2,1,0:T(8,128)(2,1)} %bitcast.25), calls=%async_computation.4 | async-start | bytes 2097152 | tf_op jit(solution)/shard_map/all_to_all | solution.py:613
  269.4 163.6 %all-gather.13.cloned.1.call-start = ((), (), s32[]{:S(2)}) async-start(), calls=%async_computation.11 | async-start | bytes 5242880 | tf_op jit(solution)/shard_map/all_gather | solution.py:648
  270.0 189.5 %all-gather.11.cloned.1.call-start = ((), (), s32[]{:S(2)}) async-start(), calls=%async_computation.10 | async-start | bytes 5242880 | tf_op jit(solution)/shard_map/all_gather | solution.py:648
  296.7 1.0 copy-start.5
  344.0 35.7 %collective-permute-start.15 = (bf16[64,3584]{1,0:T(8,128)(2,1)S(1)}, bf16[64,3584]{1,0:T(8,128)(2,1)S(1)}, u32[]{:S(2)}, u32[]{:S(2)}) collective-permute-start(bf16[64,3584]{1,0:T(8,128)(2,1)S(1)} %post.6), channel_id=1, source_target_pairs={{128,192},{64,0},{129,193},{65,1},{130,194},{66,2},{131,195},{67,3... | collective-permute-start | bytes 1376264 | tf_op jit(solution)/shard_map/ppermute | solution.py:720
  426.1 30.8 %all-to-all-start.7 = ((bf16[16,8,4096]{2,1,0:T(8,128)(2,1)}), bf16[16,8,4096]{2,1,0:T(8,128)(2,1)S(1)}, u32[]{:S(2)}, u32[]{:S(2)}) async-start(bf16[16,8,4096]{2,1,0:T(8,128)(2,1)} %bitcast.79), calls=%async_computation.7 | async-start | bytes 2097152 | tf_op jit(solution)/shard_map/all_to_all | solution.py:613
Sparse Core Ops, SparseCore 0:
  123.0 92.3 all-gather.6
  217.2 89.7 all-gather.8
  308.8 36.4 all-gather.14
  347.0 50.9 all-gather.12
  412.6 46.8 all-gather.10

commit v8 on v7

--- a/solution.py
+++ b/solution.py
@@ -693,11 +693,13 @@
             dgu = hidden_far(at, me, rows, fup, fgate, dgu_part, *wd_outer[3:])
             ready = tie(dgu, *wg_near)
             others = [shift_dp(ready, step_dp, outer) for step_dp in (1, -1, 2)]
-            sent = own_grads(me, dgu, *others, wg_own, wu_own)
+            wg_halves = tie(wg_near[0], others[0])[: CH // 2], tie(wg_near[1], others[0])[CH // 2 :]
+            far_dgu, top, low = lax.optimization_barrier((others[2],) + wg_halves)
+            sent = own_grads(me, dgu, *others[:2], far_dgu, wg_own, wu_own)
             wd = (wd_own,) + wd_near + hop(*[tie(h, dgu_part) for h in halves], inner)
             sent = tie(sent, *wd)
             wu_full = gather(tie(wu_own, sent))
-            wg = (wg_own,) + wg_near + far(*[tie(w, sent) for w in wg_near], inner)
+            wg = (wg_own,) + wg_near + hop(tie(top, sent), tie(low, sent), inner)
             home = lax.all_to_all(
                 sent.reshape(4 * EXP, 8, PCH), ("dp", "expert"), split_axis=0, concat_axis=0, tiled=True
             ).reshape(4, MAIN, PCH)

time: 473 us -> 467 us (0.987)
    ppermute x3, waiting for transfers between devices: 44.4 us -> 37.8 us  [per_device(): cur = lax.ppermute(result, 'pipe', moves[step])]
where the time goes in v8:
time: 467 us; the launch traced here: 466 us
  waiting for transfers between devices  159 us (34%)
  blocking collectives  129 us (28%)
  Pallas kernels  81.6 us (17%)
  starting transfers between devices  62.2 us (13%)
  local copies, waits for them, and re-layouts  16.7 us (4%)
  between operations  14.2 us (3%)
    all_to_all x4, blocking collectives, exchange(): lax.all_to_all(buf.reshape(EXP, 8, NCH * PCH), 'expert', split_axis=0, co...  129 us
    ppermute x13, waiting for transfers between devices, shift_dp(): return lax.ppermute(value, ('pipe', 'dp'), pairs)  48 us
    all_to_all x3, waiting for transfers between devices, exchange(): lax.all_to_all(buf.reshape(EXP, 8, NCH * PCH), 'expert', split_axis=0, co...  45.2 us
    ppermute x3, waiting for transfers between devices, per_device(): cur = lax.ppermute(result, 'pipe', moves[step])  37.8 us
    ppermute x13, starting transfers between devices, shift_dp(): return lax.ppermute(value, ('pipe', 'dp'), pairs)  28.8 us
    pallas_call x2, Pallas kernels, expert_pass(): pl.pallas_call(functools.partial(expert_kernel, at_dir, whole), in_specs=...  27.4 us
    all_to_all x1, waiting for transfers between devices, per_device(): lax.all_to_all(sent.reshape(4 * EXP, 8, PCH), ('dp', 'expert'), split_axi...  26.1 us
    all_to_all x3, starting transfers between devices, exchange(): lax.all_to_all(buf.reshape(EXP, 8, NCH * PCH), 'expert', split_axis=0, co...  16.9 us
  transfers between devices with their start and end apart: 25, of which 14 were waited for; matrix products, arithmetic and copies ran while one was open for 3% of the time, Pallas kernels for 16%

profile of v8, /device:TPU:1, one launch (start us, length us, event | category | flops | bytes accessed | tf_op | source)
XLA Modules:
  0.0 465.8 jit_solution(17695495831796993393)
XLA Ops:
  7.2 2.2 collective-permute-start
  9.4 1.5 collective-permute-start.1
  10.9 0.8 copy.29
  12.3 0.7 select_bitcast_fusion.3
  13.0 1.2 select_bitcast_fusion.2.old_ref.new_ref.cur_ref
  14.2 1.6 pre.4
  15.8 9.6 %all-to-all-start = ((bf16[16,8,4096]{2,1,0:T(8,128)(2,1)}), bf16[16,8,4096]{2,1,0:T(8,128)(2,1)}, u32[]{:S(2)}, u32[]{:S(2)}) async-start(bf16[16,8,4096]{2,1,0:T(8,128)(2,1)} %bitcast.5), calls=%async_computation | async-start | bytes 2097152 | tf_op jit(solution)/shard_map/all_to_all | solution.py:613
  25.5 2.2 prep.1
  27.8 1.0 copy-done
  28.8 1.0 copy-done.1
  29.8 19.0 %collective-permute-done.rest_1_ = bf16[256,3584]{1,0:T(8,128)(2,1)} collective-permute-done((bf16[256,3584]{1,0:T(8,128)(2,1)}, bf16[256,3584]{1,0:T(8,128)(2,1)}, u32[]{:S(2)}, u32[]{:S(2)}) %collective-permute-start) | collective-permute-done | bytes 1835040 | tf_op jit(solution)/shard_map/ppermute | solution.py:629
  48.8 1.2 collective-permute-done.1.rest_2_
  50.0 0.8 collective-permute-start.4
  50.8 1.9 collective-permute-start.5
  52.6 0.8 all-to-all-done
  53.4 2.2 slice.52
  55.6 2.7 collective-permute-start.2
  58.3 2.2 slice.53
  60.4 3.8 collective-permute-start.3
  64.3 6.3 %hidden_near.1 = (bf16[144,3584]{1,0:T(8,128)(2,1)}, bf16[2,144,1024]{2,1,0:T(8,128)(2,1)}) custom-call(s32[1]{0:T(128)} %bitcast.1.me_ref, bf16[128,4096]{1,0:T(8,128)(2,1)} %bitcast.6.buf_hbm, f32[2,144,1024]{2,1,0:T(8,128)} %copy-done, f32[2,144,1024]{2,1,0:T(8,128)} %copy-done.1, bf16[256,3584]{1,0:T(8,128)(2,1)} %bitcast.65, ...), custom_call_target="tpu_custom_call" | custom-call | flops 800000000 | bytes 10000000 | tf_op jit(solution)/shard_map/hidden_near/pallas_call | solution.py:272
  70.5 1.6 collective-permute-start.9
  72.2 7.4 %collective-permute-done.2.top_hbm.rest_3_ = bf16[128,3584]{1,0:T(8,128)(2,1)} collective-permute-done((bf16[128,3584]{1,0:T(8,128)(2,1)}, bf16[128,3584]{1,0:T(8,128)(2,1)}, u32[]{:S(2)}, u32[]{:S(2)}) %collective-permute-start.2) | collective-permute-done | bytes 917536 | tf_op jit(solution)/shard_map/ppermute | solution.py:629
  79.5 1.6 collective-permute-start.10
  81.1 1.5 collective-permute-done.3.low_hbm.rest_4_
  82.6 3.5 hidden_far.1.own
  86.1 2.6 collective-permute-start.6
  88.8 5.8 %collective-permute-start.8 = (bf16[2,144,1024]{2,1,0:T(8,128)(2,1)}, bf16[2,144,1024]{2,1,0:T(8,128)(2,1)S(1)}, u32[]{:S(2)}, u32[]{:S(2)}) collective-permute-start(bf16[2,144,1024]{2,1,0:T(8,128)(2,1)} %hidden_far.1.own), channel_id=1, source_target_pairs={{0,2},{1,3},{2,0},{3,1},{192,194},{193,195},{194,192},{195,193},{4... | collective-permute-start | bytes 1769480 | tf_op jit(solution)/shard_map/ppermute | solution.py:629
  94.5 1.9 collective-permute-start.7
  96.4 6.3 %collective-permute-done.6.left = bf16[2,144,1024]{2,1,0:T(8,128)(2,1)S(1)} collective-permute-done((bf16[2,144,1024]{2,1,0:T(8,128)(2,1)}, bf16[2,144,1024]{2,1,0:T(8,128)(2,1)S(1)}, u32[]{:S(2)}, u32[]{:S(2)}) %collective-permute-start.6) | collective-permute-done | bytes 589856 | tf_op jit(solution)/shard_map/ppermute | solution.py:629
  102.7 1.1 slice.54
  103.8 2.2 slice.55
  106.0 10.3 %collective-permute-done.8.far = bf16[2,144,1024]{2,1,0:T(8,128)(2,1)S(1)} collective-permute-done((bf16[2,144,1024]{2,1,0:T(8,128)(2,1)}, bf16[2,144,1024]{2,1,0:T(8,128)(2,1)S(1)}, u32[]{:S(2)}, u32[]{:S(2)}) %collective-permute-start.8) | collective-permute-done | bytes 589856 | tf_op jit(solution)/shard_map/ppermute | solution.py:629
  116.3 0.9 copy-done.8
  117.1 2.5 collective-permute-done.7.right
  119.6 0.9 copy-done.9
  120.5 6.5 %own_grads.1 = bf16[4,128,1024]{2,1,0:T(8,128)(2,1)} custom-call(s32[1]{0:T(128)} %bitcast.1.me_ref, bf16[2,144,1024]{2,1,0:T(8,128)(2,1)} %hidden_far.1.own, bf16[2,144,1024]{2,1,0:T(8,128)(2,1)} %copy-done.7, bf16[2,144,1024]{2,1,0:T(8,128)(2,1)} %copy-done.9, bf16[2,144,1024]{2,1,0:T(8,128)(2,1)} %copy-done.8, bf16[896,1024]{1,0:T(8,128)(2,1)} %bitcast.71, ...), custom_call_target="tpu_custom_call" | custom-call | flops 2120000000 | bytes 8000000 | tf_op jit(solution)/shard_map/own_grads/pallas_call | solution.py:357
  127.0 12.6 %all-to-all-start.1 = ((bf16[64,8,1024]{2,1,0:T(8,128)(2,1)}), bf16[64,8,1024]{2,1,0:T(8,128)(2,1)S(1)}, u32[]{:S(2)}, u32[]{:S(2)}) async-start(bf16[64,8,1024]{2,1,0:T(8,128)(2,1)} %bitcast.14), calls=%async_computation.1 | async-start | bytes 2097152 | tf_op jit(solution)/shard_map/all_to_all | solution.py:703
  139.7 0.7 collective-permute-start.12
  140.4 1.6 collective-permute-start.13
  142.0 26.1 %all-to-all-done.1 = bf16[64,8,1024]{2,1,0:T(8,128)(2,1)S(1)} async-done(((bf16[64,8,1024]{2,1,0:T(8,128)(2,1)}), bf16[64,8,1024]{2,1,0:T(8,128)(2,1)S(1)}, u32[]{:S(2)}, u32[]{:S(2)}) %all-to-all-start.1) | async-done | bytes 1048608 | tf_op jit(solution)/shard_map/all_to_all | solution.py:703
  168.7 1.3 collective-permute-start.11
  170.0 10.0 %collective-permute-done.11.new_ref.cur_ref.old_ref = bf16[64,3584]{1,0:T(8,128)(2,1)S(1)} collective-permute-done((bf16[64,3584]{1,0:T(8,128)(2,1)S(1)}, bf16[64,3584]{1,0:T(8,128)(2,1)S(1)}, u32[]{:S(2)}, u32[]{:S(2)}) %collective-permute-start.11) | collective-permute-done | bytes 458784 | tf_op jit(solution)/shard_map/ppermute | solution.py:722
  180.7 33.4 %all_to_all.40 = bf16[16,8,4096]{2,1,0:T(8,128)(2,1)} all-to-all(bf16[16,8,4096]{2,1,0:T(8,128)(2,1)S(1)} %bitcast.51), channel_id=1, replica_groups=mesh['pipe'=4,'expert'=16,'dp'=4] {'expert'}, dimensions={0} | all-to-all | bytes 2097152 | tf_op jit(solution)/shard_map/all_to_all | solution.py:613
  214.9 11.4 %front_pass.1 = (f32[4,144,896]{2,1,0:T(8,128)}, bf16[144,1024]{1,0:T(8,128)(2,1)}) custom-call(s32[1]{0:T(128)} %bitcast.1.me_ref, bf16[128,4096]{1,0:T(8,128)(2,1)} %bitcast.77, f32[2,144,1024]{2,1,0:T(8,128)} %copy-done, f32[2,144,1024]{2,1,0:T(8,128)} %copy-done.1, bf16[256,3584]{1,0:T(8,128)(2,1)} %bitcast.66, ...), custom_call_target="tpu_custom_call" | custom-call | flops 2100000000 | bytes 20000000 | tf_op jit(solution)/shard_map/front_pass/pallas_call | solution.py:484
  226.3 6.4 %back_pass.1 = bf16[128,4096]{1,0:T(8,128)(2,1)} custom-call(bf16[144,1024]{1,0:T(8,128)(2,1)} %get-tuple-element.47.du_hbm, f32[4,144,896]{2,1,0:T(8,128)} %get-tuple-element.48.part_hbm, bf16[3584,1024]{1,0:T(8,128)(2,1)} %all-gather.7.cloned.1.call-done.wu_hbm.rest_10_.rest_6_), custom_call_target="tpu_custom_call" | custom-call | flops 1060000000 | bytes 10000000 | tf_op jit(solution)/shard_map/back_pass/pallas_call | solution.py:523
  232.7 31.4 %all_to_all.41 = bf16[16,8,4096]{2,1,0:T(8,128)(2,1)S(1)} all-to-all(bf16[16,8,4096]{2,1,0:T(8,128)(2,1)} %bitcast.82), channel_id=1, replica_groups=mesh['pipe'=4,'expert'=16,'dp'=4] {'expert'}, dimensions={0} | all-to-all | bytes 2097152 | tf_op jit(solution)/shard_map/all_to_all | solution.py:613
  265.5 1.7 pre.6
  267.2 3.5 all-to-all-start.4
  271.6 26.5 %all-to-all-done.4 = bf16[16,8,4096]{2,1,0:T(8,128)(2,1)S(1)} async-done(((bf16[16,8,4096]{2,1,0:T(8,128)(2,1)}), bf16[16,8,4096]{2,1,0:T(8,128)(2,1)S(1)}, u32[]{:S(2)}, u32[]{:S(2)}) %all-to-all-start.4) | async-done | bytes 1048608 | tf_op jit(solution)/shard_map/all_to_all | solution.py:613
  298.1 1.0 copy-done.5
  299.1 13.7 %expert_pass.2 = bf16[128,4096]{1,0:T(8,128)(2,1)} custom-call(s32[1]{0:T(128)} %bitcast.1.me_ref, bf16[128,4096]{1,0:T(8,128)(2,1)} %bitcast.80, f32[2,144,1024]{2,1,0:T(8,128)} %copy-done, f32[2,144,1024]{2,1,0:T(8,128)} %copy-done.1, bf16[256,3584]{1,0:T(8,128)(2,1)} %bitcast.67, bf16[256,3584]{1,0:T(8,128)(2,1)} %collective-permute-done.rest_1_, ...), custom_call_target="tpu_custom_call" | custom-call | flops 3200000000 | bytes 28000000 | tf_op jit(solution)/shard_map/expert_pass/pallas_call | solution.py:424
  312.8 32.1 %all_to_all.42 = bf16[16,8,4096]{2,1,0:T(8,128)(2,1)S(1)} all-to-all(bf16[16,8,4096]{2,1,0:T(8,128)(2,1)} %bitcast.81), channel_id=1, replica_groups=mesh['pipe'=4,'expert'=16,'dp'=4] {'expert'}, dimensions={0} | all-to-all | bytes 2097152 | tf_op jit(solution)/shard_map/all_to_all | solution.py:613
  345.4 1.3 collective-permute-start.15
  346.7 27.8 %collective-permute-done.15.new_ref.cur_ref = bf16[64,3584]{1,0:T(8,128)(2,1)S(1)} collective-permute-done((bf16[64,3584]{1,0:T(8,128)(2,1)S(1)}, bf16[64,3584]{1,0:T(8,128)(2,1)S(1)}, u32[]{:S(2)}, u32[]{:S(2)}) %collective-permute-start.15) | collective-permute-done | bytes 458784 | tf_op jit(solution)/shard_map/ppermute | solution.py:722
  375.1 32.3 %all_to_all.43 = bf16[16,8,4096]{2,1,0:T(8,128)(2,1)} all-to-all(bf16[16,8,4096]{2,1,0:T(8,128)(2,1)S(1)} %bitcast.52), channel_id=1, replica_groups=mesh['pipe'=4,'expert'=16,'dp'=4] {'expert'}, dimensions={0} | all-to-all | bytes 2097152 | tf_op jit(solution)/shard_map/all_to_all | solution.py:613
  407.4 13.7 %expert_pass.3 = bf16[128,4096]{1,0:T(8,128)(2,1)} custom-call(s32[1]{0:T(128)} %bitcast.1.me_ref, bf16[128,4096]{1,0:T(8,128)(2,1)} %bitcast.76, f32[2,144,1024]{2,1,0:T(8,128)} %copy-done, f32[2,144,1024]{2,1,0:T(8,128)} %copy-done.1, bf16[256,3584]{1,0:T(8,128)(2,1)} %bitcast.68, bf16[256,3584]{1,0:T(8,128)(2,1)} %collective-permute-done.rest_1_, ...), custom_call_target="tpu_custom_call" | custom-call | flops 3200000000 | bytes 28000000 | tf_op jit(solution)/shard_map/expert_pass/pallas_call | solution.py:424
  421.1 3.8 all-to-all-start.7
  425.0 1.1 dynamic-slice_bitcast_fusion
  426.1 0.9 copy.33.h_hbm
  427.1 0.9 copy.32.h_ref
  428.0 6.1 %down_first.1.sum_hbm = f32[256,3584]{1,0:T(8,128)} custom-call(bf16[256,576]{1,0:T(8,128)(2,1)} %copy.32.h_ref, bf16[512,4096]{1,0:T(8,128)(2,1)} %all-gather.13.cloned.1.call-done.buf_ref), custom_call_target="tpu_custom_call" | custom-call | flops 1060000000 | bytes 8000000 | tf_op jit(solution)/shard_map/down_first/pallas_call | solution.py:559
  434.1 17.9 %all-to-all-done.7 = bf16[16,8,4096]{2,1,0:T(8,128)(2,1)S(1)} async-done(((bf16[16,8,4096]{2,1,0:T(8,128)(2,1)}), bf16[16,8,4096]{2,1,0:T(8,128)(2,1)S(1)}, u32[]{:S(2)}, u32[]{:S(2)}) %all-to-all-start.7) | async-done | bytes 1048608 | tf_op jit(solution)/shard_map/all_to_all | solution.py:613
  452.5 1.1 maximum_select_fusion
  453.9 5.4 %down_last.1 = bf16[256,3584]{1,0:T(8,128)(2,1)} custom-call(bf16[256,576]{1,0:T(8,128)(2,1)} %copy.33.h_hbm, bf16[512,4096]{1,0:T(8,128)(2,1)} %all-gather.11.cloned.1.call-done.buf_hbm, f32[256,3584]{1,0:T(8,128)} %down_first.1.sum_hbm), custom_call_target="tpu_custom_call" | custom-call | flops 1060000000 | bytes 10000000 | tf_op jit(solution)/shard_map/down_last/pallas_call | solution.py:592
  (57 shorter events, 7.0 us)
Async XLA Ops:
  7.2 41.7 %collective-permute-start = (bf16[256,3584]{1,0:T(8,128)(2,1)}, bf16[256,3584]{1,0:T(8,128)(2,1)}, u32[]{:S(2)}, u32[]{:S(2)}) collective-permute-start(bf16[256,3584]{1,0:T(8,128)(2,1)} %bitcast.63), channel_id=1, source_target_pairs={{0,1},{1,2},{2,3},{3,0},{64,65},{65,66},{66,67},{67,64},{128,129},... | collective-permute-start | bytes 5505032 | tf_op jit(solution)/shard_map/ppermute | solution.py:629
  9.4 40.6 %collective-permute-start.1 = (bf16[256,3584]{1,0:T(8,128)(2,1)}, bf16[256,3584]{1,0:T(8,128)(2,1)}, u32[]{:S(2)}, u32[]{:S(2)}) collective-permute-start(bf16[256,3584]{1,0:T(8,128)(2,1)} %bitcast.64), channel_id=1, source_target_pairs={{0,3},{1,0},{2,1},{3,2},{64,67},{65,64},{66,65},{67,66},{128,131},... | collective-permute-start | bytes 5505032 | tf_op jit(solution)/shard_map/ppermute | solution.py:629
  14.2 11.3 %copy-start.2 = (bf16[2,1,1,1,144,1024]{5,4,3,2,1,0:T(8,128)(2,1)S(1)}, bf16[2,1,1,1,144,1024]{5,4,3,2,1,0:T(8,128)(2,1)}, u32[]{:S(2)}) copy-start(bf16[2,1,1,1,144,1024]{5,4,3,2,1,0:T(8,128)(2,1)} %param.11) | copy-start | bytes 1769476
  14.2 11.3 %copy-start.3 = (bf16[2,1,1,1,144,1024]{5,4,3,2,1,0:T(8,128)(2,1)S(1)}, bf16[2,1,1,1,144,1024]{5,4,3,2,1,0:T(8,128)(2,1)}, u32[]{:S(2)}) copy-start(bf16[2,1,1,1,144,1024]{5,4,3,2,1,0:T(8,128)(2,1)} %param.12) | copy-start | bytes 1769476
  15.8 37.6 %all-to-all-start = ((bf16[16,8,4096]{2,1,0:T(8,128)(2,1)}), bf16[16,8,4096]{2,1,0:T(8,128)(2,1)}, u32[]{:S(2)}, u32[]{:S(2)}) async-start(bf16[16,8,4096]{2,1,0:T(8,128)(2,1)} %bitcast.5), calls=%async_computation | async-start | bytes 2097152 | tf_op jit(solution)/shard_map/all_to_all | solution.py:613
  25.4 200.9 %all-gather.7.cloned.1.call-start = ((), (), s32[]{:S(2)}) async-start(), calls=%async_computation.8 | async-start | bytes 9175040 | tf_op jit(solution)/shard_map/all_gather | solution.py:648
  27.8 1.1 copy-start
  28.8 1.0 copy-start.1
  50.0 36.1 %collective-permute-start.4 = (bf16[896,1024]{1,0:T(8,128)(2,1)}, bf16[896,1024]{1,0:T(8,128)(2,1)S(1)}, u32[]{:S(2)}, u32[]{:S(2)}) collective-permute-start(bf16[896,1024]{1,0:T(8,128)(2,1)} %bitcast.69), channel_id=1, source_target_pairs={{64,65},{65,66},{66,67},{67,64},{128,129},{129,130},{130,131},{131... | collective-permute-start | bytes 5505032 | tf_op jit(solution)/shard_map/ppermute | solution.py:629
  50.8 35.3 %collective-permute-start.5 = (bf16[896,1024]{1,0:T(8,128)(2,1)}, bf16[896,1024]{1,0:T(8,128)(2,1)}, u32[]{:S(2)}, u32[]{:S(2)}) collective-permute-start(bf16[896,1024]{1,0:T(8,128)(2,1)} %bitcast.70), channel_id=1, source_target_pairs={{64,67},{65,64},{66,65},{67,66},{128,131},{129,128},{130,129},{131... | collective-permute-start | bytes 5505032 | tf_op jit(solution)/shard_map/ppermute | solution.py:629
  55.6 23.9 %collective-permute-start.2 = (bf16[128,3584]{1,0:T(8,128)(2,1)}, bf16[128,3584]{1,0:T(8,128)(2,1)}, u32[]{:S(2)}, u32[]{:S(2)}) collective-permute-start(bf16[128,3584]{1,0:T(8,128)(2,1)} %slice.52), channel_id=1, source_target_pairs={{0,1},{1,2},{2,3},{3,0},{192,193},{193,194},{194,195},{195,192},{4... | collective-permute-start | bytes 2752520 | tf_op jit(solution)/shard_map/ppermute | solution.py:629
  60.4 22.1 %collective-permute-start.3 = (bf16[128,3584]{1,0:T(8,128)(2,1)}, bf16[128,3584]{1,0:T(8,128)(2,1)}, u32[]{:S(2)}, u32[]{:S(2)}) collective-permute-start(bf16[128,3584]{1,0:T(8,128)(2,1)} %slice.53), channel_id=1, source_target_pairs={{0,3},{1,0},{2,1},{3,2},{192,195},{193,192},{194,193},{195,194},{4... | collective-permute-start | bytes 2752520 | tf_op jit(solution)/shard_map/ppermute | solution.py:629
  70.5 56.4 %collective-permute-start.9 = (bf16[128,3584]{1,0:T(8,128)(2,1)}, bf16[128,3584]{1,0:T(8,128)(2,1)}, u32[]{:S(2)}, u32[]{:S(2)}) collective-permute-start(bf16[128,3584]{1,0:T(8,128)(2,1)} %slice.52), channel_id=1, source_target_pairs={{64,65},{65,66},{66,67},{67,64},{128,129},{129,130},{130,131},{131... | collective-permute-start | bytes 2752520 | tf_op jit(solution)/shard_map/ppermute | solution.py:629
  79.5 47.5 %collective-permute-start.10 = (bf16[128,3584]{1,0:T(8,128)(2,1)}, bf16[128,3584]{1,0:T(8,128)(2,1)}, u32[]{:S(2)}, u32[]{:S(2)}) collective-permute-start(bf16[128,3584]{1,0:T(8,128)(2,1)} %slice.53), channel_id=1, source_target_pairs={{64,67},{65,64},{66,65},{67,66},{128,131},{129,128},{130,129},{131... | collective-permute-start | bytes 2752520 | tf_op jit(solution)/shard_map/ppermute | solution.py:629
  86.1 19.9 %copy-start.4 = (bf16[896,1024]{1,0:T(8,128)(2,1)}, bf16[896,1024]{1,0:T(8,128)(2,1)S(1)}, u32[]{:S(2)}) copy-start(bf16[896,1024]{1,0:T(8,128)(2,1)S(1)} %collective-permute-done.4.rest_6_) | copy-start | bytes 5505028
  86.1 16.6 %collective-permute-start.6 = (bf16[2,144,1024]{2,1,0:T(8,128)(2,1)}, bf16[2,144,1024]{2,1,0:T(8,128)(2,1)S(1)}, u32[]{:S(2)}, u32[]{:S(2)}) collective-permute-start(bf16[2,144,1024]{2,1,0:T(8,128)(2,1)} %hidden_far.1.own), channel_id=1, source_target_pairs={{0,1},{1,2},{2,3},{3,0},{192,193},{193,194},{194,195},{195,192},{4... | collective-permute-start | bytes 1769480 | tf_op jit(solution)/shard_map/ppermute | solution.py:629
  88.8 27.5 %collective-permute-start.8 = (bf16[2,144,1024]{2,1,0:T(8,128)(2,1)}, bf16[2,144,1024]{2,1,0:T(8,128)(2,1)S(1)}, u32[]{:S(2)}, u32[]{:S(2)}) collective-permute-start(bf16[2,144,1024]{2,1,0:T(8,128)(2,1)} %hidden_far.1.own), channel_id=1, source_target_pairs={{0,2},{1,3},{2,0},{3,1},{192,194},{193,195},{194,192},{195,193},{4... | collective-permute-start | bytes 1769480 | tf_op jit(solution)/shard_map/ppermute | solution.py:629
  94.5 25.1 %collective-permute-start.7 = (bf16[2,144,1024]{2,1,0:T(8,128)(2,1)}, bf16[2,144,1024]{2,1,0:T(8,128)(2,1)S(1)}, u32[]{:S(2)}, u32[]{:S(2)}) collective-permute-start(bf16[2,144,1024]{2,1,0:T(8,128)(2,1)} %hidden_far.1.own), channel_id=1, source_target_pairs={{0,3},{1,0},{2,1},{3,2},{192,195},{193,192},{194,193},{195,194},{4... | collective-permute-start | bytes 1769480 | tf_op jit(solution)/shard_map/ppermute | solution.py:629
  102.7 3.3 copy-start.7
  116.3 0.9 copy-start.8
  119.6 0.9 copy-start.9
  127.0 41.2 %all-to-all-start.1 = ((bf16[64,8,1024]{2,1,0:T(8,128)(2,1)}), bf16[64,8,1024]{2,1,0:T(8,128)(2,1)S(1)}, u32[]{:S(2)}, u32[]{:S(2)}) async-start(bf16[64,8,1024]{2,1,0:T(8,128)(2,1)} %bitcast.14), calls=%async_computation.1 | async-start | bytes 2097152 | tf_op jit(solution)/shard_map/all_to_all | solution.py:703
  139.6 267.8 %all-gather.9.cloned.1.call-start = ((), (), s32[]{:S(2)}) async-start(), calls=%async_computation.9 | async-start | bytes 9175040 | tf_op jit(solution)/shard_map/all_gather | solution.py:648
  139.7 41.0 %collective-permute-start.12 = (bf16[448,1024]{1,0:T(8,128)(2,1)}, bf16[448,1024]{1,0:T(8,128)(2,1)S(1)}, u32[]{:S(2)}, u32[]{:S(2)}) collective-permute-start(bf16[448,1024]{1,0:T(8,128)(2,1)} %slice.54), channel_id=1, source_target_pairs={{64,65},{65,66},{66,67},{67,64},{128,129},{129,130},{130,131},{131... | collective-permute-start | bytes 2752520 | tf_op jit(solution)/shard_map/ppermute | solution.py:629
  140.4 40.3 %collective-permute-start.13 = (bf16[448,1024]{1,0:T(8,128)(2,1)}, bf16[448,1024]{1,0:T(8,128)(2,1)}, u32[]{:S(2)}, u32[]{:S(2)}) collective-permute-start(bf16[448,1024]{1,0:T(8,128)(2,1)} %slice.55), channel_id=1, source_target_pairs={{64,67},{65,64},{66,65},{67,66},{128,131},{129,128},{130,129},{131... | collective-permute-start | bytes 2752520 | tf_op jit(solution)/shard_map/ppermute | solution.py:629
  168.7 11.3 %collective-permute-start.11 = (bf16[64,3584]{1,0:T(8,128)(2,1)S(1)}, bf16[64,3584]{1,0:T(8,128)(2,1)S(1)}, u32[]{:S(2)}, u32[]{:S(2)}) collective-permute-start(bf16[64,3584]{1,0:T(8,128)(2,1)S(1)} %post.4), channel_id=1, source_target_pairs={{0,64},{192,128},{1,65},{193,129},{2,66},{194,130},{3,67},{195,131... | collective-permute-start | bytes 1376264 | tf_op jit(solution)/shard_map/ppermute | solution.py:722
  180.7 33.5 %copy-start.6 = (bf16[448,1024]{1,0:T(8,128)(2,1)}, bf16[448,1024]{1,0:T(8,128)(2,1)S(1)}, u32[]{:S(2)}) copy-start(bf16[448,1024]{1,0:T(8,128)(2,1)S(1)} %collective-permute-done.12.rest_8_) | copy-start | bytes 2752516
  214.1 210.8 %all-gather.15.cloned.1.call-start = ((), (), s32[]{:S(2)}) async-start(), calls=%async_computation.12 | async-start | bytes 2949120 | tf_op jit(solution)/shard_map/all_gather | solution.py:711
  264.6 0.9 collective-permute-start.14
  267.2 30.9 %all-to-all-start.4 = ((bf16[16,8,4096]{2,1,0:T(8,128)(2,1)}), bf16[16,8,4096]{2,1,0:T(8,128)(2,1)S(1)}, u32[]{:S(2)}, u32[]{:S(2)}) async-start(bf16[16,8,4096]{2,1,0:T(8,128)(2,1)} %bitcast.25), calls=%async_computation.4 | async-start | bytes 2097152 | tf_op jit(solution)/shard_map/all_to_all | solution.py:613
  270.8 157.2 %all-gather.13.cloned.1.call-start = ((), (), s32[]{:S(2)}) async-start(), calls=%async_computation.11 | async-start | bytes 5242880 | tf_op jit(solution)/shard_map/all_gather | solution.py:648
  271.4 182.6 %all-gather.11.cloned.1.call-start = ((), (), s32[]{:S(2)}) async-start(), calls=%async_computation.10 | async-start | bytes 5242880 | tf_op jit(solution)/shard_map/all_gather | solution.py:648
  298.1 1.0 copy-start.5
  345.4 29.1 %collective-permute-start.15 = (bf16[64,3584]{1,0:T(8,128)(2,1)S(1)}, bf16[64,3584]{1,0:T(8,128)(2,1)S(1)}, u32[]{:S(2)}, u32[]{:S(2)}) collective-permute-start(bf16[64,3584]{1,0:T(8,128)(2,1)S(1)} %post.6), channel_id=1, source_target_pairs={{128,192},{64,0},{129,193},{65,1},{130,194},{66,2},{131,195},{67,3... | collective-permute-start | bytes 1376264 | tf_op jit(solution)/shard_map/ppermute | solution.py:722
  421.1 30.8 %all-to-all-start.7 = ((bf16[16,8,4096]{2,1,0:T(8,128)(2,1)}), bf16[16,8,4096]{2,1,0:T(8,128)(2,1)S(1)}, u32[]{:S(2)}, u32[]{:S(2)}) async-start(bf16[16,8,4096]{2,1,0:T(8,128)(2,1)} %bitcast.79), calls=%async_computation.7 | async-start | bytes 2097152 | tf_op jit(solution)/shard_map/all_to_all | solution.py:613
Sparse Core Ops, SparseCore 0:
  127.1 89.6 all-gather.6
  218.6 85.7 all-gather.8
  306.2 36.4 all-gather.14
  344.4 50.9 all-gather.12
  407.5 46.3 all-gather.10

commit v9 on v8

--- a/solution.py
+++ b/solution.py
@@ -438,7 +438,7 @@
             pltpu.VMEM((SLOTS, FF), BF),
             pltpu.SemaphoreType.DMA((copies,)),
         ],
-        compiler_params=pltpu.CompilerParams(vmem_limit_bytes=60 << 20),
+        compiler_params=pltpu.CompilerParams(vmem_limit_bytes=48 << 20),
         cost_estimate=pl.CostEstimate(flops=3_200_000_000, bytes_accessed=28_000_000, transcendentals=0),
         name="expert_pass",
     )(me, buf, fup, fgate, *wd, *wg, wu)
@@ -552,7 +552,7 @@
 
 
 def down_first_kernel(h_ref, buf_ref, out_ref, rows_ref):
-    out_ref[...] = down_term(h_ref, buf_ref, rows_ref)
+    out_ref[...] = down_term(h_ref, buf_ref, rows_ref).astype(BF)
 
 
 def down_first(h, buf):
@@ -564,7 +564,7 @@
             pl.BlockSpec((4 * MAIN, PCH), lambda j: (0, j)),
         ],
         out_specs=pl.BlockSpec((256, CH), lambda j: (0, j)),
-        out_shape=jax.ShapeDtypeStruct((256, D), F32),
+        out_shape=jax.ShapeDtypeStruct((256, D), BF),
         scratch_shapes=[pltpu.VMEM((4 * SLOTS, CH), BF)],
         compiler_params=pltpu.CompilerParams(vmem_limit_bytes=60 << 20),
         cost_estimate=pl.CostEstimate(flops=1_060_000_000, bytes_accessed=8_000_000, transcendentals=0),
@@ -581,7 +581,7 @@
     outs = []
     for j in range(NCH):
         stream.wait(2 + 2 * j)
-        out_ref[j] = (sum_ref[j] + down_term(h_ref, buf_ref.at[j], rows_ref.at[j % 2])).astype(BF)
+        out_ref[j] = (sum_ref[j].astype(F32) + down_term(h_ref, buf_ref.at[j], rows_ref.at[j % 2])).astype(BF)
         outs.append(pltpu.make_async_copy(out_ref.at[j], out_hbm.at[:, pl.ds(j * CH, CH)], out_sems.at[j]))
         outs[-1].start()
     for copy in outs:
@@ -597,7 +597,7 @@
         scratch_shapes=[
             pltpu.VMEM((256, 4 * SLOTS), BF),
             pltpu.VMEM((NCH, 4 * MAIN, PCH), BF),
-            pltpu.VMEM((NCH, 256, CH), F32),
+            pltpu.VMEM((NCH, 256, CH), BF),
             pltpu.VMEM((NCH, 256, CH), BF),
             pltpu.VMEM((2, 4 * SLOTS, CH), BF),
             pltpu.SemaphoreType.DMA((9,)),

time: 467 us -> 472 us (1.011)
  transfers between devices with their start and end apart: 25 -> 25, of which waited for: 14 -> 12; matrix products, arithmetic and copies ran while one was open for 3% -> 4% of each run, Pallas kernels for 16% -> 16%
where the time goes in v9:
time: 472 us; the launch traced here: 470 us
  waiting for transfers between devices  158 us (33%)
  blocking collectives  129 us (27%)
  Pallas kernels  80.9 us (17%)
  starting transfers between devices  62.2 us (13%)
  local copies, waits for them, and re-layouts  21.3 us (5%)
  between operations  14.3 us (3%)
    all_to_all x4, blocking collectives, exchange(): lax.all_to_all(buf.reshape(EXP, 8, NCH * PCH), 'expert', split_axis=0, co...  129 us
    ppermute x13, waiting for transfers between devices, shift_dp(): return lax.ppermute(value, ('pipe', 'dp'), pairs)  49.4 us
    all_to_all x3, waiting for transfers between devices, exchange(): lax.all_to_all(buf.reshape(EXP, 8, NCH * PCH), 'expert', split_axis=0, co...  43.5 us
    ppermute x3, waiting for transfers between devices, per_device(): cur = lax.ppermute(result, 'pipe', moves[step])  36.7 us
    all_to_all x1, waiting for transfers between devices, per_device(): lax.all_to_all(sent.reshape(4 * EXP, 8, PCH), ('dp', 'expert'), split_axi...  27.1 us
    ppermute x13, starting transfers between devices, shift_dp(): return lax.ppermute(value, ('pipe', 'dp'), pairs)  26.9 us
    pallas_call x2, Pallas kernels, expert_pass(): pl.pallas_call(functools.partial(expert_kernel, at_dir, whole), in_specs=...  26.2 us
    all_to_all x3, starting transfers between devices, exchange(): lax.all_to_all(buf.reshape(EXP, 8, NCH * PCH), 'expert', split_axis=0, co...  17.1 us
  transfers between devices with their start and end apart: 25, of which 12 were waited for; matrix products, arithmetic and copies ran while one was open for 4% of the time, Pallas kernels for 16%

profile of v9, /device:TPU:1, one launch (start us, length us, event | category | flops | bytes accessed | tf_op | source)
XLA Modules:
  0.0 470.3 jit_solution(9417999345787251899)
XLA Ops:
  7.2 2.2 collective-permute-start
  9.4 1.5 collective-permute-start.1
  10.9 0.8 copy.29
  13.0 1.2 select_bitcast_fusion.2.old_ref.new_ref.cur_ref
  14.2 1.6 pre.4
  15.8 9.6 %all-to-all-start = ((bf16[16,8,4096]{2,1,0:T(8,128)(2,1)}), bf16[16,8,4096]{2,1,0:T(8,128)(2,1)S(1)}, u32[]{:S(2)}, u32[]{:S(2)}) async-start(bf16[16,8,4096]{2,1,0:T(8,128)(2,1)} %bitcast.5), calls=%async_computation | async-start | bytes 2097152 | tf_op jit(solution)/shard_map/all_to_all | solution.py:613
  25.5 2.3 prep.1
  27.8 1.0 copy-done
  28.8 1.0 copy-done.2
  29.8 19.0 %collective-permute-done.rest_1_ = bf16[256,3584]{1,0:T(8,128)(2,1)} collective-permute-done((bf16[256,3584]{1,0:T(8,128)(2,1)}, bf16[256,3584]{1,0:T(8,128)(2,1)}, u32[]{:S(2)}, u32[]{:S(2)}) %collective-permute-start) | collective-permute-done | bytes 1835040 | tf_op jit(solution)/shard_map/ppermute | solution.py:629
  48.8 1.2 collective-permute-done.1.rest_2_
  50.0 1.9 collective-permute-start.4
  51.9 1.9 collective-permute-start.5
  53.8 1.0 copy-done.20
  54.8 2.2 slice.52
  56.9 3.5 collective-permute-start.2
  60.4 2.2 slice.53
  62.6 3.0 collective-permute-start.3
  65.6 6.3 %hidden_near.1 = (bf16[144,3584]{1,0:T(8,128)(2,1)}, bf16[2,144,1024]{2,1,0:T(8,128)(2,1)}) custom-call(s32[1]{0:T(128)} %bitcast.1.me_ref, bf16[128,4096]{1,0:T(8,128)(2,1)} %bitcast.81, f32[2,144,1024]{2,1,0:T(8,128)} %copy-done, f32[2,144,1024]{2,1,0:T(8,128)} %copy-done.2, bf16[256,3584]{1,0:T(8,128)(2,1)} %bitcast.69, ...), custom_call_target="tpu_custom_call" | custom-call | flops 800000000 | bytes 10000000 | tf_op jit(solution)/shard_map/hidden_near/pallas_call | solution.py:272
  72.6 7.4 %collective-permute-done.2.top_hbm.rest_3_ = bf16[128,3584]{1,0:T(8,128)(2,1)S(1)} collective-permute-done((bf16[128,3584]{1,0:T(8,128)(2,1)}, bf16[128,3584]{1,0:T(8,128)(2,1)S(1)}, u32[]{:S(2)}, u32[]{:S(2)}) %collective-permute-start.2) | collective-permute-done | bytes 917536 | tf_op jit(solution)/shard_map/ppermute | solution.py:629
  80.0 1.6 collective-permute-start.10
  81.5 2.8 collective-permute-done.3.low_hbm.rest_4_
  84.4 0.9 copy-done.6
  85.3 3.5 hidden_far.1.own
  88.8 2.9 collective-permute-start.6
  91.7 4.2 collective-permute-start.8
  95.9 2.1 collective-permute-start.7
  98.0 5.9 %collective-permute-done.6.left = bf16[2,144,1024]{2,1,0:T(8,128)(2,1)S(1)} collective-permute-done((bf16[2,144,1024]{2,1,0:T(8,128)(2,1)}, bf16[2,144,1024]{2,1,0:T(8,128)(2,1)S(1)}, u32[]{:S(2)}, u32[]{:S(2)}) %collective-permute-start.6) | collective-permute-done | bytes 589856 | tf_op jit(solution)/shard_map/ppermute | solution.py:629
  103.9 2.4 slice.54
  106.4 2.2 slice.55
  108.5 8.3 %collective-permute-done.8.far = bf16[2,144,1024]{2,1,0:T(8,128)(2,1)S(1)} collective-permute-done((bf16[2,144,1024]{2,1,0:T(8,128)(2,1)}, bf16[2,144,1024]{2,1,0:T(8,128)(2,1)S(1)}, u32[]{:S(2)}, u32[]{:S(2)}) %collective-permute-start.8) | collective-permute-done | bytes 589856 | tf_op jit(solution)/shard_map/ppermute | solution.py:629
  116.8 4.8 %collective-permute-done.7.right = bf16[2,144,1024]{2,1,0:T(8,128)(2,1)S(1)} collective-permute-done((bf16[2,144,1024]{2,1,0:T(8,128)(2,1)}, bf16[2,144,1024]{2,1,0:T(8,128)(2,1)S(1)}, u32[]{:S(2)}, u32[]{:S(2)}) %collective-permute-start.7) | collective-permute-done | bytes 589856 | tf_op jit(solution)/shard_map/ppermute | solution.py:629
  121.6 0.8 copy-done.23
  122.4 6.5 %own_grads.1 = bf16[4,128,1024]{2,1,0:T(8,128)(2,1)} custom-call(s32[1]{0:T(128)} %bitcast.1.me_ref, bf16[2,144,1024]{2,1,0:T(8,128)(2,1)} %hidden_far.1.own, bf16[2,144,1024]{2,1,0:T(8,128)(2,1)} %copy-done.21, bf16[2,144,1024]{2,1,0:T(8,128)(2,1)} %copy-done.23, bf16[2,144,1024]{2,1,0:T(8,128)(2,1)} %copy-done.22, bf16[896,1024]{1,0:T(8,128)(2,1)} %bitcast.75, ...), custom_call_target="tpu_custom_call" | custom-call | flops 2120000000 | bytes 8000000 | tf_op jit(solution)/shard_map/own_grads/pallas_call | solution.py:357
  129.0 0.9 copy-done.8
  129.9 14.3 %all-to-all-start.1 = ((bf16[64,8,1024]{2,1,0:T(8,128)(2,1)}), bf16[64,8,1024]{2,1,0:T(8,128)(2,1)S(1)}, u32[]{:S(2)}, u32[]{:S(2)}) async-start(bf16[64,8,1024]{2,1,0:T(8,128)(2,1)} %bitcast.14), calls=%async_computation.1 | async-start | bytes 2097152 | tf_op jit(solution)/shard_map/all_to_all | solution.py:703
  145.7 27.1 %all-to-all-done.1 = bf16[64,8,1024]{2,1,0:T(8,128)(2,1)S(1)} async-done(((bf16[64,8,1024]{2,1,0:T(8,128)(2,1)}), bf16[64,8,1024]{2,1,0:T(8,128)(2,1)S(1)}, u32[]{:S(2)}, u32[]{:S(2)}) %all-to-all-start.1) | async-done | bytes 1048608 | tf_op jit(solution)/shard_map/all_to_all | solution.py:703
  172.8 1.3 post.4
  174.1 1.3 collective-permute-start.11
  175.4 10.3 %collective-permute-done.11.new_ref.cur_ref.old_ref = bf16[64,3584]{1,0:T(8,128)(2,1)S(1)} collective-permute-done((bf16[64,3584]{1,0:T(8,128)(2,1)}, bf16[64,3584]{1,0:T(8,128)(2,1)S(1)}, u32[]{:S(2)}, u32[]{:S(2)}) %collective-permute-start.11) | collective-permute-done | bytes 458784 | tf_op jit(solution)/shard_map/ppermute | solution.py:722
  186.4 33.4 %all_to_all.40 = bf16[16,8,4096]{2,1,0:T(8,128)(2,1)} all-to-all(bf16[16,8,4096]{2,1,0:T(8,128)(2,1)S(1)} %bitcast.55), channel_id=1, replica_groups=mesh['pipe'=4,'expert'=16,'dp'=4] {'expert'}, dimensions={0} | all-to-all | bytes 2097152 | tf_op jit(solution)/shard_map/all_to_all | solution.py:613
  220.6 11.4 %front_pass.1 = (f32[4,144,896]{2,1,0:T(8,128)}, bf16[144,1024]{1,0:T(8,128)(2,1)}) custom-call(s32[1]{0:T(128)} %bitcast.1.me_ref, bf16[128,4096]{1,0:T(8,128)(2,1)} %bitcast.79, f32[2,144,1024]{2,1,0:T(8,128)} %copy-done, f32[2,144,1024]{2,1,0:T(8,128)} %copy-done.2, bf16[256,3584]{1,0:T(8,128)(2,1)} %bitcast.70, ...), custom_call_target="tpu_custom_call" | custom-call | flops 2100000000 | bytes 20000000 | tf_op jit(solution)/shard_map/front_pass/pallas_call | solution.py:484
  232.0 6.4 %back_pass.1 = bf16[128,4096]{1,0:T(8,128)(2,1)} custom-call(bf16[144,1024]{1,0:T(8,128)(2,1)} %get-tuple-element.47.du_hbm, f32[4,144,896]{2,1,0:T(8,128)} %get-tuple-element.48.part_hbm, bf16[3584,1024]{1,0:T(8,128)(2,1)} %all-gather.7.cloned.1.call-done.wu_hbm.rest_10_.rest_6_), custom_call_target="tpu_custom_call" | custom-call | flops 1060000000 | bytes 10000000 | tf_op jit(solution)/shard_map/back_pass/pallas_call | solution.py:523
  238.4 31.4 %all_to_all.41 = bf16[16,8,4096]{2,1,0:T(8,128)(2,1)S(1)} all-to-all(bf16[16,8,4096]{2,1,0:T(8,128)(2,1)} %bitcast.82), channel_id=1, replica_groups=mesh['pipe'=4,'expert'=16,'dp'=4] {'expert'}, dimensions={0} | all-to-all | bytes 2097152 | tf_op jit(solution)/shard_map/all_to_all | solution.py:613
  271.3 1.6 pre.6
  272.9 3.7 all-to-all-start.4
  277.5 26.5 %all-to-all-done.4 = bf16[16,8,4096]{2,1,0:T(8,128)(2,1)S(1)} async-done(((bf16[16,8,4096]{2,1,0:T(8,128)(2,1)}), bf16[16,8,4096]{2,1,0:T(8,128)(2,1)S(1)}, u32[]{:S(2)}, u32[]{:S(2)}) %all-to-all-start.4) | async-done | bytes 1048608 | tf_op jit(solution)/shard_map/all_to_all | solution.py:613
  303.9 1.2 copy-done.13
  305.1 13.0 %expert_pass.2 = bf16[128,4096]{1,0:T(8,128)(2,1)S(1)} custom-call(s32[1]{0:T(128)} %bitcast.1.me_ref, bf16[128,4096]{1,0:T(8,128)(2,1)S(1)} %bitcast.53, f32[2,144,1024]{2,1,0:T(8,128)} %copy-done, f32[2,144,1024]{2,1,0:T(8,128)} %copy-done.2, bf16[256,3584]{1,0:T(8,128)(2,1)} %bitcast.71, bf16[256,3584]{1,0:T(8,128)(2,1)} %collective-permute-done.rest_1_, ...), custom_call_target="tpu_custom_call" | custom-call | flops 3200000000 | bytes 28000000 | tf_op jit(solution)/shard_map/expert_pass/pallas_call | solution.py:424
  318.1 31.9 %all_to_all.42 = bf16[16,8,4096]{2,1,0:T(8,128)(2,1)S(1)} all-to-all(bf16[16,8,4096]{2,1,0:T(8,128)(2,1)S(1)} %bitcast.54), channel_id=1, replica_groups=mesh['pipe'=4,'expert'=16,'dp'=4] {'expert'}, dimensions={0} | all-to-all | bytes 2097152 | tf_op jit(solution)/shard_map/all_to_all | solution.py:613
  350.5 1.3 collective-permute-start.15
  351.8 26.4 %collective-permute-done.15.new_ref.cur_ref = bf16[64,3584]{1,0:T(8,128)(2,1)S(1)} collective-permute-done((bf16[64,3584]{1,0:T(8,128)(2,1)S(1)}, bf16[64,3584]{1,0:T(8,128)(2,1)S(1)}, u32[]{:S(2)}, u32[]{:S(2)}) %collective-permute-start.15) | collective-permute-done | bytes 458784 | tf_op jit(solution)/shard_map/ppermute | solution.py:722
  378.8 32.6 %all_to_all.43 = bf16[16,8,4096]{2,1,0:T(8,128)(2,1)} all-to-all(bf16[16,8,4096]{2,1,0:T(8,128)(2,1)S(1)} %bitcast.56), channel_id=1, replica_groups=mesh['pipe'=4,'expert'=16,'dp'=4] {'expert'}, dimensions={0} | all-to-all | bytes 2097152 | tf_op jit(solution)/shard_map/all_to_all | solution.py:613
  411.6 1.2 copy-done.3
  412.8 13.2 %expert_pass.3 = bf16[128,4096]{1,0:T(8,128)(2,1)} custom-call(s32[1]{0:T(128)} %bitcast.1.me_ref, bf16[128,4096]{1,0:T(8,128)(2,1)S(1)} %bitcast.52, f32[2,144,1024]{2,1,0:T(8,128)S(1)} %copy-done.1, f32[2,144,1024]{2,1,0:T(8,128)} %copy-done.2, bf16[256,3584]{1,0:T(8,128)(2,1)} %bitcast.72, bf16[256,3584]{1,0:T(8,128)(2,1)} %collective-permute-done.rest_1_, ...), custom_call_target="tpu_custom_call" | custom-call | flops 3200000000 | bytes 28000000 | tf_op jit(solution)/shard_map/expert_pass/pallas_call | solution.py:424
  426.0 3.8 all-to-all-start.7
  429.9 1.1 dynamic-slice_bitcast_fusion
  431.1 0.9 copy.33.h_hbm
  432.0 0.9 copy.32.h_ref
  432.9 5.8 %down_first.1.sum_hbm = bf16[256,3584]{1,0:T(8,128)(2,1)} custom-call(bf16[256,576]{1,0:T(8,128)(2,1)} %copy.32.h_ref, bf16[512,4096]{1,0:T(8,128)(2,1)} %all-gather.13.cloned.1.call-done.buf_ref), custom_call_target="tpu_custom_call" | custom-call | flops 1060000000 | bytes 8000000 | tf_op jit(solution)/shard_map/down_first/pallas_call | solution.py:559
  438.8 1.1 select_bitcast_fusion
  439.9 17.0 %all-to-all-done.7 = bf16[16,8,4096]{2,1,0:T(8,128)(2,1)S(1)} async-done(((bf16[16,8,4096]{2,1,0:T(8,128)(2,1)}), bf16[16,8,4096]{2,1,0:T(8,128)(2,1)S(1)}, u32[]{:S(2)}, u32[]{:S(2)}) %all-to-all-start.7) | async-done | bytes 1048608 | tf_op jit(solution)/shard_map/all_to_all | solution.py:613
  457.4 1.1 maximum_select_fusion
  458.5 5.2 %down_last.1 = bf16[256,3584]{1,0:T(8,128)(2,1)} custom-call(bf16[256,576]{1,0:T(8,128)(2,1)} %copy.33.h_hbm, bf16[512,4096]{1,0:T(8,128)(2,1)} %all-gather.11.cloned.1.call-done.buf_hbm, bf16[256,3584]{1,0:T(8,128)(2,1)} %down_first.1.sum_hbm), custom_call_target="tpu_custom_call" | custom-call | flops 1060000000 | bytes 10000000 | tf_op jit(solution)/shard_map/down_last/pallas_call | solution.py:592
  (85 shorter events, 9.0 us)
Async XLA Ops:
  7.2 41.7 %collective-permute-start = (bf16[256,3584]{1,0:T(8,128)(2,1)}, bf16[256,3584]{1,0:T(8,128)(2,1)}, u32[]{:S(2)}, u32[]{:S(2)}) collective-permute-start(bf16[256,3584]{1,0:T(8,128)(2,1)} %bitcast.67), channel_id=1, source_target_pairs={{0,1},{1,2},{2,3},{3,0},{64,65},{65,66},{66,67},{67,64},{128,129},... | collective-permute-start | bytes 5505032 | tf_op jit(solution)/shard_map/ppermute | solution.py:629
  9.4 40.6 %collective-permute-start.1 = (bf16[256,3584]{1,0:T(8,128)(2,1)}, bf16[256,3584]{1,0:T(8,128)(2,1)}, u32[]{:S(2)}, u32[]{:S(2)}) collective-permute-start(bf16[256,3584]{1,0:T(8,128)(2,1)} %bitcast.68), channel_id=1, source_target_pairs={{0,3},{1,0},{2,1},{3,2},{64,67},{65,64},{66,65},{67,66},{128,131},... | collective-permute-start | bytes 5505032 | tf_op jit(solution)/shard_map/ppermute | solution.py:629
  14.2 11.3 %copy-start.18 = (bf16[2,1,1,1,144,1024]{5,4,3,2,1,0:T(8,128)(2,1)S(1)}, bf16[2,1,1,1,144,1024]{5,4,3,2,1,0:T(8,128)(2,1)}, u32[]{:S(2)}) copy-start(bf16[2,1,1,1,144,1024]{5,4,3,2,1,0:T(8,128)(2,1)} %param.11) | copy-start | bytes 1769476
  14.2 11.3 %copy-start.19 = (bf16[2,1,1,1,144,1024]{5,4,3,2,1,0:T(8,128)(2,1)S(1)}, bf16[2,1,1,1,144,1024]{5,4,3,2,1,0:T(8,128)(2,1)}, u32[]{:S(2)}) copy-start(bf16[2,1,1,1,144,1024]{5,4,3,2,1,0:T(8,128)(2,1)} %param.12) | copy-start | bytes 1769476
  15.8 38.0 %all-to-all-start = ((bf16[16,8,4096]{2,1,0:T(8,128)(2,1)}), bf16[16,8,4096]{2,1,0:T(8,128)(2,1)S(1)}, u32[]{:S(2)}, u32[]{:S(2)}) async-start(bf16[16,8,4096]{2,1,0:T(8,128)(2,1)} %bitcast.5), calls=%async_computation | async-start | bytes 2097152 | tf_op jit(solution)/shard_map/all_to_all | solution.py:613
  25.4 206.6 %all-gather.7.cloned.1.call-start = ((), (), s32[]{:S(2)}) async-start(), calls=%async_computation.8 | async-start | bytes 9175040 | tf_op jit(solution)/shard_map/all_gather | solution.py:648
  27.8 1.0 copy-start
  28.8 1.0 copy-start.2
  50.0 38.9 %collective-permute-start.4 = (bf16[896,1024]{1,0:T(8,128)(2,1)}, bf16[896,1024]{1,0:T(8,128)(2,1)}, u32[]{:S(2)}, u32[]{:S(2)}) collective-permute-start(bf16[896,1024]{1,0:T(8,128)(2,1)} %bitcast.73), channel_id=1, source_target_pairs={{64,65},{65,66},{66,67},{67,64},{128,129},{129,130},{130,131},{131... | collective-permute-start | bytes 5505032 | tf_op jit(solution)/shard_map/ppermute | solution.py:629
  51.9 37.0 %collective-permute-start.5 = (bf16[896,1024]{1,0:T(8,128)(2,1)}, bf16[896,1024]{1,0:T(8,128)(2,1)}, u32[]{:S(2)}, u32[]{:S(2)}) collective-permute-start(bf16[896,1024]{1,0:T(8,128)(2,1)} %bitcast.74), channel_id=1, source_target_pairs={{64,67},{65,64},{66,65},{67,66},{128,131},{129,128},{130,129},{131... | collective-permute-start | bytes 5505032 | tf_op jit(solution)/shard_map/ppermute | solution.py:629
  53.8 1.0 copy-start.20
  56.9 23.0 %collective-permute-start.2 = (bf16[128,3584]{1,0:T(8,128)(2,1)}, bf16[128,3584]{1,0:T(8,128)(2,1)S(1)}, u32[]{:S(2)}, u32[]{:S(2)}) collective-permute-start(bf16[128,3584]{1,0:T(8,128)(2,1)} %slice.52), channel_id=1, source_target_pairs={{0,1},{1,2},{2,3},{3,0},{192,193},{193,194},{194,195},{195,192},{4... | collective-permute-start | bytes 2752520 | tf_op jit(solution)/shard_map/ppermute | solution.py:629
  62.6 21.8 %collective-permute-start.3 = (bf16[128,3584]{1,0:T(8,128)(2,1)}, bf16[128,3584]{1,0:T(8,128)(2,1)S(1)}, u32[]{:S(2)}, u32[]{:S(2)}) collective-permute-start(bf16[128,3584]{1,0:T(8,128)(2,1)} %slice.53), channel_id=1, source_target_pairs={{0,3},{1,0},{2,1},{3,2},{192,195},{193,192},{194,193},{195,194},{4... | collective-permute-start | bytes 2752520 | tf_op jit(solution)/shard_map/ppermute | solution.py:629
  71.9 57.1 %collective-permute-start.9 = (bf16[128,3584]{1,0:T(8,128)(2,1)}, bf16[128,3584]{1,0:T(8,128)(2,1)S(1)}, u32[]{:S(2)}, u32[]{:S(2)}) collective-permute-start(bf16[128,3584]{1,0:T(8,128)(2,1)} %slice.52), channel_id=1, source_target_pairs={{64,65},{65,66},{66,67},{67,64},{128,129},{129,130},{130,131},{131... | collective-permute-start | bytes 2752520 | tf_op jit(solution)/shard_map/ppermute | solution.py:629
  80.0 4.4 copy-start.4
  80.0 49.0 %collective-permute-start.10 = (bf16[128,3584]{1,0:T(8,128)(2,1)}, bf16[128,3584]{1,0:T(8,128)(2,1)}, u32[]{:S(2)}, u32[]{:S(2)}) collective-permute-start(bf16[128,3584]{1,0:T(8,128)(2,1)} %slice.53), channel_id=1, source_target_pairs={{64,67},{65,64},{66,65},{67,66},{128,131},{129,128},{130,129},{131... | collective-permute-start | bytes 2752520 | tf_op jit(solution)/shard_map/ppermute | solution.py:629
  84.4 0.9 copy-start.6
  88.8 15.1 %collective-permute-start.6 = (bf16[2,144,1024]{2,1,0:T(8,128)(2,1)}, bf16[2,144,1024]{2,1,0:T(8,128)(2,1)S(1)}, u32[]{:S(2)}, u32[]{:S(2)}) collective-permute-start(bf16[2,144,1024]{2,1,0:T(8,128)(2,1)} %hidden_far.1.own), channel_id=1, source_target_pairs={{0,1},{1,2},{2,3},{3,0},{192,193},{193,194},{194,195},{195,192},{4... | collective-permute-start | bytes 1769480 | tf_op jit(solution)/shard_map/ppermute | solution.py:629
  91.7 25.1 %collective-permute-start.8 = (bf16[2,144,1024]{2,1,0:T(8,128)(2,1)}, bf16[2,144,1024]{2,1,0:T(8,128)(2,1)S(1)}, u32[]{:S(2)}, u32[]{:S(2)}) collective-permute-start(bf16[2,144,1024]{2,1,0:T(8,128)(2,1)} %hidden_far.1.own), channel_id=1, source_target_pairs={{0,2},{1,3},{2,0},{3,1},{192,194},{193,195},{194,192},{195,193},{4... | collective-permute-start | bytes 1769480 | tf_op jit(solution)/shard_map/ppermute | solution.py:629
  95.9 25.7 %collective-permute-start.7 = (bf16[2,144,1024]{2,1,0:T(8,128)(2,1)}, bf16[2,144,1024]{2,1,0:T(8,128)(2,1)S(1)}, u32[]{:S(2)}, u32[]{:S(2)}) collective-permute-start(bf16[2,144,1024]{2,1,0:T(8,128)(2,1)} %hidden_far.1.own), channel_id=1, source_target_pairs={{0,3},{1,0},{2,1},{3,2},{192,195},{193,192},{194,193},{195,194},{4... | collective-permute-start | bytes 1769480 | tf_op jit(solution)/shard_map/ppermute | solution.py:629
  103.9 4.6 copy-start.21
  116.8 4.8 %copy-start.22 = (bf16[2,144,1024]{2,1,0:T(8,128)(2,1)}, bf16[2,144,1024]{2,1,0:T(8,128)(2,1)S(1)}, u32[]{:S(2)}) copy-start(bf16[2,144,1024]{2,1,0:T(8,128)(2,1)S(1)} %collective-permute-done.8.far) | copy-start | bytes 1769476
  121.6 0.8 copy-start.23
  128.9 0.9 copy-start.8
  129.9 42.9 %all-to-all-start.1 = ((bf16[64,8,1024]{2,1,0:T(8,128)(2,1)}), bf16[64,8,1024]{2,1,0:T(8,128)(2,1)S(1)}, u32[]{:S(2)}, u32[]{:S(2)}) async-start(bf16[64,8,1024]{2,1,0:T(8,128)(2,1)} %bitcast.14), calls=%async_computation.1 | async-start | bytes 2097152 | tf_op jit(solution)/shard_map/all_to_all | solution.py:703
  144.2 267.3 %all-gather.9.cloned.1.call-start = ((), (), s32[]{:S(2)}) async-start(), calls=%async_computation.9 | async-start | bytes 9175040 | tf_op jit(solution)/shard_map/all_gather | solution.py:648
  144.3 42.1 %collective-permute-start.12 = (bf16[448,1024]{1,0:T(8,128)(2,1)}, bf16[448,1024]{1,0:T(8,128)(2,1)S(1)}, u32[]{:S(2)}, u32[]{:S(2)}) collective-permute-start(bf16[448,1024]{1,0:T(8,128)(2,1)} %slice.54), channel_id=1, source_target_pairs={{64,65},{65,66},{66,67},{67,64},{128,129},{129,130},{130,131},{131... | collective-permute-start | bytes 2752520 | tf_op jit(solution)/shard_map/ppermute | solution.py:629
  145.0 41.4 %collective-permute-start.13 = (bf16[448,1024]{1,0:T(8,128)(2,1)}, bf16[448,1024]{1,0:T(8,128)(2,1)S(1)}, u32[]{:S(2)}, u32[]{:S(2)}) collective-permute-start(bf16[448,1024]{1,0:T(8,128)(2,1)} %slice.55), channel_id=1, source_target_pairs={{64,67},{65,64},{66,65},{67,66},{128,131},{129,128},{130,129},{131... | collective-permute-start | bytes 2752520 | tf_op jit(solution)/shard_map/ppermute | solution.py:629
  174.1 11.6 %collective-permute-start.11 = (bf16[64,3584]{1,0:T(8,128)(2,1)}, bf16[64,3584]{1,0:T(8,128)(2,1)S(1)}, u32[]{:S(2)}, u32[]{:S(2)}) collective-permute-start(bf16[64,3584]{1,0:T(8,128)(2,1)} %post.4), channel_id=1, source_target_pairs={{0,64},{192,128},{1,65},{193,129},{2,66},{194,130},{3,67},{195,131... | collective-permute-start | bytes 1376264 | tf_op jit(solution)/shard_map/ppermute | solution.py:722
  186.4 33.5 %copy-start.10 = (bf16[448,1024]{1,0:T(8,128)(2,1)}, bf16[448,1024]{1,0:T(8,128)(2,1)S(1)}, u32[]{:S(2)}) copy-start(bf16[448,1024]{1,0:T(8,128)(2,1)S(1)} %collective-permute-done.12.rest_8_) | copy-start | bytes 2752516
  186.4 33.5 %copy-start.12 = (bf16[448,1024]{1,0:T(8,128)(2,1)}, bf16[448,1024]{1,0:T(8,128)(2,1)S(1)}, u32[]{:S(2)}) copy-start(bf16[448,1024]{1,0:T(8,128)(2,1)S(1)} %collective-permute-done.13.rest_9_) | copy-start | bytes 2752516
  219.8 210.0 %all-gather.15.cloned.1.call-start = ((), (), s32[]{:S(2)}) async-start(), calls=%async_computation.12 | async-start | bytes 2949120 | tf_op jit(solution)/shard_map/all_gather | solution.py:711
  270.4 2.6 copy-start.14
  270.4 0.9 collective-permute-start.14
  272.9 31.0 %copy-start.9 = (bf16[128,3584]{1,0:T(8,128)(2,1)S(1)}, bf16[128,3584]{1,0:T(8,128)(2,1)}, u32[]{:S(2)}) copy-start(bf16[128,3584]{1,0:T(8,128)(2,1)} %copy-done.8) | copy-start | bytes 2752516
  272.9 31.0 %copy-start.11 = (bf16[448,1024]{1,0:T(8,128)(2,1)S(1)}, bf16[448,1024]{1,0:T(8,128)(2,1)}, u32[]{:S(2)}) copy-start(bf16[448,1024]{1,0:T(8,128)(2,1)} %copy-done.10) | copy-start | bytes 2752516
  272.9 31.0 %all-to-all-start.4 = ((bf16[16,8,4096]{2,1,0:T(8,128)(2,1)}), bf16[16,8,4096]{2,1,0:T(8,128)(2,1)S(1)}, u32[]{:S(2)}, u32[]{:S(2)}) async-start(bf16[16,8,4096]{2,1,0:T(8,128)(2,1)} %bitcast.25), calls=%async_computation.4 | async-start | bytes 2097152 | tf_op jit(solution)/shard_map/all_to_all | solution.py:613
  276.6 156.3 %all-gather.13.cloned.1.call-start = ((), (), s32[]{:S(2)}) async-start(), calls=%async_computation.11 | async-start | bytes 5242880 | tf_op jit(solution)/shard_map/all_gather | solution.py:648
  277.2 181.3 %all-gather.11.cloned.1.call-start = ((), (), s32[]{:S(2)}) async-start(), calls=%async_computation.10 | async-start | bytes 5242880 | tf_op jit(solution)/shard_map/all_gather | solution.py:648
  303.9 1.2 copy-start.13
  350.4 1.3 copy-start.16
  350.5 27.7 %collective-permute-start.15 = (bf16[64,3584]{1,0:T(8,128)(2,1)S(1)}, bf16[64,3584]{1,0:T(8,128)(2,1)S(1)}, u32[]{:S(2)}, u32[]{:S(2)}) collective-permute-start(bf16[64,3584]{1,0:T(8,128)(2,1)S(1)} %post.6), channel_id=1, source_target_pairs={{128,192},{64,0},{129,193},{65,1},{130,194},{66,2},{131,195},{67,3... | collective-permute-start | bytes 1376264 | tf_op jit(solution)/shard_map/ppermute | solution.py:722
  378.8 32.7 %copy-start.1 = (f32[2,144,1024]{2,1,0:T(8,128)S(1)}, f32[2,144,1024]{2,1,0:T(8,128)}, u32[]{:S(2)}) copy-start(f32[2,144,1024]{2,1,0:T(8,128)} %copy-done) | copy-start | bytes 3538948
  378.8 32.7 %copy-start.5 = (bf16[128,3584]{1,0:T(8,128)(2,1)S(1)}, bf16[128,3584]{1,0:T(8,128)(2,1)}, u32[]{:S(2)}) copy-start(bf16[128,3584]{1,0:T(8,128)(2,1)} %copy-done.4) | copy-start | bytes 2752516
  378.8 32.7 %copy-start.7 = (bf16[128,3584]{1,0:T(8,128)(2,1)S(1)}, bf16[128,3584]{1,0:T(8,128)(2,1)}, u32[]{:S(2)}) copy-start(bf16[128,3584]{1,0:T(8,128)(2,1)} %copy-done.6) | copy-start | bytes 2752516
  411.5 1.2 copy-start.3
  426.0 30.9 %all-to-all-start.7 = ((bf16[16,8,4096]{2,1,0:T(8,128)(2,1)}), bf16[16,8,4096]{2,1,0:T(8,128)(2,1)S(1)}, u32[]{:S(2)}, u32[]{:S(2)}) async-start(bf16[16,8,4096]{2,1,0:T(8,128)(2,1)} %bitcast.32), calls=%async_computation.7 | async-start | bytes 2097152 | tf_op jit(solution)/shard_map/all_to_all | solution.py:613
  432.9 5.9 %copy-start.15 = (bf16[64,3584]{1,0:T(8,128)(2,1)S(1)}, bf16[64,3584]{1,0:T(8,128)(2,1)}, u32[]{:S(2)}) copy-start(bf16[64,3584]{1,0:T(8,128)(2,1)} %copy-done.14) | copy-start | bytes 1376260
  438.8 18.6 %copy-start.17 = (bf16[64,3584]{1,0:T(8,128)(2,1)S(1)}, bf16[64,3584]{1,0:T(8,128)(2,1)}, u32[]{:S(2)}) copy-start(bf16[64,3584]{1,0:T(8,128)(2,1)} %copy-done.16) | copy-start | bytes 1376260
Sparse Core Ops, SparseCore 0:
  129.1 91.4 all-gather.6
  222.4 81.9 all-gather.8
  306.2 36.4 all-gather.14
  344.3 50.9 all-gather.12
  411.6 44.6 all-gather.10
